TPU v7x, 32 devices: a whole 2x2x4 slice. The times are simulated.
32 devices in a mesh: region: 16 (over z, x, core), slab: 2 (over y).
Axes of the slice: x: 2, y: 2, z: 4, core: 2. Of those that a mesh axis runs over, the one named last changes fastest.
Arguments:
- features: bfloat16 [8192, 96], P(('region', 'slab')), may hold values from -6 to 6
- neighbours: int32 [8192, 27], P(('region', 'slab')), may hold values from 0 to 2304, as said below
- down_map: int32 [2048, 8], P(('region', 'slab')), may hold values from 0 to 256, as said below
- w_conv: bfloat16 [2592, 96], replicated, may hold values from -0.125 to 0.125
- w_down: bfloat16 [768, 128], replicated, may hold values from -0.21875 to 0.21875
- coarse_grad: bfloat16 [2048, 128], P(('region', 'slab')), may hold values from -6 to 6
Outputs:
- coarse: bfloat16 [2048, 128], P(('region', 'slab'))
- grad_input: float32 [8192, 96], P(('region', 'slab'))
- conv_weight_grad: float32 [2592, 96], replicated
- down_weight_grad: float32 [768, 128], replicated
Inputs may be any that keep to these rules, and one draw needn't show every extreme that they name: `neighbours`: device d is the device at region index d // (slab axis size) and slab index d mod (slab axis size). Each device's live voxels are its first slots; dead slots list 9 * 256 everywhere and are named by no one. An entry k * 256 + j names slot j of the device whose region index differs by k // 3 - 1 and slab index by k mod 3 - 1; that device exists. A live voxel names itself at offset 13 (k = 4), and otherwise a live voxel or 2304. When k is not 4, j is below 64, the naming voxel lies in its device's first 64 slots, and some voxel names slot 63 of another device in every draw. 9 * 256 means no source. `down_map`: every live voxel of a device is named exactly once, by a coarse voxel slot of that device, by its slot on the device; all other entries are 256.
All inputs are finite; a program needn't handle non-finite values.
Results may differ from a plain program's by a relative error of at most 0.005.
Values may be sent and summed in bfloat16 or wider, within the bound.
No kernel may reach another device: no remote copies, remote signals or barrier semaphores. Data moves between devices by JAX's collectives and lax.ppermute only.
A program may use at most 64 MiB of HBM per device.

v0:
```python
import functools

import jax
import jax.numpy as jnp
from jax import lax
from jax.experimental import pallas as pl
from jax.experimental.pallas import tpu as pltpu
from jax.sharding import Mesh, PartitionSpec as P

SPLIT = ("chips", "core", "slab")
RING = ("chips", "core")
PEERS = ("chips", "slab")
RIM = 64
LANES = 128
TILE = 16
F32 = jnp.float32
BF16 = jnp.bfloat16
NN = (((1,), (0,)), ((), ()))
NT = (((1,), (1,)), ((), ()))
VMEM_BYTES = 40 * 2**20


def mm(a, b, dims=NN):
    return lax.dot_general(a, b, dims, preferred_element_type=F32)


def table_lanes(neighbours, voxels, slabs):
    code = neighbours // voxels
    slot = neighbours - code * voxels
    row = code // 3
    col = code - row * 3
    if slabs == 2:
        rims = 2
        place = jnp.where(col == 1, 0, 1)
        beside = 0
    else:
        rims = 3
        place = col
        beside = col // 2
    rim = jnp.where(row == 1, 2 * rims + beside, (row // 2) * rims + place)
    lane = jnp.where(code == 4, slot, voxels + rim * RIM + slot)
    return jnp.where(code > 8, -1, lane)


def payload_tiles(channels, conv_columns, taps):
    tiles = []
    for column in range(0, conv_columns, LANES):
        for row in range(0, channels, TILE):
            tiles.append((0, row, column, min(LANES, conv_columns - column)))
    for row in range(0, taps * channels, TILE):
        tiles.append((1, row, 0, LANES))
    return tiles


def local_kernel(slabs, core_ref, f_ref, near_ref, down_ref, w_ref, wd_ref, cgrad_ref, *refs):
    halo_refs = refs[:3] if slabs == 2 else refs[:4]
    coarse_ref, base_ref, low_ref, high_ref, side_ref, keep_ref, send_ref = refs[
        len(halo_refs) : len(halo_refs) + 7
    ]
    rt, drt, drt_far, hot, far, w_back, conv_w, down_w = refs[len(halo_refs) + 7 :]
    channels, voxels = f_ref.shape
    offsets = near_ref.shape[0]
    taps, coarse_count = down_ref.shape
    group = low_ref.shape[1]
    rim_lanes = 2 * group + side_ref.shape[1]
    far_rows = far.shape[0]

    table_t = f_ref[...]
    halo = [h[...] for h in halo_refs]
    if far_rows > rim_lanes:
        halo.append(jnp.zeros((channels, far_rows - rim_lanes), BF16))
    halo_t = jnp.concatenate(halo, axis=1)
    lanes = table_lanes(near_ref[...], voxels, slabs)
    near_iota = lax.broadcasted_iota(jnp.int32, (voxels, voxels), 0)
    far_iota = lax.broadcasted_iota(jnp.int32, (far_rows, LANES), 0) + voxels

    for o in range(offsets):
        lane = lanes[o : o + 1, :]
        near = jnp.where(near_iota == lane, 1.0, 0.0).astype(BF16)
        away = jnp.where(far_iota == lane[:, :LANES], 1.0, 0.0).astype(BF16)
        hot[:, o * voxels : (o + 1) * voxels] = near
        far[:, o * LANES : (o + 1) * LANES] = away
        own = mm(table_t, near)
        first = own[:, :LANES] + mm(halo_t, away)
        rt[o * channels : (o + 1) * channels, :LANES] = first.astype(BF16)
        rt[o * channels : (o + 1) * channels, LANES:] = own[:, LANES:].astype(BF16)

    out_t = mm(w_ref[...], rt[...])
    sig = 1.0 / (1.0 + jnp.exp(-out_t))
    hidden_t = (table_t.astype(F32) + out_t * sig).astype(BF16)

    cgrad = cgrad_ref[...]
    cgrad_t = cgrad.astype(F32).T.astype(BF16)
    down = down_ref[...].astype(F32).T
    lane_iota = lax.broadcasted_iota(jnp.int32, (coarse_count, voxels), 1).astype(F32)
    coarse = jnp.zeros(cgrad.shape, F32)
    hgrad_t = jnp.zeros((channels, voxels), F32)
    for t in range(taps):
        pick = jnp.where(lane_iota == down[:, t : t + 1], 1.0, 0.0).astype(BF16)
        wd = wd_ref[t * channels : (t + 1) * channels, :]
        coarse += mm(mm(pick, hidden_t, NT).astype(BF16), wd)
        picked_t = mm(hidden_t, pick, NT).astype(BF16)
        down_w[t * channels : (t + 1) * channels, :] = mm(picked_t, cgrad).astype(BF16)
        hgrad_t += mm(wd, mm(cgrad_t, pick).astype(BF16))
    coarse_ref[...] = coarse.astype(BF16)

    grad_t = (hgrad_t * sig * (1.0 + out_t * (1.0 - sig))).astype(BF16)
    conv_columns = offsets * channels
    conv_w[:, :conv_columns] = mm(grad_t, rt[...], NT).astype(BF16)
    if conv_w.shape[1] > conv_columns:
        slack = conv_w.shape[1] - conv_columns
        conv_w[:, conv_columns:] = jnp.zeros((channels, slack), BF16)

    w_back[:, :channels] = w_ref[...].astype(F32).T.astype(BF16)
    w_back[:, channels:] = jnp.zeros((conv_columns, LANES - channels), BF16)
    grad_pad = jnp.concatenate([grad_t, jnp.zeros((LANES - channels, voxels), BF16)], axis=0)
    for o in range(offsets):
        spread = mm(w_back[o * channels : (o + 1) * channels, :], grad_pad).astype(BF16)
        drt[:, o * voxels : (o + 1) * voxels] = spread
        drt_far[:, o * LANES : (o + 1) * LANES] = spread[:, :LANES]
    base_ref[...] = hgrad_t + mm(drt[...], hot[...], NT)
    back_t = mm(drt_far[...], far[...], NT).astype(BF16)
    low_ref[...] = back_t[:, :group]
    high_ref[...] = back_t[:, group : 2 * group]
    side_ref[...] = back_t[:, 2 * group : rim_lanes]

    tiles = payload_tiles(channels, conv_columns, taps)
    half = keep_ref.shape[0]
    for core in range(2):

        @pl.when(core_ref[0] == core)
        def _(core=core):
            for i in range(2 * half):
                ref = keep_ref if i // half == core else send_ref
                if i < len(tiles):
                    kind, row, column, _ = tiles[i]
                    source = down_w if kind else conv_w
                    ref[i % half] = source[row : row + TILE, column : column + LANES]
                else:
                    ref[i % half] = jnp.zeros((TILE, LANES), BF16)


def unpack_kernel(taps, core_ref, mine_ref, other_ref, conv_ref, down_ref):
    channels, conv_columns = conv_ref.shape
    half = mine_ref.shape[0]
    for core in range(2):

        @pl.when(core_ref[0] == core)
        def _(core=core):
            for i, tile in enumerate(payload_tiles(channels, conv_columns, taps)):
                kind, row, column, columns = tile
                source = mine_ref if i // half == core else other_ref
                value = source[i % half].astype(F32)
                target = down_ref if kind else conv_ref
                target[row : row + TILE, column : column + columns] = value[:, :columns]


def shifts(count, step):
    return [(i, i + step) for i in range(count) if 0 <= i + step < count]


def on_device(features, neighbours, down_map, w_conv, w_down, coarse_grad):
    regions = lax.axis_size("chips") * lax.axis_size("core")
    slabs = lax.axis_size("slab")
    peers = lax.axis_size("chips") * slabs
    voxels, channels = features.shape
    offsets, taps = neighbours.shape[1], down_map.shape[1]
    conv_columns = offsets * channels
    core = lax.axis_index("core").astype(jnp.int32).reshape(1)
    swap = [(0, 1), (1, 0)]
    up, down = shifts(regions, 1), shifts(regions, -1)

    features_t = features.T
    rim = features_t[:, :RIM]
    if slabs == 2:
        side = [lax.ppermute(rim, "slab", swap)]
        row = [rim, side[0]]
    else:
        side = [
            lax.ppermute(rim, "slab", shifts(slabs, 1)),
            lax.ppermute(rim, "slab", shifts(slabs, -1)),
        ]
        row = [side[0], rim, side[1]]
    row = jnp.concatenate(row, axis=1)
    halos = [lax.ppermute(row, RING, up), lax.ppermute(row, RING, down), *side]

    tiles = len(payload_tiles(channels, conv_columns, taps))
    piece = -(-tiles // (2 * peers))
    half = piece * peers
    group, beside = row.shape[1], len(side) * RIM
    far_rows = -(-(2 * group + beside) // LANES) * LANES
    smem = pl.BlockSpec(memory_space=pltpu.SMEM)
    vmem = pl.BlockSpec(memory_space=pltpu.VMEM)
    coarse, base, low, high, own_side, keep, send = pl.pallas_call(
        functools.partial(local_kernel, slabs),
        out_shape=(
            jax.ShapeDtypeStruct(coarse_grad.shape, BF16),
            jax.ShapeDtypeStruct((channels, voxels), F32),
            jax.ShapeDtypeStruct((channels, group), BF16),
            jax.ShapeDtypeStruct((channels, group), BF16),
            jax.ShapeDtypeStruct((channels, beside), BF16),
            jax.ShapeDtypeStruct((half, TILE, LANES), BF16),
            jax.ShapeDtypeStruct((half, TILE, LANES), BF16),
        ),
        in_specs=[smem] + [vmem] * (6 + len(halos)),
        scratch_shapes=[
            pltpu.VMEM((conv_columns, voxels), BF16),
            pltpu.VMEM((channels, offsets * voxels), BF16),
            pltpu.VMEM((channels, offsets * LANES), BF16),
            pltpu.VMEM((voxels, offsets * voxels), BF16),
            pltpu.VMEM((far_rows, offsets * LANES), BF16),
            pltpu.VMEM((conv_columns, LANES), BF16),
            pltpu.VMEM((channels, -(-conv_columns // LANES) * LANES), BF16),
            pltpu.VMEM((taps * channels, LANES), BF16),
        ],
        compiler_params=pltpu.CompilerParams(vmem_limit_bytes=VMEM_BYTES),
        name="local",
    )(core, features_t, neighbours.T, down_map.T, w_conv.T, w_down, coarse_grad, *halos)

    got = lax.ppermute(send, "core", swap)
    pair = (keep.astype(F32) + got.astype(F32)).astype(BF16)
    parts = lax.all_to_all(pair.reshape(peers, piece, TILE, LANES), PEERS, 0, 0)
    total = jnp.sum(parts.astype(F32), axis=0).astype(BF16)
    spread = jnp.broadcast_to(total[None], parts.shape)
    mine = lax.all_to_all(spread, PEERS, 0, 0).reshape(half, TILE, LANES)
    other = lax.ppermute(mine, "core", swap)
    conv_wgrad_t, down_wgrad = pl.pallas_call(
        functools.partial(unpack_kernel, taps),
        out_shape=(
            jax.ShapeDtypeStruct((channels, conv_columns), F32),
            jax.ShapeDtypeStruct((taps * channels, LANES), F32),
        ),
        in_specs=[smem, vmem, vmem],
        compiler_params=pltpu.CompilerParams(vmem_limit_bytes=VMEM_BYTES),
        name="unpack",
    )(core, mine, other)

    row_grad = lax.ppermute(low, RING, down).astype(F32) + lax.ppermute(high, RING, up).astype(F32)
    columns = [row_grad[:, i : i + RIM] for i in range(0, group, RIM)]
    own = [own_side[:, i : i + RIM].astype(F32) for i in range(0, beside, RIM)]
    if slabs == 2:
        incoming = columns[0] + lax.ppermute((columns[1] + own[0]).astype(BF16), "slab", swap)
    else:
        incoming = columns[1]
        incoming += lax.ppermute((columns[0] + own[0]).astype(BF16), "slab", shifts(slabs, -1))
        incoming += lax.ppermute((columns[2] + own[1]).astype(BF16), "slab", shifts(slabs, 1))
    grad_input_t = base.at[:, :RIM].add(incoming)
    return coarse, grad_input_t.T, conv_wgrad_t.T, down_wgrad


def solution(mesh):
    regions, slabs = mesh.shape["region"], mesh.shape["slab"]
    fine = Mesh(mesh.devices.reshape(regions // 2, 2, slabs), SPLIT)
    split = P(SPLIT, None)
    return jax.shard_map(
        on_device,
        mesh=fine,
        in_specs=(split, split, split, P(), P(), split),
        out_specs=(split, split, P(), P()),
        check_vma=False,
    )
```

profile of v0, /device:TPU:0, one launch (start us, length us, event | category | flops | bytes accessed | tf_op | source)
XLA Modules:
  0.0 68.2 jit_solution(9286137792692450184)
XLA Ops:
  0.6 0.0 copy-start.4
  0.6 0.7 %slice.32 = bf16[96,64]{1,0:T(8,128)(2,1)S(1)} slice(bf16[96,256]{1,0:T(8,128)(2,1)} %bitcast.12), slice={[0:96], [0:64]} | slice | bytes 24576 | tf_op jit(solution)/shard_map/slice | solution.py:174
  1.4 0.0 copy-start.2
  1.4 0.0 copy-start.3
  1.4 3.0 %collective-permute-start = (bf16[96,64]{1,0:T(8,128)(2,1)S(1)}, bf16[96,64]{1,0:T(8,128)(2,1)S(1)}, u32[]{:S(2)}, u32[]{:S(2)}) collective-permute-start(bf16[96,64]{1,0:T(8,128)(2,1)S(1)} %slice.32), channel_id=1, source_target_pairs={{0,1},{1,0},{2,3},{3,2},{4,5},{5,4},{6,7},{7,6},{8,9},{9,8},{10,11... | collective-permute-start | bytes 36872 | tf_op jit(solution)/shard_map/ppermute | solution.py:176
  4.4 1.8 %collective-permute-done.refs_2_ = bf16[96,64]{1,0:T(8,128)(2,1)S(1)} collective-permute-done((bf16[96,64]{1,0:T(8,128)(2,1)S(1)}, bf16[96,64]{1,0:T(8,128)(2,1)S(1)}, u32[]{:S(2)}, u32[]{:S(2)}) %collective-permute-start) | collective-permute-done | bytes 12320 | tf_op jit(solution)/shard_map/ppermute | solution.py:176
  6.2 0.1 pad_maximum_fusion
  6.2 1.3 %collective-permute-start.2 = (bf16[96,128]{1,0:T(8,128)(2,1)S(1)}, bf16[96,128]{1,0:T(8,128)(2,1)S(1)}, u32[]{:S(2)}, u32[]{:S(2)}) collective-permute-start(bf16[96,128]{1,0:T(8,128)(2,1)S(1)} %pad_maximum_fusion), channel_id=1, source_target_pairs={{2,0},{4,2},{6,4},{8,6},{10,8},{12,10},{14,12},{16,14},{18,16},{20... | collective-permute-start | bytes 73736 | tf_op jit(solution)/shard_map/ppermute | solution.py:185
  7.5 3.0 %collective-permute-start.1 = (bf16[96,128]{1,0:T(8,128)(2,1)S(1)}, bf16[96,128]{1,0:T(8,128)(2,1)S(1)}, u32[]{:S(2)}, u32[]{:S(2)}) collective-permute-start(bf16[96,128]{1,0:T(8,128)(2,1)S(1)} %pad_maximum_fusion), channel_id=1, source_target_pairs={{0,2},{2,4},{4,6},{6,8},{8,10},{10,12},{12,14},{14,16},{16,18},{18... | collective-permute-start | bytes 73736 | tf_op jit(solution)/shard_map/ppermute | solution.py:185
  10.6 0.0 copy-start.5
  10.6 0.0 collective-permute-done.2.refs_1_
  10.6 0.8 %collective-permute-done.1.refs_0_ = bf16[96,128]{1,0:T(8,128)(2,1)S(1)} collective-permute-done((bf16[96,128]{1,0:T(8,128)(2,1)S(1)}, bf16[96,128]{1,0:T(8,128)(2,1)S(1)}, u32[]{:S(2)}, u32[]{:S(2)}) %collective-permute-start.1) | collective-permute-done | bytes 24608 | tf_op jit(solution)/shard_map/ppermute | solution.py:185
  11.4 0.0 copy-done.4
  11.4 0.0 copy-done.2
  11.4 0.0 copy-done.3
  11.4 0.0 copy-done.5
  11.4 0.0 copy-start
  11.4 1.0 %copy-done = bf16[2592,96]{0,1:T(8,128)(2,1)S(1)} copy-done((bf16[2592,96]{0,1:T(8,128)(2,1)S(1)}, bf16[2592,96]{0,1:T(8,128)(2,1)}, u32[]{:S(2)}) %copy-start) | copy-done | bytes 497688
  12.5 0.0 copy-start.1
  12.5 0.9 %copy-done.1 = bf16[768,128]{1,0:T(8,128)(2,1)S(1)} copy-done((bf16[768,128]{1,0:T(8,128)(2,1)S(1)}, bf16[768,128]{1,0:T(8,128)(2,1)}, u32[]{:S(2)}) %copy-start.1) | copy-done | bytes 196632
  13.4 8.0 %local.1 = (bf16[64,128]{1,0:T(8,128)(2,1)}, f32[96,256]{1,0:T(8,128)}, bf16[96,128]{1,0:T(8,128)(2,1)S(1)}, bf16[96,128]{1,0:T(8,128)(2,1)S(1)}, bf16[96,64]{1,...) custom-call(s32[1]{0:T(128)} %bitcast.core_ref, bf16[96,256]{1,0:T(8,128)(2,1)S(1)} %bitcast.13, ...), custom_call_target="tpu_custom_call" | custom-call | tf_op jit(solution)/shard_map/local/pallas_call | solution.py:194
  21.4 1.7 %collective-permute-start.6 = (bf16[96,16,128]{2,1,0:T(8,128)(2,1)S(1)}, bf16[96,16,128]{2,1,0:T(8,128)(2,1)S(1)}, u32[]{:S(2)}, u32[]{:S(2)}) collective-permute-start(bf16[96,16,128]{2,1,0:T(8,128)(2,1)S(1)} %get-tuple-element.31), channel_id=1, source_target_pairs={{0,2},{2,0},{1,3},{3,1},{4,6},{6,4},{5,7},{7,5},{8,10},{10,8},{9,1... | collective-permute-start | bytes 1179656 | tf_op jit(solution)/shard_map/ppermute | solution.py:220
  23.1 1.3 %collective-permute-done.6 = bf16[96,16,128]{2,1,0:T(8,128)(2,1)S(1)} collective-permute-done((bf16[96,16,128]{2,1,0:T(8,128)(2,1)S(1)}, bf16[96,16,128]{2,1,0:T(8,128)(2,1)S(1)}, u32[]{:S(2)}, u32[]{:S(2)}) %collective-permute-start.6) | collective-permute-done | bytes 393248 | tf_op jit(solution)/shard_map/ppermute | solution.py:220
  24.4 0.1 add_convert_fusion
  24.5 20.6 %all_to_all.10 = bf16[16,6,16,128]{3,2,1,0:T(8,128)(2,1)S(1)} all-to-all(bf16[16,6,16,128]{3,2,1,0:T(8,128)(2,1)S(1)} %bitcast.16), channel_id=1, replica_groups=mesh['chips'=8,'core'=2,'slab'=2] {'chips','slab'}, dimensions={0} | all-to-all | bytes 786432 | tf_op jit(solution)/shard_map/all_to_all | solution.py:222
  45.2 0.1 reduce_sum.12
  45.2 0.8 %broadcast_in_dim.2 = bf16[16,6,16,128]{3,2,1,0:T(8,128)(2,1)} broadcast(bf16[6,16,128]{2,1,0:T(8,128)(2,1)S(1)} %reduce_sum.12), dimensions={1,2,3} | broadcast | bytes 417792 | tf_op jit(solution)/shard_map/broadcast_in_dim | solution.py:224
  46.0 3.6 %all-to-all-start.1 = ((bf16[16,6,16,128]{3,2,1,0:T(8,128)(2,1)}), bf16[16,6,16,128]{3,2,1,0:T(8,128)(2,1)S(1)}, u32[]{:S(2)}, u32[]{:S(2)}) async-start(bf16[16,6,16,128]{3,2,1,0:T(8,128)(2,1)} %broadcast_in_dim.2), calls=%async_computation.1 | async-start | bytes 786432 | tf_op jit(solution)/shard_map/all_to_all | solution.py:225
  49.7 1.3 %collective-permute-start.3 = (bf16[96,128]{1,0:T(8,128)(2,1)S(1)}, bf16[96,128]{1,0:T(8,128)(2,1)S(1)}, u32[]{:S(2)}, u32[]{:S(2)}) collective-permute-start(bf16[96,128]{1,0:T(8,128)(2,1)S(1)} %get-tuple-element.27), channel_id=1, source_target_pairs={{2,0},{4,2},{6,4},{8,6},{10,8},{12,10},{14,12},{16,14},{18,16},{20... | collective-permute-start | bytes 73736 | tf_op jit(solution)/shard_map/ppermute | solution.py:238
  51.0 0.0 copy-start.6
  51.0 3.2 %collective-permute-start.4 = (bf16[96,128]{1,0:T(8,128)(2,1)S(1)}, bf16[96,128]{1,0:T(8,128)(2,1)S(1)}, u32[]{:S(2)}, u32[]{:S(2)}) collective-permute-start(bf16[96,128]{1,0:T(8,128)(2,1)S(1)} %get-tuple-element.28), channel_id=1, source_target_pairs={{0,2},{2,4},{4,6},{6,8},{8,10},{10,12},{12,14},{14,16},{16,18},{18... | collective-permute-start | bytes 73736 | tf_op jit(solution)/shard_map/ppermute | solution.py:238
  54.2 0.0 collective-permute-done.3
  54.2 0.8 %collective-permute-done.4 = bf16[96,128]{1,0:T(8,128)(2,1)S(1)} collective-permute-done((bf16[96,128]{1,0:T(8,128)(2,1)S(1)}, bf16[96,128]{1,0:T(8,128)(2,1)S(1)}, u32[]{:S(2)}, u32[]{:S(2)}) %collective-permute-start.4) | collective-permute-done | bytes 24608 | tf_op jit(solution)/shard_map/ppermute | solution.py:238
  55.0 6.7 %all-to-all-done.1 = bf16[16,6,16,128]{3,2,1,0:T(8,128)(2,1)S(1)} async-done(((bf16[16,6,16,128]{3,2,1,0:T(8,128)(2,1)}), bf16[16,6,16,128]{3,2,1,0:T(8,128)(2,1)S(1)}, u32[]{:S(2)}, u32[]{:S(2)}) %all-to-all-start.1) | async-done | bytes 393248 | tf_op jit(solution)/shard_map/all_to_all | solution.py:225
  61.7 0.0 collective-permute-start.7
  61.7 0.1 fusion
  61.8 0.6 collective-permute-start.5
  62.4 0.6 compare_reduce_fusion
  63.0 2.6 %collective-permute-done.5 = bf16[96,64]{1,0:T(8,128)(2,1)S(1)} collective-permute-done((bf16[96,64]{1,0:T(8,128)(2,1)S(1)}, bf16[96,64]{1,0:T(8,128)(2,1)S(1)}, u32[]{:S(2)}, u32[]{:S(2)}) %collective-permute-start.5) | collective-permute-done | bytes 12320 | tf_op jit(solution)/shard_map/ppermute | solution.py:242
  65.7 0.0 copy-done.6
  65.7 0.7 add_select_fusion
  66.3 0.6 scatter-add.4
  66.9 0.0 copy-start.7
  66.9 0.0 collective-permute-done.7.other_ref
  66.9 1.2 %unpack.1 = (f32[96,2592]{1,0:T(8,128)}, f32[768,128]{1,0:T(8,128)}) custom-call(s32[1]{0:T(128)} %bitcast.core_ref, bf16[96,16,128]{2,1,0:T(8,128)(2,1)S(1)} %bitcast.10, bf16[96,16,128]{2,1,0:T(8,128)(2,1)S(1)} %collective-permute-done.7.other_ref), custom_call_target="tpu_custom_call" | custom-call | tf_op jit(solution)/shard_map/unpack/pallas_call | solution.py:227
  68.2 0.0 copy-done.7
  (1 shorter events, 0.0 us)
Async XLA Ops:
  0.6 10.8 %copy-start.4 = (bf16[64,128]{1,0:T(8,128)(2,1)S(1)}, bf16[64,128]{1,0:T(8,128)(2,1)}, u32[]{:S(2)}) copy-start(bf16[64,128]{1,0:T(8,128)(2,1)} %cgrad_ref.1) | copy-start | bytes 49156
  1.4 10.0 %copy-start.2 = (bf16[256,96]{0,1:T(8,128)(2,1)S(1)}, bf16[256,96]{0,1:T(8,128)(2,1)}, u32[]{:S(2)}) copy-start(bf16[256,96]{0,1:T(8,128)(2,1)} %param.8) | copy-start | bytes 147460
  1.4 10.0 %copy-start.3 = (s32[256,27]{0,1:T(8,128)S(1)}, s32[256,27]{0,1:T(8,128)}, u32[]{:S(2)}) copy-start(s32[256,27]{0,1:T(8,128)} %param.9) | copy-start | bytes 82948
  1.4 4.8 %collective-permute-start = (bf16[96,64]{1,0:T(8,128)(2,1)S(1)}, bf16[96,64]{1,0:T(8,128)(2,1)S(1)}, u32[]{:S(2)}, u32[]{:S(2)}) collective-permute-start(bf16[96,64]{1,0:T(8,128)(2,1)S(1)} %slice.32), channel_id=1, source_target_pairs={{0,1},{1,0},{2,3},{3,2},{4,5},{5,4},{6,7},{7,6},{8,9},{9,8},{10,11... | collective-permute-start | bytes 36872 | tf_op jit(solution)/shard_map/ppermute | solution.py:176
  6.2 4.3 %collective-permute-start.2 = (bf16[96,128]{1,0:T(8,128)(2,1)S(1)}, bf16[96,128]{1,0:T(8,128)(2,1)S(1)}, u32[]{:S(2)}, u32[]{:S(2)}) collective-permute-start(bf16[96,128]{1,0:T(8,128)(2,1)S(1)} %pad_maximum_fusion), channel_id=1, source_target_pairs={{2,0},{4,2},{6,4},{8,6},{10,8},{12,10},{14,12},{16,14},{18,16},{20... | collective-permute-start | bytes 73736 | tf_op jit(solution)/shard_map/ppermute | solution.py:185
  7.5 3.9 %collective-permute-start.1 = (bf16[96,128]{1,0:T(8,128)(2,1)S(1)}, bf16[96,128]{1,0:T(8,128)(2,1)S(1)}, u32[]{:S(2)}, u32[]{:S(2)}) collective-permute-start(bf16[96,128]{1,0:T(8,128)(2,1)S(1)} %pad_maximum_fusion), channel_id=1, source_target_pairs={{0,2},{2,4},{4,6},{6,8},{8,10},{10,12},{12,14},{14,16},{16,18},{18... | collective-permute-start | bytes 73736 | tf_op jit(solution)/shard_map/ppermute | solution.py:185
  10.6 0.8 %copy-start.5 = (s32[64,8]{0,1:T(8,128)S(1)}, s32[64,8]{0,1:T(8,128)}, u32[]{:S(2)}) copy-start(s32[64,8]{0,1:T(8,128)} %param.10) | copy-start | bytes 6148
  11.4 1.0 %copy-start = (bf16[2592,96]{0,1:T(8,128)(2,1)S(1)}, bf16[2592,96]{0,1:T(8,128)(2,1)}, u32[]{:S(2)}) copy-start(bf16[2592,96]{0,1:T(8,128)(2,1)} %param.11) | copy-start | bytes 1492996
  12.5 0.9 %copy-start.1 = (bf16[768,128]{1,0:T(8,128)(2,1)S(1)}, bf16[768,128]{1,0:T(8,128)(2,1)}, u32[]{:S(2)}) copy-start(bf16[768,128]{1,0:T(8,128)(2,1)} %wd_ref.1) | copy-start | bytes 589828
  21.4 3.1 %collective-permute-start.6 = (bf16[96,16,128]{2,1,0:T(8,128)(2,1)S(1)}, bf16[96,16,128]{2,1,0:T(8,128)(2,1)S(1)}, u32[]{:S(2)}, u32[]{:S(2)}) collective-permute-start(bf16[96,16,128]{2,1,0:T(8,128)(2,1)S(1)} %get-tuple-element.31), channel_id=1, source_target_pairs={{0,2},{2,0},{1,3},{3,1},{4,6},{6,4},{5,7},{7,5},{8,10},{10,8},{9,1... | collective-permute-start | bytes 1179656 | tf_op jit(solution)/shard_map/ppermute | solution.py:220
  46.0 15.7 %all-to-all-start.1 = ((bf16[16,6,16,128]{3,2,1,0:T(8,128)(2,1)}), bf16[16,6,16,128]{3,2,1,0:T(8,128)(2,1)S(1)}, u32[]{:S(2)}, u32[]{:S(2)}) async-start(bf16[16,6,16,128]{3,2,1,0:T(8,128)(2,1)} %broadcast_in_dim.2), calls=%async_computation.1 | async-start | bytes 786432 | tf_op jit(solution)/shard_map/all_to_all | solution.py:225
  49.7 4.5 %collective-permute-start.3 = (bf16[96,128]{1,0:T(8,128)(2,1)S(1)}, bf16[96,128]{1,0:T(8,128)(2,1)S(1)}, u32[]{:S(2)}, u32[]{:S(2)}) collective-permute-start(bf16[96,128]{1,0:T(8,128)(2,1)S(1)} %get-tuple-element.27), channel_id=1, source_target_pairs={{2,0},{4,2},{6,4},{8,6},{10,8},{12,10},{14,12},{16,14},{18,16},{20... | collective-permute-start | bytes 73736 | tf_op jit(solution)/shard_map/ppermute | solution.py:238
  51.0 14.7 %copy-start.6 = (f32[96,256]{1,0:T(8,128)S(1)}, f32[96,256]{1,0:T(8,128)}, u32[]{:S(2)}) copy-start(f32[96,256]{1,0:T(8,128)} %get-tuple-element.26) | copy-start | bytes 294916
  51.0 4.0 %collective-permute-start.4 = (bf16[96,128]{1,0:T(8,128)(2,1)S(1)}, bf16[96,128]{1,0:T(8,128)(2,1)S(1)}, u32[]{:S(2)}, u32[]{:S(2)}) collective-permute-start(bf16[96,128]{1,0:T(8,128)(2,1)S(1)} %get-tuple-element.28), channel_id=1, source_target_pairs={{0,2},{2,4},{4,6},{6,8},{8,10},{10,12},{12,14},{14,16},{16,18},{18... | collective-permute-start | bytes 73736 | tf_op jit(solution)/shard_map/ppermute | solution.py:238
  61.7 5.2 %collective-permute-start.7 = (bf16[96,16,128]{2,1,0:T(8,128)(2,1)S(1)}, bf16[96,16,128]{2,1,0:T(8,128)(2,1)S(1)}, u32[]{:S(2)}, u32[]{:S(2)}) collective-permute-start(bf16[96,16,128]{2,1,0:T(8,128)(2,1)S(1)} %bitcast.9), channel_id=1, source_target_pairs={{0,2},{2,0},{1,3},{3,1},{4,6},{6,4},{5,7},{7,5},{8,10},{10,8},{9,1... | collective-permute-start | bytes 1179656 | tf_op jit(solution)/shard_map/ppermute | solution.py:226
  61.8 3.9 %collective-permute-start.5 = (bf16[96,64]{1,0:T(8,128)(2,1)S(1)}, bf16[96,64]{1,0:T(8,128)(2,1)S(1)}, u32[]{:S(2)}, u32[]{:S(2)}) collective-permute-start(bf16[96,64]{1,0:T(8,128)(2,1)S(1)} %fusion), channel_id=1, source_target_pairs={{0,1},{1,0},{2,3},{3,2},{4,5},{5,4},{6,7},{7,6},{8,9},{9,8},{10,11... | collective-permute-start | bytes 36872 | tf_op jit(solution)/shard_map/ppermute | solution.py:242
  66.9 1.3 %copy-start.7 = (f32[96,256]{1,0:T(8,128)}, f32[96,256]{1,0:T(8,128)S(1)}, u32[]{:S(2)}) copy-start(f32[96,256]{1,0:T(8,128)S(1)} %scatter-add.4) | copy-start | bytes 294916
where the time goes:
time: 68.7 us; the launch traced here: 68.2 us
  blocking collectives  20.6 us (30%)
  starting transfers between devices  17.7 us (26%)
  waiting for transfers between devices  14.1 us (21%)
  Pallas kernels  9.22 us (13%)
  local copies, waits for them, and re-layouts  4.1 us (6%)
  other arithmetic  1.63 us (2%)
  between operations  0.78 us (1%)
    all_to_all x1, blocking collectives, on_device(): parts = lax.all_to_all(pair.reshape(peers, piece, TILE, LANES), PEERS, 0, 0)  20.6 us
    pallas_call x1, Pallas kernels, on_device(): pl.pallas_call(functools.partial(local_kernel, slabs), out_shape=(jax.Sha...  7.98 us
    all_to_all x1, waiting for transfers between devices, on_device(): mine = lax.all_to_all(spread, PEERS, 0, 0).reshape(half, TILE, LANES)  6.69 us
    ppermute x2, starting transfers between devices, on_device(): halos = [lax.ppermute(row, RING, up), lax.ppermute(row, RING, down), *side]  4.31 us
    all_to_all x1, starting transfers between devices, on_device(): mine = lax.all_to_all(spread, PEERS, 0, 0).reshape(half, TILE, LANES)  3.63 us
    ppermute x1, starting transfers between devices, on_device(): lax.ppermute(high, RING, up).astype(F32)  3.16 us
    ppermute x1, starting transfers between devices, on_device(): side = [lax.ppermute(rim, 'slab', swap)]  2.97 us
    ppermute x1, waiting for transfers between devices, on_device(): lax.ppermute((columns[1] + own[0]).astype(BF16), 'slab', swap)  2.62 us
  transfers between devices with their start and end apart: 9, of which 6 were waited for; matrix products, arithmetic and copies ran while one was open for 3% of the time, Pallas kernels for 0%

commit v1 on v0

v1 whole, which is shorter than its diff:
```python
import functools

import jax
import jax.numpy as jnp
from jax import lax
from jax.experimental import pallas as pl
from jax.experimental.pallas import tpu as pltpu
from jax.sharding import Mesh, PartitionSpec as P

SPLIT = ("far", "near", "core", "slab")
RING = ("far", "near", "core")
AROUND = ("near", "slab")
RIM = 64
LANES = 128
TILE = 16
F32 = jnp.float32
BF16 = jnp.bfloat16
NN = (((1,), (0,)), ((), ()))
NT = (((1,), (1,)), ((), ()))
VMEM_BYTES = 20 * 2**20


def mm(a, b, dims=NN):
    return lax.dot_general(a, b, dims, preferred_element_type=F32)


def table_lanes(neighbours, voxels, slabs):
    code = neighbours // voxels
    slot = neighbours - code * voxels
    row = code // 3
    col = code - row * 3
    if slabs == 2:
        rims = 2
        place = jnp.where(col == 1, 0, 1)
        beside = 0
    else:
        rims = 3
        place = col
        beside = col // 2
    rim = jnp.where(row == 1, 2 * rims + beside, (row // 2) * rims + place)
    lane = jnp.where(code == 4, slot, voxels + rim * RIM + slot)
    return jnp.where(code > 8, -1, lane)


def payload_tiles(channels, conv_columns, taps):
    tiles = []
    for column in range(0, conv_columns, LANES):
        for row in range(0, channels, TILE):
            tiles.append((0, row, column, min(LANES, conv_columns - column)))
    for row in range(0, taps * channels, TILE):
        tiles.append((1, row, 0, LANES))
    return tiles


def padded_halo(halo_refs):
    halo = [h[...] for h in halo_refs]
    width = sum(h.shape[1] for h in halo)
    slack = -width % LANES
    if slack:
        halo.append(jnp.zeros((halo[0].shape[0], slack), BF16))
    return jnp.concatenate(halo, axis=1)


def prepare_kernel(slabs, f_ref, near_ref, down_ref, cgrad_ref, w_ref, wd_ref, *refs):
    first_ref, rest_ref, pick_ref, hgrad_ref, w_out, wd_out = refs
    channels, voxels = f_ref.shape
    offsets = near_ref.shape[0]
    taps, coarse_count = down_ref.shape
    w_out[...] = w_ref[...]
    wd_out[...] = wd_ref[...]
    cgrad_t = cgrad_ref[...].astype(F32).T.astype(BF16)
    down = down_ref[...].astype(F32).T
    lane_iota = lax.broadcasted_iota(jnp.int32, (coarse_count, voxels), 1).astype(F32)
    hgrad_t = jnp.zeros((channels, voxels), F32)
    for t in range(taps):
        pick = jnp.where(lane_iota == down[:, t : t + 1], 1.0, 0.0).astype(BF16)
        pick_ref[t] = pick
        wd = wd_ref[t * channels : (t + 1) * channels, :]
        hgrad_t += mm(wd, mm(cgrad_t, pick).astype(BF16))
    hgrad_ref[...] = hgrad_t
    table_t = f_ref[...]
    lanes = table_lanes(near_ref[...], voxels, slabs)
    near_iota = lax.broadcasted_iota(jnp.int32, (voxels, voxels), 0)
    for o in range(offsets):
        near = jnp.where(near_iota == lanes[o : o + 1, :], 1.0, 0.0).astype(BF16)
        own = mm(table_t, near).astype(BF16)
        first_ref[o * channels : (o + 1) * channels, :] = own[:, :LANES]
        rest_ref[o * channels : (o + 1) * channels, :] = own[:, LANES:]


def forward_kernel(slabs, core_ref, f_ref, near_ref, cgrad_ref, *refs):
    first_ref, rest_ref, pick_ref, hgrad_ref, w_ref, wd_ref = refs[:6]
    halo_refs, refs = (refs[6:9], refs[9:]) if slabs == 2 else (refs[6:10], refs[10:])
    coarse_ref, grad_ref, keep_ref, send_ref, rt, conv_w, down_w = refs
    channels, voxels = f_ref.shape
    offsets = near_ref.shape[0]
    taps = pick_ref.shape[0]
    conv_columns = offsets * channels
    halo_t = padded_halo(halo_refs)
    lanes = table_lanes(near_ref[:, :LANES], voxels, slabs)
    far_iota = lax.broadcasted_iota(jnp.int32, (halo_t.shape[1], LANES), 0) + voxels
    for o in range(offsets):
        rows = slice(o * channels, (o + 1) * channels)
        away = jnp.where(far_iota == lanes[o : o + 1, :], 1.0, 0.0).astype(BF16)
        first = first_ref[rows, :].astype(F32) + mm(halo_t, away)
        rt[rows, :LANES] = first.astype(BF16)
        rt[rows, LANES:] = rest_ref[rows, :]

    out_t = mm(w_ref[...], rt[...])
    sig = 1.0 / (1.0 + jnp.exp(-out_t))
    hidden_t = (f_ref[...].astype(F32) + out_t * sig).astype(BF16)
    grad_t = (hgrad_ref[...] * sig * (1.0 + out_t * (1.0 - sig))).astype(BF16)
    grad_ref[...] = grad_t
    conv_w[:, :conv_columns] = mm(grad_t, rt[...], NT).astype(BF16)
    if conv_w.shape[1] > conv_columns:
        slack = conv_w.shape[1] - conv_columns
        conv_w[:, conv_columns:] = jnp.zeros((channels, slack), BF16)

    cgrad = cgrad_ref[...]
    coarse = jnp.zeros(cgrad.shape, F32)
    for t in range(taps):
        rows = slice(t * channels, (t + 1) * channels)
        pick = pick_ref[t]
        coarse += mm(mm(pick, hidden_t, NT).astype(BF16), wd_ref[rows, :])
        picked_t = mm(hidden_t, pick, NT).astype(BF16)
        down_w[rows, :] = mm(picked_t, cgrad).astype(BF16)
    coarse_ref[...] = coarse.astype(BF16)

    tiles = payload_tiles(channels, conv_columns, taps)
    half = keep_ref.shape[0]
    for core in range(2):

        @pl.when(core_ref[0] == core)
        def _(core=core):
            for i in range(2 * half):
                ref = keep_ref if i // half == core else send_ref
                if i < len(tiles):
                    kind, row, column, _ = tiles[i]
                    source = down_w if kind else conv_w
                    ref[i % half] = source[row : row + TILE, column : column + LANES]
                else:
                    ref[i % half] = jnp.zeros((TILE, LANES), BF16)


def backward_kernel(slabs, near_ref, hgrad_ref, grad_ref, w_ref, *refs):
    base_ref, low_ref, high_ref, side_ref, drt, drt_far, hot, far, w_back = refs
    channels, voxels = hgrad_ref.shape
    offsets = near_ref.shape[0]
    group = low_ref.shape[1]
    lanes = table_lanes(near_ref[...], voxels, slabs)
    near_iota = lax.broadcasted_iota(jnp.int32, (voxels, voxels), 0)
    far_iota = lax.broadcasted_iota(jnp.int32, (far.shape[0], LANES), 0) + voxels
    w_back[:, :channels] = w_ref[...].astype(F32).T.astype(BF16)
    w_back[:, channels:] = jnp.zeros((offsets * channels, LANES - channels), BF16)
    slack = jnp.zeros((LANES - channels, voxels), BF16)
    grad_pad = jnp.concatenate([grad_ref[...], slack], axis=0)
    for o in range(offsets):
        lane = lanes[o : o + 1, :]
        near = jnp.where(near_iota == lane, 1.0, 0.0).astype(BF16)
        away = jnp.where(far_iota == lane[:, :LANES], 1.0, 0.0).astype(BF16)
        hot[:, o * voxels : (o + 1) * voxels] = near
        far[:, o * LANES : (o + 1) * LANES] = away
        spread = mm(w_back[o * channels : (o + 1) * channels, :], grad_pad).astype(BF16)
        drt[:, o * voxels : (o + 1) * voxels] = spread
        drt_far[:, o * LANES : (o + 1) * LANES] = spread[:, :LANES]
    base_ref[...] = hgrad_ref[...] + mm(drt[...], hot[...], NT)
    back_t = mm(drt_far[...], far[...], NT).astype(BF16)
    low_ref[...] = back_t[:, :group]
    high_ref[...] = back_t[:, group : 2 * group]
    side_ref[...] = back_t[:, 2 * group : 2 * group + side_ref.shape[1]]


def final_kernel(taps, core_ref, mine_ref, other_ref, base_ref, *refs):
    conv_ref, down_ref, grad_ref = refs[-3:]
    channels, conv_columns = conv_ref.shape
    half = mine_ref.shape[0]
    total = refs[0][...].astype(F32)
    for ref in refs[1:-3]:
        total += ref[...].astype(F32)
    grad_ref[:, RIM:] = base_ref[:, RIM:]
    grad_ref[:, :RIM] = base_ref[:, :RIM] + total
    for core in range(2):

        @pl.when(core_ref[0] == core)
        def _(core=core):
            for i, tile in enumerate(payload_tiles(channels, conv_columns, taps)):
                kind, row, column, columns = tile
                source = mine_ref if i // half == core else other_ref
                value = source[i % half].astype(F32)
                target = down_ref if kind else conv_ref
                target[row : row + TILE, column : column + columns] = value[:, :columns]


def shifts(count, step):
    return [(i, i + step) for i in range(count) if 0 <= i + step < count]


def on_device(features, neighbours, down_map, w_conv, w_down, coarse_grad):
    regions = lax.axis_size("far") * lax.axis_size("near") * lax.axis_size("core")
    slabs = lax.axis_size("slab")
    around, along = lax.axis_size("near") * slabs, lax.axis_size("far")
    voxels, channels = features.shape
    offsets, taps = neighbours.shape[1], down_map.shape[1]
    conv_columns = offsets * channels
    core = lax.axis_index("core").astype(jnp.int32).reshape(1)
    swap = [(0, 1), (1, 0)]
    up, down = shifts(regions, 1), shifts(regions, -1)

    features_t, neighbours_t, w_conv_t = features.T, neighbours.T, w_conv.T
    rim = features_t[:, :RIM]
    if slabs == 2:
        side = [lax.ppermute(rim, "slab", swap)]
        row = [rim, side[0]]
    else:
        side = [
            lax.ppermute(rim, "slab", shifts(slabs, 1)),
            lax.ppermute(rim, "slab", shifts(slabs, -1)),
        ]
        row = [side[0], rim, side[1]]
    row = jnp.concatenate(row, axis=1)
    halos = [lax.ppermute(row, RING, up), lax.ppermute(row, RING, down), *side]

    tiles = len(payload_tiles(channels, conv_columns, taps))
    piece = -(-tiles // (2 * around * along))
    half = piece * around * along
    group, beside = row.shape[1], len(side) * RIM
    far_rows = -(-(2 * group + beside) // LANES) * LANES
    smem = pl.BlockSpec(memory_space=pltpu.SMEM)
    vmem = pl.BlockSpec(memory_space=pltpu.VMEM)
    params = pltpu.CompilerParams(vmem_limit_bytes=VMEM_BYTES)
    own = pl.pallas_call(
        functools.partial(prepare_kernel, slabs),
        out_shape=(
            jax.ShapeDtypeStruct((conv_columns, LANES), BF16),
            jax.ShapeDtypeStruct((conv_columns, voxels - LANES), BF16),
            jax.ShapeDtypeStruct((taps, down_map.shape[0], voxels), BF16),
            jax.ShapeDtypeStruct((channels, voxels), F32),
            jax.ShapeDtypeStruct((channels, conv_columns), BF16),
            jax.ShapeDtypeStruct(w_down.shape, BF16),
        ),
        compiler_params=params,
        cost_estimate=pl.CostEstimate(flops=2 * 10**9, bytes_accessed=10**7, transcendentals=0),
        name="prepare",
    )(features_t, neighbours_t, down_map.T, coarse_grad, w_conv_t, w_down)
    hgrad, w_near = own[3], own[4]
    coarse, grad, keep, send = pl.pallas_call(
        functools.partial(forward_kernel, slabs),
        out_shape=(
            jax.ShapeDtypeStruct(coarse_grad.shape, BF16),
            jax.ShapeDtypeStruct((channels, voxels), BF16),
            jax.ShapeDtypeStruct((half, TILE, LANES), BF16),
            jax.ShapeDtypeStruct((half, TILE, LANES), BF16),
        ),
        in_specs=[smem] + [vmem] * (9 + len(halos)),
        scratch_shapes=[
            pltpu.VMEM((conv_columns, voxels), BF16),
            pltpu.VMEM((channels, -(-conv_columns // LANES) * LANES), BF16),
            pltpu.VMEM((taps * channels, LANES), BF16),
        ],
        compiler_params=params,
        name="forward",
    )(core, features_t, neighbours_t, coarse_grad, *own, *halos)
    got = lax.ppermute(send, "core", swap)
    pair = (keep.astype(F32) + got.astype(F32)).astype(BF16)
    pair, grad = lax.optimization_barrier((pair, grad))

    base, low, high, own_side = pl.pallas_call(
        functools.partial(backward_kernel, slabs),
        out_shape=(
            jax.ShapeDtypeStruct((channels, voxels), F32),
            jax.ShapeDtypeStruct((channels, group), BF16),
            jax.ShapeDtypeStruct((channels, group), BF16),
            jax.ShapeDtypeStruct((channels, beside), BF16),
        ),
        scratch_shapes=[
            pltpu.VMEM((channels, offsets * voxels), BF16),
            pltpu.VMEM((channels, offsets * LANES), BF16),
            pltpu.VMEM((voxels, offsets * voxels), BF16),
            pltpu.VMEM((far_rows, offsets * LANES), BF16),
            pltpu.VMEM((conv_columns, LANES), BF16),
        ],
        compiler_params=params,
        cost_estimate=pl.CostEstimate(flops=3 * 10**9, bytes_accessed=10**7, transcendentals=0),
        name="backward",
    )(neighbours_t, hgrad, grad, w_near)

    parts = lax.all_to_all(pair.reshape(around, along * piece, TILE, LANES), AROUND, 0, 0)
    parts, low, high, own_side, base = lax.optimization_barrier((parts, low, high, own_side, base))
    square = jnp.sum(parts.astype(F32), axis=0).astype(BF16)
    parts = lax.all_to_all(square.reshape(along, piece, TILE, LANES), "far", 0, 0)
    low, high = lax.ppermute(low, RING, down), lax.ppermute(high, RING, up)
    parts, low, high = lax.optimization_barrier((parts, low, high))
    total = jnp.sum(parts.astype(F32), axis=0).astype(BF16)
    total = jnp.broadcast_to(total[None], parts.shape)
    square = lax.all_to_all(total, "far", 0, 0).reshape(1, along * piece, TILE, LANES)
    row_grad = low.astype(F32) + high.astype(F32)
    columns = [row_grad[:, i : i + RIM] for i in range(0, group, RIM)]
    own = [own_side[:, i : i + RIM].astype(F32) for i in range(0, beside, RIM)]
    if slabs == 2:
        crossing = [(columns[1] + own[0]).astype(BF16)]
        crossing = [lax.ppermute(crossing[0], "slab", swap)]
        here = columns[0]
    else:
        crossing = [(columns[0] + own[0]).astype(BF16), (columns[2] + own[1]).astype(BF16)]
        crossing[0] = lax.ppermute(crossing[0], "slab", shifts(slabs, -1))
        crossing[1] = lax.ppermute(crossing[1], "slab", shifts(slabs, 1))
        here = columns[1]
    square = jnp.broadcast_to(square, (around,) + square.shape[1:])
    mine = lax.all_to_all(square, AROUND, 0, 0).reshape(half, TILE, LANES)
    mine, crossing, here = lax.optimization_barrier((mine, crossing, here))
    other = lax.ppermute(mine, "core", swap)
    conv_wgrad_t, down_wgrad, grad_input_t = pl.pallas_call(
        functools.partial(final_kernel, taps),
        out_shape=(
            jax.ShapeDtypeStruct((channels, conv_columns), F32),
            jax.ShapeDtypeStruct((taps * channels, LANES), F32),
            jax.ShapeDtypeStruct((channels, voxels), F32),
        ),
        in_specs=[smem] + [vmem] * (4 + len(crossing)),
        compiler_params=params,
        name="final",
    )(core, mine, other, base, here, *crossing)
    return coarse, grad_input_t.T, conv_wgrad_t.T, down_wgrad


def solution(mesh):
    regions, slabs = mesh.shape["region"], mesh.shape["slab"]
    fine = Mesh(mesh.devices.reshape(regions // 4, 2, 2, slabs), SPLIT)
    split = P(SPLIT, None)
    return jax.shard_map(
        on_device,
        mesh=fine,
        in_specs=(split, split, split, P(), P(), split),
        out_specs=(split, split, P(), P()),
        check_vma=False,
    )
```

time: 68.7 us -> 70.7 us (1.029)
  starting transfers between devices: 17.7 us -> 27.4 us
  blocking collectives: 20.6 us -> 13.3 us
  Pallas kernels: 9.22 us -> 8.11 us
  waiting for transfers between devices: 14.1 us -> 15.2 us
    all_to_all x1 -> x3, starting transfers between devices: 3.63 us -> 12.1 us  [the longest x1 4.8 us: on_device(): lax.all_to_all(square.reshape(along, piece, TILE, LANES), 'far', 0, 0)]
    all_to_all x1, blocking collectives: 20.6 us -> 13.3 us  [on_device(): lax.all_to_all(total, 'far', 0, 0).reshape(1, along * piece, TILE, LANES)]
    ppermute x1, waiting for transfers between devices: 0.01 us -> 1.72 us  [on_device(): other = lax.ppermute(mine, 'core', swap)]
    ppermute x3, waiting for transfers between devices: 3.45 us -> 4.78 us  [the longest x1 3.95 us: on_device(): crossing = [lax.ppermute(crossing[0], 'slab', swap)]]
    another operation x2 -> x0, other arithmetic: 1.3 us -> none
    ppermute x3, starting transfers between devices: 5.08 us -> 6.36 us  [the longest x2 4.31 us: on_device(): low, high = (lax.ppermute(low, RING, down), lax.ppermute(high, RING, up))]
    all_to_all x1 -> x3, waiting for transfers between devices: 6.69 us -> 5.5 us  [the longest x1 4.82 us: on_device(): lax.all_to_all(pair.reshape(around, along * piece, TILE, LANES), AROUND,...]
    pallas_call x2 -> x4, Pallas kernels: 9.22 us -> 8.11 us  [the longest x1 3.15 us: on_device(): pl.pallas_call(functools.partial(forward_kernel, slabs), out_shape=(jax.S...]
  transfers between devices with their start and end apart: 9 -> 11, of which waited for: 6 -> 7; matrix products, arithmetic and copies ran while one was open for 3% -> 0% of each run, Pallas kernels for 0% -> 5%
where the time goes in v1:
time: 70.7 us; the launch traced here: 70.1 us
  starting transfers between devices  27.4 us (39%)
  waiting for transfers between devices  15.2 us (21%)
  blocking collectives  13.3 us (19%)
  Pallas kernels  8.11 us (11%)
  local copies, waits for them, and re-layouts  3.53 us (5%)
  other arithmetic  1.76 us (2%)
  between operations  0.79 us (1%)
    all_to_all x1, blocking collectives, on_device(): lax.all_to_all(total, 'far', 0, 0).reshape(1, along * piece, TILE, LANES)  13.3 us
    all_to_all x1, waiting for transfers between devices, on_device(): lax.all_to_all(pair.reshape(around, along * piece, TILE, LANES), AROUND,...  4.82 us
    all_to_all x1, starting transfers between devices, on_device(): lax.all_to_all(square.reshape(along, piece, TILE, LANES), 'far', 0, 0)  4.8 us
    ppermute x2, starting transfers between devices, on_device(): halos = [lax.ppermute(row, RING, up), lax.ppermute(row, RING, down), *side]  4.32 us
    ppermute x2, starting transfers between devices, on_device(): low, high = (lax.ppermute(low, RING, down), lax.ppermute(high, RING, up))  4.31 us
    ppermute x1, waiting for transfers between devices, on_device(): crossing = [lax.ppermute(crossing[0], 'slab', swap)]  3.95 us
    all_to_all x1, starting transfers between devices, on_device(): lax.all_to_all(pair.reshape(around, along * piece, TILE, LANES), AROUND,...  3.8 us
    all_to_all x1, starting transfers between devices, on_device(): mine = lax.all_to_all(square, AROUND, 0, 0).reshape(half, TILE, LANES)  3.46 us
  transfers between devices with their start and end apart: 11, of which 7 were waited for; matrix products, arithmetic and copies ran while one was open for 0% of the time, Pallas kernels for 5%

profile of v1, /device:TPU:0, one launch (start us, length us, event | category | flops | bytes accessed | tf_op | source)
XLA Modules:
  0.0 70.1 jit_solution(15136579176052366128)
XLA Ops:
  0.6 0.0 copy-start.1
  0.6 0.7 %slice.12 = bf16[96,64]{1,0:T(8,128)(2,1)S(1)} slice(bf16[96,256]{1,0:T(8,128)(2,1)} %bitcast.13), slice={[0:96], [0:64]} | slice | bytes 24576 | tf_op jit(solution)/shard_map/slice | solution.py:210
  1.4 0.0 copy-start
  1.4 0.0 copy-start.2
  1.4 3.0 %collective-permute-start = (bf16[96,64]{1,0:T(8,128)(2,1)S(1)}, bf16[96,64]{1,0:T(8,128)(2,1)S(1)}, u32[]{:S(2)}, u32[]{:S(2)}) collective-permute-start(bf16[96,64]{1,0:T(8,128)(2,1)S(1)} %slice.12), channel_id=1, source_target_pairs={{0,1},{1,0},{2,3},{3,2},{4,5},{5,4},{6,7},{7,6},{8,9},{9,8},{10,11... | collective-permute-start | bytes 36872 | tf_op jit(solution)/shard_map/ppermute | solution.py:212
  4.4 1.8 %collective-permute-done.refs_8_ = bf16[96,64]{1,0:T(8,128)(2,1)S(1)} collective-permute-done((bf16[96,64]{1,0:T(8,128)(2,1)S(1)}, bf16[96,64]{1,0:T(8,128)(2,1)S(1)}, u32[]{:S(2)}, u32[]{:S(2)}) %collective-permute-start) | collective-permute-done | bytes 12320 | tf_op jit(solution)/shard_map/ppermute | solution.py:212
  6.2 0.1 pad_maximum_fusion
  6.2 0.0 copy-start.5
  6.2 1.3 %collective-permute-start.2 = (bf16[96,128]{1,0:T(8,128)(2,1)S(1)}, bf16[96,128]{1,0:T(8,128)(2,1)S(1)}, u32[]{:S(2)}, u32[]{:S(2)}) collective-permute-start(bf16[96,128]{1,0:T(8,128)(2,1)S(1)} %pad_maximum_fusion), channel_id=1, source_target_pairs={{2,0},{4,2},{6,4},{8,6},{10,8},{12,10},{14,12},{16,14},{18,16},{20... | collective-permute-start | bytes 73736 | tf_op jit(solution)/shard_map/ppermute | solution.py:221
  7.5 3.0 %collective-permute-start.1 = (bf16[96,128]{1,0:T(8,128)(2,1)S(1)}, bf16[96,128]{1,0:T(8,128)(2,1)S(1)}, u32[]{:S(2)}, u32[]{:S(2)}) collective-permute-start(bf16[96,128]{1,0:T(8,128)(2,1)S(1)} %pad_maximum_fusion), channel_id=1, source_target_pairs={{0,2},{2,4},{4,6},{6,8},{8,10},{10,12},{12,14},{14,16},{16,18},{18... | collective-permute-start | bytes 73736 | tf_op jit(solution)/shard_map/ppermute | solution.py:221
  10.6 0.0 copy-done.1
  10.6 0.0 copy-done
  10.6 0.0 copy-done.2
  10.6 0.0 copy-done.5
  10.6 0.0 copy-start.3
  10.6 1.0 %copy-done.3 = bf16[2592,96]{0,1:T(8,128)(2,1)S(1)} copy-done((bf16[2592,96]{0,1:T(8,128)(2,1)S(1)}, bf16[2592,96]{0,1:T(8,128)(2,1)}, u32[]{:S(2)}) %copy-start.3) | copy-done | bytes 497688
  11.7 0.0 copy-start.4
  11.7 0.9 %copy-done.4 = bf16[768,128]{1,0:T(8,128)(2,1)S(1)} copy-done((bf16[768,128]{1,0:T(8,128)(2,1)S(1)}, bf16[768,128]{1,0:T(8,128)(2,1)}, u32[]{:S(2)}) %copy-start.4) | copy-done | bytes 196632
  12.6 1.4 %prepare.1 = (bf16[2592,128]{1,0:T(8,128)(2,1)S(1)}, bf16[2592,128]{1,0:T(8,128)(2,1)S(1)}, bf16[8,64,256]{2,1,0:T(8,128)(2,1)S(1)}, f32[96,256]{1,0:T(8,128)S(1...) custom-call(bf16[96,256]{1,0:T(8,128)(2,1)S(1)} %bitcast.14, s32[27,256]{1,0:T(8,128)S(1)} %bitcast.16, ...), custom_call_target="tpu_custom_call" | custom-call | flops 2000000000 | bytes 10000000 | tf_op jit(solution)/shard_map/prepare/pallas_call | solution.py:231
  14.0 0.0 collective-permute-done.2.refs_7_
  14.0 0.0 collective-permute-done.1.refs_6_
  14.0 3.2 %forward.1 = (bf16[64,128]{1,0:T(8,128)(2,1)}, bf16[96,256]{1,0:T(8,128)(2,1)S(1)}, bf16[96,16,128]{2,1,0:T(8,128)(2,1)S(1)}, bf16[96,16,128]{2,1,0:T(8,128)(2,1)S(1)}) custom-call(s32[1]{0:T(128)} %bitcast.core_ref, bf16[96,256]{1,0:T(8,128)(2,1)S(1)} %bitcast.15, s32[27,256]{1,0:T(8,128)S(1)} %bitcast.17, bf16[64,128]{1,0:T(8,128)(2,1)S(1)} %copy-done.2, ...), custom_call_target="tpu_custom_call" | custom-call | tf_op jit(solution)/shard_map/forward/pallas_call | solution.py:246
  17.2 1.7 %collective-permute-start.3 = (bf16[96,16,128]{2,1,0:T(8,128)(2,1)S(1)}, bf16[96,16,128]{2,1,0:T(8,128)(2,1)S(1)}, u32[]{:S(2)}, u32[]{:S(2)}) collective-permute-start(bf16[96,16,128]{2,1,0:T(8,128)(2,1)S(1)} %get-tuple-element.42), channel_id=1, source_target_pairs={{0,2},{2,0},{1,3},{3,1},{4,6},{6,4},{5,7},{7,5},{8,10},{10,8},{9,1... | collective-permute-start | bytes 1179656 | tf_op jit(solution)/shard_map/ppermute | solution.py:263
  18.9 1.3 %collective-permute-done.3 = bf16[96,16,128]{2,1,0:T(8,128)(2,1)S(1)} collective-permute-done((bf16[96,16,128]{2,1,0:T(8,128)(2,1)S(1)}, bf16[96,16,128]{2,1,0:T(8,128)(2,1)S(1)}, u32[]{:S(2)}, u32[]{:S(2)}) %collective-permute-start.3) | collective-permute-done | bytes 393248 | tf_op jit(solution)/shard_map/ppermute | solution.py:263
  20.3 0.9 %add_convert_fusion = bf16[96,16,128]{2,1,0:T(8,128)(2,1)} fusion(bf16[96,16,128]{2,1,0:T(8,128)(2,1)S(1)} %collective-permute-done.3, bf16[96,16,128]{2,1,0:T(8,128)(2,1)S(1)} %get-tuple-element.41), kind=kLoop, calls=%fused_computation | loop fusion | flops 786432 | bytes 1179648 | tf_op jit(solution)/shard_map/convert_element_type | solution.py:264
  21.1 3.8 %all-to-all-start = ((bf16[4,24,16,128]{3,2,1,0:T(8,128)(2,1)}), bf16[4,24,16,128]{3,2,1,0:T(8,128)(2,1)S(1)}, u32[]{:S(2)}, u32[]{:S(2)}) async-start(bf16[4,24,16,128]{3,2,1,0:T(8,128)(2,1)} %bitcast.5), calls=%async_computation | async-start | bytes 786432 | tf_op jit(solution)/shard_map/all_to_all | solution.py:287
  24.9 2.3 %backward.1 = (f32[96,256]{1,0:T(8,128)S(1)}, bf16[96,128]{1,0:T(8,128)(2,1)S(1)}, bf16[96,128]{1,0:T(8,128)(2,1)S(1)}, bf16[96,64]{1,0:T(8,128)(2,1)S(1)}) custom-call(s32[27,256]{1,0:T(8,128)S(1)} %bitcast.18, f32[96,256]{1,0:T(8,128)S(1)} %get-tuple-element.37.refs_3_.hgrad_ref, bf16[96,256]{1,0:T(8,128)(2,1)S(1)} %get-tuple-element.45.grad_ref, ...), custom_call_target="tpu_custom_call" | custom-call | flops 3000000000 | bytes 10000000 | tf_op jit(solution)/shard_map/backward/pallas_call | solution.py:267
  27.2 4.8 %all-to-all-done = bf16[4,24,16,128]{3,2,1,0:T(8,128)(2,1)S(1)} async-done(((bf16[4,24,16,128]{3,2,1,0:T(8,128)(2,1)}), bf16[4,24,16,128]{3,2,1,0:T(8,128)(2,1)S(1)}, u32[]{:S(2)}, u32[]{:S(2)}) %all-to-all-start) | async-done | bytes 393248 | tf_op jit(solution)/shard_map/all_to_all | solution.py:287
  32.1 0.7 %reduce_sum.24 = bf16[24,16,128]{2,1,0:T(8,128)(2,1)} reduce(bf16[4,24,16,128]{3,2,1,0:T(8,128)(2,1)S(1)} %all-to-all-done, bf16[]{:T(256)} %constant.7.clone.1), dimensions={0}, to_apply=%region_0.0 | reduce | flops 147456 | bytes 491522 | tf_op jit(solution)/shard_map/reduce_sum | solution.py:289
  32.8 4.8 %all-to-all-start.1 = ((bf16[4,6,16,128]{3,2,1,0:T(8,128)(2,1)}), bf16[4,6,16,128]{3,2,1,0:T(8,128)(2,1)S(1)}, u32[]{:S(2)}, u32[]{:S(2)}) async-start(bf16[4,6,16,128]{3,2,1,0:T(8,128)(2,1)} %bitcast.6), calls=%async_computation.1 | async-start | bytes 196608 | tf_op jit(solution)/shard_map/all_to_all | solution.py:290
  37.6 1.3 %collective-permute-start.4 = (bf16[96,128]{1,0:T(8,128)(2,1)S(1)}, bf16[96,128]{1,0:T(8,128)(2,1)S(1)}, u32[]{:S(2)}, u32[]{:S(2)}) collective-permute-start(bf16[96,128]{1,0:T(8,128)(2,1)S(1)} %get-tuple-element.51), channel_id=1, source_target_pairs={{2,0},{4,2},{6,4},{8,6},{10,8},{12,10},{14,12},{16,14},{18,16},{20... | collective-permute-start | bytes 73736 | tf_op jit(solution)/shard_map/ppermute | solution.py:291
  38.9 3.0 %collective-permute-start.5 = (bf16[96,128]{1,0:T(8,128)(2,1)S(1)}, bf16[96,128]{1,0:T(8,128)(2,1)S(1)}, u32[]{:S(2)}, u32[]{:S(2)}) collective-permute-start(bf16[96,128]{1,0:T(8,128)(2,1)S(1)} %get-tuple-element.52), channel_id=1, source_target_pairs={{0,2},{2,4},{4,6},{6,8},{8,10},{10,12},{12,14},{14,16},{16,18},{18... | collective-permute-start | bytes 73736 | tf_op jit(solution)/shard_map/ppermute | solution.py:291
  41.9 0.0 collective-permute-done.4
  41.9 0.8 %collective-permute-done.5 = bf16[96,128]{1,0:T(8,128)(2,1)S(1)} collective-permute-done((bf16[96,128]{1,0:T(8,128)(2,1)S(1)}, bf16[96,128]{1,0:T(8,128)(2,1)S(1)}, u32[]{:S(2)}, u32[]{:S(2)}) %collective-permute-start.5) | collective-permute-done | bytes 24608 | tf_op jit(solution)/shard_map/ppermute | solution.py:291
  42.7 0.7 all-to-all-done.1
  43.5 13.3 %all_to_all.20 = bf16[4,6,16,128]{3,2,1,0:T(8,128)(2,1)S(1)} all-to-all(bf16[4,6,16,128]{3,2,1,0:T(8,128)(2,1)S(1)} %broadcast_in_dim.6), channel_id=1, replica_groups=mesh['far'=4,'near'=2,'core'=2,'slab'=2] {'far'}, dimensions={0} | all-to-all | bytes 196608 | tf_op jit(solution)/shard_map/all_to_all | solution.py:295
  56.8 0.8 %broadcast_in_dim.15 = bf16[4,24,16,128]{3,2,1,0:T(8,128)(2,1)} broadcast(bf16[24,16,128]{2,1,0:T(8,128)(2,1)S(1)} %bitcast.21), dimensions={1,2,3} | broadcast | bytes 491520 | tf_op jit(solution)/shard_map/broadcast_in_dim | solution.py:308
  57.6 3.5 %all-to-all-start.3 = ((bf16[4,24,16,128]{3,2,1,0:T(8,128)(2,1)}), bf16[4,24,16,128]{3,2,1,0:T(8,128)(2,1)S(1)}, u32[]{:S(2)}, u32[]{:S(2)}) async-start(bf16[4,24,16,128]{3,2,1,0:T(8,128)(2,1)} %broadcast_in_dim.15), calls=%async_computation.3 | async-start | bytes 786432 | tf_op jit(solution)/shard_map/all_to_all | solution.py:309
  61.1 0.1 fusion.1
  61.2 2.0 %collective-permute-start.6 = (bf16[96,64]{1,0:T(8,128)(2,1)S(1)}, bf16[96,64]{1,0:T(8,128)(2,1)S(1)}, u32[]{:S(2)}, u32[]{:S(2)}) collective-permute-start(bf16[96,64]{1,0:T(8,128)(2,1)S(1)} %get-tuple-element.65), channel_id=1, source_target_pairs={{0,1},{1,0},{2,3},{3,2},{4,5},{5,4},{6,7},{7,6},{8,9},{9,8},{10,11... | collective-permute-start | bytes 36872 | tf_op jit(solution)/shard_map/ppermute | solution.py:301
  63.2 4.0 %collective-permute-done.6.refs_1_ = bf16[96,64]{1,0:T(8,128)(2,1)S(1)} collective-permute-done((bf16[96,64]{1,0:T(8,128)(2,1)S(1)}, bf16[96,64]{1,0:T(8,128)(2,1)S(1)}, u32[]{:S(2)}, u32[]{:S(2)}) %collective-permute-start.6) | collective-permute-done | bytes 12320 | tf_op jit(solution)/shard_map/ppermute | solution.py:301
  67.2 0.0 all-to-all-done.3
  67.2 0.0 collective-permute-start.7
  67.2 1.7 %collective-permute-done.7.other_ref = bf16[96,16,128]{2,1,0:T(8,128)(2,1)S(1)} collective-permute-done((bf16[96,16,128]{2,1,0:T(8,128)(2,1)S(1)}, bf16[96,16,128]{2,1,0:T(8,128)(2,1)S(1)}, u32[]{:S(2)}, u32[]{:S(2)}) %collective-permute-start.7) | collective-permute-done | bytes 393248 | tf_op jit(solution)/shard_map/ppermute | solution.py:311
  68.9 1.2 %final.1 = (f32[96,2592]{1,0:T(8,128)}, f32[768,128]{1,0:T(8,128)}, f32[96,256]{1,0:T(8,128)}) custom-call(s32[1]{0:T(128)} %bitcast.core_ref, bf16[96,16,128]{2,1,0:T(8,128)(2,1)S(1)} %bitcast.12, bf16[96,16,128]{2,1,0:T(8,128)(2,1)S(1)} %collective-permute-done.7.other_ref, f32[96,256]{1,0:T(8,128)S(1)} %get-tuple-element.58.base_ref, ...), custom_call_target="tpu_custom_call" | custom-call | tf_op jit(solution)/shard_map/final/pallas_call | solution.py:312
  (3 shorter events, 0.0 us)
Async XLA Ops:
  0.6 10.0 %copy-start.1 = (s32[256,27]{0,1:T(8,128)S(1)}, s32[256,27]{0,1:T(8,128)}, u32[]{:S(2)}) copy-start(s32[256,27]{0,1:T(8,128)} %param.7) | copy-start | bytes 82948
  1.4 9.2 %copy-start = (bf16[256,96]{0,1:T(8,128)(2,1)S(1)}, bf16[256,96]{0,1:T(8,128)(2,1)}, u32[]{:S(2)}) copy-start(bf16[256,96]{0,1:T(8,128)(2,1)} %param.6) | copy-start | bytes 147460
  1.4 9.2 %copy-start.2 = (bf16[64,128]{1,0:T(8,128)(2,1)S(1)}, bf16[64,128]{1,0:T(8,128)(2,1)}, u32[]{:S(2)}) copy-start(bf16[64,128]{1,0:T(8,128)(2,1)} %cgrad_ref.3) | copy-start | bytes 49156
  1.4 4.8 %collective-permute-start = (bf16[96,64]{1,0:T(8,128)(2,1)S(1)}, bf16[96,64]{1,0:T(8,128)(2,1)S(1)}, u32[]{:S(2)}, u32[]{:S(2)}) collective-permute-start(bf16[96,64]{1,0:T(8,128)(2,1)S(1)} %slice.12), channel_id=1, source_target_pairs={{0,1},{1,0},{2,3},{3,2},{4,5},{5,4},{6,7},{7,6},{8,9},{9,8},{10,11... | collective-permute-start | bytes 36872 | tf_op jit(solution)/shard_map/ppermute | solution.py:212
  6.2 4.4 %copy-start.5 = (s32[64,8]{0,1:T(8,128)S(1)}, s32[64,8]{0,1:T(8,128)}, u32[]{:S(2)}) copy-start(s32[64,8]{0,1:T(8,128)} %param.8) | copy-start | bytes 6148
  6.2 7.8 %collective-permute-start.2 = (bf16[96,128]{1,0:T(8,128)(2,1)S(1)}, bf16[96,128]{1,0:T(8,128)(2,1)S(1)}, u32[]{:S(2)}, u32[]{:S(2)}) collective-permute-start(bf16[96,128]{1,0:T(8,128)(2,1)S(1)} %pad_maximum_fusion), channel_id=1, source_target_pairs={{2,0},{4,2},{6,4},{8,6},{10,8},{12,10},{14,12},{16,14},{18,16},{20... | collective-permute-start | bytes 73736 | tf_op jit(solution)/shard_map/ppermute | solution.py:221
  7.5 6.5 %collective-permute-start.1 = (bf16[96,128]{1,0:T(8,128)(2,1)S(1)}, bf16[96,128]{1,0:T(8,128)(2,1)S(1)}, u32[]{:S(2)}, u32[]{:S(2)}) collective-permute-start(bf16[96,128]{1,0:T(8,128)(2,1)S(1)} %pad_maximum_fusion), channel_id=1, source_target_pairs={{0,2},{2,4},{4,6},{6,8},{8,10},{10,12},{12,14},{14,16},{16,18},{18... | collective-permute-start | bytes 73736 | tf_op jit(solution)/shard_map/ppermute | solution.py:221
  10.6 1.0 %copy-start.3 = (bf16[2592,96]{0,1:T(8,128)(2,1)S(1)}, bf16[2592,96]{0,1:T(8,128)(2,1)}, u32[]{:S(2)}) copy-start(bf16[2592,96]{0,1:T(8,128)(2,1)} %param.9) | copy-start | bytes 1492996
  11.7 0.9 %copy-start.4 = (bf16[768,128]{1,0:T(8,128)(2,1)S(1)}, bf16[768,128]{1,0:T(8,128)(2,1)}, u32[]{:S(2)}) copy-start(bf16[768,128]{1,0:T(8,128)(2,1)} %wd_ref.1) | copy-start | bytes 589828
  17.2 3.1 %collective-permute-start.3 = (bf16[96,16,128]{2,1,0:T(8,128)(2,1)S(1)}, bf16[96,16,128]{2,1,0:T(8,128)(2,1)S(1)}, u32[]{:S(2)}, u32[]{:S(2)}) collective-permute-start(bf16[96,16,128]{2,1,0:T(8,128)(2,1)S(1)} %get-tuple-element.42), channel_id=1, source_target_pairs={{0,2},{2,0},{1,3},{3,1},{4,6},{6,4},{5,7},{7,5},{8,10},{10,8},{9,1... | collective-permute-start | bytes 1179656 | tf_op jit(solution)/shard_map/ppermute | solution.py:263
  21.1 10.9 %all-to-all-start = ((bf16[4,24,16,128]{3,2,1,0:T(8,128)(2,1)}), bf16[4,24,16,128]{3,2,1,0:T(8,128)(2,1)S(1)}, u32[]{:S(2)}, u32[]{:S(2)}) async-start(bf16[4,24,16,128]{3,2,1,0:T(8,128)(2,1)} %bitcast.5), calls=%async_computation | async-start | bytes 786432 | tf_op jit(solution)/shard_map/all_to_all | solution.py:287
  32.8 10.6 %all-to-all-start.1 = ((bf16[4,6,16,128]{3,2,1,0:T(8,128)(2,1)}), bf16[4,6,16,128]{3,2,1,0:T(8,128)(2,1)S(1)}, u32[]{:S(2)}, u32[]{:S(2)}) async-start(bf16[4,6,16,128]{3,2,1,0:T(8,128)(2,1)} %bitcast.6), calls=%async_computation.1 | async-start | bytes 196608 | tf_op jit(solution)/shard_map/all_to_all | solution.py:290
  37.6 4.3 %collective-permute-start.4 = (bf16[96,128]{1,0:T(8,128)(2,1)S(1)}, bf16[96,128]{1,0:T(8,128)(2,1)S(1)}, u32[]{:S(2)}, u32[]{:S(2)}) collective-permute-start(bf16[96,128]{1,0:T(8,128)(2,1)S(1)} %get-tuple-element.51), channel_id=1, source_target_pairs={{2,0},{4,2},{6,4},{8,6},{10,8},{12,10},{14,12},{16,14},{18,16},{20... | collective-permute-start | bytes 73736 | tf_op jit(solution)/shard_map/ppermute | solution.py:291
  38.9 3.9 %collective-permute-start.5 = (bf16[96,128]{1,0:T(8,128)(2,1)S(1)}, bf16[96,128]{1,0:T(8,128)(2,1)S(1)}, u32[]{:S(2)}, u32[]{:S(2)}) collective-permute-start(bf16[96,128]{1,0:T(8,128)(2,1)S(1)} %get-tuple-element.52), channel_id=1, source_target_pairs={{0,2},{2,4},{4,6},{6,8},{8,10},{10,12},{12,14},{14,16},{16,18},{18... | collective-permute-start | bytes 73736 | tf_op jit(solution)/shard_map/ppermute | solution.py:291
  57.6 9.6 %all-to-all-start.3 = ((bf16[4,24,16,128]{3,2,1,0:T(8,128)(2,1)}), bf16[4,24,16,128]{3,2,1,0:T(8,128)(2,1)S(1)}, u32[]{:S(2)}, u32[]{:S(2)}) async-start(bf16[4,24,16,128]{3,2,1,0:T(8,128)(2,1)} %broadcast_in_dim.15), calls=%async_computation.3 | async-start | bytes 786432 | tf_op jit(solution)/shard_map/all_to_all | solution.py:309
  61.2 6.0 %collective-permute-start.6 = (bf16[96,64]{1,0:T(8,128)(2,1)S(1)}, bf16[96,64]{1,0:T(8,128)(2,1)S(1)}, u32[]{:S(2)}, u32[]{:S(2)}) collective-permute-start(bf16[96,64]{1,0:T(8,128)(2,1)S(1)} %get-tuple-element.65), channel_id=1, source_target_pairs={{0,1},{1,0},{2,3},{3,2},{4,5},{5,4},{6,7},{7,6},{8,9},{9,8},{10,11... | collective-permute-start | bytes 36872 | tf_op jit(solution)/shard_map/ppermute | solution.py:301
  67.2 1.7 %collective-permute-start.7 = (bf16[96,16,128]{2,1,0:T(8,128)(2,1)S(1)}, bf16[96,16,128]{2,1,0:T(8,128)(2,1)S(1)}, u32[]{:S(2)}, u32[]{:S(2)}) collective-permute-start(bf16[96,16,128]{2,1,0:T(8,128)(2,1)S(1)} %bitcast.11), channel_id=1, source_target_pairs={{0,2},{2,0},{1,3},{3,1},{4,6},{6,4},{5,7},{7,5},{8,10},{10,8},{9,1... | collective-permute-start | bytes 1179656 | tf_op jit(solution)/shard_map/ppermute | solution.py:311

commit v2 on v1

--- a/solution.py
+++ b/solution.py
@@ -61,13 +61,12 @@
     return jnp.concatenate(halo, axis=1)
 
 
-def prepare_kernel(slabs, f_ref, near_ref, down_ref, cgrad_ref, w_ref, wd_ref, *refs):
-    first_ref, rest_ref, pick_ref, hgrad_ref, w_out, wd_out = refs
+def prepare_kernel(
+    slabs, f_ref, near_ref, down_ref, cgrad_ref, wd_ref, first_ref, rest_ref, pick_ref, hgrad_ref
+):
     channels, voxels = f_ref.shape
     offsets = near_ref.shape[0]
     taps, coarse_count = down_ref.shape
-    w_out[...] = w_ref[...]
-    wd_out[...] = wd_ref[...]
     cgrad_t = cgrad_ref[...].astype(F32).T.astype(BF16)
     down = down_ref[...].astype(F32).T
     lane_iota = lax.broadcasted_iota(jnp.int32, (coarse_count, voxels), 1).astype(F32)
@@ -88,9 +87,9 @@
         rest_ref[o * channels : (o + 1) * channels, :] = own[:, LANES:]
 
 
-def forward_kernel(slabs, core_ref, f_ref, near_ref, cgrad_ref, *refs):
-    first_ref, rest_ref, pick_ref, hgrad_ref, w_ref, wd_ref = refs[:6]
-    halo_refs, refs = (refs[6:9], refs[9:]) if slabs == 2 else (refs[6:10], refs[10:])
+def forward_kernel(slabs, core_ref, f_ref, near_ref, cgrad_ref, w_ref, wd_ref, *refs):
+    first_ref, rest_ref, pick_ref, hgrad_ref = refs[:4]
+    halo_refs, refs = (refs[4:7], refs[7:]) if slabs == 2 else (refs[4:8], refs[8:])
     coarse_ref, grad_ref, keep_ref, send_ref, rt, conv_w, down_w = refs
     channels, voxels = f_ref.shape
     offsets = near_ref.shape[0]
@@ -111,10 +110,10 @@
     hidden_t = (f_ref[...].astype(F32) + out_t * sig).astype(BF16)
     grad_t = (hgrad_ref[...] * sig * (1.0 + out_t * (1.0 - sig))).astype(BF16)
     grad_ref[...] = grad_t
-    conv_w[:, :conv_columns] = mm(grad_t, rt[...], NT).astype(BF16)
+    conv_w[:, :conv_columns] = mm(grad_t, rt[...], NT)
     if conv_w.shape[1] > conv_columns:
         slack = conv_w.shape[1] - conv_columns
-        conv_w[:, conv_columns:] = jnp.zeros((channels, slack), BF16)
+        conv_w[:, conv_columns:] = jnp.zeros((channels, slack), F32)
 
     cgrad = cgrad_ref[...]
     coarse = jnp.zeros(cgrad.shape, F32)
@@ -123,7 +122,7 @@
         pick = pick_ref[t]
         coarse += mm(mm(pick, hidden_t, NT).astype(BF16), wd_ref[rows, :])
         picked_t = mm(hidden_t, pick, NT).astype(BF16)
-        down_w[rows, :] = mm(picked_t, cgrad).astype(BF16)
+        down_w[rows, :] = mm(picked_t, cgrad)
     coarse_ref[...] = coarse.astype(BF16)
 
     tiles = payload_tiles(channels, conv_columns, taps)
@@ -137,9 +136,10 @@
                 if i < len(tiles):
                     kind, row, column, _ = tiles[i]
                     source = down_w if kind else conv_w
-                    ref[i % half] = source[row : row + TILE, column : column + LANES]
+                    value = source[row : row + TILE, column : column + LANES]
                 else:
-                    ref[i % half] = jnp.zeros((TILE, LANES), BF16)
+                    value = jnp.zeros((TILE, LANES), F32)
+                ref[i % half] = value.astype(ref.dtype)
 
 
 def backward_kernel(slabs, near_ref, hgrad_ref, grad_ref, w_ref, *refs):
@@ -170,6 +170,37 @@
     side_ref[...] = back_t[:, 2 * group : 2 * group + side_ref.shape[1]]
 
 
+def partner(index, step, count):
+    if count & (count - 1):
+        return (index + step) % count
+    return index ^ step
+
+
+def steps(axis_sizes, step):
+    count = functools.reduce(lambda a, b: a * b, axis_sizes)
+    return [(i, partner(i, step, count)) for i in range(count)]
+
+
+def split_kernel(count, received, index_ref, own_ref, *refs):
+    parts, pieces = refs[:received], refs[received:]
+    length = own_ref.shape[0] // count
+    for step in range(count):
+        chosen = partner(index_ref[0], step, count)
+        rows = pl.ds(chosen * length, length)
+        value = own_ref[rows].astype(F32)
+        for part in parts:
+            value += part[rows].astype(F32)
+        pieces[step][...] = value.astype(pieces[step].dtype)
+
+
+def join_kernel(count, index_ref, *refs):
+    pieces, full_ref = refs[:count], refs[count]
+    length = pieces[0].shape[0]
+    for step in range(count):
+        chosen = partner(index_ref[0], step, count)
+        full_ref[pl.ds(chosen * length, length)] = pieces[step][...]
+
+
 def final_kernel(taps, core_ref, mine_ref, other_ref, base_ref, *refs):
     conv_ref, down_ref, grad_ref = refs[-3:]
     channels, conv_columns = conv_ref.shape
@@ -207,16 +238,32 @@
     up, down = shifts(regions, 1), shifts(regions, -1)
 
     features_t, neighbours_t, w_conv_t = features.T, neighbours.T, w_conv.T
+    smem = pl.BlockSpec(memory_space=pltpu.SMEM)
+    vmem = pl.BlockSpec(memory_space=pltpu.VMEM)
+    params = pltpu.CompilerParams(vmem_limit_bytes=VMEM_BYTES)
+    down_t = down_map.T
     rim = features_t[:, :RIM]
     if slabs == 2:
         side = [lax.ppermute(rim, "slab", swap)]
-        row = [rim, side[0]]
     else:
         side = [
             lax.ppermute(rim, "slab", shifts(slabs, 1)),
             lax.ppermute(rim, "slab", shifts(slabs, -1)),
         ]
-        row = [side[0], rim, side[1]]
+    own = pl.pallas_call(
+        functools.partial(prepare_kernel, slabs),
+        out_shape=(
+            jax.ShapeDtypeStruct((conv_columns, LANES), BF16),
+            jax.ShapeDtypeStruct((conv_columns, voxels - LANES), BF16),
+            jax.ShapeDtypeStruct((taps, coarse_grad.shape[0], voxels), BF16),
+            jax.ShapeDtypeStruct((channels, voxels), F32),
+        ),
+        compiler_params=params,
+        cost_estimate=pl.CostEstimate(flops=2 * 10**9, bytes_accessed=10**7, transcendentals=0),
+        name="prepare",
+    )(features_t, neighbours_t, down_t, coarse_grad, w_down)
+    side, own = lax.optimization_barrier((side, own))
+    row = [rim, side[0]] if slabs == 2 else [side[0], rim, side[1]]
     row = jnp.concatenate(row, axis=1)
     halos = [lax.ppermute(row, RING, up), lax.ppermute(row, RING, down), *side]
 
@@ -225,44 +272,54 @@
     half = piece * around * along
     group, beside = row.shape[1], len(side) * RIM
     far_rows = -(-(2 * group + beside) // LANES) * LANES
-    smem = pl.BlockSpec(memory_space=pltpu.SMEM)
-    vmem = pl.BlockSpec(memory_space=pltpu.VMEM)
-    params = pltpu.CompilerParams(vmem_limit_bytes=VMEM_BYTES)
-    own = pl.pallas_call(
-        functools.partial(prepare_kernel, slabs),
-        out_shape=(
-            jax.ShapeDtypeStruct((conv_columns, LANES), BF16),
-            jax.ShapeDtypeStruct((conv_columns, voxels - LANES), BF16),
-            jax.ShapeDtypeStruct((taps, down_map.shape[0], voxels), BF16),
-            jax.ShapeDtypeStruct((channels, voxels), F32),
-            jax.ShapeDtypeStruct((channels, conv_columns), BF16),
-            jax.ShapeDtypeStruct(w_down.shape, BF16),
-        ),
-        compiler_params=params,
-        cost_estimate=pl.CostEstimate(flops=2 * 10**9, bytes_accessed=10**7, transcendentals=0),
-        name="prepare",
-    )(features_t, neighbours_t, down_map.T, coarse_grad, w_conv_t, w_down)
-    hgrad, w_near = own[3], own[4]
+    hgrad = own[3]
     coarse, grad, keep, send = pl.pallas_call(
         functools.partial(forward_kernel, slabs),
         out_shape=(
             jax.ShapeDtypeStruct(coarse_grad.shape, BF16),
             jax.ShapeDtypeStruct((channels, voxels), BF16),
-            jax.ShapeDtypeStruct((half, TILE, LANES), BF16),
+            jax.ShapeDtypeStruct((half, TILE, LANES), F32),
             jax.ShapeDtypeStruct((half, TILE, LANES), BF16),
         ),
         in_specs=[smem] + [vmem] * (9 + len(halos)),
         scratch_shapes=[
             pltpu.VMEM((conv_columns, voxels), BF16),
-            pltpu.VMEM((channels, -(-conv_columns // LANES) * LANES), BF16),
-            pltpu.VMEM((taps * channels, LANES), BF16),
+            pltpu.VMEM((channels, -(-conv_columns // LANES) * LANES), F32),
+            pltpu.VMEM((taps * channels, LANES), F32),
         ],
         compiler_params=params,
         name="forward",
-    )(core, features_t, neighbours_t, coarse_grad, *own, *halos)
+    )(core, features_t, neighbours_t, coarse_grad, w_conv_t, w_down, *own, *halos)
     got = lax.ppermute(send, "core", swap)
-    pair = (keep.astype(F32) + got.astype(F32)).astype(BF16)
-    pair, grad = lax.optimization_barrier((pair, grad))
+    ring = (lax.axis_size("near"), slabs)
+    line = (along,)
+    here = lax.axis_index(AROUND).astype(jnp.int32).reshape(1)
+    place = lax.axis_index("far").astype(jnp.int32).reshape(1)
+
+    def split(name, index, count, own, received):
+        shape = (own.shape[0] // count, TILE, LANES)
+        return pl.pallas_call(
+            functools.partial(split_kernel, count, len(received)),
+            out_shape=[jax.ShapeDtypeStruct(shape, F32 if i == 0 else BF16) for i in range(count)],
+            in_specs=[smem] + [vmem] * (1 + len(received)),
+            compiler_params=params,
+            name=name,
+        )(index, own, *received)
+
+    def join(name, index, pieces):
+        count = len(pieces)
+        shape = (pieces[0].shape[0] * count, TILE, LANES)
+        return pl.pallas_call(
+            functools.partial(join_kernel, count),
+            out_shape=jax.ShapeDtypeStruct(shape, BF16),
+            in_specs=[smem] + [vmem] * count,
+            compiler_params=params,
+            name=name,
+        )(index, *pieces)
+
+    square, *sent = split("split_pair", here, around, keep, [got])
+    square, sent, grad = lax.optimization_barrier((square, sent, grad))
+    sent = [lax.ppermute(x, AROUND, steps(ring, i + 1)) for i, x in enumerate(sent)]
 
     base, low, high, own_side = pl.pallas_call(
         functools.partial(backward_kernel, slabs),
@@ -282,32 +339,32 @@
         compiler_params=params,
         cost_estimate=pl.CostEstimate(flops=3 * 10**9, bytes_accessed=10**7, transcendentals=0),
         name="backward",
-    )(neighbours_t, hgrad, grad, w_near)
-
-    parts = lax.all_to_all(pair.reshape(around, along * piece, TILE, LANES), AROUND, 0, 0)
-    parts, low, high, own_side, base = lax.optimization_barrier((parts, low, high, own_side, base))
-    square = jnp.sum(parts.astype(F32), axis=0).astype(BF16)
-    parts = lax.all_to_all(square.reshape(along, piece, TILE, LANES), "far", 0, 0)
+    )(neighbours_t, hgrad, grad, w_conv_t)
+
+    sent, low, high, own_side, base = lax.optimization_barrier((sent, low, high, own_side, base))
+    piece, *sent = split("split_square", place, along, square, sent)
+    sent = [lax.ppermute(x, "far", steps(line, i + 1)) for i, x in enumerate(sent)]
+    total = piece + sum(x.astype(F32) for x in sent)
+    total = total.astype(BF16)
+    pieces = [total] + [lax.ppermute(total, "far", steps(line, i)) for i in range(1, along)]
+    square = join("join_square", place, pieces)
+    square, low, high = lax.optimization_barrier((square, low, high))
+    pieces = [square] + [lax.ppermute(square, AROUND, steps(ring, i)) for i in range(1, around)]
     low, high = lax.ppermute(low, RING, down), lax.ppermute(high, RING, up)
-    parts, low, high = lax.optimization_barrier((parts, low, high))
-    total = jnp.sum(parts.astype(F32), axis=0).astype(BF16)
-    total = jnp.broadcast_to(total[None], parts.shape)
-    square = lax.all_to_all(total, "far", 0, 0).reshape(1, along * piece, TILE, LANES)
+    pieces, low, high = lax.optimization_barrier((pieces, low, high))
+    mine = join("join_half", here, pieces)
     row_grad = low.astype(F32) + high.astype(F32)
     columns = [row_grad[:, i : i + RIM] for i in range(0, group, RIM)]
     own = [own_side[:, i : i + RIM].astype(F32) for i in range(0, beside, RIM)]
     if slabs == 2:
         crossing = [(columns[1] + own[0]).astype(BF16)]
         crossing = [lax.ppermute(crossing[0], "slab", swap)]
-        here = columns[0]
+        home = columns[0]
     else:
         crossing = [(columns[0] + own[0]).astype(BF16), (columns[2] + own[1]).astype(BF16)]
         crossing[0] = lax.ppermute(crossing[0], "slab", shifts(slabs, -1))
         crossing[1] = lax.ppermute(crossing[1], "slab", shifts(slabs, 1))
-        here = columns[1]
-    square = jnp.broadcast_to(square, (around,) + square.shape[1:])
-    mine = lax.all_to_all(square, AROUND, 0, 0).reshape(half, TILE, LANES)
-    mine, crossing, here = lax.optimization_barrier((mine, crossing, here))
+        home = columns[1]
     other = lax.ppermute(mine, "core", swap)
     conv_wgrad_t, down_wgrad, grad_input_t = pl.pallas_call(
         functools.partial(final_kernel, taps),
@@ -319,7 +376,7 @@
         in_specs=[smem] + [vmem] * (4 + len(crossing)),
         compiler_params=params,
         name="final",
-    )(core, mine, other, base, here, *crossing)
+    )(core, mine, other, base, home, *crossing)
     return coarse, grad_input_t.T, conv_wgrad_t.T, down_wgrad
 
 

time: 70.7 us -> 63.5 us (0.90)
  blocking collectives: 13.3 us -> 0 us
  waiting for transfers between devices: 15.2 us -> 19.3 us
  starting transfers between devices: 27.4 us -> 31.2 us
  other arithmetic: 1.76 us -> 0.19 us
    ppermute x0 -> x12, starting transfers between devices: none -> 16.4 us  [the longest x3 4.45 us: on_device(): lax.ppermute(x, 'far', steps(line, i + 1))]
    all_to_all x1 -> x0, blocking collectives: 13.3 us -> none  [on_device(): lax.all_to_all(total, 'far', 0, 0).reshape(1, along * piece, TILE, LANES)]
    all_to_all x3 -> x0, starting transfers between devices: 12.1 us -> none  [the longest x1 4.8 us: on_device(): lax.all_to_all(square.reshape(along, piece, TILE, LANES), 'far', 0, 0)]
    ppermute x0 -> x12, waiting for transfers between devices: none -> 10.2 us  [the longest x3 5.04 us: on_device(): lax.ppermute(x, 'far', steps(line, i + 1))]
    all_to_all x3 -> x0, waiting for transfers between devices: 5.5 us -> none  [the longest x1 4.82 us: on_device(): lax.all_to_all(pair.reshape(around, along * piece, TILE, LANES), AROUND,...]
    ppermute x2, waiting for transfers between devices: 0.01 us -> 3.33 us  [on_device(): halos = [lax.ppermute(row, RING, up), lax.ppermute(row, RING, down), *side]]
    ppermute x1, waiting for transfers between devices: 1.8 us -> 0.01 us  [on_device(): side = [lax.ppermute(rim, 'slab', swap)]]
    ppermute x1, waiting for transfers between devices: 1.72 us -> 0.01 us  [on_device(): other = lax.ppermute(mine, 'core', swap)]
  transfers between devices with their start and end apart: 11 -> 20, of which waited for: 7 -> 9; matrix products, arithmetic and copies ran while one was open for 0% -> 0% of each run, Pallas kernels for 5% -> 6%
where the time goes in v2:
time: 63.5 us; the launch traced here: 63.1 us
  starting transfers between devices  31.2 us (49%)
  waiting for transfers between devices  19.3 us (30%)
  Pallas kernels  8.41 us (13%)
  local copies, waits for them, and re-layouts  3.22 us (5%)
  between operations  0.82 us (1%)
    ppermute x3, waiting for transfers between devices, on_device(): lax.ppermute(x, 'far', steps(line, i + 1))  5.04 us
    ppermute x3, starting transfers between devices, on_device(): lax.ppermute(x, 'far', steps(line, i + 1))  4.45 us
    ppermute x3, starting transfers between devices, on_device(): lax.ppermute(total, 'far', steps(line, i))  4.44 us
    ppermute x2, starting transfers between devices, on_device(): low, high = (lax.ppermute(low, RING, down), lax.ppermute(high, RING, up))  4.31 us
    ppermute x3, starting transfers between devices, on_device(): lax.ppermute(x, AROUND, steps(ring, i + 1))  3.99 us
    ppermute x3, starting transfers between devices, on_device(): lax.ppermute(square, AROUND, steps(ring, i))  3.55 us
    ppermute x2, waiting for transfers between devices, on_device(): halos = [lax.ppermute(row, RING, up), lax.ppermute(row, RING, down), *side]  3.33 us
    ppermute x1, waiting for transfers between devices, on_device(): crossing = [lax.ppermute(crossing[0], 'slab', swap)]  3.32 us
  transfers between devices with their start and end apart: 20, of which 9 were waited for; matrix products, arithmetic and copies ran while one was open for 0% of the time, Pallas kernels for 6%

profile of v2, /device:TPU:0, one launch (start us, length us, event | category | flops | bytes accessed | tf_op | source)
XLA Modules:
  0.0 63.1 jit_solution(10886570447273281764)
XLA Ops:
  0.7 0.8 %slice.12 = bf16[96,64]{1,0:T(8,128)(2,1)S(1)} slice(bf16[96,256]{1,0:T(8,128)(2,1)} %bitcast.11), slice={[0:96], [0:64]} | slice | bytes 24576 | tf_op jit(solution)/shard_map/slice | solution.py:245
  1.4 3.0 %collective-permute-start = (bf16[96,64]{1,0:T(8,128)(2,1)S(1)}, bf16[96,64]{1,0:T(8,128)(2,1)S(1)}, u32[]{:S(2)}, u32[]{:S(2)}) collective-permute-start(bf16[96,64]{1,0:T(8,128)(2,1)S(1)} %slice.12), channel_id=1, source_target_pairs={{0,1},{1,0},{2,3},{3,2},{4,5},{5,4},{6,7},{7,6},{8,9},{9,8},{10,11... | collective-permute-start | bytes 36872 | tf_op jit(solution)/shard_map/ppermute | solution.py:247
  4.4 0.9 %copy-done.1 = bf16[768,128]{1,0:T(8,128)(2,1)S(1)} copy-done((bf16[768,128]{1,0:T(8,128)(2,1)S(1)}, bf16[768,128]{1,0:T(8,128)(2,1)}, u32[]{:S(2)}) %copy-start.1) | copy-done | bytes 196632
  5.3 0.8 %copy-done.4 = s32[256,27]{0,1:T(8,128)S(1)} copy-done((s32[256,27]{0,1:T(8,128)S(1)}, s32[256,27]{0,1:T(8,128)}, u32[]{:S(2)}) %copy-start.4) | copy-done | bytes 27672
  6.1 0.7 %copy-done.6 = bf16[64,128]{1,0:T(8,128)(2,1)S(1)} copy-done((bf16[64,128]{1,0:T(8,128)(2,1)S(1)}, bf16[64,128]{1,0:T(8,128)(2,1)}, u32[]{:S(2)}) %copy-start.6) | copy-done | bytes 16408
  6.8 1.4 %prepare.1 = (bf16[2592,128]{1,0:T(8,128)(2,1)S(1)}, bf16[2592,128]{1,0:T(8,128)(2,1)S(1)}, bf16[8,64,256]{2,1,0:T(8,128)(2,1)S(1)}, f32[96,256]{1,0:T(8,128)S(1)}) custom-call(bf16[96,256]{1,0:T(8,128)(2,1)S(1)} %bitcast.12, s32[27,256]{1,0:T(8,128)S(1)} %bitcast.14, s32[8,64]{1,0:T(8,128)S(1)} %bitcast.17, bf16[64,128]{1,0:T(8,128)(2,1)S(1)} %copy-done.6, ...), custom_call_target="tpu_custom_call" | custom-call | flops 2000000000 | bytes 10000000 | tf_op jit(solution)/shard_map/prepare/pallas_call | solution.py:253
  8.2 0.0 collective-permute-done.refs_6_
  8.2 0.0 copy-start.5
  8.3 0.0 copy-start.7
  8.3 0.1 pad_maximum_fusion
  8.4 1.5 %collective-permute-start.1 = (bf16[96,128]{1,0:T(8,128)(2,1)S(1)}, bf16[96,128]{1,0:T(8,128)(2,1)S(1)}, u32[]{:S(2)}, u32[]{:S(2)}) collective-permute-start(bf16[96,128]{1,0:T(8,128)(2,1)S(1)} %pad_maximum_fusion), channel_id=1, source_target_pairs={{0,2},{2,4},{4,6},{6,8},{8,10},{10,12},{12,14},{14,16},{16,18},{18... | collective-permute-start | bytes 73736 | tf_op jit(solution)/shard_map/ppermute | solution.py:268
  9.8 1.3 %collective-permute-start.2 = (bf16[96,128]{1,0:T(8,128)(2,1)S(1)}, bf16[96,128]{1,0:T(8,128)(2,1)S(1)}, u32[]{:S(2)}, u32[]{:S(2)}) collective-permute-start(bf16[96,128]{1,0:T(8,128)(2,1)S(1)} %pad_maximum_fusion), channel_id=1, source_target_pairs={{2,0},{4,2},{6,4},{8,6},{10,8},{12,10},{14,12},{16,14},{18,16},{20... | collective-permute-start | bytes 73736 | tf_op jit(solution)/shard_map/ppermute | solution.py:268
  11.1 0.0 collective-permute-done.1.refs_4_
  11.1 3.3 %collective-permute-done.2.refs_5_ = bf16[96,128]{1,0:T(8,128)(2,1)S(1)} collective-permute-done((bf16[96,128]{1,0:T(8,128)(2,1)S(1)}, bf16[96,128]{1,0:T(8,128)(2,1)S(1)}, u32[]{:S(2)}, u32[]{:S(2)}) %collective-permute-start.2) | collective-permute-done | bytes 24608 | tf_op jit(solution)/shard_map/ppermute | solution.py:268
  14.5 3.3 %forward.1 = (bf16[64,128]{1,0:T(8,128)(2,1)}, bf16[96,256]{1,0:T(8,128)(2,1)S(1)}, f32[96,16,128]{2,1,0:T(8,128)S(1)}, bf16[96,16,128]{2,1,0:T(8,128)(2,1)}) custom-call(s32[1]{0:T(128)} %bitcast.core_ref, bf16[96,256]{1,0:T(8,128)(2,1)S(1)} %bitcast.13, s32[27,256]{1,0:T(8,128)S(1)} %bitcast.15, bf16[64,128]{1,0:T(8,128)(2,1)S(1)} %copy-done.7, ...), custom_call_target="tpu_custom_call" | custom-call | tf_op jit(solution)/shard_map/forward/pallas_call | solution.py:276
  17.8 2.6 %collective-permute-start.3 = (bf16[96,16,128]{2,1,0:T(8,128)(2,1)}, bf16[96,16,128]{2,1,0:T(8,128)(2,1)S(1)}, u32[]{:S(2)}, u32[]{:S(2)}) collective-permute-start(bf16[96,16,128]{2,1,0:T(8,128)(2,1)} %get-tuple-element.64), channel_id=1, source_target_pairs={{0,2},{2,0},{1,3},{3,1},{4,6},{6,4},{5,7},{7,5},{8,10},{10,8},{9,1... | collective-permute-start | bytes 1179656 | tf_op jit(solution)/shard_map/ppermute | solution.py:293
  20.4 1.6 %collective-permute-done.3.refs_0_ = bf16[96,16,128]{2,1,0:T(8,128)(2,1)S(1)} collective-permute-done((bf16[96,16,128]{2,1,0:T(8,128)(2,1)}, bf16[96,16,128]{2,1,0:T(8,128)(2,1)S(1)}, u32[]{:S(2)}, u32[]{:S(2)}) %collective-permute-start.3) | collective-permute-done | bytes 393248 | tf_op jit(solution)/shard_map/ppermute | solution.py:293
  22.0 0.1 split_pair.1
  22.0 0.6 collective-permute-start.4
  22.6 2.4 %collective-permute-start.5 = (bf16[24,16,128]{2,1,0:T(8,128)(2,1)S(1)}, bf16[24,16,128]{2,1,0:T(8,128)(2,1)S(1)}, u32[]{:S(2)}, u32[]{:S(2)}) collective-permute-start(bf16[24,16,128]{2,1,0:T(8,128)(2,1)S(1)} %get-tuple-element.72), channel_id=1, source_target_pairs={{0,4},{1,5},{4,0},{5,1},{2,6},{3,7},{6,2},{7,3},{8,12},{9,13},{12,... | collective-permute-start | bytes 294920 | tf_op jit(solution)/shard_map/ppermute | solution.py:322
  25.1 1.0 %collective-permute-start.6 = (bf16[24,16,128]{2,1,0:T(8,128)(2,1)S(1)}, bf16[24,16,128]{2,1,0:T(8,128)(2,1)S(1)}, u32[]{:S(2)}, u32[]{:S(2)}) collective-permute-start(bf16[24,16,128]{2,1,0:T(8,128)(2,1)S(1)} %get-tuple-element.73), channel_id=1, source_target_pairs={{0,5},{1,4},{4,1},{5,0},{2,7},{3,6},{6,3},{7,2},{8,13},{9,12},{12,... | collective-permute-start | bytes 294920 | tf_op jit(solution)/shard_map/ppermute | solution.py:322
  26.0 2.3 %backward.1 = (f32[96,256]{1,0:T(8,128)S(1)}, bf16[96,128]{1,0:T(8,128)(2,1)S(1)}, bf16[96,128]{1,0:T(8,128)(2,1)S(1)}, bf16[96,64]{1,0:T(8,128)(2,1)S(1)}) custom-call(s32[27,256]{1,0:T(8,128)S(1)} %bitcast.16, f32[96,256]{1,0:T(8,128)S(1)} %get-tuple-element.60.refs_3_.hgrad_ref, bf16[96,256]{1,0:T(8,128)(2,1)S(1)} %get-tuple-element.74.grad_ref, ...), custom_call_target="tpu_custom_call" | custom-call | flops 3000000000 | bytes 10000000 | tf_op jit(solution)/shard_map/backward/pallas_call | solution.py:324
  28.4 0.0 collective-permute-done.4.refs_0_
  28.4 0.0 collective-permute-done.5.refs_1_
  28.4 2.8 %collective-permute-done.6.refs_2_ = bf16[24,16,128]{2,1,0:T(8,128)(2,1)S(1)} collective-permute-done((bf16[24,16,128]{2,1,0:T(8,128)(2,1)S(1)}, bf16[24,16,128]{2,1,0:T(8,128)(2,1)S(1)}, u32[]{:S(2)}, u32[]{:S(2)}) %collective-permute-start.6) | collective-permute-done | bytes 98336 | tf_op jit(solution)/shard_map/ppermute | solution.py:322
  31.2 0.1 split_square.1
  31.2 1.6 %collective-permute-start.7 = (bf16[6,16,128]{2,1,0:T(8,128)(2,1)S(1)}, bf16[6,16,128]{2,1,0:T(8,128)(2,1)S(1)}, u32[]{:S(2)}, u32[]{:S(2)}) collective-permute-start(bf16[6,16,128]{2,1,0:T(8,128)(2,1)S(1)} %get-tuple-element.83), channel_id=1, source_target_pairs={{0,8},{8,0},{16,24},{24,16},{1,9},{9,1},{17,25},{25,17},{2,10},{10... | collective-permute-start | bytes 73736 | tf_op jit(solution)/shard_map/ppermute | solution.py:346
  32.9 1.9 %collective-permute-start.8 = (bf16[6,16,128]{2,1,0:T(8,128)(2,1)S(1)}, bf16[6,16,128]{2,1,0:T(8,128)(2,1)S(1)}, u32[]{:S(2)}, u32[]{:S(2)}) collective-permute-start(bf16[6,16,128]{2,1,0:T(8,128)(2,1)S(1)} %get-tuple-element.84), channel_id=1, source_target_pairs={{0,16},{8,24},{16,0},{24,8},{1,17},{9,25},{17,1},{25,9},{2,18},{10... | collective-permute-start | bytes 73736 | tf_op jit(solution)/shard_map/ppermute | solution.py:346
  34.8 0.9 %collective-permute-start.9 = (bf16[6,16,128]{2,1,0:T(8,128)(2,1)S(1)}, bf16[6,16,128]{2,1,0:T(8,128)(2,1)S(1)}, u32[]{:S(2)}, u32[]{:S(2)}) collective-permute-start(bf16[6,16,128]{2,1,0:T(8,128)(2,1)S(1)} %get-tuple-element.85), channel_id=1, source_target_pairs={{0,24},{8,16},{16,8},{24,0},{1,25},{9,17},{17,9},{25,1},{2,26},{10... | collective-permute-start | bytes 73736 | tf_op jit(solution)/shard_map/ppermute | solution.py:346
  35.7 2.1 %collective-permute-done.8 = bf16[6,16,128]{2,1,0:T(8,128)(2,1)S(1)} collective-permute-done((bf16[6,16,128]{2,1,0:T(8,128)(2,1)S(1)}, bf16[6,16,128]{2,1,0:T(8,128)(2,1)S(1)}, u32[]{:S(2)}, u32[]{:S(2)}) %collective-permute-start.8) | collective-permute-done | bytes 24608 | tf_op jit(solution)/shard_map/ppermute | solution.py:346
  37.7 3.0 %collective-permute-done.9 = bf16[6,16,128]{2,1,0:T(8,128)(2,1)S(1)} collective-permute-done((bf16[6,16,128]{2,1,0:T(8,128)(2,1)S(1)}, bf16[6,16,128]{2,1,0:T(8,128)(2,1)S(1)}, u32[]{:S(2)}, u32[]{:S(2)}) %collective-permute-start.9) | collective-permute-done | bytes 24608 | tf_op jit(solution)/shard_map/ppermute | solution.py:346
  40.7 0.1 collective-permute-start.10
  40.8 1.1 %collective-permute-start.11 = (bf16[6,16,128]{2,1,0:T(8,128)(2,1)S(1)}, bf16[6,16,128]{2,1,0:T(8,128)(2,1)S(1)}, u32[]{:S(2)}, u32[]{:S(2)}) collective-permute-start(bf16[6,16,128]{2,1,0:T(8,128)(2,1)S(1)} %add_convert_fusion.refs_0_), channel_id=1, source_target_pairs={{0,16},{8,24},{16,0},{24,8},{1,17},{9,25},{17,1},{25,9},{2,18},{10... | collective-permute-start | bytes 73736 | tf_op jit(solution)/shard_map/ppermute | solution.py:349
  42.0 3.2 %collective-permute-start.12 = (bf16[6,16,128]{2,1,0:T(8,128)(2,1)S(1)}, bf16[6,16,128]{2,1,0:T(8,128)(2,1)S(1)}, u32[]{:S(2)}, u32[]{:S(2)}) collective-permute-start(bf16[6,16,128]{2,1,0:T(8,128)(2,1)S(1)} %add_convert_fusion.refs_0_), channel_id=1, source_target_pairs={{0,24},{8,16},{16,8},{24,0},{1,25},{9,17},{17,9},{25,1},{2,26},{10... | collective-permute-start | bytes 73736 | tf_op jit(solution)/shard_map/ppermute | solution.py:349
  45.2 0.0 collective-permute-done.10.refs_1_
  45.2 0.4 collective-permute-done.11.refs_2_
  45.6 2.0 %collective-permute-done.12.refs_3_ = bf16[6,16,128]{2,1,0:T(8,128)(2,1)S(1)} collective-permute-done((bf16[6,16,128]{2,1,0:T(8,128)(2,1)S(1)}, bf16[6,16,128]{2,1,0:T(8,128)(2,1)S(1)}, u32[]{:S(2)}, u32[]{:S(2)}) %collective-permute-start.12) | collective-permute-done | bytes 24608 | tf_op jit(solution)/shard_map/ppermute | solution.py:349
  47.6 1.0 %collective-permute-start.13 = (bf16[24,16,128]{2,1,0:T(8,128)(2,1)S(1)}, bf16[24,16,128]{2,1,0:T(8,128)(2,1)S(1)}, u32[]{:S(2)}, u32[]{:S(2)}) collective-permute-start(bf16[24,16,128]{2,1,0:T(8,128)(2,1)S(1)} %join_square.1.refs_0_), channel_id=1, source_target_pairs={{0,1},{1,0},{4,5},{5,4},{2,3},{3,2},{6,7},{7,6},{8,9},{9,8},{12,13... | collective-permute-start | bytes 294920 | tf_op jit(solution)/shard_map/ppermute | solution.py:352
  48.6 1.3 %collective-permute-start.14 = (bf16[24,16,128]{2,1,0:T(8,128)(2,1)S(1)}, bf16[24,16,128]{2,1,0:T(8,128)(2,1)S(1)}, u32[]{:S(2)}, u32[]{:S(2)}) collective-permute-start(bf16[24,16,128]{2,1,0:T(8,128)(2,1)S(1)} %join_square.1.refs_0_), channel_id=1, source_target_pairs={{0,4},{1,5},{4,0},{5,1},{2,6},{3,7},{6,2},{7,3},{8,12},{9,13},{12,... | collective-permute-start | bytes 294920 | tf_op jit(solution)/shard_map/ppermute | solution.py:352
  49.9 1.2 %collective-permute-start.15 = (bf16[24,16,128]{2,1,0:T(8,128)(2,1)S(1)}, bf16[24,16,128]{2,1,0:T(8,128)(2,1)S(1)}, u32[]{:S(2)}, u32[]{:S(2)}) collective-permute-start(bf16[24,16,128]{2,1,0:T(8,128)(2,1)S(1)} %join_square.1.refs_0_), channel_id=1, source_target_pairs={{0,5},{1,4},{4,1},{5,0},{2,7},{3,6},{6,3},{7,2},{8,13},{9,12},{12,... | collective-permute-start | bytes 294920 | tf_op jit(solution)/shard_map/ppermute | solution.py:352
  51.1 1.3 %collective-permute-start.16 = (bf16[96,128]{1,0:T(8,128)(2,1)S(1)}, bf16[96,128]{1,0:T(8,128)(2,1)S(1)}, u32[]{:S(2)}, u32[]{:S(2)}) collective-permute-start(bf16[96,128]{1,0:T(8,128)(2,1)S(1)} %get-tuple-element.89), channel_id=1, source_target_pairs={{2,0},{4,2},{6,4},{8,6},{10,8},{12,10},{14,12},{16,14},{18,16},{20... | collective-permute-start | bytes 73736 | tf_op jit(solution)/shard_map/ppermute | solution.py:353
  52.4 3.0 %collective-permute-start.17 = (bf16[96,128]{1,0:T(8,128)(2,1)S(1)}, bf16[96,128]{1,0:T(8,128)(2,1)S(1)}, u32[]{:S(2)}, u32[]{:S(2)}) collective-permute-start(bf16[96,128]{1,0:T(8,128)(2,1)S(1)} %get-tuple-element.90), channel_id=1, source_target_pairs={{0,2},{2,4},{4,6},{6,8},{8,10},{10,12},{12,14},{14,16},{16,18},{18... | collective-permute-start | bytes 73736 | tf_op jit(solution)/shard_map/ppermute | solution.py:353
  55.5 0.8 %collective-permute-done.17 = bf16[96,128]{1,0:T(8,128)(2,1)S(1)} collective-permute-done((bf16[96,128]{1,0:T(8,128)(2,1)S(1)}, bf16[96,128]{1,0:T(8,128)(2,1)S(1)}, u32[]{:S(2)}, u32[]{:S(2)}) %collective-permute-start.17) | collective-permute-done | bytes 24608 | tf_op jit(solution)/shard_map/ppermute | solution.py:353
  56.4 1.5 %collective-permute-start.18 = (bf16[96,16,128]{2,1,0:T(8,128)(2,1)S(1)}, bf16[96,16,128]{2,1,0:T(8,128)(2,1)S(1)}, u32[]{:S(2)}, u32[]{:S(2)}) collective-permute-start(bf16[96,16,128]{2,1,0:T(8,128)(2,1)S(1)} %join_half.1.mine_ref), channel_id=1, source_target_pairs={{0,2},{2,0},{1,3},{3,1},{4,6},{6,4},{5,7},{7,5},{8,10},{10,8},{9,1... | collective-permute-start | bytes 1179656 | tf_op jit(solution)/shard_map/ppermute | solution.py:368
  57.9 0.1 fusion
  58.0 0.6 collective-permute-start.19
  58.6 3.3 %collective-permute-done.19.refs_1_ = bf16[96,64]{1,0:T(8,128)(2,1)S(1)} collective-permute-done((bf16[96,64]{1,0:T(8,128)(2,1)S(1)}, bf16[96,64]{1,0:T(8,128)(2,1)S(1)}, u32[]{:S(2)}, u32[]{:S(2)}) %collective-permute-start.19) | collective-permute-done | bytes 12320 | tf_op jit(solution)/shard_map/ppermute | solution.py:361
  61.9 1.2 %final.1 = (f32[96,2592]{1,0:T(8,128)}, f32[768,128]{1,0:T(8,128)}, f32[96,256]{1,0:T(8,128)}) custom-call(s32[1]{0:T(128)} %bitcast.core_ref, bf16[96,16,128]{2,1,0:T(8,128)(2,1)S(1)} %join_half.1.mine_ref, bf16[96,16,128]{2,1,0:T(8,128)(2,1)S(1)} %collective-permute-done.18.other_ref, f32[96,256]{1,0:T(8,128)S(1)} %get-tuple-element.95.base_ref, ...), custom_call_target="tpu_custom_call" | custom-call | tf_op jit(solution)/shard_map/final/pallas_call | solution.py:369
  (23 shorter events, 0.1 us)
Async XLA Ops:
  0.6 3.8 %copy-start.3 = (bf16[256,96]{0,1:T(8,128)(2,1)S(1)}, bf16[256,96]{0,1:T(8,128)(2,1)}, u32[]{:S(2)}) copy-start(bf16[256,96]{0,1:T(8,128)(2,1)} %param.6) | copy-start | bytes 147460
  0.6 3.8 %copy-start.8 = (s32[64,8]{0,1:T(8,128)S(1)}, s32[64,8]{0,1:T(8,128)}, u32[]{:S(2)}) copy-start(s32[64,8]{0,1:T(8,128)} %param.8) | copy-start | bytes 6148
  1.4 6.8 %collective-permute-start = (bf16[96,64]{1,0:T(8,128)(2,1)S(1)}, bf16[96,64]{1,0:T(8,128)(2,1)S(1)}, u32[]{:S(2)}, u32[]{:S(2)}) collective-permute-start(bf16[96,64]{1,0:T(8,128)(2,1)S(1)} %slice.12), channel_id=1, source_target_pairs={{0,1},{1,0},{2,3},{3,2},{4,5},{5,4},{6,7},{7,6},{8,9},{9,8},{10,11... | collective-permute-start | bytes 36872 | tf_op jit(solution)/shard_map/ppermute | solution.py:247
  4.4 0.9 %copy-start.1 = (bf16[768,128]{1,0:T(8,128)(2,1)S(1)}, bf16[768,128]{1,0:T(8,128)(2,1)}, u32[]{:S(2)}) copy-start(bf16[768,128]{1,0:T(8,128)(2,1)} %wd_ref.3) | copy-start | bytes 589828
  5.3 0.8 %copy-start.4 = (s32[256,27]{0,1:T(8,128)S(1)}, s32[256,27]{0,1:T(8,128)}, u32[]{:S(2)}) copy-start(s32[256,27]{0,1:T(8,128)} %param.7) | copy-start | bytes 82948
  6.1 0.7 %copy-start.6 = (bf16[64,128]{1,0:T(8,128)(2,1)S(1)}, bf16[64,128]{1,0:T(8,128)(2,1)}, u32[]{:S(2)}) copy-start(bf16[64,128]{1,0:T(8,128)(2,1)} %cgrad_ref.3) | copy-start | bytes 49156
  6.8 7.6 %copy-start = (bf16[2592,96]{0,1:T(8,128)(2,1)S(1)}, bf16[2592,96]{0,1:T(8,128)(2,1)}, u32[]{:S(2)}) copy-start(bf16[2592,96]{0,1:T(8,128)(2,1)} %param.9) | copy-start | bytes 1492996
  6.8 7.6 %copy-start.2 = (bf16[768,128]{1,0:T(8,128)(2,1)S(1)}, bf16[768,128]{1,0:T(8,128)(2,1)}, u32[]{:S(2)}) copy-start(bf16[768,128]{1,0:T(8,128)(2,1)} %wd_ref.3) | copy-start | bytes 589828
  8.2 6.2 %copy-start.5 = (s32[256,27]{0,1:T(8,128)S(1)}, s32[256,27]{0,1:T(8,128)}, u32[]{:S(2)}) copy-start(s32[256,27]{0,1:T(8,128)} %param.7) | copy-start | bytes 82948
  8.3 6.2 %copy-start.7 = (bf16[64,128]{1,0:T(8,128)(2,1)S(1)}, bf16[64,128]{1,0:T(8,128)(2,1)}, u32[]{:S(2)}) copy-start(bf16[64,128]{1,0:T(8,128)(2,1)} %cgrad_ref.3) | copy-start | bytes 49156
  8.4 2.8 %collective-permute-start.1 = (bf16[96,128]{1,0:T(8,128)(2,1)S(1)}, bf16[96,128]{1,0:T(8,128)(2,1)S(1)}, u32[]{:S(2)}, u32[]{:S(2)}) collective-permute-start(bf16[96,128]{1,0:T(8,128)(2,1)S(1)} %pad_maximum_fusion), channel_id=1, source_target_pairs={{0,2},{2,4},{4,6},{6,8},{8,10},{10,12},{12,14},{14,16},{16,18},{18... | collective-permute-start | bytes 73736 | tf_op jit(solution)/shard_map/ppermute | solution.py:268
  9.8 4.6 %collective-permute-start.2 = (bf16[96,128]{1,0:T(8,128)(2,1)S(1)}, bf16[96,128]{1,0:T(8,128)(2,1)S(1)}, u32[]{:S(2)}, u32[]{:S(2)}) collective-permute-start(bf16[96,128]{1,0:T(8,128)(2,1)S(1)} %pad_maximum_fusion), channel_id=1, source_target_pairs={{2,0},{4,2},{6,4},{8,6},{10,8},{12,10},{14,12},{16,14},{18,16},{20... | collective-permute-start | bytes 73736 | tf_op jit(solution)/shard_map/ppermute | solution.py:268
  17.8 4.2 %collective-permute-start.3 = (bf16[96,16,128]{2,1,0:T(8,128)(2,1)}, bf16[96,16,128]{2,1,0:T(8,128)(2,1)S(1)}, u32[]{:S(2)}, u32[]{:S(2)}) collective-permute-start(bf16[96,16,128]{2,1,0:T(8,128)(2,1)} %get-tuple-element.64), channel_id=1, source_target_pairs={{0,2},{2,0},{1,3},{3,1},{4,6},{6,4},{5,7},{7,5},{8,10},{10,8},{9,1... | collective-permute-start | bytes 1179656 | tf_op jit(solution)/shard_map/ppermute | solution.py:293
  22.0 6.3 %collective-permute-start.4 = (bf16[24,16,128]{2,1,0:T(8,128)(2,1)S(1)}, bf16[24,16,128]{2,1,0:T(8,128)(2,1)S(1)}, u32[]{:S(2)}, u32[]{:S(2)}) collective-permute-start(bf16[24,16,128]{2,1,0:T(8,128)(2,1)S(1)} %get-tuple-element.71), channel_id=1, source_target_pairs={{0,1},{1,0},{4,5},{5,4},{2,3},{3,2},{6,7},{7,6},{8,9},{9,8},{12,13... | collective-permute-start | bytes 294920 | tf_op jit(solution)/shard_map/ppermute | solution.py:322
  22.6 5.7 %collective-permute-start.5 = (bf16[24,16,128]{2,1,0:T(8,128)(2,1)S(1)}, bf16[24,16,128]{2,1,0:T(8,128)(2,1)S(1)}, u32[]{:S(2)}, u32[]{:S(2)}) collective-permute-start(bf16[24,16,128]{2,1,0:T(8,128)(2,1)S(1)} %get-tuple-element.72), channel_id=1, source_target_pairs={{0,4},{1,5},{4,0},{5,1},{2,6},{3,7},{6,2},{7,3},{8,12},{9,13},{12,... | collective-permute-start | bytes 294920 | tf_op jit(solution)/shard_map/ppermute | solution.py:322
  25.1 6.1 %collective-permute-start.6 = (bf16[24,16,128]{2,1,0:T(8,128)(2,1)S(1)}, bf16[24,16,128]{2,1,0:T(8,128)(2,1)S(1)}, u32[]{:S(2)}, u32[]{:S(2)}) collective-permute-start(bf16[24,16,128]{2,1,0:T(8,128)(2,1)S(1)} %get-tuple-element.73), channel_id=1, source_target_pairs={{0,5},{1,4},{4,1},{5,0},{2,7},{3,6},{6,3},{7,2},{8,13},{9,12},{12,... | collective-permute-start | bytes 294920 | tf_op jit(solution)/shard_map/ppermute | solution.py:322
  31.2 4.5 %collective-permute-start.7 = (bf16[6,16,128]{2,1,0:T(8,128)(2,1)S(1)}, bf16[6,16,128]{2,1,0:T(8,128)(2,1)S(1)}, u32[]{:S(2)}, u32[]{:S(2)}) collective-permute-start(bf16[6,16,128]{2,1,0:T(8,128)(2,1)S(1)} %get-tuple-element.83), channel_id=1, source_target_pairs={{0,8},{8,0},{16,24},{24,16},{1,9},{9,1},{17,25},{25,17},{2,10},{10... | collective-permute-start | bytes 73736 | tf_op jit(solution)/shard_map/ppermute | solution.py:346
  32.9 4.9 %collective-permute-start.8 = (bf16[6,16,128]{2,1,0:T(8,128)(2,1)S(1)}, bf16[6,16,128]{2,1,0:T(8,128)(2,1)S(1)}, u32[]{:S(2)}, u32[]{:S(2)}) collective-permute-start(bf16[6,16,128]{2,1,0:T(8,128)(2,1)S(1)} %get-tuple-element.84), channel_id=1, source_target_pairs={{0,16},{8,24},{16,0},{24,8},{1,17},{9,25},{17,1},{25,9},{2,18},{10... | collective-permute-start | bytes 73736 | tf_op jit(solution)/shard_map/ppermute | solution.py:346
  34.8 6.0 %collective-permute-start.9 = (bf16[6,16,128]{2,1,0:T(8,128)(2,1)S(1)}, bf16[6,16,128]{2,1,0:T(8,128)(2,1)S(1)}, u32[]{:S(2)}, u32[]{:S(2)}) collective-permute-start(bf16[6,16,128]{2,1,0:T(8,128)(2,1)S(1)} %get-tuple-element.85), channel_id=1, source_target_pairs={{0,24},{8,16},{16,8},{24,0},{1,25},{9,17},{17,9},{25,1},{2,26},{10... | collective-permute-start | bytes 73736 | tf_op jit(solution)/shard_map/ppermute | solution.py:346
  40.7 4.5 %collective-permute-start.10 = (bf16[6,16,128]{2,1,0:T(8,128)(2,1)S(1)}, bf16[6,16,128]{2,1,0:T(8,128)(2,1)S(1)}, u32[]{:S(2)}, u32[]{:S(2)}) collective-permute-start(bf16[6,16,128]{2,1,0:T(8,128)(2,1)S(1)} %add_convert_fusion.refs_0_), channel_id=1, source_target_pairs={{0,8},{8,0},{16,24},{24,16},{1,9},{9,1},{17,25},{25,17},{2,10},{10... | collective-permute-start | bytes 73736 | tf_op jit(solution)/shard_map/ppermute | solution.py:349
  40.8 4.8 %collective-permute-start.11 = (bf16[6,16,128]{2,1,0:T(8,128)(2,1)S(1)}, bf16[6,16,128]{2,1,0:T(8,128)(2,1)S(1)}, u32[]{:S(2)}, u32[]{:S(2)}) collective-permute-start(bf16[6,16,128]{2,1,0:T(8,128)(2,1)S(1)} %add_convert_fusion.refs_0_), channel_id=1, source_target_pairs={{0,16},{8,24},{16,0},{24,8},{1,17},{9,25},{17,1},{25,9},{2,18},{10... | collective-permute-start | bytes 73736 | tf_op jit(solution)/shard_map/ppermute | solution.py:349
  42.0 5.6 %collective-permute-start.12 = (bf16[6,16,128]{2,1,0:T(8,128)(2,1)S(1)}, bf16[6,16,128]{2,1,0:T(8,128)(2,1)S(1)}, u32[]{:S(2)}, u32[]{:S(2)}) collective-permute-start(bf16[6,16,128]{2,1,0:T(8,128)(2,1)S(1)} %add_convert_fusion.refs_0_), channel_id=1, source_target_pairs={{0,24},{8,16},{16,8},{24,0},{1,25},{9,17},{17,9},{25,1},{2,26},{10... | collective-permute-start | bytes 73736 | tf_op jit(solution)/shard_map/ppermute | solution.py:349
  47.6 8.7 %collective-permute-start.13 = (bf16[24,16,128]{2,1,0:T(8,128)(2,1)S(1)}, bf16[24,16,128]{2,1,0:T(8,128)(2,1)S(1)}, u32[]{:S(2)}, u32[]{:S(2)}) collective-permute-start(bf16[24,16,128]{2,1,0:T(8,128)(2,1)S(1)} %join_square.1.refs_0_), channel_id=1, source_target_pairs={{0,1},{1,0},{4,5},{5,4},{2,3},{3,2},{6,7},{7,6},{8,9},{9,8},{12,13... | collective-permute-start | bytes 294920 | tf_op jit(solution)/shard_map/ppermute | solution.py:352
  48.6 7.7 %collective-permute-start.14 = (bf16[24,16,128]{2,1,0:T(8,128)(2,1)S(1)}, bf16[24,16,128]{2,1,0:T(8,128)(2,1)S(1)}, u32[]{:S(2)}, u32[]{:S(2)}) collective-permute-start(bf16[24,16,128]{2,1,0:T(8,128)(2,1)S(1)} %join_square.1.refs_0_), channel_id=1, source_target_pairs={{0,4},{1,5},{4,0},{5,1},{2,6},{3,7},{6,2},{7,3},{8,12},{9,13},{12,... | collective-permute-start | bytes 294920 | tf_op jit(solution)/shard_map/ppermute | solution.py:352
  49.9 6.4 %collective-permute-start.15 = (bf16[24,16,128]{2,1,0:T(8,128)(2,1)S(1)}, bf16[24,16,128]{2,1,0:T(8,128)(2,1)S(1)}, u32[]{:S(2)}, u32[]{:S(2)}) collective-permute-start(bf16[24,16,128]{2,1,0:T(8,128)(2,1)S(1)} %join_square.1.refs_0_), channel_id=1, source_target_pairs={{0,5},{1,4},{4,1},{5,0},{2,7},{3,6},{6,3},{7,2},{8,13},{9,12},{12,... | collective-permute-start | bytes 294920 | tf_op jit(solution)/shard_map/ppermute | solution.py:352
  51.1 4.3 %collective-permute-start.16 = (bf16[96,128]{1,0:T(8,128)(2,1)S(1)}, bf16[96,128]{1,0:T(8,128)(2,1)S(1)}, u32[]{:S(2)}, u32[]{:S(2)}) collective-permute-start(bf16[96,128]{1,0:T(8,128)(2,1)S(1)} %get-tuple-element.89), channel_id=1, source_target_pairs={{2,0},{4,2},{6,4},{8,6},{10,8},{12,10},{14,12},{16,14},{18,16},{20... | collective-permute-start | bytes 73736 | tf_op jit(solution)/shard_map/ppermute | solution.py:353
  52.4 3.9 %collective-permute-start.17 = (bf16[96,128]{1,0:T(8,128)(2,1)S(1)}, bf16[96,128]{1,0:T(8,128)(2,1)S(1)}, u32[]{:S(2)}, u32[]{:S(2)}) collective-permute-start(bf16[96,128]{1,0:T(8,128)(2,1)S(1)} %get-tuple-element.90), channel_id=1, source_target_pairs={{0,2},{2,4},{4,6},{6,8},{8,10},{10,12},{12,14},{14,16},{16,18},{18... | collective-permute-start | bytes 73736 | tf_op jit(solution)/shard_map/ppermute | solution.py:353
  56.4 5.5 %collective-permute-start.18 = (bf16[96,16,128]{2,1,0:T(8,128)(2,1)S(1)}, bf16[96,16,128]{2,1,0:T(8,128)(2,1)S(1)}, u32[]{:S(2)}, u32[]{:S(2)}) collective-permute-start(bf16[96,16,128]{2,1,0:T(8,128)(2,1)S(1)} %join_half.1.mine_ref), channel_id=1, source_target_pairs={{0,2},{2,0},{1,3},{3,1},{4,6},{6,4},{5,7},{7,5},{8,10},{10,8},{9,1... | collective-permute-start | bytes 1179656 | tf_op jit(solution)/shard_map/ppermute | solution.py:368
  58.0 3.9 %collective-permute-start.19 = (bf16[96,64]{1,0:T(8,128)(2,1)S(1)}, bf16[96,64]{1,0:T(8,128)(2,1)S(1)}, u32[]{:S(2)}, u32[]{:S(2)}) collective-permute-start(bf16[96,64]{1,0:T(8,128)(2,1)S(1)} %get-tuple-element.102), channel_id=1, source_target_pairs={{0,1},{1,0},{2,3},{3,2},{4,5},{5,4},{6,7},{7,6},{8,9},{9,8},{10,11... | collective-permute-start | bytes 36872 | tf_op jit(solution)/shard_map/ppermute | solution.py:361

commit v3 on v1

v3 whole, which is shorter than its diff:
```python
import functools

import jax
import jax.numpy as jnp
from jax import lax
from jax.experimental import pallas as pl
from jax.experimental.pallas import tpu as pltpu
from jax.sharding import Mesh, PartitionSpec as P

SPLIT = ("far", "near", "core", "slab")
RING = ("far", "near", "core")
RIM = 64
LANES = 128
TILE = 16
F32 = jnp.float32
BF16 = jnp.bfloat16
NN = (((1,), (0,)), ((), ()))
NT = (((1,), (1,)), ((), ()))
VMEM_BYTES = 20 * 2**20


def mm(a, b, dims=NN):
    return lax.dot_general(a, b, dims, preferred_element_type=F32)


def table_lanes(neighbours, voxels, slabs, core):
    code = neighbours // voxels
    slot = neighbours - code * voxels
    row = code // 3
    col = code - row * 3
    if slabs == 2:
        rims = 2
        place = jnp.where(col == 1, 0, 1)
        beside = 0
    else:
        rims = 3
        place = col
        beside = col // 2
    group = jnp.abs(row // 2 + core - 1)
    rim = jnp.where(row == 1, 2 * rims + beside, group * rims + place)
    lane = jnp.where(code == 4, slot, voxels + rim * RIM + slot)
    return jnp.where(code > 8, -1, lane)


def payload_tiles(channels, conv_columns, taps):
    tiles = []
    for column in range(0, conv_columns, LANES):
        for row in range(0, channels, TILE):
            tiles.append((0, row, column, min(LANES, conv_columns - column)))
    for row in range(0, taps * channels, TILE):
        tiles.append((1, row, 0, LANES))
    return tiles


def padded_halo(halo_refs):
    halo = [h[...] for h in halo_refs]
    width = sum(h.shape[1] for h in halo)
    slack = -width % LANES
    if slack:
        halo.append(jnp.zeros((halo[0].shape[0], slack), BF16))
    return jnp.concatenate(halo, axis=1)


def gather_kernel(slabs, f_ref, near_ref, first_ref, rest_ref):
    channels, voxels = f_ref.shape
    table_t = f_ref[...]
    lanes = table_lanes(near_ref[...], voxels, slabs, 0)
    near_iota = lax.broadcasted_iota(jnp.int32, (voxels, voxels), 0)
    for o in range(near_ref.shape[0]):
        near = jnp.where(near_iota == lanes[o : o + 1, :], 1.0, 0.0).astype(BF16)
        own = mm(table_t, near).astype(BF16)
        first_ref[o * channels : (o + 1) * channels, :] = own[:, :LANES]
        rest_ref[o * channels : (o + 1) * channels, :] = own[:, LANES:]


def taps_kernel(down_ref, cgrad_ref, wd_ref, pick_ref, hgrad_ref):
    channels, voxels = hgrad_ref.shape
    taps, coarse_count = down_ref.shape
    cgrad_t = cgrad_ref[...].astype(F32).T.astype(BF16)
    down = down_ref[...].astype(F32).T
    lane_iota = lax.broadcasted_iota(jnp.int32, (coarse_count, voxels), 1).astype(F32)
    hgrad_t = jnp.zeros((channels, voxels), F32)
    for t in range(taps):
        pick = jnp.where(lane_iota == down[:, t : t + 1], 1.0, 0.0).astype(BF16)
        pick_ref[t] = pick
        wd = wd_ref[t * channels : (t + 1) * channels, :]
        hgrad_t += mm(wd, mm(cgrad_t, pick).astype(BF16))
    hgrad_ref[...] = hgrad_t


def forward_kernel(slabs, core_ref, f_ref, near_ref, cgrad_ref, w_ref, wd_ref, *refs):
    first_ref, rest_ref, pick_ref, hgrad_ref = refs[:4]
    halo_refs, refs = (refs[4:7], refs[7:]) if slabs == 2 else (refs[4:8], refs[8:])
    coarse_ref, grad_ref, keep_ref, send_ref, rt, conv_w, down_w = refs
    channels, voxels = f_ref.shape
    offsets = near_ref.shape[0]
    taps = pick_ref.shape[0]
    conv_columns = offsets * channels
    halo_t = padded_halo(halo_refs)
    lanes = table_lanes(near_ref[:, :LANES], voxels, slabs, core_ref[0])
    far_iota = lax.broadcasted_iota(jnp.int32, (halo_t.shape[1], LANES), 0) + voxels
    for o in range(offsets):
        rows = slice(o * channels, (o + 1) * channels)
        away = jnp.where(far_iota == lanes[o : o + 1, :], 1.0, 0.0).astype(BF16)
        first = first_ref[rows, :].astype(F32) + mm(halo_t, away)
        rt[rows, :LANES] = first.astype(BF16)
        rt[rows, LANES:] = rest_ref[rows, :]

    out_t = mm(w_ref[...], rt[...])
    sig = 1.0 / (1.0 + jnp.exp(-out_t))
    hidden_t = (f_ref[...].astype(F32) + out_t * sig).astype(BF16)
    grad_t = (hgrad_ref[...] * sig * (1.0 + out_t * (1.0 - sig))).astype(BF16)
    grad_ref[...] = grad_t
    conv_w[:, :conv_columns] = mm(grad_t, rt[...], NT)
    if conv_w.shape[1] > conv_columns:
        slack = conv_w.shape[1] - conv_columns
        conv_w[:, conv_columns:] = jnp.zeros((channels, slack), F32)

    cgrad = cgrad_ref[...]
    coarse = jnp.zeros(cgrad.shape, F32)
    for t in range(taps):
        rows = slice(t * channels, (t + 1) * channels)
        pick = pick_ref[t]
        coarse += mm(mm(pick, hidden_t, NT).astype(BF16), wd_ref[rows, :])
        picked_t = mm(hidden_t, pick, NT).astype(BF16)
        down_w[rows, :] = mm(picked_t, cgrad)
    coarse_ref[...] = coarse.astype(BF16)

    tiles = payload_tiles(channels, conv_columns, taps)
    half = keep_ref.shape[0]
    for core in range(2):

        @pl.when(core_ref[0] == core)
        def _(core=core):
            for i in range(2 * half):
                ref = keep_ref if i // half == core else send_ref
                if i < len(tiles):
                    kind, row, column, _ = tiles[i]
                    source = down_w if kind else conv_w
                    value = source[row : row + TILE, column : column + LANES]
                else:
                    value = jnp.zeros((TILE, LANES), F32)
                ref[i % half] = value.astype(ref.dtype)


def backward_kernel(slabs, core_ref, near_ref, hgrad_ref, grad_ref, w_ref, *refs):
    base_ref, mate_ref, cross_ref, side_ref, drt, drt_far, hot, far, w_back = refs
    channels, voxels = hgrad_ref.shape
    offsets = near_ref.shape[0]
    group = mate_ref.shape[1]
    lanes = table_lanes(near_ref[...], voxels, slabs, core_ref[0])
    near_iota = lax.broadcasted_iota(jnp.int32, (voxels, voxels), 0)
    far_iota = lax.broadcasted_iota(jnp.int32, (far.shape[0], LANES), 0) + voxels
    w_back[:, :channels] = w_ref[...].astype(F32).T.astype(BF16)
    w_back[:, channels:] = jnp.zeros((offsets * channels, LANES - channels), BF16)
    slack = jnp.zeros((LANES - channels, voxels), BF16)
    grad_pad = jnp.concatenate([grad_ref[...], slack], axis=0)
    for o in range(offsets):
        lane = lanes[o : o + 1, :]
        near = jnp.where(near_iota == lane, 1.0, 0.0).astype(BF16)
        away = jnp.where(far_iota == lane[:, :LANES], 1.0, 0.0).astype(BF16)
        hot[:, o * voxels : (o + 1) * voxels] = near
        far[:, o * LANES : (o + 1) * LANES] = away
        spread = mm(w_back[o * channels : (o + 1) * channels, :], grad_pad).astype(BF16)
        drt[:, o * voxels : (o + 1) * voxels] = spread
        drt_far[:, o * LANES : (o + 1) * LANES] = spread[:, :LANES]
    base_ref[...] = hgrad_ref[...] + mm(drt[...], hot[...], NT)
    back_t = mm(drt_far[...], far[...], NT).astype(BF16)
    mate_ref[...] = back_t[:, :group]
    cross_ref[...] = back_t[:, group : 2 * group]
    side_ref[...] = back_t[:, 2 * group : 2 * group + side_ref.shape[1]]


def fold_kernel(bit_ref, own_ref, got_ref, keep_ref, send_ref):
    half = keep_ref.shape[0]
    for ref, part in ((keep_ref, bit_ref[0]), (send_ref, 1 - bit_ref[0])):
        rows = pl.ds(part * half, half)
        ref[...] = (own_ref[rows] + got_ref[rows].astype(F32)).astype(ref.dtype)


def join_kernel(bit_ref, own_ref, got_ref, full_ref):
    half = own_ref.shape[0]
    full_ref[pl.ds(bit_ref[0] * half, half)] = own_ref[...]
    full_ref[pl.ds((1 - bit_ref[0]) * half, half)] = got_ref[...]


def final_kernel(taps, core_ref, mine_ref, other_ref, base_ref, *refs):
    conv_ref, down_ref, grad_ref = refs[-3:]
    channels, conv_columns = conv_ref.shape
    half = mine_ref.shape[0]
    total = refs[0][...].astype(F32)
    for ref in refs[1:-3]:
        total += ref[...].astype(F32)
    grad_ref[:, RIM:] = base_ref[:, RIM:]
    grad_ref[:, :RIM] = base_ref[:, :RIM] + total
    for core in range(2):

        @pl.when(core_ref[0] == core)
        def _(core=core):
            for i, tile in enumerate(payload_tiles(channels, conv_columns, taps)):
                kind, row, column, columns = tile
                source = mine_ref if i // half == core else other_ref
                value = source[i % half].astype(F32)
                target = down_ref if kind else conv_ref
                target[row : row + TILE, column : column + columns] = value[:, :columns]


def shifts(count, step):
    return [(i, i + step) for i in range(count) if 0 <= i + step < count]


def chip_pairs(regions):
    mates = [(i, i ^ 1) for i in range(regions)]
    cross = [(i, i + 1) for i in range(1, regions - 1, 2)]
    return mates, cross + [(b, a) for a, b in cross]


def square_bits(nears, slabs, core):
    near = [("near", i) for i in range(nears.bit_length() - 1)]
    slab = [("slab", i) for i in range(slabs.bit_length() - 1)]
    return near + slab if core == 0 else slab + near


def bit_pairs(sizes, orders, phase):
    pairs = []
    for index in range(functools.reduce(lambda a, b: a * b, sizes.values())):
        place, left = {}, index
        for axis in reversed(SPLIT):
            left, place[axis] = divmod(left, sizes[axis])
        axis, bit = orders[place["core"]][phase]
        place[axis] ^= 1 << bit
        other = 0
        for name in SPLIT:
            other = other * sizes[name] + place[name]
        pairs.append((index, other))
    return pairs


def on_device(features, neighbours, down_map, w_conv, w_down, coarse_grad):
    sizes = {axis: lax.axis_size(axis) for axis in SPLIT}
    regions, slabs = sizes["far"] * sizes["near"] * sizes["core"], sizes["slab"]
    voxels, channels = features.shape
    offsets, taps = neighbours.shape[1], down_map.shape[1]
    conv_columns = offsets * channels
    core = lax.axis_index("core").astype(jnp.int32).reshape(1)
    swap = [(0, 1), (1, 0)]
    mates, crossings = chip_pairs(regions)
    orders = [square_bits(sizes["near"], slabs, c) for c in range(2)]
    phases = len(orders[0])
    bits = []
    for phase in range(phases):
        chosen = [(lax.axis_index(axis) >> bit) & 1 for axis, bit in (o[phase] for o in orders)]
        bits.append(jnp.where(core == 0, *chosen).astype(jnp.int32))

    smem = pl.BlockSpec(memory_space=pltpu.SMEM)
    vmem = pl.BlockSpec(memory_space=pltpu.VMEM)
    params = pltpu.CompilerParams(vmem_limit_bytes=VMEM_BYTES)
    light = pl.CostEstimate(flops=2 * 10**9, bytes_accessed=10**7, transcendentals=0)
    features_t, neighbours_t, w_conv_t = features.T, neighbours.T, w_conv.T
    rim = features_t[:, :RIM]
    if slabs == 2:
        side = [lax.ppermute(rim, "slab", swap)]
    else:
        side = [
            lax.ppermute(rim, "slab", shifts(slabs, 1)),
            lax.ppermute(rim, "slab", shifts(slabs, -1)),
        ]
    own = pl.pallas_call(
        functools.partial(gather_kernel, slabs),
        out_shape=(
            jax.ShapeDtypeStruct((conv_columns, LANES), BF16),
            jax.ShapeDtypeStruct((conv_columns, voxels - LANES), BF16),
        ),
        compiler_params=params,
        cost_estimate=light,
        name="gather",
    )(features_t, neighbours_t)
    side, own = lax.optimization_barrier((side, own))
    row = [rim, side[0]] if slabs == 2 else [side[0], rim, side[1]]
    row = jnp.concatenate(row, axis=1)
    cross = lax.ppermute(row, RING, crossings)
    mate = lax.ppermute(row, RING, mates)
    row, down_t = lax.optimization_barrier((row, down_map.T))
    pick, hgrad = pl.pallas_call(
        taps_kernel,
        out_shape=(
            jax.ShapeDtypeStruct((taps, coarse_grad.shape[0], voxels), BF16),
            jax.ShapeDtypeStruct((channels, voxels), F32),
        ),
        compiler_params=params,
        cost_estimate=light,
        name="taps",
    )(down_t, coarse_grad, w_down)
    halos = [mate, cross, *side]

    tiles = len(payload_tiles(channels, conv_columns, taps))
    squares = 1 << phases
    half = -(-tiles // (2 * squares)) * squares
    group, beside = row.shape[1], len(side) * RIM
    far_rows = -(-(2 * group + beside) // LANES) * LANES
    coarse, grad, keep, send = pl.pallas_call(
        functools.partial(forward_kernel, slabs),
        out_shape=(
            jax.ShapeDtypeStruct(coarse_grad.shape, BF16),
            jax.ShapeDtypeStruct((channels, voxels), BF16),
            jax.ShapeDtypeStruct((half, TILE, LANES), F32),
            jax.ShapeDtypeStruct((half, TILE, LANES), BF16),
        ),
        in_specs=[smem] + [vmem] * (9 + len(halos)),
        scratch_shapes=[
            pltpu.VMEM((conv_columns, voxels), BF16),
            pltpu.VMEM((channels, -(-conv_columns // LANES) * LANES), F32),
            pltpu.VMEM((taps * channels, LANES), F32),
        ],
        compiler_params=params,
        name="forward",
    )(core, features_t, neighbours_t, coarse_grad, w_conv_t, w_down, *own, pick, hgrad, *halos)

    def fold(phase, keep, got):
        shape = (keep.shape[0] // 2, TILE, LANES)
        return pl.pallas_call(
            fold_kernel,
            out_shape=(jax.ShapeDtypeStruct(shape, F32), jax.ShapeDtypeStruct(shape, BF16)),
            in_specs=[smem, vmem, vmem],
            compiler_params=params,
            name="fold",
        )(bits[phase], keep, got)

    def join(phase, own, got):
        return pl.pallas_call(
            join_kernel,
            out_shape=jax.ShapeDtypeStruct((own.shape[0] * 2, TILE, LANES), BF16),
            in_specs=[smem, vmem, vmem],
            compiler_params=params,
            name="join",
        )(bits[phase], own, got)

    got = lax.ppermute(send, "core", swap)
    for phase in range(phases):
        keep, send = fold(phase, keep, got)
        if phase == 0:
            send, grad = lax.optimization_barrier((send, grad))
        got = lax.ppermute(send, SPLIT, bit_pairs(sizes, orders, phase))
        if phase == 0:
            base, mate, cross, own_side = pl.pallas_call(
                functools.partial(backward_kernel, slabs),
                out_shape=(
                    jax.ShapeDtypeStruct((channels, voxels), F32),
                    jax.ShapeDtypeStruct((channels, group), BF16),
                    jax.ShapeDtypeStruct((channels, group), BF16),
                    jax.ShapeDtypeStruct((channels, beside), BF16),
                ),
                in_specs=[smem] + [vmem] * 4,
                scratch_shapes=[
                    pltpu.VMEM((channels, offsets * voxels), BF16),
                    pltpu.VMEM((channels, offsets * LANES), BF16),
                    pltpu.VMEM((voxels, offsets * voxels), BF16),
                    pltpu.VMEM((far_rows, offsets * LANES), BF16),
                    pltpu.VMEM((conv_columns, LANES), BF16),
                ],
                compiler_params=params,
                cost_estimate=light,
                name="backward",
            )(core, neighbours_t, hgrad, grad, w_conv_t)
            got, mate, cross, own_side, base = lax.optimization_barrier(
                (got, mate, cross, own_side, base)
            )
    total = (keep + got.astype(F32)).astype(BF16)
    far_bits = sizes["far"].bit_length() - 1
    for bit in range(far_bits):
        if bit == far_bits - 1:
            total, mate, cross = lax.optimization_barrier((total, mate, cross))
        pairs = [(i, i ^ (1 << bit)) for i in range(sizes["far"])]
        got = lax.ppermute(total, "far", pairs)
        if bit == far_bits - 1:
            cross, mate = lax.ppermute(cross, RING, crossings), lax.ppermute(mate, RING, mates)
            got, mate, cross = lax.optimization_barrier((got, mate, cross))
        total = (total.astype(F32) + got.astype(F32)).astype(BF16)
    row_grad = mate.astype(F32) + cross.astype(F32)
    columns = [row_grad[:, i : i + RIM] for i in range(0, group, RIM)]
    own = [own_side[:, i : i + RIM].astype(F32) for i in range(0, beside, RIM)]
    if slabs == 2:
        home = columns[0]
        edges = [((columns[1] + own[0]).astype(BF16), swap)]
    else:
        home = columns[1]
        edges = [
            ((columns[0] + own[0]).astype(BF16), shifts(slabs, -1)),
            ((columns[2] + own[1]).astype(BF16), shifts(slabs, 1)),
        ]
    for phase in reversed(range(phases)):
        got = lax.ppermute(total, SPLIT, bit_pairs(sizes, orders, phase))
        if phase == 0:
            edges = [lax.ppermute(x, "slab", pairs) for x, pairs in edges]
            got, edges = lax.optimization_barrier((got, edges))
        total = join(phase, total, got)
    other = lax.ppermute(total, "core", swap)
    conv_wgrad_t, down_wgrad, grad_input_t = pl.pallas_call(
        functools.partial(final_kernel, taps),
        out_shape=(
            jax.ShapeDtypeStruct((channels, conv_columns), F32),
            jax.ShapeDtypeStruct((taps * channels, LANES), F32),
            jax.ShapeDtypeStruct((channels, voxels), F32),
        ),
        in_specs=[smem] + [vmem] * (4 + len(edges)),
        compiler_params=params,
        name="final",
    )(core, total, other, base, home, *edges)
    return coarse, grad_input_t.T, conv_wgrad_t.T, down_wgrad


def solution(mesh):
    regions, slabs = mesh.shape["region"], mesh.shape["slab"]
    fine = Mesh(mesh.devices.reshape(regions // 4, 2, 2, slabs), SPLIT)
    split = P(SPLIT, None)
    return jax.shard_map(
        on_device,
        mesh=fine,
        in_specs=(split, split, split, P(), P(), split),
        out_specs=(split, split, P(), P()),
        check_vma=False,
    )
```

time: 70.7 us -> 54.3 us (0.77)
  blocking collectives: 13.3 us -> 0 us
  starting transfers between devices: 27.4 us -> 25.7 us
  waiting for transfers between devices: 15.2 us -> 16.9 us
  local copies, waits for them, and re-layouts: 3.53 us -> 1.87 us
  other arithmetic: 1.76 us -> 0.25 us
    all_to_all x1 -> x0, blocking collectives: 13.3 us -> none  [on_device(): lax.all_to_all(total, 'far', 0, 0).reshape(1, along * piece, TILE, LANES)]
    all_to_all x3 -> x0, starting transfers between devices: 12.1 us -> none  [the longest x1 4.8 us: on_device(): lax.all_to_all(square.reshape(along, piece, TILE, LANES), 'far', 0, 0)]
    ppermute x6 -> x12, waiting for transfers between devices: 6.5 us -> 15.6 us  [the longest x2 4.17 us: on_device(): got = lax.ppermute(send, SPLIT, bit_pairs(sizes, orders, phase))]
    ppermute x6 -> x12, starting transfers between devices: 10.7 us -> 18.8 us  [the longest x2 5.81 us: on_device(): got = lax.ppermute(total, SPLIT, bit_pairs(sizes, orders, phase))]
    all_to_all x3 -> x0, waiting for transfers between devices: 5.5 us -> none  [the longest x1 4.82 us: on_device(): lax.all_to_all(pair.reshape(around, along * piece, TILE, LANES), AROUND,...]
    ppermute x1, starting transfers between devices: 1.71 us -> 3.96 us  [on_device(): got = lax.ppermute(send, 'core', swap)]
    ppermute x1, waiting for transfers between devices: 1.8 us -> 0.05 us  [on_device(): side = [lax.ppermute(rim, 'slab', swap)]]
    unnamed x12 -> x14, local copies, waits for them, and re-layouts: 1.98 us -> 1.06 us
  transfers between devices with their start and end apart: 11 -> 14, of which waited for: 7 -> 9; matrix products, arithmetic and copies ran while one was open for 0% -> 0% of each run, Pallas kernels for 5% -> 7%
where the time goes in v3:
time: 54.3 us; the launch traced here: 54 us
  starting transfers between devices  25.7 us (47%)
  waiting for transfers between devices  16.9 us (31%)
  Pallas kernels  8.5 us (16%)
  local copies, waits for them, and re-layouts  1.87 us (3%)
  between operations  0.8 us (1%)
    ppermute x2, starting transfers between devices, on_device(): got = lax.ppermute(total, SPLIT, bit_pairs(sizes, orders, phase))  5.81 us
    ppermute x2, starting transfers between devices, on_device(): got = lax.ppermute(total, 'far', pairs)  5.4 us
    ppermute x2, starting transfers between devices, on_device(): got = lax.ppermute(send, SPLIT, bit_pairs(sizes, orders, phase))  4.54 us
    ppermute x2, waiting for transfers between devices, on_device(): got = lax.ppermute(send, SPLIT, bit_pairs(sizes, orders, phase))  4.17 us
    ppermute x1, starting transfers between devices, on_device(): got = lax.ppermute(send, 'core', swap)  3.96 us
    ppermute x2, waiting for transfers between devices, on_device(): got = lax.ppermute(total, 'far', pairs)  3.88 us
    pallas_call x1, Pallas kernels, on_device(): pl.pallas_call(functools.partial(forward_kernel, slabs), out_shape=(jax.S...  3.15 us
    ppermute x2, waiting for transfers between devices, on_device(): got = lax.ppermute(total, SPLIT, bit_pairs(sizes, orders, phase))  3 us
  transfers between devices with their start and end apart: 14, of which 9 were waited for; matrix products, arithmetic and copies ran while one was open for 0% of the time, Pallas kernels for 7%

profile of v3, /device:TPU:0, one launch (start us, length us, event | category | flops | bytes accessed | tf_op | source)
XLA Modules:
  0.0 54.0 jit_solution(8576982654172549104)
XLA Ops:
  0.6 0.0 copy-start.2
  0.6 0.8 %slice.12 = bf16[96,64]{1,0:T(8,128)(2,1)S(1)} slice(bf16[96,256]{1,0:T(8,128)(2,1)} %bitcast.11), slice={[0:96], [0:64]} | slice | bytes 24576 | tf_op jit(solution)/shard_map/slice | solution.py:260
  1.4 3.0 %collective-permute-start = (bf16[96,64]{1,0:T(8,128)(2,1)S(1)}, bf16[96,64]{1,0:T(8,128)(2,1)S(1)}, u32[]{:S(2)}, u32[]{:S(2)}) collective-permute-start(bf16[96,64]{1,0:T(8,128)(2,1)S(1)} %slice.12), channel_id=1, source_target_pairs={{0,1},{1,0},{2,3},{3,2},{4,5},{5,4},{6,7},{7,6},{8,9},{9,8},{10,11... | collective-permute-start | bytes 36872 | tf_op jit(solution)/shard_map/ppermute | solution.py:262
  4.4 0.0 copy-done.2
  4.4 0.0 copy-start.3
  4.4 0.8 %copy-done.3 = s32[256,27]{0,1:T(8,128)S(1)} copy-done((s32[256,27]{0,1:T(8,128)S(1)}, s32[256,27]{0,1:T(8,128)}, u32[]{:S(2)}) %copy-start.3) | copy-done | bytes 27672
  5.2 1.0 %gather.1 = (bf16[2592,128]{1,0:T(8,128)(2,1)S(1)}, bf16[2592,128]{1,0:T(8,128)(2,1)S(1)}) custom-call(bf16[96,256]{1,0:T(8,128)(2,1)S(1)} %bitcast.12, s32[27,256]{1,0:T(8,128)S(1)} %bitcast.14), custom_call_target="tpu_custom_call" | custom-call | flops 2000000000 | bytes 10000000 | tf_op jit(solution)/shard_map/gather/pallas_call | solution.py:268
  6.2 0.0 collective-permute-done.refs_6_
  6.2 0.1 pad_maximum_fusion
  6.3 0.0 collective-permute-start.1
  6.3 0.7 %collective-permute-start.2 = (bf16[96,128]{1,0:T(8,128)(2,1)S(1)}, bf16[96,128]{1,0:T(8,128)(2,1)S(1)}, u32[]{:S(2)}, u32[]{:S(2)}) collective-permute-start(bf16[96,128]{1,0:T(8,128)(2,1)S(1)} %pad_maximum_fusion), channel_id=1, source_target_pairs={{2,4},{6,8},{10,12},{14,16},{18,20},{22,24},{26,28},{4,2},{8,6},{1... | collective-permute-start | bytes 73736 | tf_op jit(solution)/shard_map/ppermute | solution.py:281
  7.0 0.0 copy-done.1
  7.0 0.0 copy-done.5
  7.0 0.0 copy-done.6
  7.0 0.0 copy-start
  7.1 0.0 copy-start.4
  7.1 0.7 %taps.1 = (bf16[8,64,256]{2,1,0:T(8,128)(2,1)S(1)}, f32[96,256]{1,0:T(8,128)S(1)}) custom-call(s32[8,64]{1,0:T(8,128)S(1)} %bitcast.17, bf16[64,128]{1,0:T(8,128)(2,1)S(1)} %copy-done.5, bf16[768,128]{1,0:T(8,128)(2,1)S(1)} %copy-done.1), custom_call_target="tpu_custom_call" | custom-call | flops 2000000000 | bytes 10000000 | tf_op jit(solution)/shard_map/taps/pallas_call | solution.py:284
  7.8 0.0 collective-permute-done.1.refs_4_
  7.8 0.0 collective-permute-done.2.refs_5_
  7.8 0.3 copy-done
  8.1 0.0 copy-done.4
  8.1 3.1 %forward.1 = (bf16[64,128]{1,0:T(8,128)(2,1)}, bf16[96,256]{1,0:T(8,128)(2,1)S(1)}, f32[88,16,128]{2,1,0:T(8,128)S(1)}, bf16[88,16,128]{2,1,0:T(8,128)(2,1)S(1)}) custom-call(s32[1]{0:T(128)} %bitcast.core_ref, bf16[96,256]{1,0:T(8,128)(2,1)S(1)} %bitcast.13, s32[27,256]{1,0:T(8,128)S(1)} %bitcast.15, bf16[64,128]{1,0:T(8,128)(2,1)S(1)} %copy-done.5, ...), custom_call_target="tpu_custom_call" | custom-call | tf_op jit(solution)/shard_map/forward/pallas_call | solution.py:301
  11.2 4.0 %collective-permute-start.3 = (bf16[88,16,128]{2,1,0:T(8,128)(2,1)S(1)}, bf16[88,16,128]{2,1,0:T(8,128)(2,1)S(1)}, u32[]{:S(2)}, u32[]{:S(2)}) collective-permute-start(bf16[88,16,128]{2,1,0:T(8,128)(2,1)S(1)} %get-tuple-element.52), channel_id=1, source_target_pairs={{0,2},{2,0},{1,3},{3,1},{4,6},{6,4},{5,7},{7,5},{8,10},{10,8},{9,1... | collective-permute-start | bytes 1081352 | tf_op jit(solution)/shard_map/ppermute | solution.py:338
  15.2 1.3 %collective-permute-done.3.got_ref = bf16[88,16,128]{2,1,0:T(8,128)(2,1)S(1)} collective-permute-done((bf16[88,16,128]{2,1,0:T(8,128)(2,1)S(1)}, bf16[88,16,128]{2,1,0:T(8,128)(2,1)S(1)}, u32[]{:S(2)}, u32[]{:S(2)}) %collective-permute-start.3) | collective-permute-done | bytes 360480 | tf_op jit(solution)/shard_map/ppermute | solution.py:338
  16.5 0.1 fold.2
  16.6 3.0 %collective-permute-start.4 = (bf16[44,16,128]{2,1,0:T(8,128)(2,1)S(1)}, bf16[44,16,128]{2,1,0:T(8,128)(2,1)S(1)}, u32[]{:S(2)}, u32[]{:S(2)}) collective-permute-start(bf16[44,16,128]{2,1,0:T(8,128)(2,1)S(1)} %get-tuple-element.56), channel_id=1, source_target_pairs={{0,4},{1,5},{2,3},{3,2},{4,0},{5,1},{6,7},{7,6},{8,12},{9,13},{10,... | collective-permute-start | bytes 540680 | tf_op jit(solution)/shard_map/ppermute | solution.py:343
  19.5 2.3 %backward.1 = (f32[96,256]{1,0:T(8,128)S(1)}, bf16[96,128]{1,0:T(8,128)(2,1)S(1)}, bf16[96,128]{1,0:T(8,128)(2,1)S(1)}, bf16[96,64]{1,0:T(8,128)(2,1)S(1)}) custom-call(s32[1]{0:T(128)} %bitcast.core_ref, s32[27,256]{1,0:T(8,128)S(1)} %bitcast.16, f32[96,256]{1,0:T(8,128)S(1)} %get-tuple-element.49.refs_3_.hgrad_ref, ...), custom_call_target="tpu_custom_call" | custom-call | flops 2000000000 | bytes 10000000 | tf_op jit(solution)/shard_map/backward/pallas_call | solution.py:345
  21.8 1.2 %collective-permute-done.4.got_ref = bf16[44,16,128]{2,1,0:T(8,128)(2,1)S(1)} collective-permute-done((bf16[44,16,128]{2,1,0:T(8,128)(2,1)S(1)}, bf16[44,16,128]{2,1,0:T(8,128)(2,1)S(1)}, u32[]{:S(2)}, u32[]{:S(2)}) %collective-permute-start.4) | collective-permute-done | bytes 180256 | tf_op jit(solution)/shard_map/ppermute | solution.py:343
  23.0 1.6 %collective-permute-start.5 = (bf16[22,16,128]{2,1,0:T(8,128)(2,1)S(1)}, bf16[22,16,128]{2,1,0:T(8,128)(2,1)S(1)}, u32[]{:S(2)}, u32[]{:S(2)}) collective-permute-start(bf16[22,16,128]{2,1,0:T(8,128)(2,1)S(1)} %get-tuple-element.64), channel_id=1, source_target_pairs={{0,1},{1,0},{2,6},{3,7},{4,5},{5,4},{6,2},{7,3},{8,9},{9,8},{10,14... | collective-permute-start | bytes 270344 | tf_op jit(solution)/shard_map/ppermute | solution.py:343
  24.6 3.0 %collective-permute-done.5 = bf16[22,16,128]{2,1,0:T(8,128)(2,1)S(1)} collective-permute-done((bf16[22,16,128]{2,1,0:T(8,128)(2,1)S(1)}, bf16[22,16,128]{2,1,0:T(8,128)(2,1)S(1)}, u32[]{:S(2)}, u32[]{:S(2)}) %collective-permute-start.5) | collective-permute-done | bytes 90144 | tf_op jit(solution)/shard_map/ppermute | solution.py:343
  27.7 2.0 %collective-permute-start.6 = (bf16[22,16,128]{2,1,0:T(8,128)(2,1)S(1)}, bf16[22,16,128]{2,1,0:T(8,128)(2,1)S(1)}, u32[]{:S(2)}, u32[]{:S(2)}) collective-permute-start(bf16[22,16,128]{2,1,0:T(8,128)(2,1)S(1)} %add_convert_fusion.2), channel_id=1, source_target_pairs={{0,8},{8,0},{16,24},{24,16},{1,9},{9,1},{17,25},{25,17},{2,10},{10... | collective-permute-start | bytes 270344 | tf_op jit(solution)/shard_map/ppermute | solution.py:374
  29.7 2.6 %collective-permute-done.6 = bf16[22,16,128]{2,1,0:T(8,128)(2,1)S(1)} collective-permute-done((bf16[22,16,128]{2,1,0:T(8,128)(2,1)S(1)}, bf16[22,16,128]{2,1,0:T(8,128)(2,1)S(1)}, u32[]{:S(2)}, u32[]{:S(2)}) %collective-permute-start.6) | collective-permute-done | bytes 90144 | tf_op jit(solution)/shard_map/ppermute | solution.py:374
  32.3 3.4 %collective-permute-start.7 = (bf16[22,16,128]{2,1,0:T(8,128)(2,1)S(1)}, bf16[22,16,128]{2,1,0:T(8,128)(2,1)S(1)}, u32[]{:S(2)}, u32[]{:S(2)}) collective-permute-start(bf16[22,16,128]{2,1,0:T(8,128)(2,1)S(1)} %add_convert_fusion.1), channel_id=1, source_target_pairs={{0,16},{8,24},{16,0},{24,8},{1,17},{9,25},{17,1},{25,9},{2,18},{10... | collective-permute-start | bytes 270344 | tf_op jit(solution)/shard_map/ppermute | solution.py:374
  35.7 0.0 collective-permute-start.8
  35.7 0.7 %collective-permute-start.9 = (bf16[96,128]{1,0:T(8,128)(2,1)S(1)}, bf16[96,128]{1,0:T(8,128)(2,1)S(1)}, u32[]{:S(2)}, u32[]{:S(2)}) collective-permute-start(bf16[96,128]{1,0:T(8,128)(2,1)S(1)} %get-tuple-element.69), channel_id=1, source_target_pairs={{2,4},{6,8},{10,12},{14,16},{18,20},{22,24},{26,28},{4,2},{8,6},{1... | collective-permute-start | bytes 73736 | tf_op jit(solution)/shard_map/ppermute | solution.py:376
  36.3 0.5 collective-permute-done.8
  36.9 0.0 collective-permute-done.9
  36.9 1.3 %collective-permute-done.7 = bf16[22,16,128]{2,1,0:T(8,128)(2,1)S(1)} collective-permute-done((bf16[22,16,128]{2,1,0:T(8,128)(2,1)S(1)}, bf16[22,16,128]{2,1,0:T(8,128)(2,1)S(1)}, u32[]{:S(2)}, u32[]{:S(2)}) %collective-permute-start.7) | collective-permute-done | bytes 90144 | tf_op jit(solution)/shard_map/ppermute | solution.py:374
  38.2 1.6 %collective-permute-start.10 = (bf16[22,16,128]{2,1,0:T(8,128)(2,1)S(1)}, bf16[22,16,128]{2,1,0:T(8,128)(2,1)S(1)}, u32[]{:S(2)}, u32[]{:S(2)}) collective-permute-start(bf16[22,16,128]{2,1,0:T(8,128)(2,1)S(1)} %add_convert_fusion.own_ref), channel_id=1, source_target_pairs={{0,1},{1,0},{2,6},{3,7},{4,5},{5,4},{6,2},{7,3},{8,9},{9,8},{10,14... | collective-permute-start | bytes 270344 | tf_op jit(solution)/shard_map/ppermute | solution.py:392
  39.8 3.0 %collective-permute-done.10.got_ref = bf16[22,16,128]{2,1,0:T(8,128)(2,1)S(1)} collective-permute-done((bf16[22,16,128]{2,1,0:T(8,128)(2,1)S(1)}, bf16[22,16,128]{2,1,0:T(8,128)(2,1)S(1)}, u32[]{:S(2)}, u32[]{:S(2)}) %collective-permute-start.10) | collective-permute-done | bytes 90144 | tf_op jit(solution)/shard_map/ppermute | solution.py:392
  42.8 4.2 %collective-permute-start.11 = (bf16[44,16,128]{2,1,0:T(8,128)(2,1)S(1)}, bf16[44,16,128]{2,1,0:T(8,128)(2,1)S(1)}, u32[]{:S(2)}, u32[]{:S(2)}) collective-permute-start(bf16[44,16,128]{2,1,0:T(8,128)(2,1)S(1)} %join.2.own_ref), channel_id=1, source_target_pairs={{0,4},{1,5},{2,3},{3,2},{4,0},{5,1},{6,7},{7,6},{8,12},{9,13},{10,... | collective-permute-start | bytes 540680 | tf_op jit(solution)/shard_map/ppermute | solution.py:392
  47.1 0.1 fusion.1
  47.1 1.6 %collective-permute-start.12 = (bf16[96,64]{1,0:T(8,128)(2,1)S(1)}, bf16[96,64]{1,0:T(8,128)(2,1)S(1)}, u32[]{:S(2)}, u32[]{:S(2)}) collective-permute-start(bf16[96,64]{1,0:T(8,128)(2,1)S(1)} %get-tuple-element.81), channel_id=1, source_target_pairs={{0,1},{1,0},{2,3},{3,2},{4,5},{5,4},{6,7},{7,6},{8,9},{9,8},{10,11... | collective-permute-start | bytes 36872 | tf_op jit(solution)/shard_map/ppermute | solution.py:394
  48.7 2.3 %collective-permute-done.12.refs_1_ = bf16[96,64]{1,0:T(8,128)(2,1)S(1)} collective-permute-done((bf16[96,64]{1,0:T(8,128)(2,1)S(1)}, bf16[96,64]{1,0:T(8,128)(2,1)S(1)}, u32[]{:S(2)}, u32[]{:S(2)}) %collective-permute-start.12) | collective-permute-done | bytes 12320 | tf_op jit(solution)/shard_map/ppermute | solution.py:394
  51.0 0.0 collective-permute-done.11.got_ref
  51.1 0.1 collective-permute-start.13
  51.1 1.7 %collective-permute-done.13.other_ref = bf16[88,16,128]{2,1,0:T(8,128)(2,1)S(1)} collective-permute-done((bf16[88,16,128]{2,1,0:T(8,128)(2,1)S(1)}, bf16[88,16,128]{2,1,0:T(8,128)(2,1)S(1)}, u32[]{:S(2)}, u32[]{:S(2)}) %collective-permute-start.13) | collective-permute-done | bytes 360480 | tf_op jit(solution)/shard_map/ppermute | solution.py:397
  52.8 1.2 %final.1 = (f32[96,2592]{1,0:T(8,128)}, f32[768,128]{1,0:T(8,128)}, f32[96,256]{1,0:T(8,128)}) custom-call(s32[1]{0:T(128)} %bitcast.core_ref, bf16[88,16,128]{2,1,0:T(8,128)(2,1)S(1)} %join.3.mine_ref, bf16[88,16,128]{2,1,0:T(8,128)(2,1)S(1)} %collective-permute-done.13.other_ref, f32[96,256]{1,0:T(8,128)S(1)} %get-tuple-element.75.base_ref, ...), custom_call_target="tpu_custom_call" | custom-call | tf_op jit(solution)/shard_map/final/pallas_call | solution.py:398
  (10 shorter events, 0.2 us)
Async XLA Ops:
  0.6 3.8 %copy-start.2 = (bf16[256,96]{0,1:T(8,128)(2,1)S(1)}, bf16[256,96]{0,1:T(8,128)(2,1)}, u32[]{:S(2)}) copy-start(bf16[256,96]{0,1:T(8,128)(2,1)} %param.6) | copy-start | bytes 147460
  1.4 4.8 %collective-permute-start = (bf16[96,64]{1,0:T(8,128)(2,1)S(1)}, bf16[96,64]{1,0:T(8,128)(2,1)S(1)}, u32[]{:S(2)}, u32[]{:S(2)}) collective-permute-start(bf16[96,64]{1,0:T(8,128)(2,1)S(1)} %slice.12), channel_id=1, source_target_pairs={{0,1},{1,0},{2,3},{3,2},{4,5},{5,4},{6,7},{7,6},{8,9},{9,8},{10,11... | collective-permute-start | bytes 36872 | tf_op jit(solution)/shard_map/ppermute | solution.py:262
  4.4 0.8 %copy-start.3 = (s32[256,27]{0,1:T(8,128)S(1)}, s32[256,27]{0,1:T(8,128)}, u32[]{:S(2)}) copy-start(s32[256,27]{0,1:T(8,128)} %param.7) | copy-start | bytes 82948
  5.2 1.8 %copy-start.1 = (bf16[768,128]{1,0:T(8,128)(2,1)S(1)}, bf16[768,128]{1,0:T(8,128)(2,1)}, u32[]{:S(2)}) copy-start(bf16[768,128]{1,0:T(8,128)(2,1)} %wd_ref.3) | copy-start | bytes 589828
  6.2 0.8 %copy-start.5 = (bf16[64,128]{1,0:T(8,128)(2,1)S(1)}, bf16[64,128]{1,0:T(8,128)(2,1)}, u32[]{:S(2)}) copy-start(bf16[64,128]{1,0:T(8,128)(2,1)} %cgrad_ref.3) | copy-start | bytes 49156
  6.2 0.8 %copy-start.6 = (s32[64,8]{0,1:T(8,128)S(1)}, s32[64,8]{0,1:T(8,128)}, u32[]{:S(2)}) copy-start(s32[64,8]{0,1:T(8,128)} %param.8) | copy-start | bytes 6148
  6.3 1.5 %collective-permute-start.1 = (bf16[96,128]{1,0:T(8,128)(2,1)S(1)}, bf16[96,128]{1,0:T(8,128)(2,1)S(1)}, u32[]{:S(2)}, u32[]{:S(2)}) collective-permute-start(bf16[96,128]{1,0:T(8,128)(2,1)S(1)} %pad_maximum_fusion), channel_id=1, source_target_pairs={{0,2},{2,0},{4,6},{6,4},{8,10},{10,8},{12,14},{14,12},{16,18},{18,... | collective-permute-start | bytes 73736 | tf_op jit(solution)/shard_map/ppermute | solution.py:282
  6.3 1.5 %collective-permute-start.2 = (bf16[96,128]{1,0:T(8,128)(2,1)S(1)}, bf16[96,128]{1,0:T(8,128)(2,1)S(1)}, u32[]{:S(2)}, u32[]{:S(2)}) collective-permute-start(bf16[96,128]{1,0:T(8,128)(2,1)S(1)} %pad_maximum_fusion), channel_id=1, source_target_pairs={{2,4},{6,8},{10,12},{14,16},{18,20},{22,24},{26,28},{4,2},{8,6},{1... | collective-permute-start | bytes 73736 | tf_op jit(solution)/shard_map/ppermute | solution.py:281
  7.0 1.0 %copy-start = (bf16[2592,96]{0,1:T(8,128)(2,1)S(1)}, bf16[2592,96]{0,1:T(8,128)(2,1)}, u32[]{:S(2)}) copy-start(bf16[2592,96]{0,1:T(8,128)(2,1)} %param.9) | copy-start | bytes 1492996
  7.1 1.0 %copy-start.4 = (s32[256,27]{0,1:T(8,128)S(1)}, s32[256,27]{0,1:T(8,128)}, u32[]{:S(2)}) copy-start(s32[256,27]{0,1:T(8,128)} %param.7) | copy-start | bytes 82948
  11.2 5.3 %collective-permute-start.3 = (bf16[88,16,128]{2,1,0:T(8,128)(2,1)S(1)}, bf16[88,16,128]{2,1,0:T(8,128)(2,1)S(1)}, u32[]{:S(2)}, u32[]{:S(2)}) collective-permute-start(bf16[88,16,128]{2,1,0:T(8,128)(2,1)S(1)} %get-tuple-element.52), channel_id=1, source_target_pairs={{0,2},{2,0},{1,3},{3,1},{4,6},{6,4},{5,7},{7,5},{8,10},{10,8},{9,1... | collective-permute-start | bytes 1081352 | tf_op jit(solution)/shard_map/ppermute | solution.py:338
  16.6 6.4 %collective-permute-start.4 = (bf16[44,16,128]{2,1,0:T(8,128)(2,1)S(1)}, bf16[44,16,128]{2,1,0:T(8,128)(2,1)S(1)}, u32[]{:S(2)}, u32[]{:S(2)}) collective-permute-start(bf16[44,16,128]{2,1,0:T(8,128)(2,1)S(1)} %get-tuple-element.56), channel_id=1, source_target_pairs={{0,4},{1,5},{2,3},{3,2},{4,0},{5,1},{6,7},{7,6},{8,12},{9,13},{10,... | collective-permute-start | bytes 540680 | tf_op jit(solution)/shard_map/ppermute | solution.py:343
  23.0 4.6 %collective-permute-start.5 = (bf16[22,16,128]{2,1,0:T(8,128)(2,1)S(1)}, bf16[22,16,128]{2,1,0:T(8,128)(2,1)S(1)}, u32[]{:S(2)}, u32[]{:S(2)}) collective-permute-start(bf16[22,16,128]{2,1,0:T(8,128)(2,1)S(1)} %get-tuple-element.64), channel_id=1, source_target_pairs={{0,1},{1,0},{2,6},{3,7},{4,5},{5,4},{6,2},{7,3},{8,9},{9,8},{10,14... | collective-permute-start | bytes 270344 | tf_op jit(solution)/shard_map/ppermute | solution.py:343
  27.7 4.6 %collective-permute-start.6 = (bf16[22,16,128]{2,1,0:T(8,128)(2,1)S(1)}, bf16[22,16,128]{2,1,0:T(8,128)(2,1)S(1)}, u32[]{:S(2)}, u32[]{:S(2)}) collective-permute-start(bf16[22,16,128]{2,1,0:T(8,128)(2,1)S(1)} %add_convert_fusion.2), channel_id=1, source_target_pairs={{0,8},{8,0},{16,24},{24,16},{1,9},{9,1},{17,25},{25,17},{2,10},{10... | collective-permute-start | bytes 270344 | tf_op jit(solution)/shard_map/ppermute | solution.py:374
  32.3 5.9 %collective-permute-start.7 = (bf16[22,16,128]{2,1,0:T(8,128)(2,1)S(1)}, bf16[22,16,128]{2,1,0:T(8,128)(2,1)S(1)}, u32[]{:S(2)}, u32[]{:S(2)}) collective-permute-start(bf16[22,16,128]{2,1,0:T(8,128)(2,1)S(1)} %add_convert_fusion.1), channel_id=1, source_target_pairs={{0,16},{8,24},{16,0},{24,8},{1,17},{9,25},{17,1},{25,9},{2,18},{10... | collective-permute-start | bytes 270344 | tf_op jit(solution)/shard_map/ppermute | solution.py:374
  35.7 1.2 %collective-permute-start.8 = (bf16[96,128]{1,0:T(8,128)(2,1)S(1)}, bf16[96,128]{1,0:T(8,128)(2,1)S(1)}, u32[]{:S(2)}, u32[]{:S(2)}) collective-permute-start(bf16[96,128]{1,0:T(8,128)(2,1)S(1)} %get-tuple-element.68), channel_id=1, source_target_pairs={{0,2},{2,0},{4,6},{6,4},{8,10},{10,8},{12,14},{14,12},{16,18},{18,... | collective-permute-start | bytes 73736 | tf_op jit(solution)/shard_map/ppermute | solution.py:376
  35.7 1.2 %collective-permute-start.9 = (bf16[96,128]{1,0:T(8,128)(2,1)S(1)}, bf16[96,128]{1,0:T(8,128)(2,1)S(1)}, u32[]{:S(2)}, u32[]{:S(2)}) collective-permute-start(bf16[96,128]{1,0:T(8,128)(2,1)S(1)} %get-tuple-element.69), channel_id=1, source_target_pairs={{2,4},{6,8},{10,12},{14,16},{18,20},{22,24},{26,28},{4,2},{8,6},{1... | collective-permute-start | bytes 73736 | tf_op jit(solution)/shard_map/ppermute | solution.py:376
  38.2 4.6 %collective-permute-start.10 = (bf16[22,16,128]{2,1,0:T(8,128)(2,1)S(1)}, bf16[22,16,128]{2,1,0:T(8,128)(2,1)S(1)}, u32[]{:S(2)}, u32[]{:S(2)}) collective-permute-start(bf16[22,16,128]{2,1,0:T(8,128)(2,1)S(1)} %add_convert_fusion.own_ref), channel_id=1, source_target_pairs={{0,1},{1,0},{2,6},{3,7},{4,5},{5,4},{6,2},{7,3},{8,9},{9,8},{10,14... | collective-permute-start | bytes 270344 | tf_op jit(solution)/shard_map/ppermute | solution.py:392
  42.8 8.2 %collective-permute-start.11 = (bf16[44,16,128]{2,1,0:T(8,128)(2,1)S(1)}, bf16[44,16,128]{2,1,0:T(8,128)(2,1)S(1)}, u32[]{:S(2)}, u32[]{:S(2)}) collective-permute-start(bf16[44,16,128]{2,1,0:T(8,128)(2,1)S(1)} %join.2.own_ref), channel_id=1, source_target_pairs={{0,4},{1,5},{2,3},{3,2},{4,0},{5,1},{6,7},{7,6},{8,12},{9,13},{10,... | collective-permute-start | bytes 540680 | tf_op jit(solution)/shard_map/ppermute | solution.py:392
  47.1 3.9 %collective-permute-start.12 = (bf16[96,64]{1,0:T(8,128)(2,1)S(1)}, bf16[96,64]{1,0:T(8,128)(2,1)S(1)}, u32[]{:S(2)}, u32[]{:S(2)}) collective-permute-start(bf16[96,64]{1,0:T(8,128)(2,1)S(1)} %get-tuple-element.81), channel_id=1, source_target_pairs={{0,1},{1,0},{2,3},{3,2},{4,5},{5,4},{6,7},{7,6},{8,9},{9,8},{10,11... | collective-permute-start | bytes 36872 | tf_op jit(solution)/shard_map/ppermute | solution.py:394
  51.1 1.7 %collective-permute-start.13 = (bf16[88,16,128]{2,1,0:T(8,128)(2,1)S(1)}, bf16[88,16,128]{2,1,0:T(8,128)(2,1)S(1)}, u32[]{:S(2)}, u32[]{:S(2)}) collective-permute-start(bf16[88,16,128]{2,1,0:T(8,128)(2,1)S(1)} %join.3.mine_ref), channel_id=1, source_target_pairs={{0,2},{2,0},{1,3},{3,1},{4,6},{6,4},{5,7},{7,5},{8,10},{10,8},{9,1... | collective-permute-start | bytes 1081352 | tf_op jit(solution)/shard_map/ppermute | solution.py:397

commit v4 on v3

v4 whole, which is shorter than its diff:
```python
import functools

import jax
import jax.numpy as jnp
from jax import lax
from jax.experimental import pallas as pl
from jax.experimental.pallas import tpu as pltpu
from jax.sharding import Mesh, PartitionSpec as P

SPLIT = ("far", "near", "core", "slab")
RING = ("far", "near", "core")
RIM = 64
LANES = 128
TILE = 16
CHUNKS = 2
F32 = jnp.float32
BF16 = jnp.bfloat16
NN = (((1,), (0,)), ((), ()))
NT = (((1,), (1,)), ((), ()))
VMEM_BYTES = 20 * 2**20


def mm(a, b, dims=NN):
    return lax.dot_general(a, b, dims, preferred_element_type=F32)


def table_lanes(neighbours, voxels, slabs, core):
    code = neighbours // voxels
    slot = neighbours - code * voxels
    row = code // 3
    col = code - row * 3
    if slabs == 2:
        rims = 2
        place = jnp.where(col == 1, 0, 1)
        beside = 0
    else:
        rims = 3
        place = col
        beside = col // 2
    group = jnp.abs(row // 2 + core - 1)
    rim = jnp.where(row == 1, 2 * rims + beside, group * rims + place)
    lane = jnp.where(code == 4, slot, voxels + rim * RIM + slot)
    return jnp.where(code > 8, -1, lane)


def payload_tiles(channels, conv_columns, taps):
    tiles = []
    for column in range(0, conv_columns, LANES):
        for row in range(0, channels, TILE):
            tiles.append((0, row, column, min(LANES, conv_columns - column)))
    for row in range(0, taps * channels, TILE):
        tiles.append((1, row, 0, LANES))
    return tiles


def padded_halo(halo_refs):
    halo = [h[...] for h in halo_refs]
    width = sum(h.shape[1] for h in halo)
    slack = -width % LANES
    if slack:
        halo.append(jnp.zeros((halo[0].shape[0], slack), BF16))
    return jnp.concatenate(halo, axis=1)


def gather_kernel(slabs, core_ref, f_ref, near_ref, first_ref, rest_ref, far_ref):
    channels, voxels = f_ref.shape
    table_t = f_ref[...]
    lanes = table_lanes(near_ref[...], voxels, slabs, core_ref[0])
    far_iota = lax.broadcasted_iota(jnp.int32, (far_ref.shape[0], LANES), 0) + voxels
    near_iota = lax.broadcasted_iota(jnp.int32, (voxels, voxels), 0)
    for o in range(near_ref.shape[0]):
        near = jnp.where(near_iota == lanes[o : o + 1, :], 1.0, 0.0).astype(BF16)
        own = mm(table_t, near).astype(BF16)
        first_ref[o * channels : (o + 1) * channels, :] = own[:, :LANES]
        rest_ref[o * channels : (o + 1) * channels, :] = own[:, LANES:]
        away = jnp.where(far_iota == lanes[o : o + 1, :LANES], 1.0, 0.0).astype(BF16)
        far_ref[:, o * LANES : (o + 1) * LANES] = away


def taps_kernel(down_ref, cgrad_ref, wd_ref, pick_ref, hgrad_ref):
    channels, voxels = hgrad_ref.shape
    taps, coarse_count = down_ref.shape
    cgrad_t = cgrad_ref[...].astype(F32).T.astype(BF16)
    down = down_ref[...].astype(F32).T
    lane_iota = lax.broadcasted_iota(jnp.int32, (coarse_count, voxels), 1).astype(F32)
    hgrad_t = jnp.zeros((channels, voxels), F32)
    for t in range(taps):
        pick = jnp.where(lane_iota == down[:, t : t + 1], 1.0, 0.0).astype(BF16)
        pick_ref[t] = pick
        wd = wd_ref[t * channels : (t + 1) * channels, :]
        hgrad_t += mm(wd, mm(cgrad_t, pick).astype(BF16))
    hgrad_ref[...] = hgrad_t


def forward_kernel(halo_count, core_ref, f_ref, cgrad_ref, w_ref, *refs):
    first_ref, rest_ref, far_ref, pick_ref, hgrad_ref = refs[:5]
    halo_refs, refs = refs[5 : 5 + halo_count], refs[5 + halo_count :]
    grad_ref, hidden_ref, *chunks, rt, conv_w, down_w = refs
    channels = f_ref.shape[0]
    offsets = far_ref.shape[1] // LANES
    taps = pick_ref.shape[0]
    conv_columns = offsets * channels
    halo_t = padded_halo(halo_refs)
    for pair in range(0, offsets, 2):
        away = mm(halo_t, far_ref[:, pair * LANES : min(pair + 2, offsets) * LANES])
        for o in range(pair, min(pair + 2, offsets)):
            rows = slice(o * channels, (o + 1) * channels)
            lanes = slice((o - pair) * LANES, (o - pair + 1) * LANES)
            first = first_ref[rows, :].astype(F32) + away[:, lanes]
            rt[rows, :LANES] = first.astype(BF16)
            rt[rows, LANES:] = rest_ref[rows, :]

    out_t = mm(w_ref[...], rt[...])
    sig = 1.0 / (1.0 + jnp.exp(-out_t))
    hidden_t = (f_ref[...].astype(F32) + out_t * sig).astype(BF16)
    grad_t = (hgrad_ref[...] * sig * (1.0 + out_t * (1.0 - sig))).astype(BF16)
    grad_ref[...] = grad_t
    conv_w[:, :conv_columns] = mm(grad_t, rt[...], NT)
    if conv_w.shape[1] > conv_columns:
        slack = conv_w.shape[1] - conv_columns
        conv_w[:, conv_columns:] = jnp.zeros((channels, slack), F32)

    hidden_ref[...] = hidden_t
    cgrad = cgrad_ref[...]
    for t in range(taps):
        picked_t = mm(hidden_t, pick_ref[t], NT).astype(BF16)
        down_w[t * channels : (t + 1) * channels, :] = mm(picked_t, cgrad)

    tiles = payload_tiles(channels, conv_columns, taps)
    count = len(chunks) // 2
    size = chunks[0].shape[0]
    for core in range(2):

        @pl.when(core_ref[0] == core)
        def _(core=core):
            for i in range(2 * count * size):
                half, chunk, place = i // (count * size), i // size % count, i % size
                ref = chunks[2 * chunk + (half != core)]
                if i < len(tiles):
                    kind, row, column, _ = tiles[i]
                    source = down_w if kind else conv_w
                    value = source[row : row + TILE, column : column + LANES]
                else:
                    value = jnp.zeros((TILE, LANES), F32)
                ref[place] = value.astype(ref.dtype)


def backward_kernel(slabs, core_ref, near_ref, far_ref, hgrad_ref, grad_ref, w_ref, *refs):
    pick_ref, hidden_ref, wd_ref, *refs = refs
    coarse_ref, base_ref, mate_ref, cross_ref, side_ref, drt, drt_far, hot, w_back = refs
    channels, voxels = hgrad_ref.shape
    offsets = near_ref.shape[0]
    group = mate_ref.shape[1]
    coarse = jnp.zeros(coarse_ref.shape, F32)
    for t in range(pick_ref.shape[0]):
        picked = mm(pick_ref[t], hidden_ref[...], NT).astype(BF16)
        coarse += mm(picked, wd_ref[t * channels : (t + 1) * channels, :])
    coarse_ref[...] = coarse.astype(BF16)
    lanes = table_lanes(near_ref[...], voxels, slabs, core_ref[0])
    near_iota = lax.broadcasted_iota(jnp.int32, (voxels, voxels), 0)
    w_back[:, :channels] = w_ref[...].astype(F32).T.astype(BF16)
    w_back[:, channels:] = jnp.zeros((offsets * channels, LANES - channels), BF16)
    slack = jnp.zeros((LANES - channels, voxels), BF16)
    grad_pad = jnp.concatenate([grad_ref[...], slack], axis=0)
    for o in range(offsets):
        near = jnp.where(near_iota == lanes[o : o + 1, :], 1.0, 0.0).astype(BF16)
        hot[:, o * voxels : (o + 1) * voxels] = near
        spread = mm(w_back[o * channels : (o + 1) * channels, :], grad_pad).astype(BF16)
        drt[:, o * voxels : (o + 1) * voxels] = spread
        drt_far[:, o * LANES : (o + 1) * LANES] = spread[:, :LANES]
    base_ref[...] = hgrad_ref[...] + mm(drt[...], hot[...], NT)
    back_t = mm(drt_far[...], far_ref[...], NT).astype(BF16)
    mate_ref[...] = back_t[:, :group]
    cross_ref[...] = back_t[:, group : 2 * group]
    side_ref[...] = back_t[:, 2 * group : 2 * group + side_ref.shape[1]]


def fold_kernel(bit_ref, own_ref, got_ref, keep_ref, send_ref):
    half = keep_ref.shape[0]
    for ref, part in ((keep_ref, bit_ref[0]), (send_ref, 1 - bit_ref[0])):
        rows = pl.ds(part * half, half)
        ref[...] = (own_ref[rows] + got_ref[rows].astype(F32)).astype(ref.dtype)


def join_kernel(bit_ref, own_ref, got_ref, full_ref):
    half = own_ref.shape[0]
    full_ref[pl.ds(bit_ref[0] * half, half)] = own_ref[...]
    full_ref[pl.ds((1 - bit_ref[0]) * half, half)] = got_ref[...]


def final_kernel(taps, count, core_ref, *refs):
    mine, other, refs = refs[:count], refs[count : 2 * count], refs[2 * count :]
    base_ref, *parts, conv_ref, down_ref, grad_ref = refs
    channels, conv_columns = conv_ref.shape
    size = mine[0].shape[0]
    total = parts[0][...].astype(F32)
    for ref in parts[1:]:
        total += ref[...].astype(F32)
    grad_ref[:, RIM:] = base_ref[:, RIM:]
    grad_ref[:, :RIM] = base_ref[:, :RIM] + total
    for core in range(2):

        @pl.when(core_ref[0] == core)
        def _(core=core):
            for i, tile in enumerate(payload_tiles(channels, conv_columns, taps)):
                kind, row, column, columns = tile
                source = mine if i // (count * size) == core else other
                value = source[i // size % count][i % size].astype(F32)
                target = down_ref if kind else conv_ref
                target[row : row + TILE, column : column + columns] = value[:, :columns]


def shifts(count, step):
    return [(i, i + step) for i in range(count) if 0 <= i + step < count]


def chip_pairs(regions):
    mates = [(i, i ^ 1) for i in range(regions)]
    cross = [(i, i + 1) for i in range(1, regions - 1, 2)]
    return mates, cross + [(b, a) for a, b in cross]


def halo_pairs(regions, slabs, links, step):
    pairs = []
    for owner, reader in links:
        for slab in range(slabs):
            other = (slab + step) % 2 if slabs == 2 else slab + step
            if 0 <= other < slabs:
                pairs.append((owner * slabs + other, reader * slabs + slab))
    return pairs


def square_bits(nears, slabs, core):
    near = [("near", i) for i in range(nears.bit_length() - 1)]
    slab = [("slab", i) for i in range(slabs.bit_length() - 1)]
    return near + slab if core == 0 else slab + near


def bit_pairs(sizes, orders, phase):
    pairs = []
    for index in range(functools.reduce(lambda a, b: a * b, sizes.values())):
        place, left = {}, index
        for axis in reversed(SPLIT):
            left, place[axis] = divmod(left, sizes[axis])
        axis, bit = orders[place["core"]][phase]
        place[axis] ^= 1 << bit
        other = 0
        for name in SPLIT:
            other = other * sizes[name] + place[name]
        pairs.append((index, other))
    return pairs


def on_device(features, neighbours, down_map, w_conv, w_down, coarse_grad):
    sizes = {axis: lax.axis_size(axis) for axis in SPLIT}
    regions, slabs = sizes["far"] * sizes["near"] * sizes["core"], sizes["slab"]
    voxels, channels = features.shape
    offsets, taps = neighbours.shape[1], down_map.shape[1]
    conv_columns = offsets * channels
    core = lax.axis_index("core").astype(jnp.int32).reshape(1)
    swap = [(0, 1), (1, 0)]
    mates, crossings = chip_pairs(regions)
    orders = [square_bits(sizes["near"], slabs, c) for c in range(2)]
    phases = len(orders[0])
    bits = []
    for phase in range(phases):
        chosen = [(lax.axis_index(axis) >> bit) & 1 for axis, bit in (o[phase] for o in orders)]
        bits.append(jnp.where(core == 0, *chosen).astype(jnp.int32))

    smem = pl.BlockSpec(memory_space=pltpu.SMEM)
    vmem = pl.BlockSpec(memory_space=pltpu.VMEM)
    params = pltpu.CompilerParams(vmem_limit_bytes=VMEM_BYTES)
    light = pl.CostEstimate(flops=2 * 10**9, bytes_accessed=10**7, transcendentals=0)
    features_t, neighbours_t, w_conv_t = features.T, neighbours.T, w_conv.T
    rim = features_t[:, :RIM]
    here = [(i, i) for i in range(regions)]
    around = (0, 1) if slabs == 2 else (-1, 0, 1)
    beside = (1,) if slabs == 2 else (-1, 1)
    sections = [(x, s) for x in (mates, crossings) for s in around] + [(here, s) for s in beside]
    halos = [None] * len(sections)
    for wanted in (crossings, mates, here):
        for i, (links, step) in sorted(enumerate(sections), key=lambda x: -abs(x[1][1])):
            if links is wanted:
                halos[i] = lax.ppermute(rim, SPLIT, halo_pairs(regions, slabs, links, step))
    group, beside = len(around) * RIM, len(beside) * RIM
    far_rows = -(-(2 * group + beside) // LANES) * LANES
    own = pl.pallas_call(
        functools.partial(gather_kernel, slabs),
        out_shape=(
            jax.ShapeDtypeStruct((conv_columns, LANES), BF16),
            jax.ShapeDtypeStruct((conv_columns, voxels - LANES), BF16),
            jax.ShapeDtypeStruct((far_rows, offsets * LANES), BF16),
        ),
        in_specs=[smem, vmem, vmem],
        compiler_params=params,
        cost_estimate=light,
        name="gather",
    )(core, features_t, neighbours_t)
    far = own[2]
    pick, hgrad = pl.pallas_call(
        taps_kernel,
        out_shape=(
            jax.ShapeDtypeStruct((taps, coarse_grad.shape[0], voxels), BF16),
            jax.ShapeDtypeStruct((channels, voxels), F32),
        ),
        compiler_params=params,
        cost_estimate=light,
        name="taps",
    )(down_map.T, coarse_grad, w_down)

    tiles = len(payload_tiles(channels, conv_columns, taps))
    size = -(-tiles // (2 * CHUNKS << phases)) << phases
    grad, hidden, *chunks = pl.pallas_call(
        functools.partial(forward_kernel, len(halos)),
        out_shape=[
            jax.ShapeDtypeStruct((channels, voxels), BF16),
            jax.ShapeDtypeStruct((channels, voxels), BF16),
        ]
        + [jax.ShapeDtypeStruct((size, TILE, LANES), kind) for kind in (F32, BF16)] * CHUNKS,
        in_specs=[smem] + [vmem] * (8 + len(halos)),
        scratch_shapes=[
            pltpu.VMEM((conv_columns, voxels), BF16),
            pltpu.VMEM((channels, -(-conv_columns // LANES) * LANES), F32),
            pltpu.VMEM((taps * channels, LANES), F32),
        ],
        compiler_params=params,
        name="forward",
    )(core, features_t, coarse_grad, w_conv_t, *own, pick, hgrad, *halos)

    def fold(phase, keep, got):
        shape = (keep.shape[0] // 2, TILE, LANES)
        return pl.pallas_call(
            fold_kernel,
            out_shape=(jax.ShapeDtypeStruct(shape, F32), jax.ShapeDtypeStruct(shape, BF16)),
            in_specs=[smem, vmem, vmem],
            compiler_params=params,
            name="fold",
        )(bits[phase], keep, got)

    def join(phase, own, got):
        return pl.pallas_call(
            join_kernel,
            out_shape=jax.ShapeDtypeStruct((own.shape[0] * 2, TILE, LANES), BF16),
            in_specs=[smem, vmem, vmem],
            compiler_params=params,
            name="join",
        )(bits[phase], own, got)

    keep, send = chunks[0::2], chunks[1::2]
    got = [lax.ppermute(x, "core", swap) for x in send]
    for phase in range(phases):
        pairs = bit_pairs(sizes, orders, phase)
        for i in range(CHUNKS):
            keep[i], send[i] = fold(phase, keep[i], got[i])
            if phase == 0 and i == 0:
                send[0], grad = lax.optimization_barrier((send[0], grad))
            got[i] = lax.ppermute(send[i], SPLIT, pairs)
        if phase == 0:
            coarse, base, mate, cross, own_side = pl.pallas_call(
                functools.partial(backward_kernel, slabs),
                out_shape=(
                    jax.ShapeDtypeStruct(coarse_grad.shape, BF16),
                    jax.ShapeDtypeStruct((channels, voxels), F32),
                    jax.ShapeDtypeStruct((channels, group), BF16),
                    jax.ShapeDtypeStruct((channels, group), BF16),
                    jax.ShapeDtypeStruct((channels, beside), BF16),
                ),
                in_specs=[smem] + [vmem] * 8,
                scratch_shapes=[
                    pltpu.VMEM((channels, offsets * voxels), BF16),
                    pltpu.VMEM((channels, offsets * LANES), BF16),
                    pltpu.VMEM((voxels, offsets * voxels), BF16),
                    pltpu.VMEM((conv_columns, LANES), BF16),
                ],
                compiler_params=params,
                cost_estimate=light,
                name="backward",
            )(core, neighbours_t, far, hgrad, grad, w_conv_t, pick, hidden, w_down)
            got[0], mate, cross, own_side, base = lax.optimization_barrier(
                (got[0], mate, cross, own_side, base)
            )
    total = [(x + y.astype(F32)).astype(BF16) for x, y in zip(keep, got)]
    far_bits = sizes["far"].bit_length() - 1
    for bit in range(far_bits):
        pairs = [(i, i ^ (1 << bit)) for i in range(sizes["far"])]
        if bit == far_bits - 1:
            total[0], mate, cross = lax.optimization_barrier((total[0], mate, cross))
        for i in range(CHUNKS):
            got[i] = lax.ppermute(total[i], "far", pairs)
            total[i] = (total[i].astype(F32) + got[i].astype(F32)).astype(BF16)
    cross, mate = lax.ppermute(cross, RING, crossings), lax.ppermute(mate, RING, mates)
    for phase in reversed(range(phases)):
        pairs = bit_pairs(sizes, orders, phase)
        got = [lax.ppermute(x, SPLIT, pairs) for x in total]
        if phase == phases - 1:
            got[0], mate, cross = lax.optimization_barrier((got[0], mate, cross))
            row_grad = mate.astype(F32) + cross.astype(F32)
            columns = [row_grad[:, i : i + RIM] for i in range(0, group, RIM)]
            own = [own_side[:, i : i + RIM].astype(F32) for i in range(0, beside, RIM)]
            if slabs == 2:
                home = columns[0]
                edges = [((columns[1] + own[0]).astype(BF16), swap)]
            else:
                home = columns[1]
                edges = [
                    ((columns[0] + own[0]).astype(BF16), shifts(slabs, -1)),
                    ((columns[2] + own[1]).astype(BF16), shifts(slabs, 1)),
                ]
            edges = [lax.ppermute(x, "slab", p) for x, p in edges]
        if phase == 0:
            got[0], edges = lax.optimization_barrier((got[0], edges))
        total = [join(phase, x, y) for x, y in zip(total, got)]
    other = [lax.ppermute(x, "core", swap) for x in total]
    conv_wgrad_t, down_wgrad, grad_input_t = pl.pallas_call(
        functools.partial(final_kernel, taps, CHUNKS),
        out_shape=(
            jax.ShapeDtypeStruct((channels, conv_columns), F32),
            jax.ShapeDtypeStruct((taps * channels, LANES), F32),
            jax.ShapeDtypeStruct((channels, voxels), F32),
        ),
        in_specs=[smem] + [vmem] * (2 * CHUNKS + 2 + len(edges)),
        compiler_params=params,
        name="final",
    )(core, *total, *other, base, home, *edges)
    return coarse, grad_input_t.T, conv_wgrad_t.T, down_wgrad


def solution(mesh):
    regions, slabs = mesh.shape["region"], mesh.shape["slab"]
    fine = Mesh(mesh.devices.reshape(regions // 4, 2, 2, slabs), SPLIT)
    split = P(SPLIT, None)
    return jax.shard_map(
        on_device,
        mesh=fine,
        in_specs=(split, split, split, P(), P(), split),
        out_specs=(split, split, P(), P()),
        check_vma=False,
    )
```

time: 54.3 us -> 73 us (1.34); the launches traced: 54 us -> 71.9 us
  local copies, waits for them, and re-layouts: 1.87 us -> 15.9 us
  starting transfers between devices: 25.7 us -> 35.7 us
  waiting for transfers between devices: 16.9 us -> 7.52 us
  Pallas kernels: 8.5 us -> 11.8 us
    unnamed x14 -> x54, local copies, waits for them, and re-layouts: 1.06 us -> 15.1 us
    ppermute x12 -> x22, starting transfers between devices: 25 us -> 35.1 us  [the longest x4 10.4 us: on_device(): got[i] = lax.ppermute(total[i], 'far', pairs)]
    ppermute x12 -> x22, waiting for transfers between devices: 16.4 us -> 7.52 us  [the longest x1 2.51 us: on_device(): edges = [lax.ppermute(x, 'slab', p) for x, p in edges]]
    pallas_call x2 -> x4, Pallas kernels: 0.1 us -> 1.97 us  [fold(): pl.pallas_call(fold_kernel, out_shape=(jax.ShapeDtypeStruct(shape, F32),...]
    pallas_call x1, Pallas kernels: 2.31 us -> 3.15 us  [on_device(): pl.pallas_call(functools.partial(backward_kernel, slabs), out_shape=(jax....]
  transfers between devices with their start and end apart: 14 -> 24, of which waited for: 9 -> 5; matrix products, arithmetic and copies ran while one was open for 0% -> 0% of each run, Pallas kernels for 7% -> 10%
where the time goes in v4:
time: 73 us; the launch traced here: 71.9 us
  starting transfers between devices  35.7 us (49%)
  local copies, waits for them, and re-layouts  15.9 us (22%)
  Pallas kernels  11.8 us (16%)
  waiting for transfers between devices  7.52 us (10%)
  between operations  0.91 us (1%)
    unnamed x54, local copies, waits for them, and re-layouts  15.1 us
    ppermute x4, starting transfers between devices, on_device(): got[i] = lax.ppermute(total[i], 'far', pairs)  10.4 us
    ppermute x4, starting transfers between devices, on_device(): got = [lax.ppermute(x, SPLIT, pairs) for x in total]  8.64 us
    ppermute x2, starting transfers between devices, on_device(): got = [lax.ppermute(x, 'core', swap) for x in send]  5.47 us
    ppermute x4, starting transfers between devices, on_device(): got[i] = lax.ppermute(send[i], SPLIT, pairs)  4.7 us
    ppermute x5, starting transfers between devices, on_device(): halos[i] = lax.ppermute(rim, SPLIT, halo_pairs(regions, slabs, links, step))  4.47 us
    pallas_call x1, Pallas kernels, on_device(): pl.pallas_call(functools.partial(backward_kernel, slabs), out_shape=(jax....  3.15 us
    pallas_call x1, Pallas kernels, on_device(): pl.pallas_call(functools.partial(forward_kernel, len(halos)), out_shape=[...  2.99 us
  transfers between devices with their start and end apart: 24, of which 5 were waited for; matrix products, arithmetic and copies ran while one was open for 0% of the time, Pallas kernels for 10%

profile of v4, /device:TPU:0, one launch (start us, length us, event | category | flops | bytes accessed | tf_op | source)
XLA Modules:
  0.0 71.9 jit_solution(6887512371543469299)
XLA Ops:
  0.6 0.7 %slice.12 = bf16[96,64]{1,0:T(8,128)(2,1)S(1)} slice(bf16[96,256]{1,0:T(8,128)(2,1)} %bitcast.11), slice={[0:96], [0:64]} | slice | bytes 24576 | tf_op jit(solution)/shard_map/slice | solution.py:275
  1.8 2.6 %collective-permute-start.1 = (bf16[96,64]{1,0:T(8,128)(2,1)S(1)}, bf16[96,64]{1,0:T(8,128)(2,1)S(1)}, u32[]{:S(2)}, u32[]{:S(2)}) collective-permute-start(bf16[96,64]{1,0:T(8,128)(2,1)S(1)} %slice.12), channel_id=1, source_target_pairs={{1,2},{0,3},{3,0},{2,1},{5,6},{4,7},{7,4},{6,5},{9,10},{8,11},{11,... | collective-permute-start | bytes 36872 | tf_op jit(solution)/shard_map/ppermute | solution.py:284
  4.5 0.7 collective-permute-start.2
  5.1 0.7 collective-permute-start.3
  5.9 0.8 %copy-done.5 = bf16[256,96]{0,1:T(8,128)(2,1)S(1)} copy-done((bf16[256,96]{0,1:T(8,128)(2,1)S(1)}, bf16[256,96]{0,1:T(8,128)(2,1)}, u32[]{:S(2)}) %copy-start.5) | copy-done | bytes 49176
  6.7 0.8 %copy-done.24 = s32[256,27]{0,1:T(8,128)S(1)} copy-done((s32[256,27]{0,1:T(8,128)S(1)}, s32[256,27]{0,1:T(8,128)}, u32[]{:S(2)}) %copy-start.24) | copy-done | bytes 27672
  7.4 1.7 %gather.1 = (bf16[2592,128]{1,0:T(8,128)(2,1)S(1)}, bf16[2592,128]{1,0:T(8,128)(2,1)S(1)}, bf16[384,3456]{1,0:T(8,128)(2,1)S(1)}) custom-call(s32[1]{0:T(128)} %bitcast.core_ref, bf16[96,256]{1,0:T(8,128)(2,1)S(1)} %bitcast.12, s32[27,256]{1,0:T(8,128)S(1)} %bitcast.14), custom_call_target="tpu_custom_call" | custom-call | flops 2000000000 | bytes 10000000 | tf_op jit(solution)/shard_map/gather/pallas_call | solution.py:287
  9.2 0.7 taps.1
  9.9 0.7 copy-done.9
  10.6 0.6 copy-done.11
  11.8 0.6 copy-done.15
  12.5 0.7 %copy-done.10 = bf16[96,64]{1,0:T(8,128)(2,1)S(1)} copy-done((bf16[96,64]{1,0:T(8,128)(2,1)S(1)}, bf16[96,64]{1,0:T(8,128)(2,1)}, u32[]{:S(2)}) %copy-start.10) | copy-done | bytes 12312
  13.2 0.7 %copy-done.12 = bf16[96,64]{1,0:T(8,128)(2,1)S(1)} copy-done((bf16[96,64]{1,0:T(8,128)(2,1)S(1)}, bf16[96,64]{1,0:T(8,128)(2,1)}, u32[]{:S(2)}) %copy-start.12) | copy-done | bytes 12312
  13.9 0.7 %copy-done.14 = bf16[96,64]{1,0:T(8,128)(2,1)S(1)} copy-done((bf16[96,64]{1,0:T(8,128)(2,1)S(1)}, bf16[96,64]{1,0:T(8,128)(2,1)}, u32[]{:S(2)}) %copy-start.14) | copy-done | bytes 12312
  14.7 0.7 %copy-done.16 = bf16[96,64]{1,0:T(8,128)(2,1)S(1)} copy-done((bf16[96,64]{1,0:T(8,128)(2,1)S(1)}, bf16[96,64]{1,0:T(8,128)(2,1)}, u32[]{:S(2)}) %copy-start.16) | copy-done | bytes 12312
  15.4 3.0 %forward.1 = (bf16[96,256]{1,0:T(8,128)(2,1)S(1)}, bf16[96,256]{1,0:T(8,128)(2,1)S(1)}, f32[44,16,128]{2,1,0:T(8,128)S(1)}, bf16[44,16,128]{2,1,0:T(8,128)(2,1)}...) custom-call(s32[1]{0:T(128)} %bitcast.core_ref, bf16[96,256]{1,0:T(8,128)(2,1)S(1)} %bitcast.13, ...), custom_call_target="tpu_custom_call" | custom-call | tf_op jit(solution)/shard_map/forward/pallas_call | solution.py:313
  18.4 0.7 %copy-done.1 = f32[44,16,128]{2,1,0:T(8,128)} copy-done((f32[44,16,128]{2,1,0:T(8,128)}, f32[44,16,128]{2,1,0:T(8,128)S(1)}, u32[]{:S(2)}) %copy-start.1) | copy-done | bytes 360472
  19.1 0.6 copy-done.20
  19.8 0.6 copy-done.22
  20.4 5.5 %collective-permute-start.15 = (bf16[44,16,128]{2,1,0:T(8,128)(2,1)}, bf16[44,16,128]{2,1,0:T(8,128)(2,1)}, u32[]{:S(2)}, u32[]{:S(2)}) collective-permute-start(bf16[44,16,128]{2,1,0:T(8,128)(2,1)} %get-tuple-element.78), channel_id=1, source_target_pairs={{0,2},{2,0},{1,3},{3,1},{4,6},{6,4},{5,7},{7,5},{8,10},{10,8},{9,1... | collective-permute-start | bytes 540680 | tf_op jit(solution)/shard_map/ppermute | solution.py:350
  25.8 1.4 %collective-permute-done.15.got_ref = bf16[44,16,128]{2,1,0:T(8,128)(2,1)} collective-permute-done((bf16[44,16,128]{2,1,0:T(8,128)(2,1)}, bf16[44,16,128]{2,1,0:T(8,128)(2,1)}, u32[]{:S(2)}, u32[]{:S(2)}) %collective-permute-start.15) | collective-permute-done | bytes 180256 | tf_op jit(solution)/shard_map/ppermute | solution.py:350
  27.2 1.0 %copy-done.2 = f32[44,16,128]{2,1,0:T(8,128)S(1)} copy-done((f32[44,16,128]{2,1,0:T(8,128)S(1)}, f32[44,16,128]{2,1,0:T(8,128)}, u32[]{:S(2)}) %copy-start.2) | copy-done | bytes 360472
  28.2 1.0 %fold.6 = (f32[22,16,128]{2,1,0:T(8,128)S(1)}, bf16[22,16,128]{2,1,0:T(8,128)(2,1)S(1)}) custom-call(s32[1]{0:T(128)S(6)} %select_n.7.bit_ref, f32[44,16,128]{2,1,0:T(8,128)S(1)} %copy-done.2, bf16[44,16,128]{2,1,0:T(8,128)(2,1)} %collective-permute-done.15.got_ref), custom_call_target="tpu_custom_call" | custom-call | tf_op jit(solution)/shard_map/fold/pallas_call | solution.py:332
  29.2 2.5 %collective-permute-start.16 = (bf16[22,16,128]{2,1,0:T(8,128)(2,1)S(1)}, bf16[22,16,128]{2,1,0:T(8,128)(2,1)S(1)}, u32[]{:S(2)}, u32[]{:S(2)}) collective-permute-start(bf16[22,16,128]{2,1,0:T(8,128)(2,1)S(1)} %get-tuple-element.80), channel_id=1, source_target_pairs={{0,4},{1,5},{2,3},{3,2},{4,0},{5,1},{6,7},{7,6},{8,12},{9,13},{10,... | collective-permute-start | bytes 270344 | tf_op jit(solution)/shard_map/ppermute | solution.py:357
  31.6 1.0 %fold.4 = (f32[22,16,128]{2,1,0:T(8,128)S(1)}, bf16[22,16,128]{2,1,0:T(8,128)(2,1)S(1)}) custom-call(s32[1]{0:T(128)S(6)} %select_n.7.bit_ref, f32[44,16,128]{2,1,0:T(8,128)S(1)} %get-tuple-element.51.own_ref, bf16[44,16,128]{2,1,0:T(8,128)(2,1)} %collective-permute-done.5.got_ref), custom_call_target="tpu_custom_call" | custom-call | tf_op jit(solution)/shard_map/fold/pallas_call | solution.py:332
  32.7 1.4 %collective-permute-done.16.got_ref = bf16[22,16,128]{2,1,0:T(8,128)(2,1)S(1)} collective-permute-done((bf16[22,16,128]{2,1,0:T(8,128)(2,1)S(1)}, bf16[22,16,128]{2,1,0:T(8,128)(2,1)S(1)}, u32[]{:S(2)}, u32[]{:S(2)}) %collective-permute-start.16) | collective-permute-done | bytes 90144 | tf_op jit(solution)/shard_map/ppermute | solution.py:357
  34.8 0.9 %copy-done.4 = bf16[8,64,256]{2,1,0:T(8,128)(2,1)S(1)} copy-done((bf16[8,64,256]{2,1,0:T(8,128)(2,1)S(1)}, bf16[8,64,256]{2,1,0:T(8,128)(2,1)}, u32[]{:S(2)}) %copy-start.4) | copy-done | bytes 262168
  35.7 0.9 %copy-done.8 = f32[96,256]{1,0:T(8,128)S(1)} copy-done((f32[96,256]{1,0:T(8,128)S(1)}, f32[96,256]{1,0:T(8,128)}, u32[]{:S(2)}) %copy-start.8) | copy-done | bytes 98328
  36.6 0.9 %copy-done.19 = bf16[768,128]{1,0:T(8,128)(2,1)S(1)} copy-done((bf16[768,128]{1,0:T(8,128)(2,1)S(1)}, bf16[768,128]{1,0:T(8,128)(2,1)}, u32[]{:S(2)}) %copy-start.19) | copy-done | bytes 196632
  37.5 0.8 %copy-done.21 = bf16[96,256]{1,0:T(8,128)(2,1)S(1)} copy-done((bf16[96,256]{1,0:T(8,128)(2,1)S(1)}, bf16[96,256]{1,0:T(8,128)(2,1)}, u32[]{:S(2)}) %copy-start.21) | copy-done | bytes 49176
  38.3 0.8 %copy-done.23 = bf16[96,256]{1,0:T(8,128)(2,1)S(1)} copy-done((bf16[96,256]{1,0:T(8,128)(2,1)S(1)}, bf16[96,256]{1,0:T(8,128)(2,1)}, u32[]{:S(2)}) %copy-start.23) | copy-done | bytes 49176
  39.1 0.8 %copy-done.25 = s32[256,27]{0,1:T(8,128)S(1)} copy-done((s32[256,27]{0,1:T(8,128)S(1)}, s32[256,27]{0,1:T(8,128)}, u32[]{:S(2)}) %copy-start.25) | copy-done | bytes 27672
  39.9 3.2 %backward.1 = (bf16[64,128]{1,0:T(8,128)(2,1)}, f32[96,256]{1,0:T(8,128)S(1)}, bf16[96,128]{1,0:T(8,128)(2,1)S(1)}, bf16[96,128]{1,0:T(8,128)(2,1)S(1)}, bf16[96,64]{1,0:T(8,128)(2,1)S(1)}) custom-call(s32[1]{0:T(128)} %bitcast.core_ref, s32[27,256]{1,0:T(8,128)S(1)} %bitcast.15, bf16[384,3456]{1,0:T(8,128)(2,1)S(1)} %get-tuple-element.46.refs_2_.far_ref, ...), custom_call_target="tpu_custom_call" | custom-call | flops 2000000000 | bytes 10000000 | tf_op jit(solution)/shard_map/backward/pallas_call | solution.py:359
  43.1 1.6 %collective-permute-start.7 = (bf16[11,16,128]{2,1,0:T(8,128)(2,1)S(1)}, bf16[11,16,128]{2,1,0:T(8,128)(2,1)S(1)}, u32[]{:S(2)}, u32[]{:S(2)}) collective-permute-start(bf16[11,16,128]{2,1,0:T(8,128)(2,1)S(1)} %get-tuple-element.66), channel_id=1, source_target_pairs={{0,1},{1,0},{2,6},{3,7},{4,5},{5,4},{6,2},{7,3},{8,9},{9,8},{10,14... | collective-permute-start | bytes 135176 | tf_op jit(solution)/shard_map/ppermute | solution.py:357
  44.7 2.8 %collective-permute-start.18 = (bf16[11,16,128]{2,1,0:T(8,128)(2,1)S(1)}, bf16[11,16,128]{2,1,0:T(8,128)(2,1)S(1)}, u32[]{:S(2)}, u32[]{:S(2)}) collective-permute-start(bf16[11,16,128]{2,1,0:T(8,128)(2,1)S(1)} %add_convert_fusion.2), channel_id=1, source_target_pairs={{0,8},{8,0},{16,24},{24,16},{1,9},{9,1},{17,25},{25,17},{2,10},{10... | collective-permute-start | bytes 135176 | tf_op jit(solution)/shard_map/ppermute | solution.py:389
  47.4 2.5 %collective-permute-start.8 = (bf16[11,16,128]{2,1,0:T(8,128)(2,1)S(1)}, bf16[11,16,128]{2,1,0:T(8,128)(2,1)S(1)}, u32[]{:S(2)}, u32[]{:S(2)}) collective-permute-start(bf16[11,16,128]{2,1,0:T(8,128)(2,1)S(1)} %add_convert_fusion.5), channel_id=1, source_target_pairs={{0,8},{8,0},{16,24},{24,16},{1,9},{9,1},{17,25},{25,17},{2,10},{10... | collective-permute-start | bytes 135176 | tf_op jit(solution)/shard_map/ppermute | solution.py:389
  50.0 3.0 %collective-permute-start.19 = (bf16[11,16,128]{2,1,0:T(8,128)(2,1)S(1)}, bf16[11,16,128]{2,1,0:T(8,128)(2,1)S(1)}, u32[]{:S(2)}, u32[]{:S(2)}) collective-permute-start(bf16[11,16,128]{2,1,0:T(8,128)(2,1)S(1)} %add_convert_fusion.1), channel_id=1, source_target_pairs={{0,16},{8,24},{16,0},{24,8},{1,17},{9,25},{17,1},{25,9},{2,18},{10... | collective-permute-start | bytes 135176 | tf_op jit(solution)/shard_map/ppermute | solution.py:389
  53.0 2.1 %collective-permute-start.9 = (bf16[11,16,128]{2,1,0:T(8,128)(2,1)S(1)}, bf16[11,16,128]{2,1,0:T(8,128)(2,1)S(1)}, u32[]{:S(2)}, u32[]{:S(2)}) collective-permute-start(bf16[11,16,128]{2,1,0:T(8,128)(2,1)S(1)} %add_convert_fusion.4), channel_id=1, source_target_pairs={{0,16},{8,24},{16,0},{24,8},{1,17},{9,25},{17,1},{25,9},{2,18},{10... | collective-permute-start | bytes 135176 | tf_op jit(solution)/shard_map/ppermute | solution.py:389
  55.1 2.2 %collective-permute-start.20 = (bf16[11,16,128]{2,1,0:T(8,128)(2,1)S(1)}, bf16[11,16,128]{2,1,0:T(8,128)(2,1)S(1)}, u32[]{:S(2)}, u32[]{:S(2)}) collective-permute-start(bf16[11,16,128]{2,1,0:T(8,128)(2,1)S(1)} %add_convert_fusion.own_ref), channel_id=1, source_target_pairs={{0,1},{1,0},{2,6},{3,7},{4,5},{5,4},{6,2},{7,3},{8,9},{9,8},{10,14... | collective-permute-start | bytes 135176 | tf_op jit(solution)/shard_map/ppermute | solution.py:394
  57.3 0.7 %collective-permute-done.9 = bf16[11,16,128]{2,1,0:T(8,128)(2,1)S(1)} collective-permute-done((bf16[11,16,128]{2,1,0:T(8,128)(2,1)S(1)}, bf16[11,16,128]{2,1,0:T(8,128)(2,1)S(1)}, u32[]{:S(2)}, u32[]{:S(2)}) %collective-permute-start.9) | collective-permute-done | bytes 45088 | tf_op jit(solution)/shard_map/ppermute | solution.py:389
  58.0 1.2 %collective-permute-start.10 = (bf16[11,16,128]{2,1,0:T(8,128)(2,1)S(1)}, bf16[11,16,128]{2,1,0:T(8,128)(2,1)S(1)}, u32[]{:S(2)}, u32[]{:S(2)}) collective-permute-start(bf16[11,16,128]{2,1,0:T(8,128)(2,1)S(1)} %add_convert_fusion.3.own_ref), channel_id=1, source_target_pairs={{0,1},{1,0},{2,6},{3,7},{4,5},{5,4},{6,2},{7,3},{8,9},{9,8},{10,14... | collective-permute-start | bytes 135176 | tf_op jit(solution)/shard_map/ppermute | solution.py:394
  59.3 0.7 collective-permute-start.12
  59.9 3.4 %collective-permute-start.21 = (bf16[22,16,128]{2,1,0:T(8,128)(2,1)S(1)}, bf16[22,16,128]{2,1,0:T(8,128)(2,1)S(1)}, u32[]{:S(2)}, u32[]{:S(2)}) collective-permute-start(bf16[22,16,128]{2,1,0:T(8,128)(2,1)S(1)} %join.6.own_ref), channel_id=1, source_target_pairs={{0,4},{1,5},{2,3},{3,2},{4,0},{5,1},{6,7},{7,6},{8,12},{9,13},{10,... | collective-permute-start | bytes 270344 | tf_op jit(solution)/shard_map/ppermute | solution.py:394
  63.4 1.8 %collective-permute-start.13 = (bf16[22,16,128]{2,1,0:T(8,128)(2,1)S(1)}, bf16[22,16,128]{2,1,0:T(8,128)(2,1)S(1)}, u32[]{:S(2)}, u32[]{:S(2)}) collective-permute-start(bf16[22,16,128]{2,1,0:T(8,128)(2,1)S(1)} %join.4.own_ref), channel_id=1, source_target_pairs={{0,4},{1,5},{2,3},{3,2},{4,0},{5,1},{6,7},{7,6},{8,12},{9,13},{10,... | collective-permute-start | bytes 270344 | tf_op jit(solution)/shard_map/ppermute | solution.py:394
  65.3 1.1 %collective-permute-start.14 = (bf16[96,64]{1,0:T(8,128)(2,1)S(1)}, bf16[96,64]{1,0:T(8,128)(2,1)S(1)}, u32[]{:S(2)}, u32[]{:S(2)}) collective-permute-start(bf16[96,64]{1,0:T(8,128)(2,1)S(1)} %get-tuple-element.89), channel_id=1, source_target_pairs={{0,1},{1,0},{2,3},{3,2},{4,5},{5,4},{6,7},{7,6},{8,9},{9,8},{10,11... | collective-permute-start | bytes 36872 | tf_op jit(solution)/shard_map/ppermute | solution.py:409
  66.7 2.5 %collective-permute-done.14.refs_6_ = bf16[96,64]{1,0:T(8,128)(2,1)S(1)} collective-permute-done((bf16[96,64]{1,0:T(8,128)(2,1)S(1)}, bf16[96,64]{1,0:T(8,128)(2,1)S(1)}, u32[]{:S(2)}, u32[]{:S(2)}) %collective-permute-start.14) | collective-permute-done | bytes 12320 | tf_op jit(solution)/shard_map/ppermute | solution.py:409
  69.3 1.4 %collective-permute-done.22.refs_2_ = bf16[44,16,128]{2,1,0:T(8,128)(2,1)S(1)} collective-permute-done((bf16[44,16,128]{2,1,0:T(8,128)(2,1)S(1)}, bf16[44,16,128]{2,1,0:T(8,128)(2,1)S(1)}, u32[]{:S(2)}, u32[]{:S(2)}) %collective-permute-start.22) | collective-permute-done | bytes 180256 | tf_op jit(solution)/shard_map/ppermute | solution.py:413
  70.7 1.2 %final.1 = (f32[96,2592]{1,0:T(8,128)}, f32[768,128]{1,0:T(8,128)}, f32[96,256]{1,0:T(8,128)}) custom-call(s32[1]{0:T(128)} %bitcast.core_ref, bf16[44,16,128]{2,1,0:T(8,128)(2,1)S(1)} %join.5.refs_0_, bf16[44,16,128]{2,1,0:T(8,128)(2,1)S(1)} %join.7.refs_1_, bf16[44,16,128]{2,1,0:T(8,128)(2,1)S(1)} %collective-permute-done.22.refs_2_, ...), custom_call_target="tpu_custom_call" | custom-call | tf_op jit(solution)/shard_map/final/pallas_call | solution.py:414
  (76 shorter events, 2.5 us)
Async XLA Ops:
  1.4 8.5 %collective-permute-start = (bf16[96,64]{1,0:T(8,128)(2,1)S(1)}, bf16[96,64]{1,0:T(8,128)(2,1)S(1)}, u32[]{:S(2)}, u32[]{:S(2)}) collective-permute-start(bf16[96,64]{1,0:T(8,128)(2,1)S(1)} %slice.12), channel_id=1, source_target_pairs={{0,2},{1,3},{2,0},{3,1},{4,6},{5,7},{6,4},{7,5},{8,10},{9,11},{10,... | collective-permute-start | bytes 36872 | tf_op jit(solution)/shard_map/ppermute | solution.py:284
  1.8 8.1 %collective-permute-start.1 = (bf16[96,64]{1,0:T(8,128)(2,1)S(1)}, bf16[96,64]{1,0:T(8,128)(2,1)S(1)}, u32[]{:S(2)}, u32[]{:S(2)}) collective-permute-start(bf16[96,64]{1,0:T(8,128)(2,1)S(1)} %slice.12), channel_id=1, source_target_pairs={{1,2},{0,3},{3,0},{2,1},{5,6},{4,7},{7,4},{6,5},{9,10},{8,11},{11,... | collective-permute-start | bytes 36872 | tf_op jit(solution)/shard_map/ppermute | solution.py:284
  4.5 6.2 %collective-permute-start.2 = (bf16[96,64]{1,0:T(8,128)(2,1)S(1)}, bf16[96,64]{1,0:T(8,128)(2,1)S(1)}, u32[]{:S(2)}, u32[]{:S(2)}) collective-permute-start(bf16[96,64]{1,0:T(8,128)(2,1)S(1)} %slice.12), channel_id=1, source_target_pairs={{2,4},{3,5},{6,8},{7,9},{10,12},{11,13},{14,16},{15,17},{18,20},{1... | collective-permute-start | bytes 36872 | tf_op jit(solution)/shard_map/ppermute | solution.py:284
  5.1 6.1 %collective-permute-start.3 = (bf16[96,64]{1,0:T(8,128)(2,1)S(1)}, bf16[96,64]{1,0:T(8,128)(2,1)S(1)}, u32[]{:S(2)}, u32[]{:S(2)}) collective-permute-start(bf16[96,64]{1,0:T(8,128)(2,1)S(1)} %slice.12), channel_id=1, source_target_pairs={{3,4},{2,5},{7,8},{6,9},{11,12},{10,13},{15,16},{14,17},{19,20},{1... | collective-permute-start | bytes 36872 | tf_op jit(solution)/shard_map/ppermute | solution.py:284
  5.8 6.1 %collective-permute-start.4 = (bf16[96,64]{1,0:T(8,128)(2,1)S(1)}, bf16[96,64]{1,0:T(8,128)(2,1)S(1)}, u32[]{:S(2)}, u32[]{:S(2)}) collective-permute-start(bf16[96,64]{1,0:T(8,128)(2,1)S(1)} %slice.12), channel_id=1, source_target_pairs={{1,0},{0,1},{3,2},{2,3},{5,4},{4,5},{7,6},{6,7},{9,8},{8,9},{11,10... | collective-permute-start | bytes 36872 | tf_op jit(solution)/shard_map/ppermute | solution.py:284
  5.9 0.8 %copy-start.5 = (bf16[256,96]{0,1:T(8,128)(2,1)S(1)}, bf16[256,96]{0,1:T(8,128)(2,1)}, u32[]{:S(2)}) copy-start(bf16[256,96]{0,1:T(8,128)(2,1)} %param.6) | copy-start | bytes 147460
  6.7 0.8 %copy-start.24 = (s32[256,27]{0,1:T(8,128)S(1)}, s32[256,27]{0,1:T(8,128)}, u32[]{:S(2)}) copy-start(s32[256,27]{0,1:T(8,128)} %param.7) | copy-start | bytes 82948
  7.4 1.7 %copy-start.17 = (bf16[64,128]{1,0:T(8,128)(2,1)S(1)}, bf16[64,128]{1,0:T(8,128)(2,1)}, u32[]{:S(2)}) copy-start(bf16[64,128]{1,0:T(8,128)(2,1)} %cgrad_ref.3) | copy-start | bytes 49156
  7.4 1.7 %copy-start.18 = (bf16[768,128]{1,0:T(8,128)(2,1)S(1)}, bf16[768,128]{1,0:T(8,128)(2,1)}, u32[]{:S(2)}) copy-start(bf16[768,128]{1,0:T(8,128)(2,1)} %refs_2_.1) | copy-start | bytes 589828
  7.4 1.7 %copy-start.26 = (s32[64,8]{0,1:T(8,128)S(1)}, s32[64,8]{0,1:T(8,128)}, u32[]{:S(2)}) copy-start(s32[64,8]{0,1:T(8,128)} %param.8) | copy-start | bytes 6148
  9.1 3.3 %copy-start = (bf16[2592,96]{0,1:T(8,128)(2,1)S(1)}, bf16[2592,96]{0,1:T(8,128)(2,1)}, u32[]{:S(2)}) copy-start(bf16[2592,96]{0,1:T(8,128)(2,1)} %param.9) | copy-start | bytes 1492996
  9.2 3.3 %copy-start.6 = (bf16[256,96]{0,1:T(8,128)(2,1)S(1)}, bf16[256,96]{0,1:T(8,128)(2,1)}, u32[]{:S(2)}) copy-start(bf16[256,96]{0,1:T(8,128)(2,1)} %param.6) | copy-start | bytes 147460
  9.9 8.5 %copy-start.3 = (bf16[8,64,256]{2,1,0:T(8,128)(2,1)}, bf16[8,64,256]{2,1,0:T(8,128)(2,1)S(1)}, u32[]{:S(2)}) copy-start(bf16[8,64,256]{2,1,0:T(8,128)(2,1)S(1)} %get-tuple-element.50.refs_3_.refs_0_) | copy-start | bytes 786436
  9.9 10.5 %copy-start.7 = (f32[96,256]{1,0:T(8,128)}, f32[96,256]{1,0:T(8,128)S(1)}, u32[]{:S(2)}) copy-start(f32[96,256]{1,0:T(8,128)S(1)} %get-tuple-element.47.refs_4_.hgrad_ref) | copy-start | bytes 294916
  9.9 0.7 copy-start.9
  10.6 0.6 copy-start.11
  12.5 0.7 %copy-start.10 = (bf16[96,64]{1,0:T(8,128)(2,1)S(1)}, bf16[96,64]{1,0:T(8,128)(2,1)}, u32[]{:S(2)}) copy-start(bf16[96,64]{1,0:T(8,128)(2,1)} %copy-done.9) | copy-start | bytes 36868
  13.2 0.7 %copy-start.12 = (bf16[96,64]{1,0:T(8,128)(2,1)S(1)}, bf16[96,64]{1,0:T(8,128)(2,1)}, u32[]{:S(2)}) copy-start(bf16[96,64]{1,0:T(8,128)(2,1)} %copy-done.11) | copy-start | bytes 36868
  13.9 0.7 %copy-start.14 = (bf16[96,64]{1,0:T(8,128)(2,1)S(1)}, bf16[96,64]{1,0:T(8,128)(2,1)}, u32[]{:S(2)}) copy-start(bf16[96,64]{1,0:T(8,128)(2,1)} %copy-done.13) | copy-start | bytes 36868
  14.7 0.7 %copy-start.16 = (bf16[96,64]{1,0:T(8,128)(2,1)S(1)}, bf16[96,64]{1,0:T(8,128)(2,1)}, u32[]{:S(2)}) copy-start(bf16[96,64]{1,0:T(8,128)(2,1)} %copy-done.15) | copy-start | bytes 36868
  18.4 0.7 %copy-start.1 = (f32[44,16,128]{2,1,0:T(8,128)}, f32[44,16,128]{2,1,0:T(8,128)S(1)}, u32[]{:S(2)}) copy-start(f32[44,16,128]{2,1,0:T(8,128)S(1)} %get-tuple-element.77.own_ref) | copy-start | bytes 1081348
  19.8 0.6 copy-start.22
  20.4 6.9 %collective-permute-start.15 = (bf16[44,16,128]{2,1,0:T(8,128)(2,1)}, bf16[44,16,128]{2,1,0:T(8,128)(2,1)}, u32[]{:S(2)}, u32[]{:S(2)}) collective-permute-start(bf16[44,16,128]{2,1,0:T(8,128)(2,1)} %get-tuple-element.78), channel_id=1, source_target_pairs={{0,2},{2,0},{1,3},{3,1},{4,6},{6,4},{5,7},{7,5},{8,10},{10,8},{9,1... | collective-permute-start | bytes 540680 | tf_op jit(solution)/shard_map/ppermute | solution.py:350
  25.8 5.8 %collective-permute-start.5 = (bf16[44,16,128]{2,1,0:T(8,128)(2,1)}, bf16[44,16,128]{2,1,0:T(8,128)(2,1)}, u32[]{:S(2)}, u32[]{:S(2)}) collective-permute-start(bf16[44,16,128]{2,1,0:T(8,128)(2,1)} %get-tuple-element.52), channel_id=1, source_target_pairs={{0,2},{2,0},{1,3},{3,1},{4,6},{6,4},{5,7},{7,5},{8,10},{10,8},{9,1... | collective-permute-start | bytes 540680 | tf_op jit(solution)/shard_map/ppermute | solution.py:350
  27.2 1.0 %copy-start.2 = (f32[44,16,128]{2,1,0:T(8,128)S(1)}, f32[44,16,128]{2,1,0:T(8,128)}, u32[]{:S(2)}) copy-start(f32[44,16,128]{2,1,0:T(8,128)} %copy-done.1) | copy-start | bytes 1081348
  29.2 5.0 %collective-permute-start.16 = (bf16[22,16,128]{2,1,0:T(8,128)(2,1)S(1)}, bf16[22,16,128]{2,1,0:T(8,128)(2,1)S(1)}, u32[]{:S(2)}, u32[]{:S(2)}) collective-permute-start(bf16[22,16,128]{2,1,0:T(8,128)(2,1)S(1)} %get-tuple-element.80), channel_id=1, source_target_pairs={{0,4},{1,5},{2,3},{3,2},{4,0},{5,1},{6,7},{7,6},{8,12},{9,13},{10,... | collective-permute-start | bytes 270344 | tf_op jit(solution)/shard_map/ppermute | solution.py:357
  32.6 10.4 %collective-permute-start.6 = (bf16[22,16,128]{2,1,0:T(8,128)(2,1)S(1)}, bf16[22,16,128]{2,1,0:T(8,128)(2,1)S(1)}, u32[]{:S(2)}, u32[]{:S(2)}) collective-permute-start(bf16[22,16,128]{2,1,0:T(8,128)(2,1)S(1)} %get-tuple-element.59), channel_id=1, source_target_pairs={{0,4},{1,5},{2,3},{3,2},{4,0},{5,1},{6,7},{7,6},{8,12},{9,13},{10,... | collective-permute-start | bytes 270344 | tf_op jit(solution)/shard_map/ppermute | solution.py:357
  34.2 10.5 %collective-permute-start.17 = (bf16[11,16,128]{2,1,0:T(8,128)(2,1)S(1)}, bf16[11,16,128]{2,1,0:T(8,128)(2,1)S(1)}, u32[]{:S(2)}, u32[]{:S(2)}) collective-permute-start(bf16[11,16,128]{2,1,0:T(8,128)(2,1)S(1)} %get-tuple-element.82), channel_id=1, source_target_pairs={{0,1},{1,0},{2,6},{3,7},{4,5},{5,4},{6,2},{7,3},{8,9},{9,8},{10,14... | collective-permute-start | bytes 135176 | tf_op jit(solution)/shard_map/ppermute | solution.py:357
  34.7 0.9 %copy-start.4 = (bf16[8,64,256]{2,1,0:T(8,128)(2,1)S(1)}, bf16[8,64,256]{2,1,0:T(8,128)(2,1)}, u32[]{:S(2)}) copy-start(bf16[8,64,256]{2,1,0:T(8,128)(2,1)} %copy-done.3) | copy-start | bytes 786436
  35.7 0.9 %copy-start.8 = (f32[96,256]{1,0:T(8,128)S(1)}, f32[96,256]{1,0:T(8,128)}, u32[]{:S(2)}) copy-start(f32[96,256]{1,0:T(8,128)} %copy-done.7) | copy-start | bytes 294916
  36.6 0.9 %copy-start.19 = (bf16[768,128]{1,0:T(8,128)(2,1)S(1)}, bf16[768,128]{1,0:T(8,128)(2,1)}, u32[]{:S(2)}) copy-start(bf16[768,128]{1,0:T(8,128)(2,1)} %refs_2_.1) | copy-start | bytes 589828
  37.5 0.8 %copy-start.21 = (bf16[96,256]{1,0:T(8,128)(2,1)S(1)}, bf16[96,256]{1,0:T(8,128)(2,1)}, u32[]{:S(2)}) copy-start(bf16[96,256]{1,0:T(8,128)(2,1)} %copy-done.20) | copy-start | bytes 147460
  38.3 0.8 %copy-start.23 = (bf16[96,256]{1,0:T(8,128)(2,1)S(1)}, bf16[96,256]{1,0:T(8,128)(2,1)}, u32[]{:S(2)}) copy-start(bf16[96,256]{1,0:T(8,128)(2,1)} %copy-done.22) | copy-start | bytes 147460
  39.1 0.8 %copy-start.25 = (s32[256,27]{0,1:T(8,128)S(1)}, s32[256,27]{0,1:T(8,128)}, u32[]{:S(2)}) copy-start(s32[256,27]{0,1:T(8,128)} %param.7) | copy-start | bytes 82948
  43.1 4.4 %collective-permute-start.7 = (bf16[11,16,128]{2,1,0:T(8,128)(2,1)S(1)}, bf16[11,16,128]{2,1,0:T(8,128)(2,1)S(1)}, u32[]{:S(2)}, u32[]{:S(2)}) collective-permute-start(bf16[11,16,128]{2,1,0:T(8,128)(2,1)S(1)} %get-tuple-element.66), channel_id=1, source_target_pairs={{0,1},{1,0},{2,6},{3,7},{4,5},{5,4},{6,2},{7,3},{8,9},{9,8},{10,14... | collective-permute-start | bytes 135176 | tf_op jit(solution)/shard_map/ppermute | solution.py:357
  44.7 5.3 %collective-permute-start.18 = (bf16[11,16,128]{2,1,0:T(8,128)(2,1)S(1)}, bf16[11,16,128]{2,1,0:T(8,128)(2,1)S(1)}, u32[]{:S(2)}, u32[]{:S(2)}) collective-permute-start(bf16[11,16,128]{2,1,0:T(8,128)(2,1)S(1)} %add_convert_fusion.2), channel_id=1, source_target_pairs={{0,8},{8,0},{16,24},{24,16},{1,9},{9,1},{17,25},{25,17},{2,10},{10... | collective-permute-start | bytes 135176 | tf_op jit(solution)/shard_map/ppermute | solution.py:389
  47.4 5.6 %collective-permute-start.8 = (bf16[11,16,128]{2,1,0:T(8,128)(2,1)S(1)}, bf16[11,16,128]{2,1,0:T(8,128)(2,1)S(1)}, u32[]{:S(2)}, u32[]{:S(2)}) collective-permute-start(bf16[11,16,128]{2,1,0:T(8,128)(2,1)S(1)} %add_convert_fusion.5), channel_id=1, source_target_pairs={{0,8},{8,0},{16,24},{24,16},{1,9},{9,1},{17,25},{25,17},{2,10},{10... | collective-permute-start | bytes 135176 | tf_op jit(solution)/shard_map/ppermute | solution.py:389
  50.0 5.1 %collective-permute-start.19 = (bf16[11,16,128]{2,1,0:T(8,128)(2,1)S(1)}, bf16[11,16,128]{2,1,0:T(8,128)(2,1)S(1)}, u32[]{:S(2)}, u32[]{:S(2)}) collective-permute-start(bf16[11,16,128]{2,1,0:T(8,128)(2,1)S(1)} %add_convert_fusion.1), channel_id=1, source_target_pairs={{0,16},{8,24},{16,0},{24,8},{1,17},{9,25},{17,1},{25,9},{2,18},{10... | collective-permute-start | bytes 135176 | tf_op jit(solution)/shard_map/ppermute | solution.py:389
  53.0 5.0 %collective-permute-start.9 = (bf16[11,16,128]{2,1,0:T(8,128)(2,1)S(1)}, bf16[11,16,128]{2,1,0:T(8,128)(2,1)S(1)}, u32[]{:S(2)}, u32[]{:S(2)}) collective-permute-start(bf16[11,16,128]{2,1,0:T(8,128)(2,1)S(1)} %add_convert_fusion.4), channel_id=1, source_target_pairs={{0,16},{8,24},{16,0},{24,8},{1,17},{9,25},{17,1},{25,9},{2,18},{10... | collective-permute-start | bytes 135176 | tf_op jit(solution)/shard_map/ppermute | solution.py:389
  55.1 4.8 %collective-permute-start.20 = (bf16[11,16,128]{2,1,0:T(8,128)(2,1)S(1)}, bf16[11,16,128]{2,1,0:T(8,128)(2,1)S(1)}, u32[]{:S(2)}, u32[]{:S(2)}) collective-permute-start(bf16[11,16,128]{2,1,0:T(8,128)(2,1)S(1)} %add_convert_fusion.own_ref), channel_id=1, source_target_pairs={{0,1},{1,0},{2,6},{3,7},{4,5},{5,4},{6,2},{7,3},{8,9},{9,8},{10,14... | collective-permute-start | bytes 135176 | tf_op jit(solution)/shard_map/ppermute | solution.py:394
  58.0 5.4 %collective-permute-start.10 = (bf16[11,16,128]{2,1,0:T(8,128)(2,1)S(1)}, bf16[11,16,128]{2,1,0:T(8,128)(2,1)S(1)}, u32[]{:S(2)}, u32[]{:S(2)}) collective-permute-start(bf16[11,16,128]{2,1,0:T(8,128)(2,1)S(1)} %add_convert_fusion.3.own_ref), channel_id=1, source_target_pairs={{0,1},{1,0},{2,6},{3,7},{4,5},{5,4},{6,2},{7,3},{8,9},{9,8},{10,14... | collective-permute-start | bytes 135176 | tf_op jit(solution)/shard_map/ppermute | solution.py:394
  59.3 4.1 %collective-permute-start.11 = (bf16[96,128]{1,0:T(8,128)(2,1)S(1)}, bf16[96,128]{1,0:T(8,128)(2,1)S(1)}, u32[]{:S(2)}, u32[]{:S(2)}) collective-permute-start(bf16[96,128]{1,0:T(8,128)(2,1)S(1)} %get-tuple-element.70), channel_id=1, source_target_pairs={{0,2},{2,0},{4,6},{6,4},{8,10},{10,8},{12,14},{14,12},{16,18},{18,... | collective-permute-start | bytes 73736 | tf_op jit(solution)/shard_map/ppermute | solution.py:391
  59.3 4.1 %collective-permute-start.12 = (bf16[96,128]{1,0:T(8,128)(2,1)S(1)}, bf16[96,128]{1,0:T(8,128)(2,1)S(1)}, u32[]{:S(2)}, u32[]{:S(2)}) collective-permute-start(bf16[96,128]{1,0:T(8,128)(2,1)S(1)} %get-tuple-element.71), channel_id=1, source_target_pairs={{2,4},{6,8},{10,12},{14,16},{18,20},{22,24},{26,28},{4,2},{8,6},{1... | collective-permute-start | bytes 73736 | tf_op jit(solution)/shard_map/ppermute | solution.py:391
  59.9 6.5 %collective-permute-start.21 = (bf16[22,16,128]{2,1,0:T(8,128)(2,1)S(1)}, bf16[22,16,128]{2,1,0:T(8,128)(2,1)S(1)}, u32[]{:S(2)}, u32[]{:S(2)}) collective-permute-start(bf16[22,16,128]{2,1,0:T(8,128)(2,1)S(1)} %join.6.own_ref), channel_id=1, source_target_pairs={{0,4},{1,5},{2,3},{3,2},{4,0},{5,1},{6,7},{7,6},{8,12},{9,13},{10,... | collective-permute-start | bytes 270344 | tf_op jit(solution)/shard_map/ppermute | solution.py:394
  63.4 5.8 %collective-permute-start.13 = (bf16[22,16,128]{2,1,0:T(8,128)(2,1)S(1)}, bf16[22,16,128]{2,1,0:T(8,128)(2,1)S(1)}, u32[]{:S(2)}, u32[]{:S(2)}) collective-permute-start(bf16[22,16,128]{2,1,0:T(8,128)(2,1)S(1)} %join.4.own_ref), channel_id=1, source_target_pairs={{0,4},{1,5},{2,3},{3,2},{4,0},{5,1},{6,7},{7,6},{8,12},{9,13},{10,... | collective-permute-start | bytes 270344 | tf_op jit(solution)/shard_map/ppermute | solution.py:394
  65.3 3.9 %collective-permute-start.14 = (bf16[96,64]{1,0:T(8,128)(2,1)S(1)}, bf16[96,64]{1,0:T(8,128)(2,1)S(1)}, u32[]{:S(2)}, u32[]{:S(2)}) collective-permute-start(bf16[96,64]{1,0:T(8,128)(2,1)S(1)} %get-tuple-element.89), channel_id=1, source_target_pairs={{0,1},{1,0},{2,3},{3,2},{4,5},{5,4},{6,7},{7,6},{8,9},{9,8},{10,11... | collective-permute-start | bytes 36872 | tf_op jit(solution)/shard_map/ppermute | solution.py:409
  66.5 2.8 %collective-permute-start.23 = (bf16[44,16,128]{2,1,0:T(8,128)(2,1)S(1)}, bf16[44,16,128]{2,1,0:T(8,128)(2,1)S(1)}, u32[]{:S(2)}, u32[]{:S(2)}) collective-permute-start(bf16[44,16,128]{2,1,0:T(8,128)(2,1)S(1)} %join.7.refs_1_), channel_id=1, source_target_pairs={{0,2},{2,0},{1,3},{3,1},{4,6},{6,4},{5,7},{7,5},{8,10},{10,8},{9,1... | collective-permute-start | bytes 540680 | tf_op jit(solution)/shard_map/ppermute | solution.py:413
  69.2 1.5 %collective-permute-start.22 = (bf16[44,16,128]{2,1,0:T(8,128)(2,1)S(1)}, bf16[44,16,128]{2,1,0:T(8,128)(2,1)S(1)}, u32[]{:S(2)}, u32[]{:S(2)}) collective-permute-start(bf16[44,16,128]{2,1,0:T(8,128)(2,1)S(1)} %join.5.refs_0_), channel_id=1, source_target_pairs={{0,2},{2,0},{1,3},{3,1},{4,6},{6,4},{5,7},{7,5},{8,10},{10,8},{9,1... | collective-permute-start | bytes 540680 | tf_op jit(solution)/shard_map/ppermute | solution.py:413
  (3 other events, 1.8 us)

commit v5 on v4

--- a/solution.py
+++ b/solution.py
@@ -62,19 +62,16 @@
     return jnp.concatenate(halo, axis=1)
 
 
-def gather_kernel(slabs, core_ref, f_ref, near_ref, first_ref, rest_ref, far_ref):
+def gather_kernel(slabs, f_ref, near_ref, first_ref, rest_ref):
     channels, voxels = f_ref.shape
     table_t = f_ref[...]
-    lanes = table_lanes(near_ref[...], voxels, slabs, core_ref[0])
-    far_iota = lax.broadcasted_iota(jnp.int32, (far_ref.shape[0], LANES), 0) + voxels
+    lanes = table_lanes(near_ref[...], voxels, slabs, 0)
     near_iota = lax.broadcasted_iota(jnp.int32, (voxels, voxels), 0)
     for o in range(near_ref.shape[0]):
         near = jnp.where(near_iota == lanes[o : o + 1, :], 1.0, 0.0).astype(BF16)
         own = mm(table_t, near).astype(BF16)
         first_ref[o * channels : (o + 1) * channels, :] = own[:, :LANES]
         rest_ref[o * channels : (o + 1) * channels, :] = own[:, LANES:]
-        away = jnp.where(far_iota == lanes[o : o + 1, :LANES], 1.0, 0.0).astype(BF16)
-        far_ref[:, o * LANES : (o + 1) * LANES] = away
 
 
 def taps_kernel(down_ref, cgrad_ref, wd_ref, pick_ref, hgrad_ref):
@@ -92,21 +89,28 @@
     hgrad_ref[...] = hgrad_t
 
 
-def forward_kernel(halo_count, core_ref, f_ref, cgrad_ref, w_ref, *refs):
-    first_ref, rest_ref, far_ref, pick_ref, hgrad_ref = refs[:5]
-    halo_refs, refs = refs[5 : 5 + halo_count], refs[5 + halo_count :]
+def far_one_hots(lanes, rows, voxels, offsets):
+    iota = lax.broadcasted_iota(jnp.int32, (rows, LANES), 0) + voxels
+    hots = [jnp.where(iota == lanes[o : o + 1, :LANES], 1.0, 0.0).astype(BF16) for o in offsets]
+    return jnp.concatenate(hots, axis=1)
+
+
+def forward_kernel(slabs, core_ref, f_ref, near_ref, cgrad_ref, w_ref, *refs):
+    first_ref, rest_ref, pick_ref, hgrad_ref = refs[:4]
+    halo_refs, refs = (refs[4:7], refs[7:]) if slabs == 2 else (refs[4:8], refs[8:])
     grad_ref, hidden_ref, *chunks, rt, conv_w, down_w = refs
-    channels = f_ref.shape[0]
-    offsets = far_ref.shape[1] // LANES
+    channels, voxels = f_ref.shape
+    offsets = near_ref.shape[0]
     taps = pick_ref.shape[0]
     conv_columns = offsets * channels
     halo_t = padded_halo(halo_refs)
+    lanes = table_lanes(near_ref[:, :LANES], voxels, slabs, core_ref[0])
     for pair in range(0, offsets, 2):
-        away = mm(halo_t, far_ref[:, pair * LANES : min(pair + 2, offsets) * LANES])
-        for o in range(pair, min(pair + 2, offsets)):
+        pair = range(pair, min(pair + 2, offsets))
+        away = mm(halo_t, far_one_hots(lanes, halo_t.shape[1], voxels, pair))
+        for i, o in enumerate(pair):
             rows = slice(o * channels, (o + 1) * channels)
-            lanes = slice((o - pair) * LANES, (o - pair + 1) * LANES)
-            first = first_ref[rows, :].astype(F32) + away[:, lanes]
+            first = first_ref[rows, :].astype(F32) + away[:, i * LANES : (i + 1) * LANES]
             rt[rows, :LANES] = first.astype(BF16)
             rt[rows, LANES:] = rest_ref[rows, :]
 
@@ -145,12 +149,11 @@
                 ref[place] = value.astype(ref.dtype)
 
 
-def backward_kernel(slabs, core_ref, near_ref, far_ref, hgrad_ref, grad_ref, w_ref, *refs):
-    pick_ref, hidden_ref, wd_ref, *refs = refs
-    coarse_ref, base_ref, mate_ref, cross_ref, side_ref, drt, drt_far, hot, w_back = refs
+def backward_kernel(slabs, core_ref, near_ref, hgrad_ref, grad_ref, w_ref, *refs):
+    pick_ref, hidden_ref, wd_ref, coarse_ref, base_ref, keep_ref, *refs = refs
+    cross_refs, (drt, drt_far, hot, far, w_back) = refs[:-5], refs[-5:]
     channels, voxels = hgrad_ref.shape
     offsets = near_ref.shape[0]
-    group = mate_ref.shape[1]
     coarse = jnp.zeros(coarse_ref.shape, F32)
     for t in range(pick_ref.shape[0]):
         picked = mm(pick_ref[t], hidden_ref[...], NT).astype(BF16)
@@ -168,11 +171,31 @@
         spread = mm(w_back[o * channels : (o + 1) * channels, :], grad_pad).astype(BF16)
         drt[:, o * voxels : (o + 1) * voxels] = spread
         drt_far[:, o * LANES : (o + 1) * LANES] = spread[:, :LANES]
+        far[:, o * LANES : (o + 1) * LANES] = far_one_hots(lanes, far.shape[0], voxels, (o,))
     base_ref[...] = hgrad_ref[...] + mm(drt[...], hot[...], NT)
-    back_t = mm(drt_far[...], far_ref[...], NT).astype(BF16)
-    mate_ref[...] = back_t[:, :group]
-    cross_ref[...] = back_t[:, group : 2 * group]
-    side_ref[...] = back_t[:, 2 * group : 2 * group + side_ref.shape[1]]
+    back_t = mm(drt_far[...], far[...], NT)
+    rims = 2 if slabs == 2 else 3
+    mid = 0 if slabs == 2 else 1
+    rim = [back_t[:, i * RIM : (i + 1) * RIM] for i in range(2 * rims + len(cross_refs))]
+    keep_ref[...] = jnp.concatenate([rim[mid], rim[rims + mid]], axis=1)
+    for i, ref in enumerate(cross_refs):
+        place = 1 if slabs == 2 else 2 * i
+        parts = [rim[place], rim[rims + place], rim[2 * rims + i], jnp.zeros_like(rim[0])]
+        ref[...] = jnp.concatenate(parts, axis=1).astype(BF16)
+
+
+def turn_kernel(base_ref, keep_ref, *refs):
+    got_refs, (sum_ref, cross_ref, mate_ref) = refs[:-3], refs[-3:]
+    got = got_refs[0][...].astype(F32)
+    for ref in got_refs[1:]:
+        got += ref[...].astype(F32)
+    sum_ref[:, RIM:] = base_ref[:, RIM:]
+    sum_ref[:, :RIM] = base_ref[:, :RIM] + got[:, 2 * RIM : 3 * RIM]
+    pair = keep_ref[...] + got[:, : 2 * RIM]
+    cross_ref[...] = pair[:, RIM:].astype(BF16)
+    pair = pair.astype(BF16)
+    for i in range(mate_ref.shape[0]):
+        mate_ref[i] = pair[i * TILE : (i + 1) * TILE, :]
 
 
 def fold_kernel(bit_ref, own_ref, got_ref, keep_ref, send_ref):
@@ -182,22 +205,24 @@
         ref[...] = (own_ref[rows] + got_ref[rows].astype(F32)).astype(ref.dtype)
 
 
-def join_kernel(bit_ref, own_ref, got_ref, full_ref):
+def join_kernel(bit_ref, own_ref, got_ref, *refs):
+    riders, full_ref = refs[:-1], refs[-1]
     half = own_ref.shape[0]
+    for rider in riders:
+        full_ref[2 * half :] = rider[...]
     full_ref[pl.ds(bit_ref[0] * half, half)] = own_ref[...]
     full_ref[pl.ds((1 - bit_ref[0]) * half, half)] = got_ref[...]
 
 
-def final_kernel(taps, count, core_ref, *refs):
+def final_kernel(taps, count, size, core_ref, *refs):
     mine, other, refs = refs[:count], refs[count : 2 * count], refs[2 * count :]
-    base_ref, *parts, conv_ref, down_ref, grad_ref = refs
+    base_ref, cross_ref, conv_ref, down_ref, grad_ref = refs
     channels, conv_columns = conv_ref.shape
-    size = mine[0].shape[0]
-    total = parts[0][...].astype(F32)
-    for ref in parts[1:]:
-        total += ref[...].astype(F32)
     grad_ref[:, RIM:] = base_ref[:, RIM:]
-    grad_ref[:, :RIM] = base_ref[:, :RIM] + total
+    for i in range(channels // TILE):
+        rows = slice(i * TILE, (i + 1) * TILE)
+        total = base_ref[rows, :RIM] + cross_ref[rows, :].astype(F32)
+        grad_ref[rows, :RIM] = total + other[-1][size + i][:, :RIM].astype(F32)
     for core in range(2):
 
         @pl.when(core_ref[0] == core)
@@ -218,16 +243,6 @@
     mates = [(i, i ^ 1) for i in range(regions)]
     cross = [(i, i + 1) for i in range(1, regions - 1, 2)]
     return mates, cross + [(b, a) for a, b in cross]
-
-
-def halo_pairs(regions, slabs, links, step):
-    pairs = []
-    for owner, reader in links:
-        for slab in range(slabs):
-            other = (slab + step) % 2 if slabs == 2 else slab + step
-            if 0 <= other < slabs:
-                pairs.append((owner * slabs + other, reader * slabs + slab))
-    return pairs
 
 
 def square_bits(nears, slabs, core):
@@ -273,30 +288,27 @@
     light = pl.CostEstimate(flops=2 * 10**9, bytes_accessed=10**7, transcendentals=0)
     features_t, neighbours_t, w_conv_t = features.T, neighbours.T, w_conv.T
     rim = features_t[:, :RIM]
-    here = [(i, i) for i in range(regions)]
-    around = (0, 1) if slabs == 2 else (-1, 0, 1)
-    beside = (1,) if slabs == 2 else (-1, 1)
-    sections = [(x, s) for x in (mates, crossings) for s in around] + [(here, s) for s in beside]
-    halos = [None] * len(sections)
-    for wanted in (crossings, mates, here):
-        for i, (links, step) in sorted(enumerate(sections), key=lambda x: -abs(x[1][1])):
-            if links is wanted:
-                halos[i] = lax.ppermute(rim, SPLIT, halo_pairs(regions, slabs, links, step))
-    group, beside = len(around) * RIM, len(beside) * RIM
-    far_rows = -(-(2 * group + beside) // LANES) * LANES
+    if slabs == 2:
+        beside = [swap]
+    else:
+        beside = [shifts(slabs, 1), shifts(slabs, -1)]
+    side = [lax.ppermute(rim, "slab", pairs) for pairs in beside]
     own = pl.pallas_call(
         functools.partial(gather_kernel, slabs),
         out_shape=(
             jax.ShapeDtypeStruct((conv_columns, LANES), BF16),
             jax.ShapeDtypeStruct((conv_columns, voxels - LANES), BF16),
-            jax.ShapeDtypeStruct((far_rows, offsets * LANES), BF16),
         ),
-        in_specs=[smem, vmem, vmem],
         compiler_params=params,
         cost_estimate=light,
         name="gather",
-    )(core, features_t, neighbours_t)
-    far = own[2]
+    )(features_t, neighbours_t)
+    side, own = lax.optimization_barrier((side, own))
+    row = [rim, side[0]] if slabs == 2 else [side[0], rim, side[1]]
+    row = jnp.concatenate(row, axis=1)
+    cross = lax.ppermute(row, RING, crossings)
+    mate = lax.ppermute(row, RING, mates)
+    row, down_t = lax.optimization_barrier((row, down_map.T))
     pick, hgrad = pl.pallas_call(
         taps_kernel,
         out_shape=(
@@ -306,12 +318,14 @@
         compiler_params=params,
         cost_estimate=light,
         name="taps",
-    )(down_map.T, coarse_grad, w_down)
+    )(down_t, coarse_grad, w_down)
+    halos = [mate, cross, *side]
+    far_rows = -(-sum(x.shape[1] for x in halos) // LANES) * LANES
 
     tiles = len(payload_tiles(channels, conv_columns, taps))
     size = -(-tiles // (2 * CHUNKS << phases)) << phases
     grad, hidden, *chunks = pl.pallas_call(
-        functools.partial(forward_kernel, len(halos)),
+        functools.partial(forward_kernel, slabs),
         out_shape=[
             jax.ShapeDtypeStruct((channels, voxels), BF16),
             jax.ShapeDtypeStruct((channels, voxels), BF16),
@@ -325,7 +339,7 @@
         ],
         compiler_params=params,
         name="forward",
-    )(core, features_t, coarse_grad, w_conv_t, *own, pick, hgrad, *halos)
+    )(core, features_t, neighbours_t, coarse_grad, w_conv_t, *own, pick, hgrad, *halos)
 
     def fold(phase, keep, got):
         shape = (keep.shape[0] // 2, TILE, LANES)
@@ -337,14 +351,15 @@
             name="fold",
         )(bits[phase], keep, got)
 
-    def join(phase, own, got):
+    def join(phase, own, got, *riders):
+        count = own.shape[0] * 2 + sum(x.shape[0] for x in riders)
         return pl.pallas_call(
             join_kernel,
-            out_shape=jax.ShapeDtypeStruct((own.shape[0] * 2, TILE, LANES), BF16),
-            in_specs=[smem, vmem, vmem],
+            out_shape=jax.ShapeDtypeStruct((count, TILE, LANES), BF16),
+            in_specs=[smem] + [vmem] * (2 + len(riders)),
             compiler_params=params,
             name="join",
-        )(bits[phase], own, got)
+        )(bits[phase], own, got, *riders)
 
     keep, send = chunks[0::2], chunks[1::2]
     got = [lax.ppermute(x, "core", swap) for x in send]
@@ -356,72 +371,67 @@
                 send[0], grad = lax.optimization_barrier((send[0], grad))
             got[i] = lax.ppermute(send[i], SPLIT, pairs)
         if phase == 0:
-            coarse, base, mate, cross, own_side = pl.pallas_call(
+            coarse, base, stay, *edges = pl.pallas_call(
                 functools.partial(backward_kernel, slabs),
-                out_shape=(
+                out_shape=[
                     jax.ShapeDtypeStruct(coarse_grad.shape, BF16),
                     jax.ShapeDtypeStruct((channels, voxels), F32),
-                    jax.ShapeDtypeStruct((channels, group), BF16),
-                    jax.ShapeDtypeStruct((channels, group), BF16),
-                    jax.ShapeDtypeStruct((channels, beside), BF16),
-                ),
-                in_specs=[smem] + [vmem] * 8,
+                    jax.ShapeDtypeStruct((channels, 2 * RIM), F32),
+                ]
+                + [jax.ShapeDtypeStruct((channels, 4 * RIM), BF16)] * len(beside),
+                in_specs=[smem] + [vmem] * 7,
                 scratch_shapes=[
                     pltpu.VMEM((channels, offsets * voxels), BF16),
                     pltpu.VMEM((channels, offsets * LANES), BF16),
                     pltpu.VMEM((voxels, offsets * voxels), BF16),
+                    pltpu.VMEM((far_rows, offsets * LANES), BF16),
                     pltpu.VMEM((conv_columns, LANES), BF16),
                 ],
                 compiler_params=params,
                 cost_estimate=light,
                 name="backward",
-            )(core, neighbours_t, far, hgrad, grad, w_conv_t, pick, hidden, w_down)
-            got[0], mate, cross, own_side, base = lax.optimization_barrier(
-                (got[0], mate, cross, own_side, base)
-            )
+            )(core, neighbours_t, hgrad, grad, w_conv_t, pick, hidden, w_down)
+            got[0], stay, edges, base = lax.optimization_barrier((got[0], stay, edges, base))
+        if phase == phases - 1:
+            back = beside if slabs == 2 else beside[::-1]
+            edges = [lax.ppermute(x, "slab", p) for x, p in zip(edges, back)]
+            got[-1], edges = lax.optimization_barrier((got[-1], edges))
+            base, cross, mate = pl.pallas_call(
+                turn_kernel,
+                out_shape=(
+                    jax.ShapeDtypeStruct((channels, voxels), F32),
+                    jax.ShapeDtypeStruct((channels, RIM), BF16),
+                    jax.ShapeDtypeStruct((channels // TILE, TILE, LANES), BF16),
+                ),
+                compiler_params=params,
+                name="turn",
+            )(base, stay, *edges)
     total = [(x + y.astype(F32)).astype(BF16) for x, y in zip(keep, got)]
     far_bits = sizes["far"].bit_length() - 1
     for bit in range(far_bits):
         pairs = [(i, i ^ (1 << bit)) for i in range(sizes["far"])]
+        got = [lax.ppermute(x, "far", pairs) for x in total]
         if bit == far_bits - 1:
-            total[0], mate, cross = lax.optimization_barrier((total[0], mate, cross))
-        for i in range(CHUNKS):
-            got[i] = lax.ppermute(total[i], "far", pairs)
-            total[i] = (total[i].astype(F32) + got[i].astype(F32)).astype(BF16)
-    cross, mate = lax.ppermute(cross, RING, crossings), lax.ppermute(mate, RING, mates)
+            cross = lax.ppermute(cross, RING, crossings)
+            got[-1], cross, mate = lax.optimization_barrier((got[-1], cross, mate))
+        total = [(x.astype(F32) + y.astype(F32)).astype(BF16) for x, y in zip(total, got)]
     for phase in reversed(range(phases)):
         pairs = bit_pairs(sizes, orders, phase)
         got = [lax.ppermute(x, SPLIT, pairs) for x in total]
-        if phase == phases - 1:
-            got[0], mate, cross = lax.optimization_barrier((got[0], mate, cross))
-            row_grad = mate.astype(F32) + cross.astype(F32)
-            columns = [row_grad[:, i : i + RIM] for i in range(0, group, RIM)]
-            own = [own_side[:, i : i + RIM].astype(F32) for i in range(0, beside, RIM)]
-            if slabs == 2:
-                home = columns[0]
-                edges = [((columns[1] + own[0]).astype(BF16), swap)]
-            else:
-                home = columns[1]
-                edges = [
-                    ((columns[0] + own[0]).astype(BF16), shifts(slabs, -1)),
-                    ((columns[2] + own[1]).astype(BF16), shifts(slabs, 1)),
-                ]
-            edges = [lax.ppermute(x, "slab", p) for x, p in edges]
-        if phase == 0:
-            got[0], edges = lax.optimization_barrier((got[0], edges))
-        total = [join(phase, x, y) for x, y in zip(total, got)]
+        riders = [()] * (CHUNKS - 1) + [(mate,) if phase == 0 else ()]
+        total = [join(phase, x, y, *z) for x, y, z in zip(total, got, riders)]
     other = [lax.ppermute(x, "core", swap) for x in total]
     conv_wgrad_t, down_wgrad, grad_input_t = pl.pallas_call(
-        functools.partial(final_kernel, taps, CHUNKS),
+        functools.partial(final_kernel, taps, CHUNKS, size),
         out_shape=(
             jax.ShapeDtypeStruct((channels, conv_columns), F32),
             jax.ShapeDtypeStruct((taps * channels, LANES), F32),
             jax.ShapeDtypeStruct((channels, voxels), F32),
         ),
-        in_specs=[smem] + [vmem] * (2 * CHUNKS + 2 + len(edges)),
+        in_specs=[smem] + [vmem] * (2 * CHUNKS + 2),
         compiler_params=params,
         name="final",
-    )(core, *total, *other, base, home, *edges)
+    )(core, *total, *other, base, cross)
     return coarse, grad_input_t.T, conv_wgrad_t.T, down_wgrad
 
 

time: 73 us -> 54.9 us (0.75)
  local copies, waits for them, and re-layouts: 15.9 us -> 1.87 us
  starting transfers between devices: 35.7 us -> 24.9 us
  waiting for transfers between devices: 7.52 us -> 17.5 us
  Pallas kernels: 11.8 us -> 9.27 us
    unnamed x54 -> x14, local copies, waits for them, and re-layouts: 15.1 us -> 1.06 us
    ppermute x4, waiting for transfers between devices: 0.01 us -> 5.29 us  [on_device(): got = [lax.ppermute(x, SPLIT, pairs) for x in total]]
    ppermute x12 -> x9, starting transfers between devices: 16.6 us -> 11.6 us  [the longest x4 5.75 us: on_device(): got = [lax.ppermute(x, 'far', pairs) for x in total]]
    ppermute x4, starting transfers between devices: 8.64 us -> 4 us  [on_device(): got = [lax.ppermute(x, SPLIT, pairs) for x in total]]
    ppermute x12 -> x9, waiting for transfers between devices: 3.27 us -> 6.12 us  [the longest x4 6.06 us: on_device(): got = [lax.ppermute(x, 'far', pairs) for x in total]]
    pallas_call x4, Pallas kernels: 1.97 us -> 0.12 us  [fold(): pl.pallas_call(fold_kernel, out_shape=(jax.ShapeDtypeStruct(shape, F32),...]
    ppermute x4, waiting for transfers between devices: 1.46 us -> 3.24 us  [on_device(): got[i] = lax.ppermute(send[i], SPLIT, pairs)]
    ppermute x2, starting transfers between devices: 5.47 us -> 3.96 us  [on_device(): got = [lax.ppermute(x, 'core', swap) for x in send]]
  transfers between devices with their start and end apart: 24 -> 21, of which waited for: 5 -> 9; matrix products, arithmetic and copies ran while one was open for 0% -> 0% of each run, Pallas kernels for 10% -> 9%
where the time goes in v5:
time: 54.9 us; the launch traced here: 54.6 us
  starting transfers between devices  24.9 us (45%)
  waiting for transfers between devices  17.5 us (32%)
  Pallas kernels  9.27 us (17%)
  local copies, waits for them, and re-layouts  1.87 us (3%)
  between operations  0.83 us (2%)
    ppermute x4, waiting for transfers between devices, on_device(): got = [lax.ppermute(x, 'far', pairs) for x in total]  6.06 us
    ppermute x4, starting transfers between devices, on_device(): got = [lax.ppermute(x, 'far', pairs) for x in total]  5.75 us
    ppermute x4, waiting for transfers between devices, on_device(): got = [lax.ppermute(x, SPLIT, pairs) for x in total]  5.29 us
    ppermute x4, starting transfers between devices, on_device(): got[i] = lax.ppermute(send[i], SPLIT, pairs)  5.21 us
    ppermute x4, starting transfers between devices, on_device(): got = [lax.ppermute(x, SPLIT, pairs) for x in total]  4 us
    ppermute x2, starting transfers between devices, on_device(): got = [lax.ppermute(x, 'core', swap) for x in send]  3.96 us
    ppermute x4, waiting for transfers between devices, on_device(): got[i] = lax.ppermute(send[i], SPLIT, pairs)  3.24 us
    pallas_call x1, Pallas kernels, on_device(): pl.pallas_call(functools.partial(backward_kernel, slabs), out_shape=[jax....  3.19 us
  transfers between devices with their start and end apart: 21, of which 9 were waited for; matrix products, arithmetic and copies ran while one was open for 0% of the time, Pallas kernels for 9%

profile of v5, /device:TPU:0, one launch (start us, length us, event | category | flops | bytes accessed | tf_op | source)
XLA Modules:
  0.0 54.6 jit_solution(11608327025171267330)
XLA Ops:
  0.6 0.8 %slice.4 = bf16[96,64]{1,0:T(8,128)(2,1)S(1)} slice(bf16[96,256]{1,0:T(8,128)(2,1)} %bitcast.11), slice={[0:96], [0:64]} | slice | bytes 24576 | tf_op jit(solution)/shard_map/slice | solution.py:290
  1.4 3.0 %collective-permute-start = (bf16[96,64]{1,0:T(8,128)(2,1)S(1)}, bf16[96,64]{1,0:T(8,128)(2,1)S(1)}, u32[]{:S(2)}, u32[]{:S(2)}) collective-permute-start(bf16[96,64]{1,0:T(8,128)(2,1)S(1)} %slice.4), channel_id=1, source_target_pairs={{0,1},{1,0},{2,3},{3,2},{4,5},{5,4},{6,7},{7,6},{8,9},{9,8},{10,11... | collective-permute-start | bytes 36872 | tf_op jit(solution)/shard_map/ppermute | solution.py:295
  4.4 0.8 %copy-done.2 = s32[256,27]{0,1:T(8,128)S(1)} copy-done((s32[256,27]{0,1:T(8,128)S(1)}, s32[256,27]{0,1:T(8,128)}, u32[]{:S(2)}) %copy-start.2) | copy-done | bytes 27672
  5.2 1.0 %gather.1 = (bf16[2592,128]{1,0:T(8,128)(2,1)S(1)}, bf16[2592,128]{1,0:T(8,128)(2,1)S(1)}) custom-call(bf16[96,256]{1,0:T(8,128)(2,1)S(1)} %bitcast.12, s32[27,256]{1,0:T(8,128)S(1)} %bitcast.14), custom_call_target="tpu_custom_call" | custom-call | flops 2000000000 | bytes 10000000 | tf_op jit(solution)/shard_map/gather/pallas_call | solution.py:296
  6.2 0.0 collective-permute-done.refs_6_
  6.2 0.1 pad_maximum_fusion
  6.3 0.0 collective-permute-start.1
  6.3 0.7 %collective-permute-start.2 = (bf16[96,128]{1,0:T(8,128)(2,1)S(1)}, bf16[96,128]{1,0:T(8,128)(2,1)S(1)}, u32[]{:S(2)}, u32[]{:S(2)}) collective-permute-start(bf16[96,128]{1,0:T(8,128)(2,1)S(1)} %pad_maximum_fusion), channel_id=1, source_target_pairs={{2,4},{6,8},{10,12},{14,16},{18,20},{22,24},{26,28},{4,2},{8,6},{1... | collective-permute-start | bytes 73736 | tf_op jit(solution)/shard_map/ppermute | solution.py:309
  7.0 0.0 copy-start
  7.1 0.0 copy-start.3
  7.1 0.7 %taps.1 = (bf16[8,64,256]{2,1,0:T(8,128)(2,1)S(1)}, f32[96,256]{1,0:T(8,128)S(1)}) custom-call(s32[8,64]{1,0:T(8,128)S(1)} %bitcast.17, bf16[64,128]{1,0:T(8,128)(2,1)S(1)} %copy-done.4, bf16[768,128]{1,0:T(8,128)(2,1)S(1)} %copy-done.5), custom_call_target="tpu_custom_call" | custom-call | flops 2000000000 | bytes 10000000 | tf_op jit(solution)/shard_map/taps/pallas_call | solution.py:312
  7.8 0.0 collective-permute-done.1.refs_4_
  7.8 0.3 copy-done
  8.1 2.9 %forward.1 = (bf16[96,256]{1,0:T(8,128)(2,1)S(1)}, bf16[96,256]{1,0:T(8,128)(2,1)S(1)}, f32[44,16,128]{2,1,0:T(8,128)S(1)}, bf16[44,16,128]{2,1,0:T(8,128)(2,1)S...) custom-call(s32[1]{0:T(128)} %bitcast.core_ref, bf16[96,256]{1,0:T(8,128)(2,1)S(1)} %bitcast.13, ...), custom_call_target="tpu_custom_call" | custom-call | tf_op jit(solution)/shard_map/forward/pallas_call | solution.py:327
  11.0 4.0 %collective-permute-start.10 = (bf16[44,16,128]{2,1,0:T(8,128)(2,1)}, bf16[44,16,128]{2,1,0:T(8,128)(2,1)S(1)}, u32[]{:S(2)}, u32[]{:S(2)}) collective-permute-start(bf16[44,16,128]{2,1,0:T(8,128)(2,1)} %get-tuple-element.71), channel_id=1, source_target_pairs={{0,2},{2,0},{1,3},{3,1},{4,6},{6,4},{5,7},{7,5},{8,10},{10,8},{9,1... | collective-permute-start | bytes 540680 | tf_op jit(solution)/shard_map/ppermute | solution.py:365
  15.0 1.5 %collective-permute-done.10.got_ref = bf16[44,16,128]{2,1,0:T(8,128)(2,1)S(1)} collective-permute-done((bf16[44,16,128]{2,1,0:T(8,128)(2,1)}, bf16[44,16,128]{2,1,0:T(8,128)(2,1)S(1)}, u32[]{:S(2)}, u32[]{:S(2)}) %collective-permute-start.10) | collective-permute-done | bytes 180256 | tf_op jit(solution)/shard_map/ppermute | solution.py:365
  16.5 3.0 %collective-permute-start.11 = (bf16[22,16,128]{2,1,0:T(8,128)(2,1)S(1)}, bf16[22,16,128]{2,1,0:T(8,128)(2,1)S(1)}, u32[]{:S(2)}, u32[]{:S(2)}) collective-permute-start(bf16[22,16,128]{2,1,0:T(8,128)(2,1)S(1)} %get-tuple-element.73), channel_id=1, source_target_pairs={{0,4},{1,5},{2,3},{3,2},{4,0},{5,1},{6,7},{7,6},{8,12},{9,13},{10,... | collective-permute-start | bytes 270344 | tf_op jit(solution)/shard_map/ppermute | solution.py:372
  19.4 0.0 collective-permute-done.3.got_ref
  19.5 0.1 collective-permute-start.4
  19.6 3.2 %backward.1 = (bf16[64,128]{1,0:T(8,128)(2,1)}, f32[96,256]{1,0:T(8,128)S(1)}, f32[96,128]{1,0:T(8,128)S(1)}, bf16[96,256]{1,0:T(8,128)(2,1)S(1)}) custom-call(s32[1]{0:T(128)} %bitcast.core_ref, s32[27,256]{1,0:T(8,128)S(1)} %bitcast.16, f32[96,256]{1,0:T(8,128)S(1)} %get-tuple-element.51.refs_3_.hgrad_ref, bf16[96,256]{1,0:T(8,128)(2,1)S(1)} %get-tuple-element.59.grad_ref, ...), custom_call_target="tpu_custom_call" | custom-call | flops 2000000000 | bytes 10000000 | tf_op jit(solution)/shard_map/backward/pallas_call | solution.py:374
  22.8 1.3 %collective-permute-done.4.got_ref = bf16[22,16,128]{2,1,0:T(8,128)(2,1)S(1)} collective-permute-done((bf16[22,16,128]{2,1,0:T(8,128)(2,1)S(1)}, bf16[22,16,128]{2,1,0:T(8,128)(2,1)S(1)}, u32[]{:S(2)}, u32[]{:S(2)}) %collective-permute-start.4) | collective-permute-done | bytes 90144 | tf_op jit(solution)/shard_map/ppermute | solution.py:372
  24.1 1.5 %collective-permute-start.13 = (bf16[96,256]{1,0:T(8,128)(2,1)S(1)}, bf16[96,256]{1,0:T(8,128)(2,1)S(1)}, u32[]{:S(2)}, u32[]{:S(2)}) collective-permute-start(bf16[96,256]{1,0:T(8,128)(2,1)S(1)} %get-tuple-element.76), channel_id=1, source_target_pairs={{0,1},{1,0},{2,3},{3,2},{4,5},{5,4},{6,7},{7,6},{8,9},{9,8},{10,11... | collective-permute-start | bytes 147464 | tf_op jit(solution)/shard_map/ppermute | solution.py:397
  25.6 0.6 %collective-permute-start.12 = (bf16[11,16,128]{2,1,0:T(8,128)(2,1)S(1)}, bf16[11,16,128]{2,1,0:T(8,128)(2,1)S(1)}, u32[]{:S(2)}, u32[]{:S(2)}) collective-permute-start(bf16[11,16,128]{2,1,0:T(8,128)(2,1)S(1)} %get-tuple-element.75), channel_id=1, source_target_pairs={{0,1},{1,0},{2,6},{3,7},{4,5},{5,4},{6,2},{7,3},{8,9},{9,8},{10,14... | collective-permute-start | bytes 135176 | tf_op jit(solution)/shard_map/ppermute | solution.py:372
  26.2 1.6 %collective-permute-start.5 = (bf16[11,16,128]{2,1,0:T(8,128)(2,1)S(1)}, bf16[11,16,128]{2,1,0:T(8,128)(2,1)S(1)}, u32[]{:S(2)}, u32[]{:S(2)}) collective-permute-start(bf16[11,16,128]{2,1,0:T(8,128)(2,1)S(1)} %get-tuple-element.69), channel_id=1, source_target_pairs={{0,1},{1,0},{2,6},{3,7},{4,5},{5,4},{6,2},{7,3},{8,9},{9,8},{10,14... | collective-permute-start | bytes 135176 | tf_op jit(solution)/shard_map/ppermute | solution.py:372
  27.8 1.9 %collective-permute-done.12 = bf16[11,16,128]{2,1,0:T(8,128)(2,1)S(1)} collective-permute-done((bf16[11,16,128]{2,1,0:T(8,128)(2,1)S(1)}, bf16[11,16,128]{2,1,0:T(8,128)(2,1)S(1)}, u32[]{:S(2)}, u32[]{:S(2)}) %collective-permute-start.12) | collective-permute-done | bytes 45088 | tf_op jit(solution)/shard_map/ppermute | solution.py:372
  29.7 0.0 collective-permute-done.13.refs_0_
  29.8 1.6 %collective-permute-start.14 = (bf16[11,16,128]{2,1,0:T(8,128)(2,1)S(1)}, bf16[11,16,128]{2,1,0:T(8,128)(2,1)S(1)}, u32[]{:S(2)}, u32[]{:S(2)}) collective-permute-start(bf16[11,16,128]{2,1,0:T(8,128)(2,1)S(1)} %add_convert_fusion.2), channel_id=1, source_target_pairs={{0,8},{8,0},{16,24},{24,16},{1,9},{9,1},{17,25},{25,17},{2,10},{10... | collective-permute-start | bytes 135176 | tf_op jit(solution)/shard_map/ppermute | solution.py:413
  31.4 0.0 collective-permute-done.5
  31.4 0.6 %collective-permute-start.6 = (bf16[11,16,128]{2,1,0:T(8,128)(2,1)S(1)}, bf16[11,16,128]{2,1,0:T(8,128)(2,1)S(1)}, u32[]{:S(2)}, u32[]{:S(2)}) collective-permute-start(bf16[11,16,128]{2,1,0:T(8,128)(2,1)S(1)} %add_convert_fusion.5), channel_id=1, source_target_pairs={{0,8},{8,0},{16,24},{24,16},{1,9},{9,1},{17,25},{25,17},{2,10},{10... | collective-permute-start | bytes 135176 | tf_op jit(solution)/shard_map/ppermute | solution.py:413
  32.0 0.1 turn.1
  32.1 0.7 %collective-permute-start.16 = (bf16[96,64]{1,0:T(8,128)(2,1)S(1)}, bf16[96,64]{1,0:T(8,128)(2,1)S(1)}, u32[]{:S(2)}, u32[]{:S(2)}) collective-permute-start(bf16[96,64]{1,0:T(8,128)(2,1)S(1)} %get-tuple-element.81), channel_id=1, source_target_pairs={{2,4},{6,8},{10,12},{14,16},{18,20},{22,24},{26,28},{4,2},{8,6},{1... | collective-permute-start | bytes 36872 | tf_op jit(solution)/shard_map/ppermute | solution.py:415
  32.8 1.1 %collective-permute-done.14 = bf16[11,16,128]{2,1,0:T(8,128)(2,1)S(1)} collective-permute-done((bf16[11,16,128]{2,1,0:T(8,128)(2,1)S(1)}, bf16[11,16,128]{2,1,0:T(8,128)(2,1)S(1)}, u32[]{:S(2)}, u32[]{:S(2)}) %collective-permute-start.14) | collective-permute-done | bytes 45088 | tf_op jit(solution)/shard_map/ppermute | solution.py:413
  33.9 2.8 %collective-permute-start.15 = (bf16[11,16,128]{2,1,0:T(8,128)(2,1)S(1)}, bf16[11,16,128]{2,1,0:T(8,128)(2,1)S(1)}, u32[]{:S(2)}, u32[]{:S(2)}) collective-permute-start(bf16[11,16,128]{2,1,0:T(8,128)(2,1)S(1)} %add_convert_fusion.1), channel_id=1, source_target_pairs={{0,16},{8,24},{16,0},{24,8},{1,17},{9,25},{17,1},{25,9},{2,18},{10... | collective-permute-start | bytes 135176 | tf_op jit(solution)/shard_map/ppermute | solution.py:413
  36.7 0.8 %collective-permute-start.7 = (bf16[11,16,128]{2,1,0:T(8,128)(2,1)S(1)}, bf16[11,16,128]{2,1,0:T(8,128)(2,1)S(1)}, u32[]{:S(2)}, u32[]{:S(2)}) collective-permute-start(bf16[11,16,128]{2,1,0:T(8,128)(2,1)S(1)} %add_convert_fusion.4), channel_id=1, source_target_pairs={{0,16},{8,24},{16,0},{24,8},{1,17},{9,25},{17,1},{25,9},{2,18},{10... | collective-permute-start | bytes 135176 | tf_op jit(solution)/shard_map/ppermute | solution.py:413
  37.4 0.0 collective-permute-done.16.refs_5_
  37.5 1.8 %collective-permute-done.15 = bf16[11,16,128]{2,1,0:T(8,128)(2,1)S(1)} collective-permute-done((bf16[11,16,128]{2,1,0:T(8,128)(2,1)S(1)}, bf16[11,16,128]{2,1,0:T(8,128)(2,1)S(1)}, u32[]{:S(2)}, u32[]{:S(2)}) %collective-permute-start.15) | collective-permute-done | bytes 45088 | tf_op jit(solution)/shard_map/ppermute | solution.py:413
  39.3 0.4 collective-permute-start.17
  39.7 3.2 %collective-permute-done.7 = bf16[11,16,128]{2,1,0:T(8,128)(2,1)S(1)} collective-permute-done((bf16[11,16,128]{2,1,0:T(8,128)(2,1)S(1)}, bf16[11,16,128]{2,1,0:T(8,128)(2,1)S(1)}, u32[]{:S(2)}, u32[]{:S(2)}) %collective-permute-start.7) | collective-permute-done | bytes 45088 | tf_op jit(solution)/shard_map/ppermute | solution.py:413
  42.9 1.1 %collective-permute-start.8 = (bf16[11,16,128]{2,1,0:T(8,128)(2,1)S(1)}, bf16[11,16,128]{2,1,0:T(8,128)(2,1)S(1)}, u32[]{:S(2)}, u32[]{:S(2)}) collective-permute-start(bf16[11,16,128]{2,1,0:T(8,128)(2,1)S(1)} %add_convert_fusion.3.own_ref), channel_id=1, source_target_pairs={{0,1},{1,0},{2,6},{3,7},{4,5},{5,4},{6,2},{7,3},{8,9},{9,8},{10,14... | collective-permute-start | bytes 135176 | tf_op jit(solution)/shard_map/ppermute | solution.py:420
  44.0 1.0 %collective-permute-start.18 = (bf16[22,16,128]{2,1,0:T(8,128)(2,1)S(1)}, bf16[22,16,128]{2,1,0:T(8,128)(2,1)S(1)}, u32[]{:S(2)}, u32[]{:S(2)}) collective-permute-start(bf16[22,16,128]{2,1,0:T(8,128)(2,1)S(1)} %join.6.own_ref), channel_id=1, source_target_pairs={{0,4},{1,5},{2,3},{3,2},{4,0},{5,1},{6,7},{7,6},{8,12},{9,13},{10,... | collective-permute-start | bytes 270344 | tf_op jit(solution)/shard_map/ppermute | solution.py:420
  45.0 2.2 %collective-permute-done.8.got_ref = bf16[11,16,128]{2,1,0:T(8,128)(2,1)S(1)} collective-permute-done((bf16[11,16,128]{2,1,0:T(8,128)(2,1)S(1)}, bf16[11,16,128]{2,1,0:T(8,128)(2,1)S(1)}, u32[]{:S(2)}, u32[]{:S(2)}) %collective-permute-start.8) | collective-permute-done | bytes 45088 | tf_op jit(solution)/shard_map/ppermute | solution.py:420
  47.3 1.4 %collective-permute-start.9 = (bf16[22,16,128]{2,1,0:T(8,128)(2,1)S(1)}, bf16[22,16,128]{2,1,0:T(8,128)(2,1)S(1)}, u32[]{:S(2)}, u32[]{:S(2)}) collective-permute-start(bf16[22,16,128]{2,1,0:T(8,128)(2,1)S(1)} %join.4.own_ref), channel_id=1, source_target_pairs={{0,4},{1,5},{2,3},{3,2},{4,0},{5,1},{6,7},{7,6},{8,12},{9,13},{10,... | collective-permute-start | bytes 270344 | tf_op jit(solution)/shard_map/ppermute | solution.py:420
  48.7 0.1 collective-permute-start.20
  48.8 3.1 %collective-permute-done.9.got_ref = bf16[22,16,128]{2,1,0:T(8,128)(2,1)S(1)} collective-permute-done((bf16[22,16,128]{2,1,0:T(8,128)(2,1)S(1)}, bf16[22,16,128]{2,1,0:T(8,128)(2,1)S(1)}, u32[]{:S(2)}, u32[]{:S(2)}) %collective-permute-start.9) | collective-permute-done | bytes 90144 | tf_op jit(solution)/shard_map/ppermute | solution.py:420
  51.9 0.1 collective-permute-start.19
  51.9 1.4 %collective-permute-done.19.refs_2_ = bf16[44,16,128]{2,1,0:T(8,128)(2,1)S(1)} collective-permute-done((bf16[44,16,128]{2,1,0:T(8,128)(2,1)S(1)}, bf16[44,16,128]{2,1,0:T(8,128)(2,1)S(1)}, u32[]{:S(2)}, u32[]{:S(2)}) %collective-permute-start.19) | collective-permute-done | bytes 180256 | tf_op jit(solution)/shard_map/ppermute | solution.py:423
  53.4 0.0 collective-permute-done.20.refs_3_
  53.4 1.2 %final.1 = (f32[96,2592]{1,0:T(8,128)}, f32[768,128]{1,0:T(8,128)}, f32[96,256]{1,0:T(8,128)}) custom-call(s32[1]{0:T(128)} %bitcast.core_ref, bf16[44,16,128]{2,1,0:T(8,128)(2,1)S(1)} %join.5.refs_0_, bf16[50,16,128]{2,1,0:T(8,128)(2,1)S(1)} %join.7.refs_1_, bf16[44,16,128]{2,1,0:T(8,128)(2,1)S(1)} %collective-permute-done.19.refs_2_, ...), custom_call_target="tpu_custom_call" | custom-call | tf_op jit(solution)/shard_map/final/pallas_call | solution.py:424
  (30 shorter events, 0.3 us)
Async XLA Ops:
  0.6 3.8 %copy-start.1 = (bf16[256,96]{0,1:T(8,128)(2,1)S(1)}, bf16[256,96]{0,1:T(8,128)(2,1)}, u32[]{:S(2)}) copy-start(bf16[256,96]{0,1:T(8,128)(2,1)} %param.6) | copy-start | bytes 147460
  1.4 4.8 %collective-permute-start = (bf16[96,64]{1,0:T(8,128)(2,1)S(1)}, bf16[96,64]{1,0:T(8,128)(2,1)S(1)}, u32[]{:S(2)}, u32[]{:S(2)}) collective-permute-start(bf16[96,64]{1,0:T(8,128)(2,1)S(1)} %slice.4), channel_id=1, source_target_pairs={{0,1},{1,0},{2,3},{3,2},{4,5},{5,4},{6,7},{7,6},{8,9},{9,8},{10,11... | collective-permute-start | bytes 36872 | tf_op jit(solution)/shard_map/ppermute | solution.py:295
  4.4 0.8 %copy-start.2 = (s32[256,27]{0,1:T(8,128)S(1)}, s32[256,27]{0,1:T(8,128)}, u32[]{:S(2)}) copy-start(s32[256,27]{0,1:T(8,128)} %param.7) | copy-start | bytes 82948
  5.2 1.8 %copy-start.5 = (bf16[768,128]{1,0:T(8,128)(2,1)S(1)}, bf16[768,128]{1,0:T(8,128)(2,1)}, u32[]{:S(2)}) copy-start(bf16[768,128]{1,0:T(8,128)(2,1)} %refs_2_.1) | copy-start | bytes 589828
  6.2 0.8 %copy-start.4 = (bf16[64,128]{1,0:T(8,128)(2,1)S(1)}, bf16[64,128]{1,0:T(8,128)(2,1)}, u32[]{:S(2)}) copy-start(bf16[64,128]{1,0:T(8,128)(2,1)} %cgrad_ref.3) | copy-start | bytes 49156
  6.2 0.8 %copy-start.6 = (s32[64,8]{0,1:T(8,128)S(1)}, s32[64,8]{0,1:T(8,128)}, u32[]{:S(2)}) copy-start(s32[64,8]{0,1:T(8,128)} %param.8) | copy-start | bytes 6148
  6.3 1.5 %collective-permute-start.1 = (bf16[96,128]{1,0:T(8,128)(2,1)S(1)}, bf16[96,128]{1,0:T(8,128)(2,1)S(1)}, u32[]{:S(2)}, u32[]{:S(2)}) collective-permute-start(bf16[96,128]{1,0:T(8,128)(2,1)S(1)} %pad_maximum_fusion), channel_id=1, source_target_pairs={{0,2},{2,0},{4,6},{6,4},{8,10},{10,8},{12,14},{14,12},{16,18},{18,... | collective-permute-start | bytes 73736 | tf_op jit(solution)/shard_map/ppermute | solution.py:310
  6.3 1.5 %collective-permute-start.2 = (bf16[96,128]{1,0:T(8,128)(2,1)S(1)}, bf16[96,128]{1,0:T(8,128)(2,1)S(1)}, u32[]{:S(2)}, u32[]{:S(2)}) collective-permute-start(bf16[96,128]{1,0:T(8,128)(2,1)S(1)} %pad_maximum_fusion), channel_id=1, source_target_pairs={{2,4},{6,8},{10,12},{14,16},{18,20},{22,24},{26,28},{4,2},{8,6},{1... | collective-permute-start | bytes 73736 | tf_op jit(solution)/shard_map/ppermute | solution.py:309
  7.0 1.0 %copy-start = (bf16[2592,96]{0,1:T(8,128)(2,1)S(1)}, bf16[2592,96]{0,1:T(8,128)(2,1)}, u32[]{:S(2)}) copy-start(bf16[2592,96]{0,1:T(8,128)(2,1)} %param.9) | copy-start | bytes 1492996
  7.1 1.0 %copy-start.3 = (s32[256,27]{0,1:T(8,128)S(1)}, s32[256,27]{0,1:T(8,128)}, u32[]{:S(2)}) copy-start(s32[256,27]{0,1:T(8,128)} %param.7) | copy-start | bytes 82948
  11.0 5.4 %collective-permute-start.10 = (bf16[44,16,128]{2,1,0:T(8,128)(2,1)}, bf16[44,16,128]{2,1,0:T(8,128)(2,1)S(1)}, u32[]{:S(2)}, u32[]{:S(2)}) collective-permute-start(bf16[44,16,128]{2,1,0:T(8,128)(2,1)} %get-tuple-element.71), channel_id=1, source_target_pairs={{0,2},{2,0},{1,3},{3,1},{4,6},{6,4},{5,7},{7,5},{8,10},{10,8},{9,1... | collective-permute-start | bytes 540680 | tf_op jit(solution)/shard_map/ppermute | solution.py:365
  15.0 4.5 %collective-permute-start.3 = (bf16[44,16,128]{2,1,0:T(8,128)(2,1)S(1)}, bf16[44,16,128]{2,1,0:T(8,128)(2,1)S(1)}, u32[]{:S(2)}, u32[]{:S(2)}) collective-permute-start(bf16[44,16,128]{2,1,0:T(8,128)(2,1)S(1)} %get-tuple-element.56), channel_id=1, source_target_pairs={{0,2},{2,0},{1,3},{3,1},{4,6},{6,4},{5,7},{7,5},{8,10},{10,8},{9,1... | collective-permute-start | bytes 540680 | tf_op jit(solution)/shard_map/ppermute | solution.py:365
  16.5 9.1 %collective-permute-start.11 = (bf16[22,16,128]{2,1,0:T(8,128)(2,1)S(1)}, bf16[22,16,128]{2,1,0:T(8,128)(2,1)S(1)}, u32[]{:S(2)}, u32[]{:S(2)}) collective-permute-start(bf16[22,16,128]{2,1,0:T(8,128)(2,1)S(1)} %get-tuple-element.73), channel_id=1, source_target_pairs={{0,4},{1,5},{2,3},{3,2},{4,0},{5,1},{6,7},{7,6},{8,12},{9,13},{10,... | collective-permute-start | bytes 270344 | tf_op jit(solution)/shard_map/ppermute | solution.py:372
  19.5 4.6 %collective-permute-start.4 = (bf16[22,16,128]{2,1,0:T(8,128)(2,1)S(1)}, bf16[22,16,128]{2,1,0:T(8,128)(2,1)S(1)}, u32[]{:S(2)}, u32[]{:S(2)}) collective-permute-start(bf16[22,16,128]{2,1,0:T(8,128)(2,1)S(1)} %get-tuple-element.63), channel_id=1, source_target_pairs={{0,4},{1,5},{2,3},{3,2},{4,0},{5,1},{6,7},{7,6},{8,12},{9,13},{10,... | collective-permute-start | bytes 270344 | tf_op jit(solution)/shard_map/ppermute | solution.py:372
  24.1 5.7 %collective-permute-start.13 = (bf16[96,256]{1,0:T(8,128)(2,1)S(1)}, bf16[96,256]{1,0:T(8,128)(2,1)S(1)}, u32[]{:S(2)}, u32[]{:S(2)}) collective-permute-start(bf16[96,256]{1,0:T(8,128)(2,1)S(1)} %get-tuple-element.76), channel_id=1, source_target_pairs={{0,1},{1,0},{2,3},{3,2},{4,5},{5,4},{6,7},{7,6},{8,9},{9,8},{10,11... | collective-permute-start | bytes 147464 | tf_op jit(solution)/shard_map/ppermute | solution.py:397
  25.6 4.1 %collective-permute-start.12 = (bf16[11,16,128]{2,1,0:T(8,128)(2,1)S(1)}, bf16[11,16,128]{2,1,0:T(8,128)(2,1)S(1)}, u32[]{:S(2)}, u32[]{:S(2)}) collective-permute-start(bf16[11,16,128]{2,1,0:T(8,128)(2,1)S(1)} %get-tuple-element.75), channel_id=1, source_target_pairs={{0,1},{1,0},{2,6},{3,7},{4,5},{5,4},{6,2},{7,3},{8,9},{9,8},{10,14... | collective-permute-start | bytes 135176 | tf_op jit(solution)/shard_map/ppermute | solution.py:372
  26.2 5.2 %collective-permute-start.5 = (bf16[11,16,128]{2,1,0:T(8,128)(2,1)S(1)}, bf16[11,16,128]{2,1,0:T(8,128)(2,1)S(1)}, u32[]{:S(2)}, u32[]{:S(2)}) collective-permute-start(bf16[11,16,128]{2,1,0:T(8,128)(2,1)S(1)} %get-tuple-element.69), channel_id=1, source_target_pairs={{0,1},{1,0},{2,6},{3,7},{4,5},{5,4},{6,2},{7,3},{8,9},{9,8},{10,14... | collective-permute-start | bytes 135176 | tf_op jit(solution)/shard_map/ppermute | solution.py:372
  29.8 4.1 %collective-permute-start.14 = (bf16[11,16,128]{2,1,0:T(8,128)(2,1)S(1)}, bf16[11,16,128]{2,1,0:T(8,128)(2,1)S(1)}, u32[]{:S(2)}, u32[]{:S(2)}) collective-permute-start(bf16[11,16,128]{2,1,0:T(8,128)(2,1)S(1)} %add_convert_fusion.2), channel_id=1, source_target_pairs={{0,8},{8,0},{16,24},{24,16},{1,9},{9,1},{17,25},{25,17},{2,10},{10... | collective-permute-start | bytes 135176 | tf_op jit(solution)/shard_map/ppermute | solution.py:413
  31.4 5.2 %collective-permute-start.6 = (bf16[11,16,128]{2,1,0:T(8,128)(2,1)S(1)}, bf16[11,16,128]{2,1,0:T(8,128)(2,1)S(1)}, u32[]{:S(2)}, u32[]{:S(2)}) collective-permute-start(bf16[11,16,128]{2,1,0:T(8,128)(2,1)S(1)} %add_convert_fusion.5), channel_id=1, source_target_pairs={{0,8},{8,0},{16,24},{24,16},{1,9},{9,1},{17,25},{25,17},{2,10},{10... | collective-permute-start | bytes 135176 | tf_op jit(solution)/shard_map/ppermute | solution.py:413
  32.1 5.4 %collective-permute-start.16 = (bf16[96,64]{1,0:T(8,128)(2,1)S(1)}, bf16[96,64]{1,0:T(8,128)(2,1)S(1)}, u32[]{:S(2)}, u32[]{:S(2)}) collective-permute-start(bf16[96,64]{1,0:T(8,128)(2,1)S(1)} %get-tuple-element.81), channel_id=1, source_target_pairs={{2,4},{6,8},{10,12},{14,16},{18,20},{22,24},{26,28},{4,2},{8,6},{1... | collective-permute-start | bytes 36872 | tf_op jit(solution)/shard_map/ppermute | solution.py:415
  33.9 5.3 %collective-permute-start.15 = (bf16[11,16,128]{2,1,0:T(8,128)(2,1)S(1)}, bf16[11,16,128]{2,1,0:T(8,128)(2,1)S(1)}, u32[]{:S(2)}, u32[]{:S(2)}) collective-permute-start(bf16[11,16,128]{2,1,0:T(8,128)(2,1)S(1)} %add_convert_fusion.1), channel_id=1, source_target_pairs={{0,16},{8,24},{16,0},{24,8},{1,17},{9,25},{17,1},{25,9},{2,18},{10... | collective-permute-start | bytes 135176 | tf_op jit(solution)/shard_map/ppermute | solution.py:413
  36.7 6.2 %collective-permute-start.7 = (bf16[11,16,128]{2,1,0:T(8,128)(2,1)S(1)}, bf16[11,16,128]{2,1,0:T(8,128)(2,1)S(1)}, u32[]{:S(2)}, u32[]{:S(2)}) collective-permute-start(bf16[11,16,128]{2,1,0:T(8,128)(2,1)S(1)} %add_convert_fusion.4), channel_id=1, source_target_pairs={{0,16},{8,24},{16,0},{24,8},{1,17},{9,25},{17,1},{25,9},{2,18},{10... | collective-permute-start | bytes 135176 | tf_op jit(solution)/shard_map/ppermute | solution.py:413
  39.3 4.7 %collective-permute-start.17 = (bf16[11,16,128]{2,1,0:T(8,128)(2,1)S(1)}, bf16[11,16,128]{2,1,0:T(8,128)(2,1)S(1)}, u32[]{:S(2)}, u32[]{:S(2)}) collective-permute-start(bf16[11,16,128]{2,1,0:T(8,128)(2,1)S(1)} %add_convert_fusion.own_ref), channel_id=1, source_target_pairs={{0,1},{1,0},{2,6},{3,7},{4,5},{5,4},{6,2},{7,3},{8,9},{9,8},{10,14... | collective-permute-start | bytes 135176 | tf_op jit(solution)/shard_map/ppermute | solution.py:420
  42.9 4.4 %collective-permute-start.8 = (bf16[11,16,128]{2,1,0:T(8,128)(2,1)S(1)}, bf16[11,16,128]{2,1,0:T(8,128)(2,1)S(1)}, u32[]{:S(2)}, u32[]{:S(2)}) collective-permute-start(bf16[11,16,128]{2,1,0:T(8,128)(2,1)S(1)} %add_convert_fusion.3.own_ref), channel_id=1, source_target_pairs={{0,1},{1,0},{2,6},{3,7},{4,5},{5,4},{6,2},{7,3},{8,9},{9,8},{10,14... | collective-permute-start | bytes 135176 | tf_op jit(solution)/shard_map/ppermute | solution.py:420
  44.0 4.7 %collective-permute-start.18 = (bf16[22,16,128]{2,1,0:T(8,128)(2,1)S(1)}, bf16[22,16,128]{2,1,0:T(8,128)(2,1)S(1)}, u32[]{:S(2)}, u32[]{:S(2)}) collective-permute-start(bf16[22,16,128]{2,1,0:T(8,128)(2,1)S(1)} %join.6.own_ref), channel_id=1, source_target_pairs={{0,4},{1,5},{2,3},{3,2},{4,0},{5,1},{6,7},{7,6},{8,12},{9,13},{10,... | collective-permute-start | bytes 270344 | tf_op jit(solution)/shard_map/ppermute | solution.py:420
  47.3 4.6 %collective-permute-start.9 = (bf16[22,16,128]{2,1,0:T(8,128)(2,1)S(1)}, bf16[22,16,128]{2,1,0:T(8,128)(2,1)S(1)}, u32[]{:S(2)}, u32[]{:S(2)}) collective-permute-start(bf16[22,16,128]{2,1,0:T(8,128)(2,1)S(1)} %join.4.own_ref), channel_id=1, source_target_pairs={{0,4},{1,5},{2,3},{3,2},{4,0},{5,1},{6,7},{7,6},{8,12},{9,13},{10,... | collective-permute-start | bytes 270344 | tf_op jit(solution)/shard_map/ppermute | solution.py:420
  48.7 4.6 %collective-permute-start.20 = (bf16[50,16,128]{2,1,0:T(8,128)(2,1)S(1)}, bf16[50,16,128]{2,1,0:T(8,128)(2,1)S(1)}, u32[]{:S(2)}, u32[]{:S(2)}) collective-permute-start(bf16[50,16,128]{2,1,0:T(8,128)(2,1)S(1)} %join.7.refs_1_), channel_id=1, source_target_pairs={{0,2},{2,0},{1,3},{3,1},{4,6},{6,4},{5,7},{7,5},{8,10},{10,8},{9,1... | collective-permute-start | bytes 614408 | tf_op jit(solution)/shard_map/ppermute | solution.py:423
  51.9 1.5 %collective-permute-start.19 = (bf16[44,16,128]{2,1,0:T(8,128)(2,1)S(1)}, bf16[44,16,128]{2,1,0:T(8,128)(2,1)S(1)}, u32[]{:S(2)}, u32[]{:S(2)}) collective-permute-start(bf16[44,16,128]{2,1,0:T(8,128)(2,1)S(1)} %join.5.refs_0_), channel_id=1, source_target_pairs={{0,2},{2,0},{1,3},{3,1},{4,6},{6,4},{5,7},{7,5},{8,10},{10,8},{9,1... | collective-permute-start | bytes 540680 | tf_op jit(solution)/shard_map/ppermute | solution.py:423

commit v6 on v5

--- a/solution.py
+++ b/solution.py
@@ -12,7 +12,7 @@
 RIM = 64
 LANES = 128
 TILE = 16
-CHUNKS = 2
+CHUNKS = 1
 F32 = jnp.float32
 BF16 = jnp.bfloat16
 NN = (((1,), (0,)), ((), ()))
@@ -149,16 +149,19 @@
                 ref[place] = value.astype(ref.dtype)
 
 
-def backward_kernel(slabs, core_ref, near_ref, hgrad_ref, grad_ref, w_ref, *refs):
-    pick_ref, hidden_ref, wd_ref, coarse_ref, base_ref, keep_ref, *refs = refs
-    cross_refs, (drt, drt_far, hot, far, w_back) = refs[:-5], refs[-5:]
-    channels, voxels = hgrad_ref.shape
-    offsets = near_ref.shape[0]
+def coarse_kernel(pick_ref, hidden_ref, wd_ref, coarse_ref):
+    channels = hidden_ref.shape[0]
     coarse = jnp.zeros(coarse_ref.shape, F32)
     for t in range(pick_ref.shape[0]):
         picked = mm(pick_ref[t], hidden_ref[...], NT).astype(BF16)
         coarse += mm(picked, wd_ref[t * channels : (t + 1) * channels, :])
     coarse_ref[...] = coarse.astype(BF16)
+
+
+def backward_kernel(slabs, core_ref, near_ref, hgrad_ref, grad_ref, w_ref, *refs):
+    base_ref, mate_ref, first_ref, second_ref, drt, drt_far, hot, far, w_back = refs
+    channels, voxels = hgrad_ref.shape
+    offsets = near_ref.shape[0]
     lanes = table_lanes(near_ref[...], voxels, slabs, core_ref[0])
     near_iota = lax.broadcasted_iota(jnp.int32, (voxels, voxels), 0)
     w_back[:, :channels] = w_ref[...].astype(F32).T.astype(BF16)
@@ -175,54 +178,144 @@
     base_ref[...] = hgrad_ref[...] + mm(drt[...], hot[...], NT)
     back_t = mm(drt_far[...], far[...], NT)
     rims = 2 if slabs == 2 else 3
-    mid = 0 if slabs == 2 else 1
-    rim = [back_t[:, i * RIM : (i + 1) * RIM] for i in range(2 * rims + len(cross_refs))]
-    keep_ref[...] = jnp.concatenate([rim[mid], rim[rims + mid]], axis=1)
-    for i, ref in enumerate(cross_refs):
-        place = 1 if slabs == 2 else 2 * i
-        parts = [rim[place], rim[rims + place], rim[2 * rims + i], jnp.zeros_like(rim[0])]
-        ref[...] = jnp.concatenate(parts, axis=1).astype(BF16)
-
-
-def turn_kernel(base_ref, keep_ref, *refs):
-    got_refs, (sum_ref, cross_ref, mate_ref) = refs[:-3], refs[-3:]
-    got = got_refs[0][...].astype(F32)
-    for ref in got_refs[1:]:
-        got += ref[...].astype(F32)
-    sum_ref[:, RIM:] = base_ref[:, RIM:]
-    sum_ref[:, :RIM] = base_ref[:, :RIM] + got[:, 2 * RIM : 3 * RIM]
-    pair = keep_ref[...] + got[:, : 2 * RIM]
-    cross_ref[...] = pair[:, RIM:].astype(BF16)
-    pair = pair.astype(BF16)
-    for i in range(mate_ref.shape[0]):
-        mate_ref[i] = pair[i * TILE : (i + 1) * TILE, :]
-
-
-def fold_kernel(bit_ref, own_ref, got_ref, keep_ref, send_ref):
+    rim = [back_t[:, i * RIM : (i + 1) * RIM] for i in range(back_t.shape[1] // RIM)]
+    mate, cross, side = rim[:rims], rim[rims : 2 * rims], rim[2 * rims : 3 * rims - 1]
+    if slabs == 2:
+        mate_ref[...] = mate[0]
+        slots = [cross[0], cross[1], mate[1], side[0]]
+    else:
+        mate_ref[...] = mate[1]
+        slots = [cross[1], cross[0], cross[2], jnp.zeros_like(cross[0])]
+        slots += [mate[0], mate[2], side[0], side[1]]
+    pairs = [jnp.concatenate(slots[i : i + 2], axis=1).astype(BF16) for i in range(0, len(slots), 2)]
+    rows = channels // TILE
+    for ref, part in ((first_ref, pairs[: len(pairs) // 2]), (second_ref, pairs[len(pairs) // 2 :])):
+        for i, pair in enumerate(part):
+            for j in range(rows):
+                ref[i * rows + j] = pair[j * TILE : (j + 1) * TILE, :]
+
+
+def slot_table(slabs):
+    if slabs == 2:
+        return [("cross", 1, 0), ("cross", 1, 1), ("mate", 0, 1), ("side", 0, 1)]
+    table = [("cross", 1, 0), ("cross", 1, -1), ("cross", 1, 1), ("none", 0, 0)]
+    return table + [("mate", 0, -1), ("mate", 0, 1), ("side", 0, -1), ("side", 0, 1)]
+
+
+def place_of(me, sizes):
+    place = {}
+    for axis in reversed(SPLIT):
+        place[axis] = me & (sizes[axis] - 1)
+        me = me >> (sizes[axis].bit_length() - 1)
+    return place
+
+
+def goes(slot, axis, bit, place, sizes):
+    _, chips, step = slot
+    low = (1 << bit) - 1
+    yes, no = jnp.int32(1), jnp.int32(0)
+    if axis == "far":
+        if not chips:
+            return no
+        far = place["far"] & low
+        up = (place["near"] == 1) & (far == 0)
+        down = (place["near"] == 0) & (far == low)
+        return jnp.where(place["core"] == 1, up.astype(jnp.int32), down.astype(jnp.int32))
+    if axis == "near":
+        return yes if chips else no
+    if step == 0:
+        return no
+    if sizes["slab"] == 2:
+        return yes
+    return ((place["slab"] & low) == (0 if step > 0 else low)).astype(jnp.int32)
+
+
+def chosen_bit(choice, place):
+    return jnp.where(place["core"] == 0, *[(place[axis] >> bit) & 1 for axis, bit in choice])
+
+
+def riders_after(choice, sizes, place, rows, mine, got):
+    slots = slot_table(sizes["slab"])
+    lane = lax.broadcasted_iota(jnp.int32, (TILE, LANES), 1)
+    masks = []
+    for i in range(0, len(slots), 2):
+        flags = []
+        for slot in slots[i : i + 2]:
+            each = [goes(slot, axis, bit, place, sizes) for axis, bit in choice]
+            flags.append(jnp.where(place["core"] == 0, *each))
+        masks.append(jnp.where(lane < RIM, flags[0], flags[1]) > 0)
+    return [
+        jnp.where(masks[i // rows], got[i].astype(F32), mine[i].astype(F32))
+        for i in range(mine.shape[0])
+    ]
+
+
+def close_kernel(keep_ref, got_ref, *refs):
+    riders, full_ref = refs[:-1], refs[-1]
+    count = keep_ref.shape[0]
+    full_ref[:count] = (keep_ref[...] + got_ref[...].astype(F32)).astype(BF16)
+    for rider in riders:
+        full_ref[count : count + rider.shape[0]] = rider[...]
+        count += rider.shape[0]
+
+
+def meet_kernel(choice, sizes, rows, count, me_ref, own_ref, got_ref, *refs):
+    riders, full_ref = refs[:-1], refs[-1]
+    place = place_of(me_ref[0], sizes)
+    total = own_ref[:count].astype(F32) + got_ref[:count].astype(F32)
+    full_ref[:count] = total.astype(BF16)
+    parts = riders_after(choice, sizes, place, rows, own_ref.at[count:], got_ref.at[count:])
+    for part in parts:
+        full_ref[count] = part.astype(BF16)
+        count += 1
+    for rider in riders:
+        full_ref[count : count + rider.shape[0]] = rider[...]
+
+
+def fold_kernel(choice, sizes, me_ref, own_ref, got_ref, keep_ref, send_ref):
     half = keep_ref.shape[0]
-    for ref, part in ((keep_ref, bit_ref[0]), (send_ref, 1 - bit_ref[0])):
+    bit = chosen_bit(choice, place_of(me_ref[0], sizes))
+    for ref, part in ((keep_ref, bit), (send_ref, 1 - bit)):
         rows = pl.ds(part * half, half)
         ref[...] = (own_ref[rows] + got_ref[rows].astype(F32)).astype(ref.dtype)
 
 
-def join_kernel(bit_ref, own_ref, got_ref, *refs):
-    riders, full_ref = refs[:-1], refs[-1]
-    half = own_ref.shape[0]
-    for rider in riders:
-        full_ref[2 * half :] = rider[...]
-    full_ref[pl.ds(bit_ref[0] * half, half)] = own_ref[...]
-    full_ref[pl.ds((1 - bit_ref[0]) * half, half)] = got_ref[...]
+def join_kernel(choice, sizes, rows, half, last, me_ref, own_ref, got_ref, *refs):
+    full_ref = refs[1] if last else refs[0]
+    place = place_of(me_ref[0], sizes)
+    bit = chosen_bit(choice, place)
+    full_ref[pl.ds(bit * half, half)] = own_ref[:half]
+    full_ref[pl.ds((1 - bit) * half, half)] = got_ref[:half]
+    if own_ref.shape[0] == half:
+        return
+    parts = riders_after(choice, sizes, place, rows, own_ref.at[half:], got_ref.at[half:])
+    if not last:
+        for i, part in enumerate(parts):
+            full_ref[2 * half + i] = part.astype(BF16)
+        return
+    mate_ref, side_ref = refs[0], refs[2]
+    for j in range(rows):
+        mate, side = mate_ref[j * TILE : (j + 1) * TILE, :], jnp.zeros((TILE, RIM), F32)
+        for i, (kind, _, _) in enumerate(slot_table(sizes["slab"])):
+            value = parts[i // 2 * rows + j][:, i % 2 * RIM : (i % 2 + 1) * RIM]
+            if kind == "side":
+                side += value
+            elif kind != "none":
+                mate += value
+        pair = jnp.concatenate([mate, jnp.zeros_like(mate)], axis=1)
+        full_ref[2 * half + j] = pair.astype(BF16)
+        side_ref[j * TILE : (j + 1) * TILE, :] = side
 
 
 def final_kernel(taps, count, size, core_ref, *refs):
     mine, other, refs = refs[:count], refs[count : 2 * count], refs[2 * count :]
-    base_ref, cross_ref, conv_ref, down_ref, grad_ref = refs
+    base_ref, side_ref, conv_ref, down_ref, grad_ref = refs
     channels, conv_columns = conv_ref.shape
     grad_ref[:, RIM:] = base_ref[:, RIM:]
     for i in range(channels // TILE):
         rows = slice(i * TILE, (i + 1) * TILE)
-        total = base_ref[rows, :RIM] + cross_ref[rows, :].astype(F32)
-        grad_ref[rows, :RIM] = total + other[-1][size + i][:, :RIM].astype(F32)
+        total = base_ref[rows, :RIM] + side_ref[rows, :]
+        grad_ref[rows, :RIM] = total + other[0][size + i][:, :RIM].astype(F32)
     for core in range(2):
 
         @pl.when(core_ref[0] == core)
@@ -247,7 +340,7 @@
 
 def square_bits(nears, slabs, core):
     near = [("near", i) for i in range(nears.bit_length() - 1)]
-    slab = [("slab", i) for i in range(slabs.bit_length() - 1)]
+    slab = [("slab", i) for i in reversed(range(slabs.bit_length() - 1))]
     return near + slab if core == 0 else slab + near
 
 
@@ -277,11 +370,8 @@
     mates, crossings = chip_pairs(regions)
     orders = [square_bits(sizes["near"], slabs, c) for c in range(2)]
     phases = len(orders[0])
-    bits = []
-    for phase in range(phases):
-        chosen = [(lax.axis_index(axis) >> bit) & 1 for axis, bit in (o[phase] for o in orders)]
-        bits.append(jnp.where(core == 0, *chosen).astype(jnp.int32))
-
+    me = lax.axis_index(SPLIT).astype(jnp.int32).reshape(1)
+    choices = [tuple(order[phase] for order in orders) for phase in range(phases)]
     smem = pl.BlockSpec(memory_space=pltpu.SMEM)
     vmem = pl.BlockSpec(memory_space=pltpu.VMEM)
     params = pltpu.CompilerParams(vmem_limit_bytes=VMEM_BYTES)
@@ -341,25 +431,24 @@
         name="forward",
     )(core, features_t, neighbours_t, coarse_grad, w_conv_t, *own, pick, hgrad, *halos)
 
+    rows = channels // TILE
+
+    def tile_shape(count, kind=BF16):
+        return jax.ShapeDtypeStruct((count, TILE, LANES), kind)
+
+    def call(name, kernel, out_shape, *operands):
+        return pl.pallas_call(
+            kernel,
+            out_shape=out_shape,
+            in_specs=[smem] + [vmem] * (len(operands) - 1),
+            compiler_params=params,
+            name=name,
+        )(*operands)
+
     def fold(phase, keep, got):
-        shape = (keep.shape[0] // 2, TILE, LANES)
-        return pl.pallas_call(
-            fold_kernel,
-            out_shape=(jax.ShapeDtypeStruct(shape, F32), jax.ShapeDtypeStruct(shape, BF16)),
-            in_specs=[smem, vmem, vmem],
-            compiler_params=params,
-            name="fold",
-        )(bits[phase], keep, got)
-
-    def join(phase, own, got, *riders):
-        count = own.shape[0] * 2 + sum(x.shape[0] for x in riders)
-        return pl.pallas_call(
-            join_kernel,
-            out_shape=jax.ShapeDtypeStruct((count, TILE, LANES), BF16),
-            in_specs=[smem] + [vmem] * (2 + len(riders)),
-            compiler_params=params,
-            name="join",
-        )(bits[phase], own, got, *riders)
+        half = keep.shape[0] // 2
+        kernel = functools.partial(fold_kernel, choices[phase], sizes)
+        return call("fold", kernel, (tile_shape(half, F32), tile_shape(half)), me, keep, got)
 
     keep, send = chunks[0::2], chunks[1::2]
     got = [lax.ppermute(x, "core", swap) for x in send]
@@ -367,19 +456,20 @@
         pairs = bit_pairs(sizes, orders, phase)
         for i in range(CHUNKS):
             keep[i], send[i] = fold(phase, keep[i], got[i])
-            if phase == 0 and i == 0:
-                send[0], grad = lax.optimization_barrier((send[0], grad))
+            if i == CHUNKS - 1 and phase == 0:
+                send[i], grad = lax.optimization_barrier((send[i], grad))
             got[i] = lax.ppermute(send[i], SPLIT, pairs)
         if phase == 0:
-            coarse, base, stay, *edges = pl.pallas_call(
+            slots = len(slot_table(slabs)) // 4 * rows
+            base, stay, *riders = pl.pallas_call(
                 functools.partial(backward_kernel, slabs),
-                out_shape=[
-                    jax.ShapeDtypeStruct(coarse_grad.shape, BF16),
+                out_shape=(
                     jax.ShapeDtypeStruct((channels, voxels), F32),
-                    jax.ShapeDtypeStruct((channels, 2 * RIM), F32),
-                ]
-                + [jax.ShapeDtypeStruct((channels, 4 * RIM), BF16)] * len(beside),
-                in_specs=[smem] + [vmem] * 7,
+                    jax.ShapeDtypeStruct((channels, RIM), F32),
+                    tile_shape(slots),
+                    tile_shape(slots),
+                ),
+                in_specs=[smem] + [vmem] * 4,
                 scratch_shapes=[
                     pltpu.VMEM((channels, offsets * voxels), BF16),
                     pltpu.VMEM((channels, offsets * LANES), BF16),
@@ -390,36 +480,49 @@
                 compiler_params=params,
                 cost_estimate=light,
                 name="backward",
-            )(core, neighbours_t, hgrad, grad, w_conv_t, pick, hidden, w_down)
-            got[0], stay, edges, base = lax.optimization_barrier((got[0], stay, edges, base))
+            )(core, neighbours_t, hgrad, grad, w_conv_t)
+            got[0], stay, riders, base = lax.optimization_barrier((got[0], stay, riders, base))
         if phase == phases - 1:
-            back = beside if slabs == 2 else beside[::-1]
-            edges = [lax.ppermute(x, "slab", p) for x, p in zip(edges, back)]
-            got[-1], edges = lax.optimization_barrier((got[-1], edges))
-            base, cross, mate = pl.pallas_call(
-                turn_kernel,
-                out_shape=(
-                    jax.ShapeDtypeStruct((channels, voxels), F32),
-                    jax.ShapeDtypeStruct((channels, RIM), BF16),
-                    jax.ShapeDtypeStruct((channels // TILE, TILE, LANES), BF16),
-                ),
+            coarse = pl.pallas_call(
+                coarse_kernel,
+                out_shape=jax.ShapeDtypeStruct(coarse_grad.shape, BF16),
                 compiler_params=params,
-                name="turn",
-            )(base, stay, *edges)
+                cost_estimate=light,
+                name="coarse",
+            )(pick, hidden, w_down)
+
+    far_bits = sizes["far"].bit_length() - 1
+    count = keep[0].shape[0]
+    first = riders[:1] if far_bits else riders
     total = [(x + y.astype(F32)).astype(BF16) for x, y in zip(keep, got)]
-    far_bits = sizes["far"].bit_length() - 1
+    total[0] = pl.pallas_call(
+        close_kernel,
+        out_shape=tile_shape(count + sum(x.shape[0] for x in first)),
+        compiler_params=params,
+        name="close",
+    )(keep[0], got[0], *first)
     for bit in range(far_bits):
         pairs = [(i, i ^ (1 << bit)) for i in range(sizes["far"])]
         got = [lax.ppermute(x, "far", pairs) for x in total]
-        if bit == far_bits - 1:
-            cross = lax.ppermute(cross, RING, crossings)
-            got[-1], cross, mate = lax.optimization_barrier((got[-1], cross, mate))
+        more = riders[1:] if bit == far_bits - 1 else []
+        kernel = functools.partial(meet_kernel, (("far", bit),) * 2, sizes, rows, count)
+        shape = tile_shape(total[0].shape[0] + sum(x.shape[0] for x in more))
+        carried = call("meet", kernel, shape, me, total[0], got[0], *more)
         total = [(x.astype(F32) + y.astype(F32)).astype(BF16) for x, y in zip(total, got)]
+        total[0] = carried
     for phase in reversed(range(phases)):
         pairs = bit_pairs(sizes, orders, phase)
         got = [lax.ppermute(x, SPLIT, pairs) for x in total]
-        riders = [()] * (CHUNKS - 1) + [(mate,) if phase == 0 else ()]
-        total = [join(phase, x, y, *z) for x, y, z in zip(total, got, riders)]
+        for i in range(CHUNKS):
+            last = i == 0 and phase == 0
+            kernel = functools.partial(join_kernel, choices[phase], sizes, rows, count, last)
+            if last:
+                shape = (tile_shape(2 * count + rows), jax.ShapeDtypeStruct((channels, RIM), F32))
+                total[0], side = call("join", kernel, shape, me, total[0], got[0], stay)
+            else:
+                shape = tile_shape(total[i].shape[0] + count)
+                total[i] = call("join", kernel, shape, me, total[i], got[i])
+        count *= 2
     other = [lax.ppermute(x, "core", swap) for x in total]
     conv_wgrad_t, down_wgrad, grad_input_t = pl.pallas_call(
         functools.partial(final_kernel, taps, CHUNKS, size),
@@ -431,7 +534,7 @@
         in_specs=[smem] + [vmem] * (2 * CHUNKS + 2),
         compiler_params=params,
         name="final",
-    )(core, *total, *other, base, cross)
+    )(core, *total, *other, base, side)
     return coarse, grad_input_t.T, conv_wgrad_t.T, down_wgrad
 
 

time: 54.9 us -> 54.2 us (0.987)
  starting transfers between devices: 24.9 us -> 20.5 us
  waiting for transfers between devices: 17.5 us -> 21.8 us
    ppermute x4 -> x2, waiting for transfers between devices: 5.29 us -> 9 us  [on_device(): got = [lax.ppermute(x, SPLIT, pairs) for x in total]]
    ppermute x2 -> x1, starting transfers between devices: 3.96 us -> 0.54 us  [on_device(): got = [lax.ppermute(x, 'core', swap) for x in send]]
    ppermute x1, starting transfers between devices: 0.04 us -> 3.42 us  [on_device(): mate = lax.ppermute(row, RING, mates)]
    ppermute x2 -> x0, starting transfers between devices: 2.18 us -> none  [the longest x1 1.52 us: on_device(): edges = [lax.ppermute(x, 'slab', p) for x, p in zip(edges, back)]]
    ppermute x4 -> x2, starting transfers between devices: 4 us -> 2.61 us  [on_device(): got = [lax.ppermute(x, SPLIT, pairs) for x in total]]
    ppermute x4 -> x2, starting transfers between devices: 5.21 us -> 3.84 us  [on_device(): got[i] = lax.ppermute(send[i], SPLIT, pairs)]
    ppermute x2 -> x1, waiting for transfers between devices: 1.41 us -> 0.55 us  [on_device(): other = [lax.ppermute(x, 'core', swap) for x in total]]
    ppermute x4 -> x2, waiting for transfers between devices: 3.24 us -> 4.05 us  [on_device(): got[i] = lax.ppermute(send[i], SPLIT, pairs)]
  transfers between devices with their start and end apart: 21 -> 11, of which waited for: 9 -> 9; matrix products, arithmetic and copies ran while one was open for 0% -> 0% of each run, Pallas kernels for 9% -> 10%
where the time goes in v6:
time: 54.2 us; the launch traced here: 53.9 us
  waiting for transfers between devices  21.8 us (40%)
  starting transfers between devices  20.5 us (38%)
  Pallas kernels  9 us (17%)
  local copies, waits for them, and re-layouts  1.79 us (3%)
  between operations  0.76 us (1%)
    ppermute x2, waiting for transfers between devices, on_device(): got = [lax.ppermute(x, SPLIT, pairs) for x in total]  9 us
    ppermute x2, waiting for transfers between devices, on_device(): got = [lax.ppermute(x, 'far', pairs) for x in total]  6.77 us
    ppermute x2, starting transfers between devices, on_device(): got = [lax.ppermute(x, 'far', pairs) for x in total]  6.37 us
    ppermute x2, waiting for transfers between devices, on_device(): got[i] = lax.ppermute(send[i], SPLIT, pairs)  4.05 us
    ppermute x2, starting transfers between devices, on_device(): got[i] = lax.ppermute(send[i], SPLIT, pairs)  3.84 us
    ppermute x1, starting transfers between devices, on_device(): mate = lax.ppermute(row, RING, mates)  3.42 us
    ppermute x1, starting transfers between devices, on_device(): side = [lax.ppermute(rim, 'slab', pairs) for pairs in beside]  2.97 us
    ppermute x2, starting transfers between devices, on_device(): got = [lax.ppermute(x, SPLIT, pairs) for x in total]  2.61 us
  transfers between devices with their start and end apart: 11, of which 9 were waited for; matrix products, arithmetic and copies ran while one was open for 0% of the time, Pallas kernels for 10%

profile of v6, /device:TPU:0, one launch (start us, length us, event | category | flops | bytes accessed | tf_op | source)
XLA Modules:
  0.0 53.9 jit_solution(4946709705033256795)
XLA Ops:
  0.6 0.0 copy-start.1
  0.6 0.8 %slice.4 = bf16[96,64]{1,0:T(8,128)(2,1)S(1)} slice(bf16[96,256]{1,0:T(8,128)(2,1)} %bitcast.10), slice={[0:96], [0:64]} | slice | bytes 24576 | tf_op jit(solution)/shard_map/slice | solution.py:380
  1.4 3.0 %collective-permute-start = (bf16[96,64]{1,0:T(8,128)(2,1)S(1)}, bf16[96,64]{1,0:T(8,128)(2,1)S(1)}, u32[]{:S(2)}, u32[]{:S(2)}) collective-permute-start(bf16[96,64]{1,0:T(8,128)(2,1)S(1)} %slice.4), channel_id=1, source_target_pairs={{0,1},{1,0},{2,3},{3,2},{4,5},{5,4},{6,7},{7,6},{8,9},{9,8},{10,11... | collective-permute-start | bytes 36872 | tf_op jit(solution)/shard_map/ppermute | solution.py:385
  4.4 0.0 copy-done.1
  4.4 0.0 copy-start.2
  4.4 0.8 %copy-done.2 = s32[256,27]{0,1:T(8,128)S(1)} copy-done((s32[256,27]{0,1:T(8,128)S(1)}, s32[256,27]{0,1:T(8,128)}, u32[]{:S(2)}) %copy-start.2) | copy-done | bytes 27672
  5.2 0.0 copy-start.5
  5.2 1.0 %gather.1 = (bf16[2592,128]{1,0:T(8,128)(2,1)S(1)}, bf16[2592,128]{1,0:T(8,128)(2,1)S(1)}) custom-call(bf16[96,256]{1,0:T(8,128)(2,1)S(1)} %bitcast.11, s32[27,256]{1,0:T(8,128)S(1)} %bitcast.13), custom_call_target="tpu_custom_call" | custom-call | flops 2000000000 | bytes 10000000 | tf_op jit(solution)/shard_map/gather/pallas_call | solution.py:386
  6.2 0.0 collective-permute-done.refs_6_
  6.2 0.0 copy-start.4
  6.2 0.0 copy-start.7
  6.2 0.1 pad_maximum_fusion
  6.3 0.7 %collective-permute-start.2 = (bf16[96,128]{1,0:T(8,128)(2,1)S(1)}, bf16[96,128]{1,0:T(8,128)(2,1)S(1)}, u32[]{:S(2)}, u32[]{:S(2)}) collective-permute-start(bf16[96,128]{1,0:T(8,128)(2,1)S(1)} %pad_maximum_fusion), channel_id=1, source_target_pairs={{2,4},{6,8},{10,12},{14,16},{18,20},{22,24},{26,28},{4,2},{8,6},{1... | collective-permute-start | bytes 73736 | tf_op jit(solution)/shard_map/ppermute | solution.py:399
  7.0 3.4 %collective-permute-start.1 = (bf16[96,128]{1,0:T(8,128)(2,1)S(1)}, bf16[96,128]{1,0:T(8,128)(2,1)S(1)}, u32[]{:S(2)}, u32[]{:S(2)}) collective-permute-start(bf16[96,128]{1,0:T(8,128)(2,1)S(1)} %pad_maximum_fusion), channel_id=1, source_target_pairs={{0,2},{2,0},{4,6},{6,4},{8,10},{10,8},{12,14},{14,12},{16,18},{18,... | collective-permute-start | bytes 73736 | tf_op jit(solution)/shard_map/ppermute | solution.py:400
  10.4 0.0 copy-done.5
  10.4 0.0 copy-done.4
  10.4 0.0 copy-done.7
  10.4 0.0 copy-start
  10.4 0.0 copy-start.3
  10.4 0.7 %taps.1 = (bf16[8,64,256]{2,1,0:T(8,128)(2,1)S(1)}, f32[96,256]{1,0:T(8,128)S(1)}) custom-call(s32[8,64]{1,0:T(8,128)S(1)} %bitcast.16, bf16[64,128]{1,0:T(8,128)(2,1)S(1)} %copy-done.4, bf16[768,128]{1,0:T(8,128)(2,1)S(1)} %copy-done.5), custom_call_target="tpu_custom_call" | custom-call | flops 2000000000 | bytes 10000000 | tf_op jit(solution)/shard_map/taps/pallas_call | solution.py:402
  11.1 0.0 collective-permute-done.2.refs_5_
  11.1 0.1 collective-permute-done.1.refs_4_
  11.2 0.2 copy-done
  11.4 0.0 copy-done.3
  11.4 2.2 %forward.1 = (bf16[96,256]{1,0:T(8,128)(2,1)S(1)}, bf16[96,256]{1,0:T(8,128)(2,1)S(1)}, f32[88,16,128]{2,1,0:T(8,128)S(1)}, bf16[88,16,128]{2,1,0:T(8,128)(2,1)S(1)}) custom-call(s32[1]{0:T(128)} %bitcast.3.core_ref, bf16[96,256]{1,0:T(8,128)(2,1)S(1)} %bitcast.12, s32[27,256]{1,0:T(8,128)S(1)} %bitcast.14, bf16[64,128]{1,0:T(8,128)(2,1)S(1)} %copy-done.4, ...), custom_call_target="tpu_custom_call" | custom-call | tf_op jit(solution)/shard_map/forward/pallas_call | solution.py:417
  13.7 0.5 collective-permute-start.3
  14.2 1.3 %collective-permute-done.3.got_ref = bf16[88,16,128]{2,1,0:T(8,128)(2,1)S(1)} collective-permute-done((bf16[88,16,128]{2,1,0:T(8,128)(2,1)S(1)}, bf16[88,16,128]{2,1,0:T(8,128)(2,1)S(1)}, u32[]{:S(2)}, u32[]{:S(2)}) %collective-permute-start.3) | collective-permute-done | bytes 360480 | tf_op jit(solution)/shard_map/ppermute | solution.py:454
  15.5 0.1 fold.2
  15.6 2.3 %collective-permute-start.4 = (bf16[44,16,128]{2,1,0:T(8,128)(2,1)S(1)}, bf16[44,16,128]{2,1,0:T(8,128)(2,1)S(1)}, u32[]{:S(2)}, u32[]{:S(2)}) collective-permute-start(bf16[44,16,128]{2,1,0:T(8,128)(2,1)S(1)} %get-tuple-element.50), channel_id=1, source_target_pairs={{0,4},{1,5},{2,3},{3,2},{4,0},{5,1},{6,7},{7,6},{8,12},{9,13},{10,... | collective-permute-start | bytes 540680 | tf_op jit(solution)/shard_map/ppermute | solution.py:461
  17.8 2.4 %backward.1 = (f32[96,256]{1,0:T(8,128)S(1)}, f32[96,64]{1,0:T(8,128)S(1)}, bf16[6,16,128]{2,1,0:T(8,128)(2,1)S(1)}, bf16[6,16,128]{2,1,0:T(8,128)(2,1)S(1)}) custom-call(s32[1]{0:T(128)} %bitcast.3.core_ref, s32[27,256]{1,0:T(8,128)S(1)} %bitcast.15, f32[96,256]{1,0:T(8,128)S(1)} %get-tuple-element.43.refs_3_.hgrad_ref, ...), custom_call_target="tpu_custom_call" | custom-call | flops 2000000000 | bytes 10000000 | tf_op jit(solution)/shard_map/backward/pallas_call | solution.py:464
  20.3 1.0 %collective-permute-done.4.got_ref = bf16[44,16,128]{2,1,0:T(8,128)(2,1)S(1)} collective-permute-done((bf16[44,16,128]{2,1,0:T(8,128)(2,1)S(1)}, bf16[44,16,128]{2,1,0:T(8,128)(2,1)S(1)}, u32[]{:S(2)}, u32[]{:S(2)}) %collective-permute-start.4) | collective-permute-done | bytes 180256 | tf_op jit(solution)/shard_map/ppermute | solution.py:461
  21.3 1.6 %collective-permute-start.5 = (bf16[22,16,128]{2,1,0:T(8,128)(2,1)S(1)}, bf16[22,16,128]{2,1,0:T(8,128)(2,1)S(1)}, u32[]{:S(2)}, u32[]{:S(2)}) collective-permute-start(bf16[22,16,128]{2,1,0:T(8,128)(2,1)S(1)} %get-tuple-element.58), channel_id=1, source_target_pairs={{0,1},{1,0},{2,6},{3,7},{4,5},{5,4},{6,2},{7,3},{8,9},{9,8},{10,14... | collective-permute-start | bytes 270344 | tf_op jit(solution)/shard_map/ppermute | solution.py:461
  22.9 3.0 %collective-permute-done.5.got_ref = bf16[22,16,128]{2,1,0:T(8,128)(2,1)S(1)} collective-permute-done((bf16[22,16,128]{2,1,0:T(8,128)(2,1)S(1)}, bf16[22,16,128]{2,1,0:T(8,128)(2,1)S(1)}, u32[]{:S(2)}, u32[]{:S(2)}) %collective-permute-start.5) | collective-permute-done | bytes 90144 | tf_op jit(solution)/shard_map/ppermute | solution.py:461
  26.0 2.8 %collective-permute-start.6 = (bf16[28,16,128]{2,1,0:T(8,128)(2,1)S(1)}, bf16[28,16,128]{2,1,0:T(8,128)(2,1)S(1)}, u32[]{:S(2)}, u32[]{:S(2)}) collective-permute-start(bf16[28,16,128]{2,1,0:T(8,128)(2,1)S(1)} %close.1.own_ref), channel_id=1, source_target_pairs={{0,8},{8,0},{16,24},{24,16},{1,9},{9,1},{17,25},{25,17},{2,10},{10... | collective-permute-start | bytes 344072 | tf_op jit(solution)/shard_map/ppermute | solution.py:506
  28.8 2.8 %collective-permute-done.6.got_ref = bf16[28,16,128]{2,1,0:T(8,128)(2,1)S(1)} collective-permute-done((bf16[28,16,128]{2,1,0:T(8,128)(2,1)S(1)}, bf16[28,16,128]{2,1,0:T(8,128)(2,1)S(1)}, u32[]{:S(2)}, u32[]{:S(2)}) %collective-permute-start.6) | collective-permute-done | bytes 114720 | tf_op jit(solution)/shard_map/ppermute | solution.py:506
  31.6 3.6 %collective-permute-start.7 = (bf16[28,16,128]{2,1,0:T(8,128)(2,1)S(1)}, bf16[28,16,128]{2,1,0:T(8,128)(2,1)S(1)}, u32[]{:S(2)}, u32[]{:S(2)}) collective-permute-start(bf16[28,16,128]{2,1,0:T(8,128)(2,1)S(1)} %meet.2.own_ref), channel_id=1, source_target_pairs={{0,16},{8,24},{16,0},{24,8},{1,17},{9,25},{17,1},{25,9},{2,18},{10... | collective-permute-start | bytes 344072 | tf_op jit(solution)/shard_map/ppermute | solution.py:506
  35.1 4.0 %collective-permute-done.7.got_ref = bf16[28,16,128]{2,1,0:T(8,128)(2,1)S(1)} collective-permute-done((bf16[28,16,128]{2,1,0:T(8,128)(2,1)S(1)}, bf16[28,16,128]{2,1,0:T(8,128)(2,1)S(1)}, u32[]{:S(2)}, u32[]{:S(2)}) %collective-permute-start.7) | collective-permute-done | bytes 114720 | tf_op jit(solution)/shard_map/ppermute | solution.py:506
  39.2 1.6 %collective-permute-start.8 = (bf16[34,16,128]{2,1,0:T(8,128)(2,1)S(1)}, bf16[34,16,128]{2,1,0:T(8,128)(2,1)S(1)}, u32[]{:S(2)}, u32[]{:S(2)}) collective-permute-start(bf16[34,16,128]{2,1,0:T(8,128)(2,1)S(1)} %meet.3.own_ref), channel_id=1, source_target_pairs={{0,1},{1,0},{2,6},{3,7},{4,5},{5,4},{6,2},{7,3},{8,9},{9,8},{10,14... | collective-permute-start | bytes 417800 | tf_op jit(solution)/shard_map/ppermute | solution.py:515
  40.8 3.9 %collective-permute-done.8.got_ref = bf16[34,16,128]{2,1,0:T(8,128)(2,1)S(1)} collective-permute-done((bf16[34,16,128]{2,1,0:T(8,128)(2,1)S(1)}, bf16[34,16,128]{2,1,0:T(8,128)(2,1)S(1)}, u32[]{:S(2)}, u32[]{:S(2)}) %collective-permute-start.8) | collective-permute-done | bytes 139296 | tf_op jit(solution)/shard_map/ppermute | solution.py:515
  44.7 0.0 copy-start.6
  44.7 1.0 %collective-permute-start.9 = (bf16[56,16,128]{2,1,0:T(8,128)(2,1)S(1)}, bf16[56,16,128]{2,1,0:T(8,128)(2,1)S(1)}, u32[]{:S(2)}, u32[]{:S(2)}) collective-permute-start(bf16[56,16,128]{2,1,0:T(8,128)(2,1)S(1)} %join.2.own_ref), channel_id=1, source_target_pairs={{0,4},{1,5},{2,3},{3,2},{4,0},{5,1},{6,7},{7,6},{8,12},{9,13},{10,... | collective-permute-start | bytes 688136 | tf_op jit(solution)/shard_map/ppermute | solution.py:515
  45.8 5.1 %collective-permute-done.9.got_ref = bf16[56,16,128]{2,1,0:T(8,128)(2,1)S(1)} collective-permute-done((bf16[56,16,128]{2,1,0:T(8,128)(2,1)S(1)}, bf16[56,16,128]{2,1,0:T(8,128)(2,1)S(1)}, u32[]{:S(2)}, u32[]{:S(2)}) %collective-permute-start.9) | collective-permute-done | bytes 229408 | tf_op jit(solution)/shard_map/ppermute | solution.py:515
  50.8 0.1 join.3
  50.9 0.1 collective-permute-start.10
  51.0 0.0 copy-done.6
  51.0 1.1 %coarse.1 = bf16[64,128]{1,0:T(8,128)(2,1)} custom-call(bf16[8,64,256]{2,1,0:T(8,128)(2,1)S(1)} %get-tuple-element.40.refs_2_.pick_ref, bf16[96,256]{1,0:T(8,128)(2,1)S(1)} %get-tuple-element.44.hidden_ref, bf16[768,128]{1,0:T(8,128)(2,1)S(1)} %copy-done.6), custom_call_target="tpu_custom_call" | custom-call | flops 2000000000 | bytes 10000000 | tf_op jit(solution)/shard_map/coarse/pallas_call | solution.py:486
  52.1 0.6 %collective-permute-done.10.refs_1_ = bf16[94,16,128]{2,1,0:T(8,128)(2,1)S(1)} collective-permute-done((bf16[94,16,128]{2,1,0:T(8,128)(2,1)S(1)}, bf16[94,16,128]{2,1,0:T(8,128)(2,1)S(1)}, u32[]{:S(2)}, u32[]{:S(2)}) %collective-permute-start.10) | collective-permute-done | bytes 385056 | tf_op jit(solution)/shard_map/ppermute | solution.py:526
  52.7 1.2 %final.1 = (f32[96,2592]{1,0:T(8,128)}, f32[768,128]{1,0:T(8,128)}, f32[96,256]{1,0:T(8,128)}) custom-call(s32[1]{0:T(128)} %bitcast.3.core_ref, bf16[94,16,128]{2,1,0:T(8,128)(2,1)S(1)} %get-tuple-element.62.refs_0_, bf16[94,16,128]{2,1,0:T(8,128)(2,1)S(1)} %collective-permute-done.10.refs_1_, f32[96,256]{1,0:T(8,128)S(1)} %get-tuple-element.63.refs_2_, ...), custom_call_target="tpu_custom_call" | custom-call | tf_op jit(solution)/shard_map/final/pallas_call | solution.py:527
  (5 shorter events, 0.1 us)
Async XLA Ops:
  0.6 3.8 %copy-start.1 = (bf16[256,96]{0,1:T(8,128)(2,1)S(1)}, bf16[256,96]{0,1:T(8,128)(2,1)}, u32[]{:S(2)}) copy-start(bf16[256,96]{0,1:T(8,128)(2,1)} %param.6) | copy-start | bytes 147460
  1.4 4.8 %collective-permute-start = (bf16[96,64]{1,0:T(8,128)(2,1)S(1)}, bf16[96,64]{1,0:T(8,128)(2,1)S(1)}, u32[]{:S(2)}, u32[]{:S(2)}) collective-permute-start(bf16[96,64]{1,0:T(8,128)(2,1)S(1)} %slice.4), channel_id=1, source_target_pairs={{0,1},{1,0},{2,3},{3,2},{4,5},{5,4},{6,7},{7,6},{8,9},{9,8},{10,11... | collective-permute-start | bytes 36872 | tf_op jit(solution)/shard_map/ppermute | solution.py:385
  4.4 0.8 %copy-start.2 = (s32[256,27]{0,1:T(8,128)S(1)}, s32[256,27]{0,1:T(8,128)}, u32[]{:S(2)}) copy-start(s32[256,27]{0,1:T(8,128)} %param.7) | copy-start | bytes 82948
  5.2 5.2 %copy-start.5 = (bf16[768,128]{1,0:T(8,128)(2,1)S(1)}, bf16[768,128]{1,0:T(8,128)(2,1)}, u32[]{:S(2)}) copy-start(bf16[768,128]{1,0:T(8,128)(2,1)} %wd_ref.3) | copy-start | bytes 589828
  6.2 4.2 %copy-start.4 = (bf16[64,128]{1,0:T(8,128)(2,1)S(1)}, bf16[64,128]{1,0:T(8,128)(2,1)}, u32[]{:S(2)}) copy-start(bf16[64,128]{1,0:T(8,128)(2,1)} %cgrad_ref.3) | copy-start | bytes 49156
  6.2 4.2 %copy-start.7 = (s32[64,8]{0,1:T(8,128)S(1)}, s32[64,8]{0,1:T(8,128)}, u32[]{:S(2)}) copy-start(s32[64,8]{0,1:T(8,128)} %param.8) | copy-start | bytes 6148
  6.3 4.8 %collective-permute-start.2 = (bf16[96,128]{1,0:T(8,128)(2,1)S(1)}, bf16[96,128]{1,0:T(8,128)(2,1)S(1)}, u32[]{:S(2)}, u32[]{:S(2)}) collective-permute-start(bf16[96,128]{1,0:T(8,128)(2,1)S(1)} %pad_maximum_fusion), channel_id=1, source_target_pairs={{2,4},{6,8},{10,12},{14,16},{18,20},{22,24},{26,28},{4,2},{8,6},{1... | collective-permute-start | bytes 73736 | tf_op jit(solution)/shard_map/ppermute | solution.py:399
  7.0 4.3 %collective-permute-start.1 = (bf16[96,128]{1,0:T(8,128)(2,1)S(1)}, bf16[96,128]{1,0:T(8,128)(2,1)S(1)}, u32[]{:S(2)}, u32[]{:S(2)}) collective-permute-start(bf16[96,128]{1,0:T(8,128)(2,1)S(1)} %pad_maximum_fusion), channel_id=1, source_target_pairs={{0,2},{2,0},{4,6},{6,4},{8,10},{10,8},{12,14},{14,12},{16,18},{18,... | collective-permute-start | bytes 73736 | tf_op jit(solution)/shard_map/ppermute | solution.py:400
  10.4 1.0 %copy-start = (bf16[2592,96]{0,1:T(8,128)(2,1)S(1)}, bf16[2592,96]{0,1:T(8,128)(2,1)}, u32[]{:S(2)}) copy-start(bf16[2592,96]{0,1:T(8,128)(2,1)} %param.9) | copy-start | bytes 1492996
  10.4 1.0 %copy-start.3 = (s32[256,27]{0,1:T(8,128)S(1)}, s32[256,27]{0,1:T(8,128)}, u32[]{:S(2)}) copy-start(s32[256,27]{0,1:T(8,128)} %param.7) | copy-start | bytes 82948
  13.7 1.8 %collective-permute-start.3 = (bf16[88,16,128]{2,1,0:T(8,128)(2,1)S(1)}, bf16[88,16,128]{2,1,0:T(8,128)(2,1)S(1)}, u32[]{:S(2)}, u32[]{:S(2)}) collective-permute-start(bf16[88,16,128]{2,1,0:T(8,128)(2,1)S(1)} %get-tuple-element.46), channel_id=1, source_target_pairs={{0,2},{2,0},{1,3},{3,1},{4,6},{6,4},{5,7},{7,5},{8,10},{10,8},{9,1... | collective-permute-start | bytes 1081352 | tf_op jit(solution)/shard_map/ppermute | solution.py:454
  15.6 5.7 %collective-permute-start.4 = (bf16[44,16,128]{2,1,0:T(8,128)(2,1)S(1)}, bf16[44,16,128]{2,1,0:T(8,128)(2,1)S(1)}, u32[]{:S(2)}, u32[]{:S(2)}) collective-permute-start(bf16[44,16,128]{2,1,0:T(8,128)(2,1)S(1)} %get-tuple-element.50), channel_id=1, source_target_pairs={{0,4},{1,5},{2,3},{3,2},{4,0},{5,1},{6,7},{7,6},{8,12},{9,13},{10,... | collective-permute-start | bytes 540680 | tf_op jit(solution)/shard_map/ppermute | solution.py:461
  21.3 4.6 %collective-permute-start.5 = (bf16[22,16,128]{2,1,0:T(8,128)(2,1)S(1)}, bf16[22,16,128]{2,1,0:T(8,128)(2,1)S(1)}, u32[]{:S(2)}, u32[]{:S(2)}) collective-permute-start(bf16[22,16,128]{2,1,0:T(8,128)(2,1)S(1)} %get-tuple-element.58), channel_id=1, source_target_pairs={{0,1},{1,0},{2,6},{3,7},{4,5},{5,4},{6,2},{7,3},{8,9},{9,8},{10,14... | collective-permute-start | bytes 270344 | tf_op jit(solution)/shard_map/ppermute | solution.py:461
  26.0 5.6 %collective-permute-start.6 = (bf16[28,16,128]{2,1,0:T(8,128)(2,1)S(1)}, bf16[28,16,128]{2,1,0:T(8,128)(2,1)S(1)}, u32[]{:S(2)}, u32[]{:S(2)}) collective-permute-start(bf16[28,16,128]{2,1,0:T(8,128)(2,1)S(1)} %close.1.own_ref), channel_id=1, source_target_pairs={{0,8},{8,0},{16,24},{24,16},{1,9},{9,1},{17,25},{25,17},{2,10},{10... | collective-permute-start | bytes 344072 | tf_op jit(solution)/shard_map/ppermute | solution.py:506
  31.6 7.6 %collective-permute-start.7 = (bf16[28,16,128]{2,1,0:T(8,128)(2,1)S(1)}, bf16[28,16,128]{2,1,0:T(8,128)(2,1)S(1)}, u32[]{:S(2)}, u32[]{:S(2)}) collective-permute-start(bf16[28,16,128]{2,1,0:T(8,128)(2,1)S(1)} %meet.2.own_ref), channel_id=1, source_target_pairs={{0,16},{8,24},{16,0},{24,8},{1,17},{9,25},{17,1},{25,9},{2,18},{10... | collective-permute-start | bytes 344072 | tf_op jit(solution)/shard_map/ppermute | solution.py:506
  39.2 5.5 %collective-permute-start.8 = (bf16[34,16,128]{2,1,0:T(8,128)(2,1)S(1)}, bf16[34,16,128]{2,1,0:T(8,128)(2,1)S(1)}, u32[]{:S(2)}, u32[]{:S(2)}) collective-permute-start(bf16[34,16,128]{2,1,0:T(8,128)(2,1)S(1)} %meet.3.own_ref), channel_id=1, source_target_pairs={{0,1},{1,0},{2,6},{3,7},{4,5},{5,4},{6,2},{7,3},{8,9},{9,8},{10,14... | collective-permute-start | bytes 417800 | tf_op jit(solution)/shard_map/ppermute | solution.py:515
  44.7 6.3 %copy-start.6 = (bf16[768,128]{1,0:T(8,128)(2,1)S(1)}, bf16[768,128]{1,0:T(8,128)(2,1)}, u32[]{:S(2)}) copy-start(bf16[768,128]{1,0:T(8,128)(2,1)} %wd_ref.3) | copy-start | bytes 589828
  44.7 6.1 %collective-permute-start.9 = (bf16[56,16,128]{2,1,0:T(8,128)(2,1)S(1)}, bf16[56,16,128]{2,1,0:T(8,128)(2,1)S(1)}, u32[]{:S(2)}, u32[]{:S(2)}) collective-permute-start(bf16[56,16,128]{2,1,0:T(8,128)(2,1)S(1)} %join.2.own_ref), channel_id=1, source_target_pairs={{0,4},{1,5},{2,3},{3,2},{4,0},{5,1},{6,7},{7,6},{8,12},{9,13},{10,... | collective-permute-start | bytes 688136 | tf_op jit(solution)/shard_map/ppermute | solution.py:515
  50.9 1.8 %collective-permute-start.10 = (bf16[94,16,128]{2,1,0:T(8,128)(2,1)S(1)}, bf16[94,16,128]{2,1,0:T(8,128)(2,1)S(1)}, u32[]{:S(2)}, u32[]{:S(2)}) collective-permute-start(bf16[94,16,128]{2,1,0:T(8,128)(2,1)S(1)} %get-tuple-element.62.refs_0_), channel_id=1, source_target_pairs={{0,2},{2,0},{1,3},{3,1},{4,6},{6,4},{5,7},{7,5},{8,10},{10,8},{9,1... | collective-permute-start | bytes 1155080 | tf_op jit(solution)/shard_map/ppermute | solution.py:526

commit v7 on v6

--- a/solution.py
+++ b/solution.py
@@ -12,7 +12,7 @@
 RIM = 64
 LANES = 128
 TILE = 16
-CHUNKS = 1
+EXTRA = 0.27
 F32 = jnp.float32
 BF16 = jnp.bfloat16
 NN = (((1,), (0,)), ((), ()))
@@ -98,7 +98,8 @@
 def forward_kernel(slabs, core_ref, f_ref, near_ref, cgrad_ref, w_ref, *refs):
     first_ref, rest_ref, pick_ref, hgrad_ref = refs[:4]
     halo_refs, refs = (refs[4:7], refs[7:]) if slabs == 2 else (refs[4:8], refs[8:])
-    grad_ref, hidden_ref, *chunks, rt, conv_w, down_w = refs
+    grad_ref, hidden_ref, keep_ref, send_ref, more_keep_ref, more_send_ref, *refs = refs
+    rt, conv_w, down_w = refs
     channels, voxels = f_ref.shape
     offsets = near_ref.shape[0]
     taps = pick_ref.shape[0]
@@ -131,15 +132,16 @@
         down_w[t * channels : (t + 1) * channels, :] = mm(picked_t, cgrad)
 
     tiles = payload_tiles(channels, conv_columns, taps)
-    count = len(chunks) // 2
-    size = chunks[0].shape[0]
+    shared = keep_ref.shape[0]
     for core in range(2):
 
         @pl.when(core_ref[0] == core)
         def _(core=core):
-            for i in range(2 * count * size):
-                half, chunk, place = i // (count * size), i // size % count, i % size
-                ref = chunks[2 * chunk + (half != core)]
+            for i in range(2 * shared + more_keep_ref.shape[0]):
+                if i < 2 * shared:
+                    ref, place = keep_ref if i // shared == core else send_ref, i % shared
+                else:
+                    ref, place = more_keep_ref if core else more_send_ref, i - 2 * shared
                 if i < len(tiles):
                     kind, row, column, _ = tiles[i]
                     source = down_w if kind else conv_w
@@ -307,25 +309,28 @@
         side_ref[j * TILE : (j + 1) * TILE, :] = side
 
 
-def final_kernel(taps, count, size, core_ref, *refs):
-    mine, other, refs = refs[:count], refs[count : 2 * count], refs[2 * count :]
-    base_ref, side_ref, conv_ref, down_ref, grad_ref = refs
+def final_kernel(taps, shared, core_ref, *refs):
+    mine_ref, more_ref, other_ref, other_more_ref, base_ref, side_ref, *refs = refs
+    conv_ref, down_ref, grad_ref = refs
     channels, conv_columns = conv_ref.shape
     grad_ref[:, RIM:] = base_ref[:, RIM:]
     for i in range(channels // TILE):
         rows = slice(i * TILE, (i + 1) * TILE)
         total = base_ref[rows, :RIM] + side_ref[rows, :]
-        grad_ref[rows, :RIM] = total + other[0][size + i][:, :RIM].astype(F32)
+        grad_ref[rows, :RIM] = total + other_ref[shared + i][:, :RIM].astype(F32)
     for core in range(2):
 
         @pl.when(core_ref[0] == core)
         def _(core=core):
             for i, tile in enumerate(payload_tiles(channels, conv_columns, taps)):
                 kind, row, column, columns = tile
-                source = mine if i // (count * size) == core else other
-                value = source[i // size % count][i % size].astype(F32)
+                if i < 2 * shared:
+                    value = (mine_ref if i // shared == core else other_ref)[i % shared]
+                else:
+                    value = (more_ref if core else other_more_ref)[i - 2 * shared]
                 target = down_ref if kind else conv_ref
-                target[row : row + TILE, column : column + columns] = value[:, :columns]
+                value = value.astype(F32)[:, :columns]
+                target[row : row + TILE, column : column + columns] = value
 
 
 def shifts(count, step):
@@ -344,13 +349,15 @@
     return near + slab if core == 0 else slab + near
 
 
-def bit_pairs(sizes, orders, phase):
+def bit_pairs(sizes, choice, cores):
     pairs = []
     for index in range(functools.reduce(lambda a, b: a * b, sizes.values())):
         place, left = {}, index
         for axis in reversed(SPLIT):
             left, place[axis] = divmod(left, sizes[axis])
-        axis, bit = orders[place["core"]][phase]
+        if place["core"] not in cores:
+            continue
+        axis, bit = choice[place["core"]]
         place[axis] ^= 1 << bit
         other = 0
         for name in SPLIT:
@@ -382,7 +389,7 @@
         beside = [swap]
     else:
         beside = [shifts(slabs, 1), shifts(slabs, -1)]
-    side = [lax.ppermute(rim, "slab", pairs) for pairs in beside]
+    side = [lax.ppermute(features_t, "slab", pairs) for pairs in beside]
     own = pl.pallas_call(
         functools.partial(gather_kernel, slabs),
         out_shape=(
@@ -394,6 +401,7 @@
         name="gather",
     )(features_t, neighbours_t)
     side, own = lax.optimization_barrier((side, own))
+    side = [x[:, :RIM] for x in side]
     row = [rim, side[0]] if slabs == 2 else [side[0], rim, side[1]]
     row = jnp.concatenate(row, axis=1)
     cross = lax.ppermute(row, RING, crossings)
@@ -413,14 +421,19 @@
     far_rows = -(-sum(x.shape[1] for x in halos) // LANES) * LANES
 
     tiles = len(payload_tiles(channels, conv_columns, taps))
-    size = -(-tiles // (2 * CHUNKS << phases)) << phases
+    more = round(tiles * EXTRA / (1 << phases)) << phases
+    shared = -(-(tiles - more) // (2 << phases)) << phases
     grad, hidden, *chunks = pl.pallas_call(
         functools.partial(forward_kernel, slabs),
         out_shape=[
             jax.ShapeDtypeStruct((channels, voxels), BF16),
             jax.ShapeDtypeStruct((channels, voxels), BF16),
         ]
-        + [jax.ShapeDtypeStruct((size, TILE, LANES), kind) for kind in (F32, BF16)] * CHUNKS,
+        + [
+            jax.ShapeDtypeStruct((size, TILE, LANES), kind)
+            for size in (shared, more)
+            for kind in (F32, BF16)
+        ],
         in_specs=[smem] + [vmem] * (8 + len(halos)),
         scratch_shapes=[
             pltpu.VMEM((conv_columns, voxels), BF16),
@@ -451,14 +464,16 @@
         return call("fold", kernel, (tile_shape(half, F32), tile_shape(half)), me, keep, got)
 
     keep, send = chunks[0::2], chunks[1::2]
-    got = [lax.ppermute(x, "core", swap) for x in send]
+    cores = ((0, 1), (1,))
+    got = [lax.ppermute(x, "core", p) for x, p in zip(send, (swap, swap[:1]))]
     for phase in range(phases):
-        pairs = bit_pairs(sizes, orders, phase)
-        for i in range(CHUNKS):
+        for i in (1, 0):
             keep[i], send[i] = fold(phase, keep[i], got[i])
-            if i == CHUNKS - 1 and phase == 0:
-                send[i], grad = lax.optimization_barrier((send[i], grad))
-            got[i] = lax.ppermute(send[i], SPLIT, pairs)
+            if i == 0:
+                send[0], _ = lax.optimization_barrier((send[0], send[1]))
+            if i == 0 and phase == 0:
+                send[0], grad = lax.optimization_barrier((send[0], grad))
+            got[i] = lax.ppermute(send[i], SPLIT, bit_pairs(sizes, choices[phase], cores[i]))
         if phase == 0:
             slots = len(slot_table(slabs)) // 4 * rows
             base, stay, *riders = pl.pallas_call(
@@ -492,46 +507,49 @@
             )(pick, hidden, w_down)
 
     far_bits = sizes["far"].bit_length() - 1
-    count = keep[0].shape[0]
+    count = [x.shape[0] for x in keep]
     first = riders[:1] if far_bits else riders
     total = [(x + y.astype(F32)).astype(BF16) for x, y in zip(keep, got)]
     total[0] = pl.pallas_call(
         close_kernel,
-        out_shape=tile_shape(count + sum(x.shape[0] for x in first)),
+        out_shape=tile_shape(count[0] + sum(x.shape[0] for x in first)),
         compiler_params=params,
         name="close",
     )(keep[0], got[0], *first)
     for bit in range(far_bits):
-        pairs = [(i, i ^ (1 << bit)) for i in range(sizes["far"])]
-        got = [lax.ppermute(x, "far", pairs) for x in total]
-        more = riders[1:] if bit == far_bits - 1 else []
-        kernel = functools.partial(meet_kernel, (("far", bit),) * 2, sizes, rows, count)
-        shape = tile_shape(total[0].shape[0] + sum(x.shape[0] for x in more))
-        carried = call("meet", kernel, shape, me, total[0], got[0], *more)
+        choice = (("far", bit),) * 2
+        total[0], _ = lax.optimization_barrier((total[0], total[1]))
+        got = [lax.ppermute(x, SPLIT, bit_pairs(sizes, choice, c)) for x, c in zip(total, cores)]
+        late = riders[1:] if bit == far_bits - 1 else []
+        kernel = functools.partial(meet_kernel, choice, sizes, rows, count[0])
+        shape = tile_shape(total[0].shape[0] + sum(x.shape[0] for x in late))
+        carried = call("meet", kernel, shape, me, total[0], got[0], *late)
         total = [(x.astype(F32) + y.astype(F32)).astype(BF16) for x, y in zip(total, got)]
         total[0] = carried
     for phase in reversed(range(phases)):
-        pairs = bit_pairs(sizes, orders, phase)
-        got = [lax.ppermute(x, SPLIT, pairs) for x in total]
-        for i in range(CHUNKS):
+        choice = choices[phase]
+        total[0], _ = lax.optimization_barrier((total[0], total[1]))
+        got = [lax.ppermute(x, SPLIT, bit_pairs(sizes, choice, c)) for x, c in zip(total, cores)]
+        for i in range(2):
             last = i == 0 and phase == 0
-            kernel = functools.partial(join_kernel, choices[phase], sizes, rows, count, last)
+            kernel = functools.partial(join_kernel, choice, sizes, rows, count[i], last)
             if last:
-                shape = (tile_shape(2 * count + rows), jax.ShapeDtypeStruct((channels, RIM), F32))
+                shape = (tile_shape(2 * count[0] + rows), jax.ShapeDtypeStruct((channels, RIM), F32))
                 total[0], side = call("join", kernel, shape, me, total[0], got[0], stay)
             else:
-                shape = tile_shape(total[i].shape[0] + count)
+                shape = tile_shape(total[i].shape[0] + count[i])
                 total[i] = call("join", kernel, shape, me, total[i], got[i])
-        count *= 2
-    other = [lax.ppermute(x, "core", swap) for x in total]
+            count[i] *= 2
+    total[0], _ = lax.optimization_barrier((total[0], total[1]))
+    other = [lax.ppermute(x, "core", p) for x, p in zip(total, (swap, swap[1:]))]
     conv_wgrad_t, down_wgrad, grad_input_t = pl.pallas_call(
-        functools.partial(final_kernel, taps, CHUNKS, size),
+        functools.partial(final_kernel, taps, shared),
         out_shape=(
             jax.ShapeDtypeStruct((channels, conv_columns), F32),
             jax.ShapeDtypeStruct((taps * channels, LANES), F32),
             jax.ShapeDtypeStruct((channels, voxels), F32),
         ),
-        in_specs=[smem] + [vmem] * (2 * CHUNKS + 2),
+        in_specs=[smem] + [vmem] * 6,
         compiler_params=params,
         name="final",
     )(core, *total, *other, base, side)

time: 54.2 us -> 62.3 us (1.15)
  starting transfers between devices: 20.5 us -> 33.3 us
  waiting for transfers between devices: 21.8 us -> 15.9 us
  Pallas kernels: 9 us -> 9.78 us
    ppermute x9 -> x17, starting transfers between devices: 16.4 us -> 29.6 us  [the longest x8 10.7 us: on_device(): lax.ppermute(x, SPLIT, bit_pairs(sizes, choice, c))]
    ppermute x9 -> x17, waiting for transfers between devices: 21.7 us -> 15.8 us  [the longest x8 11.5 us: on_device(): lax.ppermute(x, SPLIT, bit_pairs(sizes, choice, c))]
    unnamed x16 -> x18, local copies, waits for them, and re-layouts: 0.99 us -> 1.82 us
    slice x1, local copies, waits for them, and re-layouts: 0.8 us -> 0.01 us  [on_device(): rim = features_t[:, :RIM]]
    pallas_call x1, Pallas kernels: 2.22 us -> 2.91 us  [on_device(): pl.pallas_call(functools.partial(forward_kernel, slabs), out_shape=[jax.S...]
  transfers between devices with their start and end apart: 11 -> 19, of which waited for: 9 -> 8; matrix products, arithmetic and copies ran while one was open for 0% -> 0% of each run, Pallas kernels for 10% -> 9%
where the time goes in v7:
time: 62.3 us; the launch traced here: 61.9 us
  starting transfers between devices  33.3 us (53%)
  waiting for transfers between devices  15.9 us (26%)
  Pallas kernels  9.78 us (16%)
  local copies, waits for them, and re-layouts  1.83 us (3%)
  between operations  0.94 us (2%)
    ppermute x8, waiting for transfers between devices, on_device(): lax.ppermute(x, SPLIT, bit_pairs(sizes, choice, c))  11.5 us
    ppermute x8, starting transfers between devices, on_device(): lax.ppermute(x, SPLIT, bit_pairs(sizes, choice, c))  10.7 us
    ppermute x2, starting transfers between devices, on_device(): lax.ppermute(x, 'core', p)  8.62 us
    ppermute x4, starting transfers between devices, on_device(): lax.ppermute(send[i], SPLIT, bit_pairs(sizes, choices[phase], cores[i]))  4.78 us
    ppermute x1, starting transfers between devices, on_device(): mate = lax.ppermute(row, RING, mates)  3.07 us
    ppermute x1, starting transfers between devices, on_device(): side = [lax.ppermute(features_t, 'slab', pairs) for pairs in beside]  3.03 us
    pallas_call x1, Pallas kernels, on_device(): pl.pallas_call(functools.partial(forward_kernel, slabs), out_shape=[jax.S...  2.91 us
    ppermute x2, starting transfers between devices, on_device(): got = [lax.ppermute(x, 'core', p) for x, p in zip(send, (swap, swap[:1]))]  2.45 us
  transfers between devices with their start and end apart: 19, of which 8 were waited for; matrix products, arithmetic and copies ran while one was open for 0% of the time, Pallas kernels for 9%

profile of v7, /device:TPU:0, one launch (start us, length us, event | category | flops | bytes accessed | tf_op | source)
XLA Modules:
  0.0 61.9 jit_solution(5195199621537648801)
XLA Ops:
  0.6 3.0 %collective-permute-start = (bf16[96,256]{1,0:T(8,128)(2,1)}, bf16[96,256]{1,0:T(8,128)(2,1)S(1)}, u32[]{:S(2)}, u32[]{:S(2)}) collective-permute-start(bf16[96,256]{1,0:T(8,128)(2,1)} %bitcast.10), channel_id=1, source_target_pairs={{0,1},{1,0},{2,3},{3,2},{4,5},{5,4},{6,7},{7,6},{8,9},{9,8},{10,11... | collective-permute-start | bytes 147464 | tf_op jit(solution)/shard_map/ppermute | solution.py:392
  3.7 0.8 %copy-done.1 = bf16[256,96]{0,1:T(8,128)(2,1)S(1)} copy-done((bf16[256,96]{0,1:T(8,128)(2,1)S(1)}, bf16[256,96]{0,1:T(8,128)(2,1)}, u32[]{:S(2)}) %copy-start.1) | copy-done | bytes 49176
  4.5 0.8 %copy-done.3 = s32[256,27]{0,1:T(8,128)S(1)} copy-done((s32[256,27]{0,1:T(8,128)S(1)}, s32[256,27]{0,1:T(8,128)}, u32[]{:S(2)}) %copy-start.3) | copy-done | bytes 27672
  5.3 1.0 %gather.1 = (bf16[2592,128]{1,0:T(8,128)(2,1)S(1)}, bf16[2592,128]{1,0:T(8,128)(2,1)S(1)}) custom-call(bf16[96,256]{1,0:T(8,128)(2,1)S(1)} %bitcast.11, s32[27,256]{1,0:T(8,128)S(1)} %bitcast.14), custom_call_target="tpu_custom_call" | custom-call | flops 2000000000 | bytes 10000000 | tf_op jit(solution)/shard_map/gather/pallas_call | solution.py:393
  6.3 0.0 collective-permute-done
  6.3 0.0 copy-start.5
  6.3 0.0 copy-start.8
  6.3 0.1 pad_maximum_fusion
  6.4 0.7 %collective-permute-start.2 = (bf16[96,128]{1,0:T(8,128)(2,1)S(1)}, bf16[96,128]{1,0:T(8,128)(2,1)S(1)}, u32[]{:S(2)}, u32[]{:S(2)}) collective-permute-start(bf16[96,128]{1,0:T(8,128)(2,1)S(1)} %pad_maximum_fusion), channel_id=1, source_target_pairs={{2,4},{6,8},{10,12},{14,16},{18,20},{22,24},{26,28},{4,2},{8,6},{1... | collective-permute-start | bytes 73736 | tf_op jit(solution)/shard_map/ppermute | solution.py:407
  7.0 3.1 %collective-permute-start.1 = (bf16[96,128]{1,0:T(8,128)(2,1)S(1)}, bf16[96,128]{1,0:T(8,128)(2,1)S(1)}, u32[]{:S(2)}, u32[]{:S(2)}) collective-permute-start(bf16[96,128]{1,0:T(8,128)(2,1)S(1)} %pad_maximum_fusion), channel_id=1, source_target_pairs={{0,2},{2,0},{4,6},{6,4},{8,10},{10,8},{12,14},{14,12},{16,18},{18,... | collective-permute-start | bytes 73736 | tf_op jit(solution)/shard_map/ppermute | solution.py:408
  10.1 0.0 copy-start.2
  10.1 0.0 copy-start.4
  10.2 0.7 %taps.1 = (bf16[8,64,256]{2,1,0:T(8,128)(2,1)S(1)}, f32[96,256]{1,0:T(8,128)S(1)}) custom-call(s32[8,64]{1,0:T(8,128)S(1)} %bitcast.17, bf16[64,128]{1,0:T(8,128)(2,1)S(1)} %copy-done.5, bf16[768,128]{1,0:T(8,128)(2,1)S(1)} %copy-done.6), custom_call_target="tpu_custom_call" | custom-call | flops 2000000000 | bytes 10000000 | tf_op jit(solution)/shard_map/taps/pallas_call | solution.py:410
  10.9 0.1 collective-permute-done.1.refs_4_
  11.0 0.2 copy-done
  11.2 2.9 %forward.1 = (bf16[96,256]{1,0:T(8,128)(2,1)S(1)}, bf16[96,256]{1,0:T(8,128)(2,1)S(1)}, f32[64,16,128]{2,1,0:T(8,128)S(1)}, bf16[64,16,128]{2,1,0:T(8,128)(2,1)S...) custom-call(s32[1]{0:T(128)} %bitcast.3.core_ref, bf16[96,256]{1,0:T(8,128)(2,1)S(1)} %bitcast.13, ...), custom_call_target="tpu_custom_call" | custom-call | tf_op jit(solution)/shard_map/forward/pallas_call | solution.py:426
  14.1 2.4 %collective-permute-start.4 = (bf16[48,16,128]{2,1,0:T(8,128)(2,1)}, bf16[48,16,128]{2,1,0:T(8,128)(2,1)S(1)}, u32[]{:S(2)}, u32[]{:S(2)}) collective-permute-start(bf16[48,16,128]{2,1,0:T(8,128)(2,1)} %get-tuple-element.63), channel_id=1, source_target_pairs={{0,2},{1,3},{4,6},{5,7},{8,10},{9,11},{12,14},{13,15},{16,18},{17,... | collective-permute-start | bytes 589832 | tf_op jit(solution)/shard_map/ppermute | solution.py:468
  16.5 0.1 collective-permute-start.3
  16.6 1.2 %collective-permute-done.4.got_ref = bf16[48,16,128]{2,1,0:T(8,128)(2,1)S(1)} collective-permute-done((bf16[48,16,128]{2,1,0:T(8,128)(2,1)}, bf16[48,16,128]{2,1,0:T(8,128)(2,1)S(1)}, u32[]{:S(2)}, u32[]{:S(2)}) %collective-permute-start.4) | collective-permute-done | bytes 196640 | tf_op jit(solution)/shard_map/ppermute | solution.py:468
  17.8 0.7 %collective-permute-start.6 = (bf16[24,16,128]{2,1,0:T(8,128)(2,1)S(1)}, bf16[24,16,128]{2,1,0:T(8,128)(2,1)S(1)}, u32[]{:S(2)}, u32[]{:S(2)}) collective-permute-start(bf16[24,16,128]{2,1,0:T(8,128)(2,1)S(1)} %get-tuple-element.64), channel_id=1, source_target_pairs={{2,3},{3,2},{6,7},{7,6},{10,11},{11,10},{14,15},{15,14},{18,19},{1... | collective-permute-start | bytes 294920 | tf_op jit(solution)/shard_map/ppermute | solution.py:476
  18.5 0.1 fold.4
  18.5 2.0 %collective-permute-start.5 = (bf16[32,16,128]{2,1,0:T(8,128)(2,1)S(1)}, bf16[32,16,128]{2,1,0:T(8,128)(2,1)S(1)}, u32[]{:S(2)}, u32[]{:S(2)}) collective-permute-start(bf16[32,16,128]{2,1,0:T(8,128)(2,1)S(1)} %get-tuple-element.67), channel_id=1, source_target_pairs={{0,4},{1,5},{2,3},{3,2},{4,0},{5,1},{6,7},{7,6},{8,12},{9,13},{10,... | collective-permute-start | bytes 393224 | tf_op jit(solution)/shard_map/ppermute | solution.py:476
  20.5 0.0 collective-permute-done.6.got_ref
  20.5 0.7 %collective-permute-start.8 = (bf16[12,16,128]{2,1,0:T(8,128)(2,1)S(1)}, bf16[12,16,128]{2,1,0:T(8,128)(2,1)S(1)}, u32[]{:S(2)}, u32[]{:S(2)}) collective-permute-start(bf16[12,16,128]{2,1,0:T(8,128)(2,1)S(1)} %get-tuple-element.77), channel_id=1, source_target_pairs={{2,6},{3,7},{6,2},{7,3},{10,14},{11,15},{14,10},{15,11},{18,22},{1... | collective-permute-start | bytes 147464 | tf_op jit(solution)/shard_map/ppermute | solution.py:476
  21.2 2.4 %backward.1 = (f32[96,256]{1,0:T(8,128)S(1)}, f32[96,64]{1,0:T(8,128)S(1)}, bf16[6,16,128]{2,1,0:T(8,128)(2,1)S(1)}, bf16[6,16,128]{2,1,0:T(8,128)(2,1)S(1)}) custom-call(s32[1]{0:T(128)} %bitcast.3.core_ref, s32[27,256]{1,0:T(8,128)S(1)} %bitcast.16, f32[96,256]{1,0:T(8,128)S(1)} %get-tuple-element.56.refs_3_.hgrad_ref, ...), custom_call_target="tpu_custom_call" | custom-call | flops 2000000000 | bytes 10000000 | tf_op jit(solution)/shard_map/backward/pallas_call | solution.py:479
  23.7 1.5 %collective-permute-start.7 = (bf16[16,16,128]{2,1,0:T(8,128)(2,1)S(1)}, bf16[16,16,128]{2,1,0:T(8,128)(2,1)S(1)}, u32[]{:S(2)}, u32[]{:S(2)}) collective-permute-start(bf16[16,16,128]{2,1,0:T(8,128)(2,1)S(1)} %get-tuple-element.78), channel_id=1, source_target_pairs={{0,1},{1,0},{2,6},{3,7},{4,5},{5,4},{6,2},{7,3},{8,9},{9,8},{10,14... | collective-permute-start | bytes 196616 | tf_op jit(solution)/shard_map/ppermute | solution.py:476
  25.2 0.0 collective-permute-done.8
  25.2 0.7 %collective-permute-start.10 = (bf16[12,16,128]{2,1,0:T(8,128)(2,1)S(1)}, bf16[12,16,128]{2,1,0:T(8,128)(2,1)S(1)}, u32[]{:S(2)}, u32[]{:S(2)}) collective-permute-start(bf16[12,16,128]{2,1,0:T(8,128)(2,1)S(1)} %add_convert_fusion.2), channel_id=1, source_target_pairs={{2,10},{3,11},{6,14},{7,15},{10,2},{11,3},{14,6},{15,7},{18,26},{1... | collective-permute-start | bytes 147464 | tf_op jit(solution)/shard_map/ppermute | solution.py:522
  25.9 2.2 %collective-permute-done.7.got_ref = bf16[16,16,128]{2,1,0:T(8,128)(2,1)S(1)} collective-permute-done((bf16[16,16,128]{2,1,0:T(8,128)(2,1)S(1)}, bf16[16,16,128]{2,1,0:T(8,128)(2,1)S(1)}, u32[]{:S(2)}, u32[]{:S(2)}) %collective-permute-start.7) | collective-permute-done | bytes 65568 | tf_op jit(solution)/shard_map/ppermute | solution.py:476
  28.1 1.9 %collective-permute-start.9 = (bf16[22,16,128]{2,1,0:T(8,128)(2,1)S(1)}, bf16[22,16,128]{2,1,0:T(8,128)(2,1)S(1)}, u32[]{:S(2)}, u32[]{:S(2)}) collective-permute-start(bf16[22,16,128]{2,1,0:T(8,128)(2,1)S(1)} %close.1.own_ref), channel_id=1, source_target_pairs={{0,8},{1,9},{2,10},{3,11},{4,12},{5,13},{6,14},{7,15},{8,0},{9,1},... | collective-permute-start | bytes 270344 | tf_op jit(solution)/shard_map/ppermute | solution.py:522
  29.9 0.0 collective-permute-done.10
  30.0 0.7 %collective-permute-start.12 = (bf16[12,16,128]{2,1,0:T(8,128)(2,1)S(1)}, bf16[12,16,128]{2,1,0:T(8,128)(2,1)S(1)}, u32[]{:S(2)}, u32[]{:S(2)}) collective-permute-start(bf16[12,16,128]{2,1,0:T(8,128)(2,1)S(1)} %add_convert_fusion.1), channel_id=1, source_target_pairs={{2,18},{3,19},{6,22},{7,23},{10,26},{11,27},{14,30},{15,31},{18,2}... | collective-permute-start | bytes 147464 | tf_op jit(solution)/shard_map/ppermute | solution.py:522
  30.6 2.0 %collective-permute-done.9.got_ref = bf16[22,16,128]{2,1,0:T(8,128)(2,1)S(1)} collective-permute-done((bf16[22,16,128]{2,1,0:T(8,128)(2,1)S(1)}, bf16[22,16,128]{2,1,0:T(8,128)(2,1)S(1)}, u32[]{:S(2)}, u32[]{:S(2)}) %collective-permute-start.9) | collective-permute-done | bytes 90144 | tf_op jit(solution)/shard_map/ppermute | solution.py:522
  32.7 2.9 %collective-permute-start.11 = (bf16[22,16,128]{2,1,0:T(8,128)(2,1)S(1)}, bf16[22,16,128]{2,1,0:T(8,128)(2,1)S(1)}, u32[]{:S(2)}, u32[]{:S(2)}) collective-permute-start(bf16[22,16,128]{2,1,0:T(8,128)(2,1)S(1)} %meet.2.own_ref), channel_id=1, source_target_pairs={{0,16},{1,17},{2,18},{3,19},{4,20},{5,21},{6,22},{7,23},{8,24},{9,... | collective-permute-start | bytes 270344 | tf_op jit(solution)/shard_map/ppermute | solution.py:522
  35.6 2.6 %collective-permute-done.11.got_ref = bf16[22,16,128]{2,1,0:T(8,128)(2,1)S(1)} collective-permute-done((bf16[22,16,128]{2,1,0:T(8,128)(2,1)S(1)}, bf16[22,16,128]{2,1,0:T(8,128)(2,1)S(1)}, u32[]{:S(2)}, u32[]{:S(2)}) %collective-permute-start.11) | collective-permute-done | bytes 90144 | tf_op jit(solution)/shard_map/ppermute | solution.py:522
  38.2 1.5 %collective-permute-start.13 = (bf16[28,16,128]{2,1,0:T(8,128)(2,1)S(1)}, bf16[28,16,128]{2,1,0:T(8,128)(2,1)S(1)}, u32[]{:S(2)}, u32[]{:S(2)}) collective-permute-start(bf16[28,16,128]{2,1,0:T(8,128)(2,1)S(1)} %meet.3.own_ref), channel_id=1, source_target_pairs={{0,1},{1,0},{2,6},{3,7},{4,5},{5,4},{6,2},{7,3},{8,9},{9,8},{10,14... | collective-permute-start | bytes 344072 | tf_op jit(solution)/shard_map/ppermute | solution.py:532
  39.7 0.7 %collective-permute-start.14 = (bf16[12,16,128]{2,1,0:T(8,128)(2,1)S(1)}, bf16[12,16,128]{2,1,0:T(8,128)(2,1)S(1)}, u32[]{:S(2)}, u32[]{:S(2)}) collective-permute-start(bf16[12,16,128]{2,1,0:T(8,128)(2,1)S(1)} %add_convert_fusion.own_ref), channel_id=1, source_target_pairs={{2,6},{3,7},{6,2},{7,3},{10,14},{11,15},{14,10},{15,11},{18,22},{1... | collective-permute-start | bytes 147464 | tf_op jit(solution)/shard_map/ppermute | solution.py:532
  40.4 2.7 %collective-permute-done.13.got_ref = bf16[28,16,128]{2,1,0:T(8,128)(2,1)S(1)} collective-permute-done((bf16[28,16,128]{2,1,0:T(8,128)(2,1)S(1)}, bf16[28,16,128]{2,1,0:T(8,128)(2,1)S(1)}, u32[]{:S(2)}, u32[]{:S(2)}) %collective-permute-start.13) | collective-permute-done | bytes 114720 | tf_op jit(solution)/shard_map/ppermute | solution.py:532
  43.1 1.9 %collective-permute-start.15 = (bf16[44,16,128]{2,1,0:T(8,128)(2,1)S(1)}, bf16[44,16,128]{2,1,0:T(8,128)(2,1)S(1)}, u32[]{:S(2)}, u32[]{:S(2)}) collective-permute-start(bf16[44,16,128]{2,1,0:T(8,128)(2,1)S(1)} %join.4.own_ref), channel_id=1, source_target_pairs={{0,4},{1,5},{2,3},{3,2},{4,0},{5,1},{6,7},{7,6},{8,12},{9,13},{10,... | collective-permute-start | bytes 540680 | tf_op jit(solution)/shard_map/ppermute | solution.py:532
  45.0 0.7 %collective-permute-start.16 = (bf16[24,16,128]{2,1,0:T(8,128)(2,1)S(1)}, bf16[24,16,128]{2,1,0:T(8,128)(2,1)S(1)}, u32[]{:S(2)}, u32[]{:S(2)}) collective-permute-start(bf16[24,16,128]{2,1,0:T(8,128)(2,1)S(1)} %join.5.own_ref), channel_id=1, source_target_pairs={{2,3},{3,2},{6,7},{7,6},{10,11},{11,10},{14,15},{15,14},{18,19},{1... | collective-permute-start | bytes 294920 | tf_op jit(solution)/shard_map/ppermute | solution.py:532
  45.7 0.0 copy-start.7
  45.7 4.2 %collective-permute-done.15.got_ref = bf16[44,16,128]{2,1,0:T(8,128)(2,1)S(1)} collective-permute-done((bf16[44,16,128]{2,1,0:T(8,128)(2,1)S(1)}, bf16[44,16,128]{2,1,0:T(8,128)(2,1)S(1)}, u32[]{:S(2)}, u32[]{:S(2)}) %collective-permute-start.15) | collective-permute-done | bytes 180256 | tf_op jit(solution)/shard_map/ppermute | solution.py:532
  49.9 0.1 join.6
  50.0 7.3 %collective-permute-start.17 = (bf16[70,16,128]{2,1,0:T(8,128)(2,1)S(1)}, bf16[70,16,128]{2,1,0:T(8,128)(2,1)S(1)}, u32[]{:S(2)}, u32[]{:S(2)}) collective-permute-start(bf16[70,16,128]{2,1,0:T(8,128)(2,1)S(1)} %get-tuple-element.88.refs_0_), channel_id=1, source_target_pairs={{0,2},{2,0},{1,3},{3,1},{4,6},{6,4},{5,7},{7,5},{8,10},{10,8},{9,1... | collective-permute-start | bytes 860168 | tf_op jit(solution)/shard_map/ppermute | solution.py:544
  57.3 1.3 %collective-permute-start.18 = (bf16[48,16,128]{2,1,0:T(8,128)(2,1)S(1)}, bf16[48,16,128]{2,1,0:T(8,128)(2,1)S(1)}, u32[]{:S(2)}, u32[]{:S(2)}) collective-permute-start(bf16[48,16,128]{2,1,0:T(8,128)(2,1)S(1)} %join.7.refs_1_), channel_id=1, source_target_pairs={{2,0},{3,1},{6,4},{7,5},{10,8},{11,9},{14,12},{15,13},{18,16},{19,... | collective-permute-start | bytes 589832 | tf_op jit(solution)/shard_map/ppermute | solution.py:544
  58.6 1.1 %coarse.1 = bf16[64,128]{1,0:T(8,128)(2,1)} custom-call(bf16[8,64,256]{2,1,0:T(8,128)(2,1)S(1)} %get-tuple-element.53.refs_2_.pick_ref, bf16[96,256]{1,0:T(8,128)(2,1)S(1)} %get-tuple-element.57.hidden_ref, bf16[768,128]{1,0:T(8,128)(2,1)S(1)} %copy-done.7), custom_call_target="tpu_custom_call" | custom-call | flops 2000000000 | bytes 10000000 | tf_op jit(solution)/shard_map/coarse/pallas_call | solution.py:501
  59.7 0.9 %collective-permute-done.18.refs_3_ = bf16[48,16,128]{2,1,0:T(8,128)(2,1)S(1)} collective-permute-done((bf16[48,16,128]{2,1,0:T(8,128)(2,1)S(1)}, bf16[48,16,128]{2,1,0:T(8,128)(2,1)S(1)}, u32[]{:S(2)}, u32[]{:S(2)}) %collective-permute-start.18) | collective-permute-done | bytes 196640 | tf_op jit(solution)/shard_map/ppermute | solution.py:544
  60.6 1.2 %final.1 = (f32[96,2592]{1,0:T(8,128)}, f32[768,128]{1,0:T(8,128)}, f32[96,256]{1,0:T(8,128)}) custom-call(s32[1]{0:T(128)} %bitcast.3.core_ref, bf16[70,16,128]{2,1,0:T(8,128)(2,1)S(1)} %get-tuple-element.88.refs_0_, bf16[48,16,128]{2,1,0:T(8,128)(2,1)S(1)} %join.7.refs_1_, bf16[70,16,128]{2,1,0:T(8,128)(2,1)S(1)} %collective-permute-done.17.refs_2_, ...), custom_call_target="tpu_custom_call" | custom-call | tf_op jit(solution)/shard_map/final/pallas_call | solution.py:545
  (31 shorter events, 0.3 us)
Async XLA Ops:
  0.6 5.6 %collective-permute-start = (bf16[96,256]{1,0:T(8,128)(2,1)}, bf16[96,256]{1,0:T(8,128)(2,1)S(1)}, u32[]{:S(2)}, u32[]{:S(2)}) collective-permute-start(bf16[96,256]{1,0:T(8,128)(2,1)} %bitcast.10), channel_id=1, source_target_pairs={{0,1},{1,0},{2,3},{3,2},{4,5},{5,4},{6,7},{7,6},{8,9},{9,8},{10,11... | collective-permute-start | bytes 147464 | tf_op jit(solution)/shard_map/ppermute | solution.py:392
  3.7 0.8 %copy-start.1 = (bf16[256,96]{0,1:T(8,128)(2,1)S(1)}, bf16[256,96]{0,1:T(8,128)(2,1)}, u32[]{:S(2)}) copy-start(bf16[256,96]{0,1:T(8,128)(2,1)} %param.6) | copy-start | bytes 147460
  4.5 0.8 %copy-start.3 = (s32[256,27]{0,1:T(8,128)S(1)}, s32[256,27]{0,1:T(8,128)}, u32[]{:S(2)}) copy-start(s32[256,27]{0,1:T(8,128)} %param.7) | copy-start | bytes 82948
  5.3 4.9 %copy-start.6 = (bf16[768,128]{1,0:T(8,128)(2,1)S(1)}, bf16[768,128]{1,0:T(8,128)(2,1)}, u32[]{:S(2)}) copy-start(bf16[768,128]{1,0:T(8,128)(2,1)} %wd_ref.3) | copy-start | bytes 589828
  6.3 3.8 %copy-start.5 = (bf16[64,128]{1,0:T(8,128)(2,1)S(1)}, bf16[64,128]{1,0:T(8,128)(2,1)}, u32[]{:S(2)}) copy-start(bf16[64,128]{1,0:T(8,128)(2,1)} %cgrad_ref.3) | copy-start | bytes 49156
  6.3 3.8 %copy-start.8 = (s32[64,8]{0,1:T(8,128)S(1)}, s32[64,8]{0,1:T(8,128)}, u32[]{:S(2)}) copy-start(s32[64,8]{0,1:T(8,128)} %param.8) | copy-start | bytes 6148
  6.4 4.5 %collective-permute-start.2 = (bf16[96,128]{1,0:T(8,128)(2,1)S(1)}, bf16[96,128]{1,0:T(8,128)(2,1)S(1)}, u32[]{:S(2)}, u32[]{:S(2)}) collective-permute-start(bf16[96,128]{1,0:T(8,128)(2,1)S(1)} %pad_maximum_fusion), channel_id=1, source_target_pairs={{2,4},{6,8},{10,12},{14,16},{18,20},{22,24},{26,28},{4,2},{8,6},{1... | collective-permute-start | bytes 73736 | tf_op jit(solution)/shard_map/ppermute | solution.py:407
  7.0 3.9 %collective-permute-start.1 = (bf16[96,128]{1,0:T(8,128)(2,1)S(1)}, bf16[96,128]{1,0:T(8,128)(2,1)S(1)}, u32[]{:S(2)}, u32[]{:S(2)}) collective-permute-start(bf16[96,128]{1,0:T(8,128)(2,1)S(1)} %pad_maximum_fusion), channel_id=1, source_target_pairs={{0,2},{2,0},{4,6},{6,4},{8,10},{10,8},{12,14},{14,12},{16,18},{18,... | collective-permute-start | bytes 73736 | tf_op jit(solution)/shard_map/ppermute | solution.py:408
  10.1 1.0 %copy-start = (bf16[2592,96]{0,1:T(8,128)(2,1)S(1)}, bf16[2592,96]{0,1:T(8,128)(2,1)}, u32[]{:S(2)}) copy-start(bf16[2592,96]{0,1:T(8,128)(2,1)} %param.9) | copy-start | bytes 1492996
  10.1 1.0 %copy-start.2 = (bf16[256,96]{0,1:T(8,128)(2,1)S(1)}, bf16[256,96]{0,1:T(8,128)(2,1)}, u32[]{:S(2)}) copy-start(bf16[256,96]{0,1:T(8,128)(2,1)} %param.6) | copy-start | bytes 147460
  10.1 1.0 %copy-start.4 = (s32[256,27]{0,1:T(8,128)S(1)}, s32[256,27]{0,1:T(8,128)}, u32[]{:S(2)}) copy-start(s32[256,27]{0,1:T(8,128)} %param.7) | copy-start | bytes 82948
  14.1 3.6 %collective-permute-start.4 = (bf16[48,16,128]{2,1,0:T(8,128)(2,1)}, bf16[48,16,128]{2,1,0:T(8,128)(2,1)S(1)}, u32[]{:S(2)}, u32[]{:S(2)}) collective-permute-start(bf16[48,16,128]{2,1,0:T(8,128)(2,1)} %get-tuple-element.63), channel_id=1, source_target_pairs={{0,2},{1,3},{4,6},{5,7},{8,10},{9,11},{12,14},{13,15},{16,18},{17,... | collective-permute-start | bytes 589832 | tf_op jit(solution)/shard_map/ppermute | solution.py:468
  16.5 2.0 %collective-permute-start.3 = (bf16[64,16,128]{2,1,0:T(8,128)(2,1)S(1)}, bf16[64,16,128]{2,1,0:T(8,128)(2,1)S(1)}, u32[]{:S(2)}, u32[]{:S(2)}) collective-permute-start(bf16[64,16,128]{2,1,0:T(8,128)(2,1)S(1)} %get-tuple-element.59), channel_id=1, source_target_pairs={{0,2},{2,0},{1,3},{3,1},{4,6},{6,4},{5,7},{7,5},{8,10},{10,8},{9,1... | collective-permute-start | bytes 786440 | tf_op jit(solution)/shard_map/ppermute | solution.py:468
  17.8 2.7 %collective-permute-start.6 = (bf16[24,16,128]{2,1,0:T(8,128)(2,1)S(1)}, bf16[24,16,128]{2,1,0:T(8,128)(2,1)S(1)}, u32[]{:S(2)}, u32[]{:S(2)}) collective-permute-start(bf16[24,16,128]{2,1,0:T(8,128)(2,1)S(1)} %get-tuple-element.64), channel_id=1, source_target_pairs={{2,3},{3,2},{6,7},{7,6},{10,11},{11,10},{14,15},{15,14},{18,19},{1... | collective-permute-start | bytes 294920 | tf_op jit(solution)/shard_map/ppermute | solution.py:476
  18.5 5.1 %collective-permute-start.5 = (bf16[32,16,128]{2,1,0:T(8,128)(2,1)S(1)}, bf16[32,16,128]{2,1,0:T(8,128)(2,1)S(1)}, u32[]{:S(2)}, u32[]{:S(2)}) collective-permute-start(bf16[32,16,128]{2,1,0:T(8,128)(2,1)S(1)} %get-tuple-element.67), channel_id=1, source_target_pairs={{0,4},{1,5},{2,3},{3,2},{4,0},{5,1},{6,7},{7,6},{8,12},{9,13},{10,... | collective-permute-start | bytes 393224 | tf_op jit(solution)/shard_map/ppermute | solution.py:476
  20.5 4.6 %collective-permute-start.8 = (bf16[12,16,128]{2,1,0:T(8,128)(2,1)S(1)}, bf16[12,16,128]{2,1,0:T(8,128)(2,1)S(1)}, u32[]{:S(2)}, u32[]{:S(2)}) collective-permute-start(bf16[12,16,128]{2,1,0:T(8,128)(2,1)S(1)} %get-tuple-element.77), channel_id=1, source_target_pairs={{2,6},{3,7},{6,2},{7,3},{10,14},{11,15},{14,10},{15,11},{18,22},{1... | collective-permute-start | bytes 147464 | tf_op jit(solution)/shard_map/ppermute | solution.py:476
  23.7 4.3 %collective-permute-start.7 = (bf16[16,16,128]{2,1,0:T(8,128)(2,1)S(1)}, bf16[16,16,128]{2,1,0:T(8,128)(2,1)S(1)}, u32[]{:S(2)}, u32[]{:S(2)}) collective-permute-start(bf16[16,16,128]{2,1,0:T(8,128)(2,1)S(1)} %get-tuple-element.78), channel_id=1, source_target_pairs={{0,1},{1,0},{2,6},{3,7},{4,5},{5,4},{6,2},{7,3},{8,9},{9,8},{10,14... | collective-permute-start | bytes 196616 | tf_op jit(solution)/shard_map/ppermute | solution.py:476
  25.2 4.7 %collective-permute-start.10 = (bf16[12,16,128]{2,1,0:T(8,128)(2,1)S(1)}, bf16[12,16,128]{2,1,0:T(8,128)(2,1)S(1)}, u32[]{:S(2)}, u32[]{:S(2)}) collective-permute-start(bf16[12,16,128]{2,1,0:T(8,128)(2,1)S(1)} %add_convert_fusion.2), channel_id=1, source_target_pairs={{2,10},{3,11},{6,14},{7,15},{10,2},{11,3},{14,6},{15,7},{18,26},{1... | collective-permute-start | bytes 147464 | tf_op jit(solution)/shard_map/ppermute | solution.py:522
  28.1 4.6 %collective-permute-start.9 = (bf16[22,16,128]{2,1,0:T(8,128)(2,1)S(1)}, bf16[22,16,128]{2,1,0:T(8,128)(2,1)S(1)}, u32[]{:S(2)}, u32[]{:S(2)}) collective-permute-start(bf16[22,16,128]{2,1,0:T(8,128)(2,1)S(1)} %close.1.own_ref), channel_id=1, source_target_pairs={{0,8},{1,9},{2,10},{3,11},{4,12},{5,13},{6,14},{7,15},{8,0},{9,1},... | collective-permute-start | bytes 270344 | tf_op jit(solution)/shard_map/ppermute | solution.py:522
  30.0 5.6 %collective-permute-start.12 = (bf16[12,16,128]{2,1,0:T(8,128)(2,1)S(1)}, bf16[12,16,128]{2,1,0:T(8,128)(2,1)S(1)}, u32[]{:S(2)}, u32[]{:S(2)}) collective-permute-start(bf16[12,16,128]{2,1,0:T(8,128)(2,1)S(1)} %add_convert_fusion.1), channel_id=1, source_target_pairs={{2,18},{3,19},{6,22},{7,23},{10,26},{11,27},{14,30},{15,31},{18,2}... | collective-permute-start | bytes 147464 | tf_op jit(solution)/shard_map/ppermute | solution.py:522
  32.7 5.5 %collective-permute-start.11 = (bf16[22,16,128]{2,1,0:T(8,128)(2,1)S(1)}, bf16[22,16,128]{2,1,0:T(8,128)(2,1)S(1)}, u32[]{:S(2)}, u32[]{:S(2)}) collective-permute-start(bf16[22,16,128]{2,1,0:T(8,128)(2,1)S(1)} %meet.2.own_ref), channel_id=1, source_target_pairs={{0,16},{1,17},{2,18},{3,19},{4,20},{5,21},{6,22},{7,23},{8,24},{9,... | collective-permute-start | bytes 270344 | tf_op jit(solution)/shard_map/ppermute | solution.py:522
  38.2 4.9 %collective-permute-start.13 = (bf16[28,16,128]{2,1,0:T(8,128)(2,1)S(1)}, bf16[28,16,128]{2,1,0:T(8,128)(2,1)S(1)}, u32[]{:S(2)}, u32[]{:S(2)}) collective-permute-start(bf16[28,16,128]{2,1,0:T(8,128)(2,1)S(1)} %meet.3.own_ref), channel_id=1, source_target_pairs={{0,1},{1,0},{2,6},{3,7},{4,5},{5,4},{6,2},{7,3},{8,9},{9,8},{10,14... | collective-permute-start | bytes 344072 | tf_op jit(solution)/shard_map/ppermute | solution.py:532
  39.7 0.7 %collective-permute-start.14 = (bf16[12,16,128]{2,1,0:T(8,128)(2,1)S(1)}, bf16[12,16,128]{2,1,0:T(8,128)(2,1)S(1)}, u32[]{:S(2)}, u32[]{:S(2)}) collective-permute-start(bf16[12,16,128]{2,1,0:T(8,128)(2,1)S(1)} %add_convert_fusion.own_ref), channel_id=1, source_target_pairs={{2,6},{3,7},{6,2},{7,3},{10,14},{11,15},{14,10},{15,11},{18,22},{1... | collective-permute-start | bytes 147464 | tf_op jit(solution)/shard_map/ppermute | solution.py:532
  43.1 6.8 %collective-permute-start.15 = (bf16[44,16,128]{2,1,0:T(8,128)(2,1)S(1)}, bf16[44,16,128]{2,1,0:T(8,128)(2,1)S(1)}, u32[]{:S(2)}, u32[]{:S(2)}) collective-permute-start(bf16[44,16,128]{2,1,0:T(8,128)(2,1)S(1)} %join.4.own_ref), channel_id=1, source_target_pairs={{0,4},{1,5},{2,3},{3,2},{4,0},{5,1},{6,7},{7,6},{8,12},{9,13},{10,... | collective-permute-start | bytes 540680 | tf_op jit(solution)/shard_map/ppermute | solution.py:532
  45.0 0.7 %collective-permute-start.16 = (bf16[24,16,128]{2,1,0:T(8,128)(2,1)S(1)}, bf16[24,16,128]{2,1,0:T(8,128)(2,1)S(1)}, u32[]{:S(2)}, u32[]{:S(2)}) collective-permute-start(bf16[24,16,128]{2,1,0:T(8,128)(2,1)S(1)} %join.5.own_ref), channel_id=1, source_target_pairs={{2,3},{3,2},{6,7},{7,6},{10,11},{11,10},{14,15},{15,14},{18,19},{1... | collective-permute-start | bytes 294920 | tf_op jit(solution)/shard_map/ppermute | solution.py:532
  45.7 12.9 %copy-start.7 = (bf16[768,128]{1,0:T(8,128)(2,1)S(1)}, bf16[768,128]{1,0:T(8,128)(2,1)}, u32[]{:S(2)}) copy-start(bf16[768,128]{1,0:T(8,128)(2,1)} %wd_ref.3) | copy-start | bytes 589828
  50.0 10.7 %collective-permute-start.17 = (bf16[70,16,128]{2,1,0:T(8,128)(2,1)S(1)}, bf16[70,16,128]{2,1,0:T(8,128)(2,1)S(1)}, u32[]{:S(2)}, u32[]{:S(2)}) collective-permute-start(bf16[70,16,128]{2,1,0:T(8,128)(2,1)S(1)} %get-tuple-element.88.refs_0_), channel_id=1, source_target_pairs={{0,2},{2,0},{1,3},{3,1},{4,6},{6,4},{5,7},{7,5},{8,10},{10,8},{9,1... | collective-permute-start | bytes 860168 | tf_op jit(solution)/shard_map/ppermute | solution.py:544
  57.3 3.3 %collective-permute-start.18 = (bf16[48,16,128]{2,1,0:T(8,128)(2,1)S(1)}, bf16[48,16,128]{2,1,0:T(8,128)(2,1)S(1)}, u32[]{:S(2)}, u32[]{:S(2)}) collective-permute-start(bf16[48,16,128]{2,1,0:T(8,128)(2,1)S(1)} %join.7.refs_1_), channel_id=1, source_target_pairs={{2,0},{3,1},{6,4},{7,5},{10,8},{11,9},{14,12},{15,13},{18,16},{19,... | collective-permute-start | bytes 589832 | tf_op jit(solution)/shard_map/ppermute | solution.py:544

commit v8 on v5

--- a/solution.py
+++ b/solution.py
@@ -12,7 +12,7 @@
 RIM = 64
 LANES = 128
 TILE = 16
-CHUNKS = 2
+CHUNKS = 1
 F32 = jnp.float32
 BF16 = jnp.bfloat16
 NN = (((1,), (0,)), ((), ()))
@@ -149,16 +149,20 @@
                 ref[place] = value.astype(ref.dtype)
 
 
-def backward_kernel(slabs, core_ref, near_ref, hgrad_ref, grad_ref, w_ref, *refs):
-    pick_ref, hidden_ref, wd_ref, coarse_ref, base_ref, keep_ref, *refs = refs
-    cross_refs, (drt, drt_far, hot, far, w_back) = refs[:-5], refs[-5:]
-    channels, voxels = hgrad_ref.shape
-    offsets = near_ref.shape[0]
+def coarse_kernel(pick_ref, hidden_ref, wd_ref, coarse_ref):
+    channels = hidden_ref.shape[0]
     coarse = jnp.zeros(coarse_ref.shape, F32)
     for t in range(pick_ref.shape[0]):
         picked = mm(pick_ref[t], hidden_ref[...], NT).astype(BF16)
         coarse += mm(picked, wd_ref[t * channels : (t + 1) * channels, :])
     coarse_ref[...] = coarse.astype(BF16)
+
+
+def backward_kernel(slabs, core_ref, near_ref, hgrad_ref, grad_ref, w_ref, *refs):
+    base_ref, keep_ref, *refs = refs
+    cross_refs, (drt, drt_far, hot, far, w_back) = refs[:-5], refs[-5:]
+    channels, voxels = hgrad_ref.shape
+    offsets = near_ref.shape[0]
     lanes = table_lanes(near_ref[...], voxels, slabs, core_ref[0])
     near_iota = lax.broadcasted_iota(jnp.int32, (voxels, voxels), 0)
     w_back[:, :channels] = w_ref[...].astype(F32).T.astype(BF16)
@@ -292,7 +296,7 @@
         beside = [swap]
     else:
         beside = [shifts(slabs, 1), shifts(slabs, -1)]
-    side = [lax.ppermute(rim, "slab", pairs) for pairs in beside]
+    side = [lax.ppermute(features_t, "slab", pairs) for pairs in beside]
     own = pl.pallas_call(
         functools.partial(gather_kernel, slabs),
         out_shape=(
@@ -304,6 +308,7 @@
         name="gather",
     )(features_t, neighbours_t)
     side, own = lax.optimization_barrier((side, own))
+    side = [x[:, :RIM] for x in side]
     row = [rim, side[0]] if slabs == 2 else [side[0], rim, side[1]]
     row = jnp.concatenate(row, axis=1)
     cross = lax.ppermute(row, RING, crossings)
@@ -371,15 +376,14 @@
                 send[0], grad = lax.optimization_barrier((send[0], grad))
             got[i] = lax.ppermute(send[i], SPLIT, pairs)
         if phase == 0:
-            coarse, base, stay, *edges = pl.pallas_call(
+            base, stay, *edges = pl.pallas_call(
                 functools.partial(backward_kernel, slabs),
                 out_shape=[
-                    jax.ShapeDtypeStruct(coarse_grad.shape, BF16),
                     jax.ShapeDtypeStruct((channels, voxels), F32),
                     jax.ShapeDtypeStruct((channels, 2 * RIM), F32),
                 ]
                 + [jax.ShapeDtypeStruct((channels, 4 * RIM), BF16)] * len(beside),
-                in_specs=[smem] + [vmem] * 7,
+                in_specs=[smem] + [vmem] * 4,
                 scratch_shapes=[
                     pltpu.VMEM((channels, offsets * voxels), BF16),
                     pltpu.VMEM((channels, offsets * LANES), BF16),
@@ -390,31 +394,38 @@
                 compiler_params=params,
                 cost_estimate=light,
                 name="backward",
-            )(core, neighbours_t, hgrad, grad, w_conv_t, pick, hidden, w_down)
+            )(core, neighbours_t, hgrad, grad, w_conv_t)
             got[0], stay, edges, base = lax.optimization_barrier((got[0], stay, edges, base))
         if phase == phases - 1:
             back = beside if slabs == 2 else beside[::-1]
             edges = [lax.ppermute(x, "slab", p) for x, p in zip(edges, back)]
-            got[-1], edges = lax.optimization_barrier((got[-1], edges))
-            base, cross, mate = pl.pallas_call(
-                turn_kernel,
-                out_shape=(
-                    jax.ShapeDtypeStruct((channels, voxels), F32),
-                    jax.ShapeDtypeStruct((channels, RIM), BF16),
-                    jax.ShapeDtypeStruct((channels // TILE, TILE, LANES), BF16),
-                ),
-                compiler_params=params,
-                name="turn",
-            )(base, stay, *edges)
+    coarse = pl.pallas_call(
+        coarse_kernel,
+        out_shape=jax.ShapeDtypeStruct(coarse_grad.shape, BF16),
+        compiler_params=params,
+        cost_estimate=light,
+        name="coarse",
+    )(pick, hidden, w_down)
     total = [(x + y.astype(F32)).astype(BF16) for x, y in zip(keep, got)]
     far_bits = sizes["far"].bit_length() - 1
     for bit in range(far_bits):
         pairs = [(i, i ^ (1 << bit)) for i in range(sizes["far"])]
         got = [lax.ppermute(x, "far", pairs) for x in total]
-        if bit == far_bits - 1:
-            cross = lax.ppermute(cross, RING, crossings)
-            got[-1], cross, mate = lax.optimization_barrier((got[-1], cross, mate))
         total = [(x.astype(F32) + y.astype(F32)).astype(BF16) for x, y in zip(total, got)]
+        if bit == 0:
+            total[-1], edges = lax.optimization_barrier((total[-1], edges))
+    base, cross, mate = pl.pallas_call(
+        turn_kernel,
+        out_shape=(
+            jax.ShapeDtypeStruct((channels, voxels), F32),
+            jax.ShapeDtypeStruct((channels, RIM), BF16),
+            jax.ShapeDtypeStruct((channels // TILE, TILE, LANES), BF16),
+        ),
+        compiler_params=params,
+        name="turn",
+    )(base, stay, *edges)
+    cross = lax.ppermute(cross, RING, crossings)
+    total[-1], cross = lax.optimization_barrier((total[-1], cross))
     for phase in reversed(range(phases)):
         pairs = bit_pairs(sizes, orders, phase)
         got = [lax.ppermute(x, SPLIT, pairs) for x in total]

time: 54.9 us -> 54.1 us (0.985)
  starting transfers between devices: 24.9 us -> 22.6 us
  local copies, waits for them, and re-layouts: 1.87 us -> 3.83 us
    unnamed x14 -> x24, local copies, waits for them, and re-layouts: 1.06 us -> 3.82 us
    ppermute x4 -> x2, waiting for transfers between devices: 6.06 us -> 4.07 us  [on_device(): got = [lax.ppermute(x, 'far', pairs) for x in total]]
    ppermute x1, waiting for transfers between devices: 0.01 us -> 1.49 us  [on_device(): edges = [lax.ppermute(x, 'slab', p) for x, p in zip(edges, back)]]
    ppermute x2 -> x1, waiting for transfers between devices: 1.41 us -> 0.01 us  [on_device(): other = [lax.ppermute(x, 'core', swap) for x in total]]
    ppermute x4 -> x2, waiting for transfers between devices: 5.29 us -> 6.48 us  [on_device(): got = [lax.ppermute(x, SPLIT, pairs) for x in total]]
    ppermute x4 -> x2, starting transfers between devices: 5.75 us -> 4.61 us  [on_device(): got = [lax.ppermute(x, 'far', pairs) for x in total]]
    pallas_call x0 -> x1, Pallas kernels: none -> 1.13 us  [on_device(): pl.pallas_call(coarse_kernel, out_shape=jax.ShapeDtypeStruct(coarse_grad....]
    ppermute x4 -> x2, starting transfers between devices: 5.21 us -> 4.2 us  [on_device(): got[i] = lax.ppermute(send[i], SPLIT, pairs)]
  transfers between devices with their start and end apart: 21 -> 13, of which waited for: 9 -> 8; matrix products, arithmetic and copies ran while one was open for 0% -> 0% of each run, Pallas kernels for 9% -> 10%
where the time goes in v8:
time: 54.1 us; the launch traced here: 53.8 us
  starting transfers between devices  22.6 us (42%)
  waiting for transfers between devices  17.5 us (32%)
  Pallas kernels  8.81 us (16%)
  local copies, waits for them, and re-layouts  3.83 us (7%)
  between operations  0.86 us (2%)
    ppermute x2, waiting for transfers between devices, on_device(): got = [lax.ppermute(x, SPLIT, pairs) for x in total]  6.48 us
    ppermute x2, starting transfers between devices, on_device(): got = [lax.ppermute(x, 'far', pairs) for x in total]  4.61 us
    ppermute x2, starting transfers between devices, on_device(): got[i] = lax.ppermute(send[i], SPLIT, pairs)  4.2 us
    ppermute x2, waiting for transfers between devices, on_device(): got[i] = lax.ppermute(send[i], SPLIT, pairs)  4.15 us
    ppermute x2, waiting for transfers between devices, on_device(): got = [lax.ppermute(x, 'far', pairs) for x in total]  4.07 us
    ppermute x1, starting transfers between devices, on_device(): got = [lax.ppermute(x, 'core', swap) for x in send]  3.95 us
    ppermute x2, starting transfers between devices, on_device(): got = [lax.ppermute(x, SPLIT, pairs) for x in total]  3.83 us
    unnamed x24, local copies, waits for them, and re-layouts  3.82 us
  transfers between devices with their start and end apart: 13, of which 8 were waited for; matrix products, arithmetic and copies ran while one was open for 0% of the time, Pallas kernels for 10%

profile of v8, /device:TPU:0, one launch (start us, length us, event | category | flops | bytes accessed | tf_op | source)
XLA Modules:
  0.0 53.8 jit_solution(2019090632228131955)
XLA Ops:
  0.6 3.0 %collective-permute-start = (bf16[96,256]{1,0:T(8,128)(2,1)}, bf16[96,256]{1,0:T(8,128)(2,1)S(1)}, u32[]{:S(2)}, u32[]{:S(2)}) collective-permute-start(bf16[96,256]{1,0:T(8,128)(2,1)} %bitcast.11), channel_id=1, source_target_pairs={{0,1},{1,0},{2,3},{3,2},{4,5},{5,4},{6,7},{7,6},{8,9},{9,8},{10,11... | collective-permute-start | bytes 147464 | tf_op jit(solution)/shard_map/ppermute | solution.py:299
  3.7 0.8 %copy-done.1 = bf16[256,96]{0,1:T(8,128)(2,1)S(1)} copy-done((bf16[256,96]{0,1:T(8,128)(2,1)S(1)}, bf16[256,96]{0,1:T(8,128)(2,1)}, u32[]{:S(2)}) %copy-start.1) | copy-done | bytes 49176
  4.5 0.8 %copy-done.3 = s32[256,27]{0,1:T(8,128)S(1)} copy-done((s32[256,27]{0,1:T(8,128)S(1)}, s32[256,27]{0,1:T(8,128)}, u32[]{:S(2)}) %copy-start.3) | copy-done | bytes 27672
  5.3 1.0 %gather.1 = (bf16[2592,128]{1,0:T(8,128)(2,1)S(1)}, bf16[2592,128]{1,0:T(8,128)(2,1)S(1)}) custom-call(bf16[96,256]{1,0:T(8,128)(2,1)S(1)} %bitcast.12, s32[27,256]{1,0:T(8,128)S(1)} %bitcast.15), custom_call_target="tpu_custom_call" | custom-call | flops 2000000000 | bytes 10000000 | tf_op jit(solution)/shard_map/gather/pallas_call | solution.py:300
  6.3 0.0 collective-permute-done
  6.3 0.0 copy-start.5
  6.3 0.0 copy-start.11
  6.3 0.1 pad_maximum_fusion
  6.4 0.0 collective-permute-start.1
  6.4 0.7 %collective-permute-start.2 = (bf16[96,128]{1,0:T(8,128)(2,1)S(1)}, bf16[96,128]{1,0:T(8,128)(2,1)S(1)}, u32[]{:S(2)}, u32[]{:S(2)}) collective-permute-start(bf16[96,128]{1,0:T(8,128)(2,1)S(1)} %pad_maximum_fusion), channel_id=1, source_target_pairs={{2,4},{6,8},{10,12},{14,16},{18,20},{22,24},{26,28},{4,2},{8,6},{1... | collective-permute-start | bytes 73736 | tf_op jit(solution)/shard_map/ppermute | solution.py:314
  7.1 0.0 copy-start
  7.1 0.0 copy-start.2
  7.2 0.0 copy-start.4
  7.2 0.7 %taps.1 = (bf16[8,64,256]{2,1,0:T(8,128)(2,1)S(1)}, f32[96,256]{1,0:T(8,128)S(1)}) custom-call(s32[8,64]{1,0:T(8,128)S(1)} %bitcast.18, bf16[64,128]{1,0:T(8,128)(2,1)S(1)} %copy-done.5, bf16[768,128]{1,0:T(8,128)(2,1)S(1)} %copy-done.6), custom_call_target="tpu_custom_call" | custom-call | flops 2000000000 | bytes 10000000 | tf_op jit(solution)/shard_map/taps/pallas_call | solution.py:317
  7.9 0.0 collective-permute-done.1.refs_4_
  7.9 0.0 collective-permute-done.2.refs_5_
  7.9 0.3 copy-done
  8.2 0.0 copy-done.4
  8.2 2.2 %forward.1 = (bf16[96,256]{1,0:T(8,128)(2,1)S(1)}, bf16[96,256]{1,0:T(8,128)(2,1)S(1)}, f32[88,16,128]{2,1,0:T(8,128)S(1)}, bf16[88,16,128]{2,1,0:T(8,128)(2,1)S(1)}) custom-call(s32[1]{0:T(128)} %bitcast.3.core_ref, bf16[96,256]{1,0:T(8,128)(2,1)S(1)} %bitcast.14, s32[27,256]{1,0:T(8,128)S(1)} %bitcast.16, bf16[64,128]{1,0:T(8,128)(2,1)S(1)} %copy-done.5, ...), custom_call_target="tpu_custom_call" | custom-call | tf_op jit(solution)/shard_map/forward/pallas_call | solution.py:332
  10.4 0.0 copy-start.7
  10.4 0.6 %copy-done.7 = bf16[96,256]{1,0:T(8,128)(2,1)} copy-done((bf16[96,256]{1,0:T(8,128)(2,1)}, bf16[96,256]{1,0:T(8,128)(2,1)S(1)}, u32[]{:S(2)}) %copy-start.7) | copy-done | bytes 49176
  11.0 0.6 %copy-done.9 = bf16[96,256]{1,0:T(8,128)(2,1)} copy-done((bf16[96,256]{1,0:T(8,128)(2,1)}, bf16[96,256]{1,0:T(8,128)(2,1)S(1)}, u32[]{:S(2)}) %copy-start.9) | copy-done | bytes 49176
  11.7 4.0 %collective-permute-start.3 = (bf16[88,16,128]{2,1,0:T(8,128)(2,1)S(1)}, bf16[88,16,128]{2,1,0:T(8,128)(2,1)S(1)}, u32[]{:S(2)}, u32[]{:S(2)}) collective-permute-start(bf16[88,16,128]{2,1,0:T(8,128)(2,1)S(1)} %get-tuple-element.49), channel_id=1, source_target_pairs={{0,2},{2,0},{1,3},{3,1},{4,6},{6,4},{5,7},{7,5},{8,10},{10,8},{9,1... | collective-permute-start | bytes 1081352 | tf_op jit(solution)/shard_map/ppermute | solution.py:370
  15.6 1.3 %collective-permute-done.3.got_ref = bf16[88,16,128]{2,1,0:T(8,128)(2,1)S(1)} collective-permute-done((bf16[88,16,128]{2,1,0:T(8,128)(2,1)S(1)}, bf16[88,16,128]{2,1,0:T(8,128)(2,1)S(1)}, u32[]{:S(2)}, u32[]{:S(2)}) %collective-permute-start.3) | collective-permute-done | bytes 360480 | tf_op jit(solution)/shard_map/ppermute | solution.py:370
  16.9 0.1 fold.2
  17.0 2.6 %collective-permute-start.4 = (bf16[44,16,128]{2,1,0:T(8,128)(2,1)S(1)}, bf16[44,16,128]{2,1,0:T(8,128)(2,1)S(1)}, u32[]{:S(2)}, u32[]{:S(2)}) collective-permute-start(bf16[44,16,128]{2,1,0:T(8,128)(2,1)S(1)} %get-tuple-element.53), channel_id=1, source_target_pairs={{0,4},{1,5},{2,3},{3,2},{4,0},{5,1},{6,7},{7,6},{8,12},{9,13},{10,... | collective-permute-start | bytes 540680 | tf_op jit(solution)/shard_map/ppermute | solution.py:377
  19.6 2.3 %backward.1 = (f32[96,256]{1,0:T(8,128)S(1)}, f32[96,128]{1,0:T(8,128)S(1)}, bf16[96,256]{1,0:T(8,128)(2,1)S(1)}) custom-call(s32[1]{0:T(128)} %bitcast.3.core_ref, s32[27,256]{1,0:T(8,128)S(1)} %bitcast.17, f32[96,256]{1,0:T(8,128)S(1)} %get-tuple-element.46.refs_3_.hgrad_ref, bf16[96,256]{1,0:T(8,128)(2,1)S(1)} %copy-done.10, bf16[96,2592]{1,0:T(8,128)(2,1)S(1)} %bitcast.10), custom_call_target="tpu_custom_call" | custom-call | flops 2000000000 | bytes 10000000 | tf_op jit(solution)/shard_map/backward/pallas_call | solution.py:379
  21.9 1.2 %collective-permute-done.4.got_ref = bf16[44,16,128]{2,1,0:T(8,128)(2,1)S(1)} collective-permute-done((bf16[44,16,128]{2,1,0:T(8,128)(2,1)S(1)}, bf16[44,16,128]{2,1,0:T(8,128)(2,1)S(1)}, u32[]{:S(2)}, u32[]{:S(2)}) %collective-permute-start.4) | collective-permute-done | bytes 180256 | tf_op jit(solution)/shard_map/ppermute | solution.py:377
  23.1 1.6 %collective-permute-start.5 = (bf16[22,16,128]{2,1,0:T(8,128)(2,1)S(1)}, bf16[22,16,128]{2,1,0:T(8,128)(2,1)S(1)}, u32[]{:S(2)}, u32[]{:S(2)}) collective-permute-start(bf16[22,16,128]{2,1,0:T(8,128)(2,1)S(1)} %get-tuple-element.60), channel_id=1, source_target_pairs={{0,1},{1,0},{2,6},{3,7},{4,5},{5,4},{6,2},{7,3},{8,9},{9,8},{10,14... | collective-permute-start | bytes 270344 | tf_op jit(solution)/shard_map/ppermute | solution.py:377
  24.7 3.0 %collective-permute-done.5 = bf16[22,16,128]{2,1,0:T(8,128)(2,1)S(1)} collective-permute-done((bf16[22,16,128]{2,1,0:T(8,128)(2,1)S(1)}, bf16[22,16,128]{2,1,0:T(8,128)(2,1)S(1)}, u32[]{:S(2)}, u32[]{:S(2)}) %collective-permute-start.5) | collective-permute-done | bytes 90144 | tf_op jit(solution)/shard_map/ppermute | solution.py:377
  27.7 2.0 %collective-permute-start.6 = (bf16[22,16,128]{2,1,0:T(8,128)(2,1)S(1)}, bf16[22,16,128]{2,1,0:T(8,128)(2,1)S(1)}, u32[]{:S(2)}, u32[]{:S(2)}) collective-permute-start(bf16[22,16,128]{2,1,0:T(8,128)(2,1)S(1)} %add_convert_fusion.2), channel_id=1, source_target_pairs={{0,8},{8,0},{16,24},{24,16},{1,9},{9,1},{17,25},{25,17},{2,10},{10... | collective-permute-start | bytes 270344 | tf_op jit(solution)/shard_map/ppermute | solution.py:413
  29.8 1.5 %collective-permute-start.7 = (bf16[96,256]{1,0:T(8,128)(2,1)S(1)}, bf16[96,256]{1,0:T(8,128)(2,1)S(1)}, u32[]{:S(2)}, u32[]{:S(2)}) collective-permute-start(bf16[96,256]{1,0:T(8,128)(2,1)S(1)} %get-tuple-element.61), channel_id=1, source_target_pairs={{0,1},{1,0},{2,3},{3,2},{4,5},{5,4},{6,7},{7,6},{8,9},{9,8},{10,11... | collective-permute-start | bytes 147464 | tf_op jit(solution)/shard_map/ppermute | solution.py:401
  31.3 1.0 %collective-permute-done.6 = bf16[22,16,128]{2,1,0:T(8,128)(2,1)S(1)} collective-permute-done((bf16[22,16,128]{2,1,0:T(8,128)(2,1)S(1)}, bf16[22,16,128]{2,1,0:T(8,128)(2,1)S(1)}, u32[]{:S(2)}, u32[]{:S(2)}) %collective-permute-start.6) | collective-permute-done | bytes 90144 | tf_op jit(solution)/shard_map/ppermute | solution.py:413
  32.4 1.5 %collective-permute-done.7.refs_0_ = bf16[96,256]{1,0:T(8,128)(2,1)S(1)} collective-permute-done((bf16[96,256]{1,0:T(8,128)(2,1)S(1)}, bf16[96,256]{1,0:T(8,128)(2,1)S(1)}, u32[]{:S(2)}, u32[]{:S(2)}) %collective-permute-start.7) | collective-permute-done | bytes 49184 | tf_op jit(solution)/shard_map/ppermute | solution.py:401
  33.9 2.6 %collective-permute-start.8 = (bf16[22,16,128]{2,1,0:T(8,128)(2,1)S(1)}, bf16[22,16,128]{2,1,0:T(8,128)(2,1)S(1)}, u32[]{:S(2)}, u32[]{:S(2)}) collective-permute-start(bf16[22,16,128]{2,1,0:T(8,128)(2,1)S(1)} %add_convert_fusion.1), channel_id=1, source_target_pairs={{0,16},{8,24},{16,0},{24,8},{1,17},{9,25},{17,1},{25,9},{2,18},{10... | collective-permute-start | bytes 270344 | tf_op jit(solution)/shard_map/ppermute | solution.py:413
  36.4 0.1 turn.1
  36.5 0.7 %collective-permute-start.9 = (bf16[96,64]{1,0:T(8,128)(2,1)S(1)}, bf16[96,64]{1,0:T(8,128)(2,1)S(1)}, u32[]{:S(2)}, u32[]{:S(2)}) collective-permute-start(bf16[96,64]{1,0:T(8,128)(2,1)S(1)} %get-tuple-element.66), channel_id=1, source_target_pairs={{2,4},{6,8},{10,12},{14,16},{18,20},{22,24},{26,28},{4,2},{8,6},{1... | collective-permute-start | bytes 36872 | tf_op jit(solution)/shard_map/ppermute | solution.py:427
  37.2 3.0 %collective-permute-done.8 = bf16[22,16,128]{2,1,0:T(8,128)(2,1)S(1)} collective-permute-done((bf16[22,16,128]{2,1,0:T(8,128)(2,1)S(1)}, bf16[22,16,128]{2,1,0:T(8,128)(2,1)S(1)}, u32[]{:S(2)}, u32[]{:S(2)}) %collective-permute-start.8) | collective-permute-done | bytes 90144 | tf_op jit(solution)/shard_map/ppermute | solution.py:413
  40.3 0.0 collective-permute-done.9.refs_3_
  40.3 1.6 %collective-permute-start.10 = (bf16[22,16,128]{2,1,0:T(8,128)(2,1)S(1)}, bf16[22,16,128]{2,1,0:T(8,128)(2,1)S(1)}, u32[]{:S(2)}, u32[]{:S(2)}) collective-permute-start(bf16[22,16,128]{2,1,0:T(8,128)(2,1)S(1)} %add_convert_fusion.own_ref), channel_id=1, source_target_pairs={{0,1},{1,0},{2,6},{3,7},{4,5},{5,4},{6,2},{7,3},{8,9},{9,8},{10,14... | collective-permute-start | bytes 270344 | tf_op jit(solution)/shard_map/ppermute | solution.py:431
  41.9 3.0 %collective-permute-done.10.got_ref = bf16[22,16,128]{2,1,0:T(8,128)(2,1)S(1)} collective-permute-done((bf16[22,16,128]{2,1,0:T(8,128)(2,1)S(1)}, bf16[22,16,128]{2,1,0:T(8,128)(2,1)S(1)}, u32[]{:S(2)}, u32[]{:S(2)}) %collective-permute-start.10) | collective-permute-done | bytes 90144 | tf_op jit(solution)/shard_map/ppermute | solution.py:431
  44.9 2.2 %collective-permute-start.11 = (bf16[44,16,128]{2,1,0:T(8,128)(2,1)S(1)}, bf16[44,16,128]{2,1,0:T(8,128)(2,1)S(1)}, u32[]{:S(2)}, u32[]{:S(2)}) collective-permute-start(bf16[44,16,128]{2,1,0:T(8,128)(2,1)S(1)} %join.2.own_ref), channel_id=1, source_target_pairs={{0,4},{1,5},{2,3},{3,2},{4,0},{5,1},{6,7},{7,6},{8,12},{9,13},{10,... | collective-permute-start | bytes 540680 | tf_op jit(solution)/shard_map/ppermute | solution.py:431
  47.1 3.5 %collective-permute-done.11.got_ref = bf16[44,16,128]{2,1,0:T(8,128)(2,1)S(1)} collective-permute-done((bf16[44,16,128]{2,1,0:T(8,128)(2,1)S(1)}, bf16[44,16,128]{2,1,0:T(8,128)(2,1)S(1)}, u32[]{:S(2)}, u32[]{:S(2)}) %collective-permute-start.11) | collective-permute-done | bytes 180256 | tf_op jit(solution)/shard_map/ppermute | solution.py:431
  50.6 0.1 collective-permute-start.12
  50.7 0.7 %copy-done.8 = bf16[96,256]{1,0:T(8,128)(2,1)S(1)} copy-done((bf16[96,256]{1,0:T(8,128)(2,1)S(1)}, bf16[96,256]{1,0:T(8,128)(2,1)}, u32[]{:S(2)}) %copy-start.8) | copy-done | bytes 49176
  51.4 1.1 %coarse.1 = bf16[64,128]{1,0:T(8,128)(2,1)} custom-call(bf16[8,64,256]{2,1,0:T(8,128)(2,1)S(1)} %get-tuple-element.43.refs_2_.pick_ref, bf16[96,256]{1,0:T(8,128)(2,1)S(1)} %copy-done.8, bf16[768,128]{1,0:T(8,128)(2,1)S(1)} %copy-done.6), custom_call_target="tpu_custom_call" | custom-call | flops 2000000000 | bytes 10000000 | tf_op jit(solution)/shard_map/coarse/pallas_call | solution.py:402
  52.5 0.0 collective-permute-done.12.refs_1_
  52.5 1.2 %final.1 = (f32[96,2592]{1,0:T(8,128)}, f32[768,128]{1,0:T(8,128)}, f32[96,256]{1,0:T(8,128)}) custom-call(s32[1]{0:T(128)} %bitcast.3.core_ref, bf16[94,16,128]{2,1,0:T(8,128)(2,1)S(1)} %join.3.refs_0_, bf16[94,16,128]{2,1,0:T(8,128)(2,1)S(1)} %collective-permute-done.12.refs_1_, f32[96,256]{1,0:T(8,128)S(1)} %get-tuple-element.69.refs_2_, ...), custom_call_target="tpu_custom_call" | custom-call | tf_op jit(solution)/shard_map/final/pallas_call | solution.py:435
  (19 shorter events, 0.2 us)
Async XLA Ops:
  0.6 5.6 %collective-permute-start = (bf16[96,256]{1,0:T(8,128)(2,1)}, bf16[96,256]{1,0:T(8,128)(2,1)S(1)}, u32[]{:S(2)}, u32[]{:S(2)}) collective-permute-start(bf16[96,256]{1,0:T(8,128)(2,1)} %bitcast.11), channel_id=1, source_target_pairs={{0,1},{1,0},{2,3},{3,2},{4,5},{5,4},{6,7},{7,6},{8,9},{9,8},{10,11... | collective-permute-start | bytes 147464 | tf_op jit(solution)/shard_map/ppermute | solution.py:299
  3.7 0.8 %copy-start.1 = (bf16[256,96]{0,1:T(8,128)(2,1)S(1)}, bf16[256,96]{0,1:T(8,128)(2,1)}, u32[]{:S(2)}) copy-start(bf16[256,96]{0,1:T(8,128)(2,1)} %param.6) | copy-start | bytes 147460
  4.5 0.8 %copy-start.3 = (s32[256,27]{0,1:T(8,128)S(1)}, s32[256,27]{0,1:T(8,128)}, u32[]{:S(2)}) copy-start(s32[256,27]{0,1:T(8,128)} %param.7) | copy-start | bytes 82948
  5.3 1.9 %copy-start.6 = (bf16[768,128]{1,0:T(8,128)(2,1)S(1)}, bf16[768,128]{1,0:T(8,128)(2,1)}, u32[]{:S(2)}) copy-start(bf16[768,128]{1,0:T(8,128)(2,1)} %wd_ref.3) | copy-start | bytes 589828
  6.3 0.8 %copy-start.5 = (bf16[64,128]{1,0:T(8,128)(2,1)S(1)}, bf16[64,128]{1,0:T(8,128)(2,1)}, u32[]{:S(2)}) copy-start(bf16[64,128]{1,0:T(8,128)(2,1)} %cgrad_ref.3) | copy-start | bytes 49156
  6.3 0.8 %copy-start.11 = (s32[64,8]{0,1:T(8,128)S(1)}, s32[64,8]{0,1:T(8,128)}, u32[]{:S(2)}) copy-start(s32[64,8]{0,1:T(8,128)} %param.8) | copy-start | bytes 6148
  6.4 1.5 %collective-permute-start.1 = (bf16[96,128]{1,0:T(8,128)(2,1)S(1)}, bf16[96,128]{1,0:T(8,128)(2,1)S(1)}, u32[]{:S(2)}, u32[]{:S(2)}) collective-permute-start(bf16[96,128]{1,0:T(8,128)(2,1)S(1)} %pad_maximum_fusion), channel_id=1, source_target_pairs={{0,2},{2,0},{4,6},{6,4},{8,10},{10,8},{12,14},{14,12},{16,18},{18,... | collective-permute-start | bytes 73736 | tf_op jit(solution)/shard_map/ppermute | solution.py:315
  6.4 1.5 %collective-permute-start.2 = (bf16[96,128]{1,0:T(8,128)(2,1)S(1)}, bf16[96,128]{1,0:T(8,128)(2,1)S(1)}, u32[]{:S(2)}, u32[]{:S(2)}) collective-permute-start(bf16[96,128]{1,0:T(8,128)(2,1)S(1)} %pad_maximum_fusion), channel_id=1, source_target_pairs={{2,4},{6,8},{10,12},{14,16},{18,20},{22,24},{26,28},{4,2},{8,6},{1... | collective-permute-start | bytes 73736 | tf_op jit(solution)/shard_map/ppermute | solution.py:314
  7.1 1.0 %copy-start = (bf16[2592,96]{0,1:T(8,128)(2,1)S(1)}, bf16[2592,96]{0,1:T(8,128)(2,1)}, u32[]{:S(2)}) copy-start(bf16[2592,96]{0,1:T(8,128)(2,1)} %param.9) | copy-start | bytes 1492996
  7.1 1.0 %copy-start.2 = (bf16[256,96]{0,1:T(8,128)(2,1)S(1)}, bf16[256,96]{0,1:T(8,128)(2,1)}, u32[]{:S(2)}) copy-start(bf16[256,96]{0,1:T(8,128)(2,1)} %param.6) | copy-start | bytes 147460
  7.2 1.0 %copy-start.4 = (s32[256,27]{0,1:T(8,128)S(1)}, s32[256,27]{0,1:T(8,128)}, u32[]{:S(2)}) copy-start(s32[256,27]{0,1:T(8,128)} %param.7) | copy-start | bytes 82948
  10.4 0.6 %copy-start.7 = (bf16[96,256]{1,0:T(8,128)(2,1)}, bf16[96,256]{1,0:T(8,128)(2,1)S(1)}, u32[]{:S(2)}) copy-start(bf16[96,256]{1,0:T(8,128)(2,1)S(1)} %get-tuple-element.47.hidden_ref) | copy-start | bytes 147460
  11.0 0.6 %copy-start.9 = (bf16[96,256]{1,0:T(8,128)(2,1)}, bf16[96,256]{1,0:T(8,128)(2,1)S(1)}, u32[]{:S(2)}) copy-start(bf16[96,256]{1,0:T(8,128)(2,1)S(1)} %get-tuple-element.54.grad_ref) | copy-start | bytes 147460
  11.7 5.3 %collective-permute-start.3 = (bf16[88,16,128]{2,1,0:T(8,128)(2,1)S(1)}, bf16[88,16,128]{2,1,0:T(8,128)(2,1)S(1)}, u32[]{:S(2)}, u32[]{:S(2)}) collective-permute-start(bf16[88,16,128]{2,1,0:T(8,128)(2,1)S(1)} %get-tuple-element.49), channel_id=1, source_target_pairs={{0,2},{2,0},{1,3},{3,1},{4,6},{6,4},{5,7},{7,5},{8,10},{10,8},{9,1... | collective-permute-start | bytes 1081352 | tf_op jit(solution)/shard_map/ppermute | solution.py:370
  16.9 2.7 %copy-start.10 = (bf16[96,256]{1,0:T(8,128)(2,1)S(1)}, bf16[96,256]{1,0:T(8,128)(2,1)}, u32[]{:S(2)}) copy-start(bf16[96,256]{1,0:T(8,128)(2,1)} %copy-done.9) | copy-start | bytes 147460
  17.0 6.1 %collective-permute-start.4 = (bf16[44,16,128]{2,1,0:T(8,128)(2,1)S(1)}, bf16[44,16,128]{2,1,0:T(8,128)(2,1)S(1)}, u32[]{:S(2)}, u32[]{:S(2)}) collective-permute-start(bf16[44,16,128]{2,1,0:T(8,128)(2,1)S(1)} %get-tuple-element.53), channel_id=1, source_target_pairs={{0,4},{1,5},{2,3},{3,2},{4,0},{5,1},{6,7},{7,6},{8,12},{9,13},{10,... | collective-permute-start | bytes 540680 | tf_op jit(solution)/shard_map/ppermute | solution.py:377
  23.1 4.6 %collective-permute-start.5 = (bf16[22,16,128]{2,1,0:T(8,128)(2,1)S(1)}, bf16[22,16,128]{2,1,0:T(8,128)(2,1)S(1)}, u32[]{:S(2)}, u32[]{:S(2)}) collective-permute-start(bf16[22,16,128]{2,1,0:T(8,128)(2,1)S(1)} %get-tuple-element.60), channel_id=1, source_target_pairs={{0,1},{1,0},{2,6},{3,7},{4,5},{5,4},{6,2},{7,3},{8,9},{9,8},{10,14... | collective-permute-start | bytes 270344 | tf_op jit(solution)/shard_map/ppermute | solution.py:377
  27.7 4.6 %collective-permute-start.6 = (bf16[22,16,128]{2,1,0:T(8,128)(2,1)S(1)}, bf16[22,16,128]{2,1,0:T(8,128)(2,1)S(1)}, u32[]{:S(2)}, u32[]{:S(2)}) collective-permute-start(bf16[22,16,128]{2,1,0:T(8,128)(2,1)S(1)} %add_convert_fusion.2), channel_id=1, source_target_pairs={{0,8},{8,0},{16,24},{24,16},{1,9},{9,1},{17,25},{25,17},{2,10},{10... | collective-permute-start | bytes 270344 | tf_op jit(solution)/shard_map/ppermute | solution.py:413
  29.8 4.1 %collective-permute-start.7 = (bf16[96,256]{1,0:T(8,128)(2,1)S(1)}, bf16[96,256]{1,0:T(8,128)(2,1)S(1)}, u32[]{:S(2)}, u32[]{:S(2)}) collective-permute-start(bf16[96,256]{1,0:T(8,128)(2,1)S(1)} %get-tuple-element.61), channel_id=1, source_target_pairs={{0,1},{1,0},{2,3},{3,2},{4,5},{5,4},{6,7},{7,6},{8,9},{9,8},{10,11... | collective-permute-start | bytes 147464 | tf_op jit(solution)/shard_map/ppermute | solution.py:401
  33.9 6.4 %collective-permute-start.8 = (bf16[22,16,128]{2,1,0:T(8,128)(2,1)S(1)}, bf16[22,16,128]{2,1,0:T(8,128)(2,1)S(1)}, u32[]{:S(2)}, u32[]{:S(2)}) collective-permute-start(bf16[22,16,128]{2,1,0:T(8,128)(2,1)S(1)} %add_convert_fusion.1), channel_id=1, source_target_pairs={{0,16},{8,24},{16,0},{24,8},{1,17},{9,25},{17,1},{25,9},{2,18},{10... | collective-permute-start | bytes 270344 | tf_op jit(solution)/shard_map/ppermute | solution.py:413
  36.5 3.7 %collective-permute-start.9 = (bf16[96,64]{1,0:T(8,128)(2,1)S(1)}, bf16[96,64]{1,0:T(8,128)(2,1)S(1)}, u32[]{:S(2)}, u32[]{:S(2)}) collective-permute-start(bf16[96,64]{1,0:T(8,128)(2,1)S(1)} %get-tuple-element.66), channel_id=1, source_target_pairs={{2,4},{6,8},{10,12},{14,16},{18,20},{22,24},{26,28},{4,2},{8,6},{1... | collective-permute-start | bytes 36872 | tf_op jit(solution)/shard_map/ppermute | solution.py:427
  40.3 4.6 %collective-permute-start.10 = (bf16[22,16,128]{2,1,0:T(8,128)(2,1)S(1)}, bf16[22,16,128]{2,1,0:T(8,128)(2,1)S(1)}, u32[]{:S(2)}, u32[]{:S(2)}) collective-permute-start(bf16[22,16,128]{2,1,0:T(8,128)(2,1)S(1)} %add_convert_fusion.own_ref), channel_id=1, source_target_pairs={{0,1},{1,0},{2,6},{3,7},{4,5},{5,4},{6,2},{7,3},{8,9},{9,8},{10,14... | collective-permute-start | bytes 270344 | tf_op jit(solution)/shard_map/ppermute | solution.py:431
  44.9 5.7 %collective-permute-start.11 = (bf16[44,16,128]{2,1,0:T(8,128)(2,1)S(1)}, bf16[44,16,128]{2,1,0:T(8,128)(2,1)S(1)}, u32[]{:S(2)}, u32[]{:S(2)}) collective-permute-start(bf16[44,16,128]{2,1,0:T(8,128)(2,1)S(1)} %join.2.own_ref), channel_id=1, source_target_pairs={{0,4},{1,5},{2,3},{3,2},{4,0},{5,1},{6,7},{7,6},{8,12},{9,13},{10,... | collective-permute-start | bytes 540680 | tf_op jit(solution)/shard_map/ppermute | solution.py:431
  50.6 0.8 %copy-start.8 = (bf16[96,256]{1,0:T(8,128)(2,1)S(1)}, bf16[96,256]{1,0:T(8,128)(2,1)}, u32[]{:S(2)}) copy-start(bf16[96,256]{1,0:T(8,128)(2,1)} %copy-done.7) | copy-start | bytes 147460
  50.6 1.9 %collective-permute-start.12 = (bf16[94,16,128]{2,1,0:T(8,128)(2,1)S(1)}, bf16[94,16,128]{2,1,0:T(8,128)(2,1)S(1)}, u32[]{:S(2)}, u32[]{:S(2)}) collective-permute-start(bf16[94,16,128]{2,1,0:T(8,128)(2,1)S(1)} %join.3.refs_0_), channel_id=1, source_target_pairs={{0,2},{2,0},{1,3},{3,1},{4,6},{6,4},{5,7},{7,5},{8,10},{10,8},{9,1... | collective-permute-start | bytes 1155080 | tf_op jit(solution)/shard_map/ppermute | solution.py:434

commit v9 on v8

--- a/solution.py
+++ b/solution.py
@@ -12,7 +12,6 @@
 RIM = 64
 LANES = 128
 TILE = 16
-CHUNKS = 1
 F32 = jnp.float32
 BF16 = jnp.bfloat16
 NN = (((1,), (0,)), ((), ()))
@@ -98,7 +97,7 @@
 def forward_kernel(slabs, core_ref, f_ref, near_ref, cgrad_ref, w_ref, *refs):
     first_ref, rest_ref, pick_ref, hgrad_ref = refs[:4]
     halo_refs, refs = (refs[4:7], refs[7:]) if slabs == 2 else (refs[4:8], refs[8:])
-    grad_ref, hidden_ref, *chunks, rt, conv_w, down_w = refs
+    grad_ref, hidden_ref, keep_ref, send_ref, rt, conv_w, down_w = refs
     channels, voxels = f_ref.shape
     offsets = near_ref.shape[0]
     taps = pick_ref.shape[0]
@@ -131,22 +130,20 @@
         down_w[t * channels : (t + 1) * channels, :] = mm(picked_t, cgrad)
 
     tiles = payload_tiles(channels, conv_columns, taps)
-    count = len(chunks) // 2
-    size = chunks[0].shape[0]
+    size = keep_ref.shape[0]
     for core in range(2):
 
         @pl.when(core_ref[0] == core)
         def _(core=core):
-            for i in range(2 * count * size):
-                half, chunk, place = i // (count * size), i // size % count, i % size
-                ref = chunks[2 * chunk + (half != core)]
+            for i in range(2 * size):
+                ref = keep_ref if i // size == core else send_ref
                 if i < len(tiles):
                     kind, row, column, _ = tiles[i]
                     source = down_w if kind else conv_w
                     value = source[row : row + TILE, column : column + LANES]
                 else:
                     value = jnp.zeros((TILE, LANES), F32)
-                ref[place] = value.astype(ref.dtype)
+                ref[i % size] = value.astype(ref.dtype)
 
 
 def coarse_kernel(pick_ref, hidden_ref, wd_ref, coarse_ref):
@@ -202,39 +199,42 @@
         mate_ref[i] = pair[i * TILE : (i + 1) * TILE, :]
 
 
-def fold_kernel(bit_ref, own_ref, got_ref, keep_ref, send_ref):
-    half = keep_ref.shape[0]
-    for ref, part in ((keep_ref, bit_ref[0]), (send_ref, 1 - bit_ref[0])):
-        rows = pl.ds(part * half, half)
+def step_of(steps, core):
+    return jnp.where(core == 0, *steps)
+
+
+def split_kernel(orders, core_ref, here_ref, own_ref, got_ref, *piece_refs):
+    length = piece_refs[0].shape[0]
+    for ref, steps in zip(piece_refs, ((0, 0),) + orders):
+        rows = pl.ds((here_ref[0] ^ step_of(steps, core_ref[0])) * length, length)
         ref[...] = (own_ref[rows] + got_ref[rows].astype(F32)).astype(ref.dtype)
 
 
-def join_kernel(bit_ref, own_ref, got_ref, *refs):
-    riders, full_ref = refs[:-1], refs[-1]
-    half = own_ref.shape[0]
-    for rider in riders:
-        full_ref[2 * half :] = rider[...]
-    full_ref[pl.ds(bit_ref[0] * half, half)] = own_ref[...]
-    full_ref[pl.ds((1 - bit_ref[0]) * half, half)] = got_ref[...]
-
-
-def final_kernel(taps, count, size, core_ref, *refs):
-    mine, other, refs = refs[:count], refs[count : 2 * count], refs[2 * count :]
+def join_kernel(orders, core_ref, here_ref, *refs):
+    piece_refs, rider_ref, full_ref = refs[:-2], refs[-2], refs[-1]
+    length = piece_refs[0].shape[0]
+    for ref, steps in zip(piece_refs, ((0, 0),) + orders):
+        place = here_ref[0] ^ step_of(steps, core_ref[0])
+        full_ref[pl.ds(place * length, length)] = ref[...]
+    full_ref[len(piece_refs) * length :] = rider_ref[...]
+
+
+def final_kernel(taps, size, core_ref, mine_ref, other_ref, *refs):
     base_ref, cross_ref, conv_ref, down_ref, grad_ref = refs
     channels, conv_columns = conv_ref.shape
     grad_ref[:, RIM:] = base_ref[:, RIM:]
     for i in range(channels // TILE):
         rows = slice(i * TILE, (i + 1) * TILE)
         total = base_ref[rows, :RIM] + cross_ref[rows, :].astype(F32)
-        grad_ref[rows, :RIM] = total + other[-1][size + i][:, :RIM].astype(F32)
+        grad_ref[rows, :RIM] = total + other_ref[size + i][:, :RIM].astype(F32)
     for core in range(2):
 
         @pl.when(core_ref[0] == core)
         def _(core=core):
             for i, tile in enumerate(payload_tiles(channels, conv_columns, taps)):
                 kind, row, column, columns = tile
-                source = mine if i // (count * size) == core else other
-                value = source[i // size % count][i % size].astype(F32)
+                source = mine_ref if i // size == core else other_ref
+                value = source[i % size].astype(F32)
                 target = down_ref if kind else conv_ref
                 target[row : row + TILE, column : column + columns] = value[:, :columns]
 
@@ -249,24 +249,24 @@
     return mates, cross + [(b, a) for a, b in cross]
 
 
-def square_bits(nears, slabs, core):
-    near = [("near", i) for i in range(nears.bit_length() - 1)]
-    slab = [("slab", i) for i in range(slabs.bit_length() - 1)]
-    return near + slab if core == 0 else slab + near
-
-
-def bit_pairs(sizes, orders, phase):
+def around_orders(nears, slabs):
+    count = nears * slabs
+    if count == 4:
+        return ((3, 3), (2, 1), (1, 2))
+    return tuple((i, i) for i in range(count - 1, 0, -1))
+
+
+def around_pairs(sizes, steps):
     pairs = []
-    for index in range(functools.reduce(lambda a, b: a * b, sizes.values())):
-        place, left = {}, index
-        for axis in reversed(SPLIT):
-            left, place[axis] = divmod(left, sizes[axis])
-        axis, bit = orders[place["core"]][phase]
-        place[axis] ^= 1 << bit
-        other = 0
-        for name in SPLIT:
-            other = other * sizes[name] + place[name]
-        pairs.append((index, other))
+    slabs = sizes["slab"]
+    for far in range(sizes["far"]):
+        for here in range(sizes["near"] * slabs):
+            for core in range(2):
+                spots = []
+                for spot in (here, here ^ steps[core]):
+                    near, slab = divmod(spot, slabs)
+                    spots.append(((far * sizes["near"] + near) * 2 + core) * slabs + slab)
+                pairs.append(tuple(spots))
     return pairs
 
 
@@ -279,12 +279,10 @@
     core = lax.axis_index("core").astype(jnp.int32).reshape(1)
     swap = [(0, 1), (1, 0)]
     mates, crossings = chip_pairs(regions)
-    orders = [square_bits(sizes["near"], slabs, c) for c in range(2)]
-    phases = len(orders[0])
-    bits = []
-    for phase in range(phases):
-        chosen = [(lax.axis_index(axis) >> bit) & 1 for axis, bit in (o[phase] for o in orders)]
-        bits.append(jnp.where(core == 0, *chosen).astype(jnp.int32))
+    here = lax.axis_index(("near", "slab")).astype(jnp.int32).reshape(1)
+    orders = around_orders(sizes["near"], slabs)
+    routes = [around_pairs(sizes, steps) for steps in orders]
+    squares = len(orders) + 1
 
     smem = pl.BlockSpec(memory_space=pltpu.SMEM)
     vmem = pl.BlockSpec(memory_space=pltpu.VMEM)
@@ -312,7 +310,6 @@
     row = [rim, side[0]] if slabs == 2 else [side[0], rim, side[1]]
     row = jnp.concatenate(row, axis=1)
     cross = lax.ppermute(row, RING, crossings)
-    mate = lax.ppermute(row, RING, mates)
     row, down_t = lax.optimization_barrier((row, down_map.T))
     pick, hgrad = pl.pallas_call(
         taps_kernel,
@@ -324,18 +321,21 @@
         cost_estimate=light,
         name="taps",
     )(down_t, coarse_grad, w_down)
+    row, pick, hgrad = lax.optimization_barrier((row, pick, hgrad))
+    mate = lax.ppermute(row, RING, mates)
     halos = [mate, cross, *side]
     far_rows = -(-sum(x.shape[1] for x in halos) // LANES) * LANES
 
     tiles = len(payload_tiles(channels, conv_columns, taps))
-    size = -(-tiles // (2 * CHUNKS << phases)) << phases
-    grad, hidden, *chunks = pl.pallas_call(
+    size = -(-tiles // (2 * squares)) * squares
+    grad, hidden, keep, send = pl.pallas_call(
         functools.partial(forward_kernel, slabs),
-        out_shape=[
+        out_shape=(
             jax.ShapeDtypeStruct((channels, voxels), BF16),
             jax.ShapeDtypeStruct((channels, voxels), BF16),
-        ]
-        + [jax.ShapeDtypeStruct((size, TILE, LANES), kind) for kind in (F32, BF16)] * CHUNKS,
+            jax.ShapeDtypeStruct((size, TILE, LANES), F32),
+            jax.ShapeDtypeStruct((size, TILE, LANES), BF16),
+        ),
         in_specs=[smem] + [vmem] * (8 + len(halos)),
         scratch_shapes=[
             pltpu.VMEM((conv_columns, voxels), BF16),
@@ -346,59 +346,41 @@
         name="forward",
     )(core, features_t, neighbours_t, coarse_grad, w_conv_t, *own, pick, hgrad, *halos)
 
-    def fold(phase, keep, got):
-        shape = (keep.shape[0] // 2, TILE, LANES)
-        return pl.pallas_call(
-            fold_kernel,
-            out_shape=(jax.ShapeDtypeStruct(shape, F32), jax.ShapeDtypeStruct(shape, BF16)),
-            in_specs=[smem, vmem, vmem],
-            compiler_params=params,
-            name="fold",
-        )(bits[phase], keep, got)
-
-    def join(phase, own, got, *riders):
-        count = own.shape[0] * 2 + sum(x.shape[0] for x in riders)
-        return pl.pallas_call(
-            join_kernel,
-            out_shape=jax.ShapeDtypeStruct((count, TILE, LANES), BF16),
-            in_specs=[smem] + [vmem] * (2 + len(riders)),
-            compiler_params=params,
-            name="join",
-        )(bits[phase], own, got, *riders)
-
-    keep, send = chunks[0::2], chunks[1::2]
-    got = [lax.ppermute(x, "core", swap) for x in send]
-    for phase in range(phases):
-        pairs = bit_pairs(sizes, orders, phase)
-        for i in range(CHUNKS):
-            keep[i], send[i] = fold(phase, keep[i], got[i])
-            if phase == 0 and i == 0:
-                send[0], grad = lax.optimization_barrier((send[0], grad))
-            got[i] = lax.ppermute(send[i], SPLIT, pairs)
-        if phase == 0:
-            base, stay, *edges = pl.pallas_call(
-                functools.partial(backward_kernel, slabs),
-                out_shape=[
-                    jax.ShapeDtypeStruct((channels, voxels), F32),
-                    jax.ShapeDtypeStruct((channels, 2 * RIM), F32),
-                ]
-                + [jax.ShapeDtypeStruct((channels, 4 * RIM), BF16)] * len(beside),
-                in_specs=[smem] + [vmem] * 4,
-                scratch_shapes=[
-                    pltpu.VMEM((channels, offsets * voxels), BF16),
-                    pltpu.VMEM((channels, offsets * LANES), BF16),
-                    pltpu.VMEM((voxels, offsets * voxels), BF16),
-                    pltpu.VMEM((far_rows, offsets * LANES), BF16),
-                    pltpu.VMEM((conv_columns, LANES), BF16),
-                ],
-                compiler_params=params,
-                cost_estimate=light,
-                name="backward",
-            )(core, neighbours_t, hgrad, grad, w_conv_t)
-            got[0], stay, edges, base = lax.optimization_barrier((got[0], stay, edges, base))
-        if phase == phases - 1:
-            back = beside if slabs == 2 else beside[::-1]
-            edges = [lax.ppermute(x, "slab", p) for x, p in zip(edges, back)]
+    got = lax.ppermute(send, "core", swap)
+    piece = size // squares
+    keep, *sent = pl.pallas_call(
+        functools.partial(split_kernel, orders),
+        out_shape=[
+            jax.ShapeDtypeStruct((piece, TILE, LANES), BF16 if i else F32) for i in range(squares)
+        ],
+        in_specs=[smem, smem, vmem, vmem],
+        compiler_params=params,
+        name="split",
+    )(core, here, keep, got)
+    sent, grad = lax.optimization_barrier((sent, grad))
+    got = [lax.ppermute(x, SPLIT, route) for x, route in zip(sent, routes)]
+    base, stay, *edges = pl.pallas_call(
+        functools.partial(backward_kernel, slabs),
+        out_shape=[
+            jax.ShapeDtypeStruct((channels, voxels), F32),
+            jax.ShapeDtypeStruct((channels, 2 * RIM), F32),
+        ]
+        + [jax.ShapeDtypeStruct((channels, 4 * RIM), BF16)] * len(beside),
+        in_specs=[smem] + [vmem] * 4,
+        scratch_shapes=[
+            pltpu.VMEM((channels, offsets * voxels), BF16),
+            pltpu.VMEM((channels, offsets * LANES), BF16),
+            pltpu.VMEM((voxels, offsets * voxels), BF16),
+            pltpu.VMEM((far_rows, offsets * LANES), BF16),
+            pltpu.VMEM((conv_columns, LANES), BF16),
+        ],
+        compiler_params=params,
+        cost_estimate=light,
+        name="backward",
+    )(core, neighbours_t, hgrad, grad, w_conv_t)
+    got, stay, edges, base = lax.optimization_barrier((got, stay, edges, base))
+    back = beside if slabs == 2 else beside[::-1]
+    edges = [lax.ppermute(x, "slab", p) for x, p in zip(edges, back)]
     coarse = pl.pallas_call(
         coarse_kernel,
         out_shape=jax.ShapeDtypeStruct(coarse_grad.shape, BF16),
@@ -406,14 +388,14 @@
         cost_estimate=light,
         name="coarse",
     )(pick, hidden, w_down)
-    total = [(x + y.astype(F32)).astype(BF16) for x, y in zip(keep, got)]
+    total = functools.reduce(lambda x, y: x + y.astype(F32), got, keep).astype(BF16)
     far_bits = sizes["far"].bit_length() - 1
     for bit in range(far_bits):
         pairs = [(i, i ^ (1 << bit)) for i in range(sizes["far"])]
-        got = [lax.ppermute(x, "far", pairs) for x in total]
-        total = [(x.astype(F32) + y.astype(F32)).astype(BF16) for x, y in zip(total, got)]
+        got = lax.ppermute(total, "far", pairs)
+        total = (total.astype(F32) + got.astype(F32)).astype(BF16)
         if bit == 0:
-            total[-1], edges = lax.optimization_barrier((total[-1], edges))
+            total, edges = lax.optimization_barrier((total, edges))
     base, cross, mate = pl.pallas_call(
         turn_kernel,
         out_shape=(
@@ -425,24 +407,27 @@
         name="turn",
     )(base, stay, *edges)
     cross = lax.ppermute(cross, RING, crossings)
-    total[-1], cross = lax.optimization_barrier((total[-1], cross))
-    for phase in reversed(range(phases)):
-        pairs = bit_pairs(sizes, orders, phase)
-        got = [lax.ppermute(x, SPLIT, pairs) for x in total]
-        riders = [()] * (CHUNKS - 1) + [(mate,) if phase == 0 else ()]
-        total = [join(phase, x, y, *z) for x, y, z in zip(total, got, riders)]
-    other = [lax.ppermute(x, "core", swap) for x in total]
+    total, cross = lax.optimization_barrier((total, cross))
+    got = [lax.ppermute(total, SPLIT, route) for route in routes[::-1]]
+    mine = pl.pallas_call(
+        functools.partial(join_kernel, orders[::-1]),
+        out_shape=jax.ShapeDtypeStruct((size + mate.shape[0], TILE, LANES), BF16),
+        in_specs=[smem, smem] + [vmem] * (squares + 1),
+        compiler_params=params,
+        name="join",
+    )(core, here, total, *got, mate)
+    other = lax.ppermute(mine, "core", swap)
     conv_wgrad_t, down_wgrad, grad_input_t = pl.pallas_call(
-        functools.partial(final_kernel, taps, CHUNKS, size),
+        functools.partial(final_kernel, taps, size),
         out_shape=(
             jax.ShapeDtypeStruct((channels, conv_columns), F32),
             jax.ShapeDtypeStruct((taps * channels, LANES), F32),
             jax.ShapeDtypeStruct((channels, voxels), F32),
         ),
-        in_specs=[smem] + [vmem] * (2 * CHUNKS + 2),
+        in_specs=[smem] + [vmem] * 4,
         compiler_params=params,
         name="final",
-    )(core, *total, *other, base, cross)
+    )(core, mine, other, base, cross)
     return coarse, grad_input_t.T, conv_wgrad_t.T, down_wgrad
 
 

time: 54.1 us -> 47.8 us (0.88)
  waiting for transfers between devices: 17.5 us -> 14.1 us
  starting transfers between devices: 22.6 us -> 21.2 us
  local copies, waits for them, and re-layouts: 3.83 us -> 2.45 us
    ppermute x8 -> x10, waiting for transfers between devices: 16 us -> 11.7 us  [the longest x2 4.37 us: on_device(): got = lax.ppermute(total, 'far', pairs)]
    ppermute x8 -> x10, starting transfers between devices: 16.7 us -> 12.6 us  [the longest x2 4.84 us: on_device(): got = lax.ppermute(total, 'far', pairs)]
    ppermute x1, starting transfers between devices: 0.04 us -> 3.08 us  [on_device(): mate = lax.ppermute(row, RING, mates)]
    unnamed x24 -> x18, local copies, waits for them, and re-layouts: 3.82 us -> 2.44 us
    ppermute x1, waiting for transfers between devices: 0.01 us -> 0.85 us  [on_device(): mate = lax.ppermute(row, RING, mates)]
    pallas_call x6 -> x4, Pallas kernels: 3.6 us -> 3.55 us  [the longest x1 2.23 us: on_device(): pl.pallas_call(functools.partial(forward_kernel, slabs), out_shape=(jax.S...]
  transfers between devices with their start and end apart: 13 -> 15, of which waited for: 8 -> 9; matrix products, arithmetic and copies ran while one was open for 0% -> 0% of each run, Pallas kernels for 10% -> 11%
where the time goes in v9:
time: 47.8 us; the launch traced here: 47.5 us
  starting transfers between devices  21.2 us (44%)
  waiting for transfers between devices  14.1 us (29%)
  Pallas kernels  8.76 us (18%)
  local copies, waits for them, and re-layouts  2.45 us (5%)
  between operations  0.82 us (2%)
    ppermute x2, starting transfers between devices, on_device(): got = lax.ppermute(total, 'far', pairs)  4.84 us
    ppermute x2, waiting for transfers between devices, on_device(): got = lax.ppermute(total, 'far', pairs)  4.37 us
    ppermute x3, waiting for transfers between devices, on_device(): got = [lax.ppermute(total, SPLIT, route) for route in routes[::-1]]  4.01 us
    ppermute x3, starting transfers between devices, on_device(): got = [lax.ppermute(total, SPLIT, route) for route in routes[::-1]]  3.68 us
    ppermute x3, starting transfers between devices, on_device(): got = [lax.ppermute(x, SPLIT, route) for x, route in zip(sent, routes)]  3.57 us
    ppermute x1, starting transfers between devices, on_device(): mate = lax.ppermute(row, RING, mates)  3.08 us
    ppermute x1, starting transfers between devices, on_device(): side = [lax.ppermute(features_t, 'slab', pairs) for pairs in beside]  3.03 us
    unnamed x18, local copies, waits for them, and re-layouts  2.44 us
  transfers between devices with their start and end apart: 15, of which 9 were waited for; matrix products, arithmetic and copies ran while one was open for 0% of the time, Pallas kernels for 11%

profile of v9, /device:TPU:0, one launch (start us, length us, event | category | flops | bytes accessed | tf_op | source)
XLA Modules:
  0.0 47.5 jit_solution(8310497092679806928)
XLA Ops:
  0.6 3.0 %collective-permute-start = (bf16[96,256]{1,0:T(8,128)(2,1)}, bf16[96,256]{1,0:T(8,128)(2,1)S(1)}, u32[]{:S(2)}, u32[]{:S(2)}) collective-permute-start(bf16[96,256]{1,0:T(8,128)(2,1)} %bitcast.10), channel_id=1, source_target_pairs={{0,1},{1,0},{2,3},{3,2},{4,5},{5,4},{6,7},{7,6},{8,9},{9,8},{10,11... | collective-permute-start | bytes 147464 | tf_op jit(solution)/shard_map/ppermute | solution.py:297
  3.7 0.8 %copy-done.1 = bf16[256,96]{0,1:T(8,128)(2,1)S(1)} copy-done((bf16[256,96]{0,1:T(8,128)(2,1)S(1)}, bf16[256,96]{0,1:T(8,128)(2,1)}, u32[]{:S(2)}) %copy-start.1) | copy-done | bytes 49176
  4.5 0.8 %copy-done.3 = s32[256,27]{0,1:T(8,128)S(1)} copy-done((s32[256,27]{0,1:T(8,128)S(1)}, s32[256,27]{0,1:T(8,128)}, u32[]{:S(2)}) %copy-start.3) | copy-done | bytes 27672
  5.3 1.0 %gather.1 = (bf16[2592,128]{1,0:T(8,128)(2,1)S(1)}, bf16[2592,128]{1,0:T(8,128)(2,1)S(1)}) custom-call(bf16[96,256]{1,0:T(8,128)(2,1)S(1)} %bitcast.11, s32[27,256]{1,0:T(8,128)S(1)} %bitcast.14), custom_call_target="tpu_custom_call" | custom-call | flops 2000000000 | bytes 10000000 | tf_op jit(solution)/shard_map/gather/pallas_call | solution.py:298
  6.2 0.0 collective-permute-done
  6.3 0.0 copy-start.5
  6.3 0.0 copy-start.8
  6.3 0.1 pad_maximum_fusion
  6.4 0.7 %collective-permute-start.2 = (bf16[96,128]{1,0:T(8,128)(2,1)S(1)}, bf16[96,128]{1,0:T(8,128)(2,1)S(1)}, u32[]{:S(2)}, u32[]{:S(2)}) collective-permute-start(bf16[96,128]{1,0:T(8,128)(2,1)S(1)} %pad_maximum_fusion), channel_id=1, source_target_pairs={{2,4},{6,8},{10,12},{14,16},{18,20},{22,24},{26,28},{4,2},{8,6},{1... | collective-permute-start | bytes 73736 | tf_op jit(solution)/shard_map/ppermute | solution.py:312
  7.1 0.0 copy-start
  7.1 0.0 copy-start.2
  7.1 0.0 copy-start.4
  7.1 0.7 %taps.1 = (bf16[8,64,256]{2,1,0:T(8,128)(2,1)S(1)}, f32[96,256]{1,0:T(8,128)S(1)}) custom-call(s32[8,64]{1,0:T(8,128)S(1)} %bitcast.17, bf16[64,128]{1,0:T(8,128)(2,1)S(1)} %copy-done.5, bf16[768,128]{1,0:T(8,128)(2,1)S(1)} %copy-done.6), custom_call_target="tpu_custom_call" | custom-call | flops 2000000000 | bytes 10000000 | tf_op jit(solution)/shard_map/taps/pallas_call | solution.py:314
  7.8 3.1 %collective-permute-start.1 = (bf16[96,128]{1,0:T(8,128)(2,1)S(1)}, bf16[96,128]{1,0:T(8,128)(2,1)S(1)}, u32[]{:S(2)}, u32[]{:S(2)}) collective-permute-start(bf16[96,128]{1,0:T(8,128)(2,1)S(1)} %pad_maximum_fusion), channel_id=1, source_target_pairs={{0,2},{2,0},{4,6},{6,4},{8,10},{10,8},{12,14},{14,12},{16,18},{18,... | collective-permute-start | bytes 73736 | tf_op jit(solution)/shard_map/ppermute | solution.py:325
  10.9 0.0 collective-permute-done.2.refs_5_
  10.9 0.8 %collective-permute-done.1.refs_4_ = bf16[96,128]{1,0:T(8,128)(2,1)S(1)} collective-permute-done((bf16[96,128]{1,0:T(8,128)(2,1)S(1)}, bf16[96,128]{1,0:T(8,128)(2,1)S(1)}, u32[]{:S(2)}, u32[]{:S(2)}) %collective-permute-start.1) | collective-permute-done | bytes 24608 | tf_op jit(solution)/shard_map/ppermute | solution.py:325
  11.8 2.2 %forward.1 = (bf16[96,256]{1,0:T(8,128)(2,1)S(1)}, bf16[96,256]{1,0:T(8,128)(2,1)S(1)}, f32[88,16,128]{2,1,0:T(8,128)S(1)}, bf16[88,16,128]{2,1,0:T(8,128)(2,1)S(1)}) custom-call(s32[1]{0:T(128)} %bitcast.3.core_ref, bf16[96,256]{1,0:T(8,128)(2,1)S(1)} %bitcast.13, s32[27,256]{1,0:T(8,128)S(1)} %bitcast.15, bf16[64,128]{1,0:T(8,128)(2,1)S(1)} %copy-done.5, ...), custom_call_target="tpu_custom_call" | custom-call | tf_op jit(solution)/shard_map/forward/pallas_call | solution.py:331
  14.0 0.5 %collective-permute-start.3 = (bf16[88,16,128]{2,1,0:T(8,128)(2,1)S(1)}, bf16[88,16,128]{2,1,0:T(8,128)(2,1)S(1)}, u32[]{:S(2)}, u32[]{:S(2)}) collective-permute-start(bf16[88,16,128]{2,1,0:T(8,128)(2,1)S(1)} %get-tuple-element.61), channel_id=1, source_target_pairs={{0,2},{2,0},{1,3},{3,1},{4,6},{6,4},{5,7},{7,5},{8,10},{10,8},{9,1... | collective-permute-start | bytes 1081352 | tf_op jit(solution)/shard_map/ppermute | solution.py:349
  14.5 1.3 %collective-permute-done.3.got_ref = bf16[88,16,128]{2,1,0:T(8,128)(2,1)S(1)} collective-permute-done((bf16[88,16,128]{2,1,0:T(8,128)(2,1)S(1)}, bf16[88,16,128]{2,1,0:T(8,128)(2,1)S(1)}, u32[]{:S(2)}, u32[]{:S(2)}) %collective-permute-start.3) | collective-permute-done | bytes 360480 | tf_op jit(solution)/shard_map/ppermute | solution.py:349
  15.8 0.1 split.1
  15.9 2.7 %collective-permute-start.4 = (bf16[22,16,128]{2,1,0:T(8,128)(2,1)S(1)}, bf16[22,16,128]{2,1,0:T(8,128)(2,1)S(1)}, u32[]{:S(2)}, u32[]{:S(2)}) collective-permute-start(bf16[22,16,128]{2,1,0:T(8,128)(2,1)S(1)} %get-tuple-element.67), channel_id=1, source_target_pairs={{0,5},{2,7},{1,4},{3,6},{4,1},{6,3},{5,0},{7,2},{8,13},{10,15},{9,... | collective-permute-start | bytes 270344 | tf_op jit(solution)/shard_map/ppermute | solution.py:361
  18.5 0.4 collective-permute-start.5
  18.9 0.5 %collective-permute-start.6 = (bf16[22,16,128]{2,1,0:T(8,128)(2,1)S(1)}, bf16[22,16,128]{2,1,0:T(8,128)(2,1)S(1)}, u32[]{:S(2)}, u32[]{:S(2)}) collective-permute-start(bf16[22,16,128]{2,1,0:T(8,128)(2,1)S(1)} %get-tuple-element.69), channel_id=1, source_target_pairs={{0,1},{2,6},{1,0},{3,7},{4,5},{6,2},{5,4},{7,3},{8,9},{10,14},{9,8... | collective-permute-start | bytes 270344 | tf_op jit(solution)/shard_map/ppermute | solution.py:361
  19.4 2.3 %backward.1 = (f32[96,256]{1,0:T(8,128)S(1)}, f32[96,128]{1,0:T(8,128)S(1)}, bf16[96,256]{1,0:T(8,128)(2,1)S(1)}) custom-call(s32[1]{0:T(128)} %bitcast.3.core_ref, s32[27,256]{1,0:T(8,128)S(1)} %bitcast.16, f32[96,256]{1,0:T(8,128)S(1)} %get-tuple-element.57.refs_3_.hgrad_ref, bf16[96,256]{1,0:T(8,128)(2,1)S(1)} %get-tuple-element.70.grad_ref, ...), custom_call_target="tpu_custom_call" | custom-call | flops 2000000000 | bytes 10000000 | tf_op jit(solution)/shard_map/backward/pallas_call | solution.py:362
  21.7 0.1 collective-permute-done.4
  21.8 1.9 %collective-permute-done.5 = bf16[22,16,128]{2,1,0:T(8,128)(2,1)S(1)} collective-permute-done((bf16[22,16,128]{2,1,0:T(8,128)(2,1)S(1)}, bf16[22,16,128]{2,1,0:T(8,128)(2,1)S(1)}, u32[]{:S(2)}, u32[]{:S(2)}) %collective-permute-start.5) | collective-permute-done | bytes 90144 | tf_op jit(solution)/shard_map/ppermute | solution.py:361
  23.7 0.0 collective-permute-done.6
  23.7 0.1 add_convert_fusion.2
  23.8 2.3 %collective-permute-start.7 = (bf16[22,16,128]{2,1,0:T(8,128)(2,1)S(1)}, bf16[22,16,128]{2,1,0:T(8,128)(2,1)S(1)}, u32[]{:S(2)}, u32[]{:S(2)}) collective-permute-start(bf16[22,16,128]{2,1,0:T(8,128)(2,1)S(1)} %add_convert_fusion.2), channel_id=1, source_target_pairs={{0,8},{8,0},{16,24},{24,16},{1,9},{9,1},{17,25},{25,17},{2,10},{10... | collective-permute-start | bytes 270344 | tf_op jit(solution)/shard_map/ppermute | solution.py:395
  26.0 1.2 %collective-permute-start.8 = (bf16[96,256]{1,0:T(8,128)(2,1)S(1)}, bf16[96,256]{1,0:T(8,128)(2,1)S(1)}, u32[]{:S(2)}, u32[]{:S(2)}) collective-permute-start(bf16[96,256]{1,0:T(8,128)(2,1)S(1)} %get-tuple-element.77), channel_id=1, source_target_pairs={{0,1},{1,0},{2,3},{3,2},{4,5},{5,4},{6,7},{7,6},{8,9},{9,8},{10,11... | collective-permute-start | bytes 147464 | tf_op jit(solution)/shard_map/ppermute | solution.py:383
  27.2 1.3 %collective-permute-done.7 = bf16[22,16,128]{2,1,0:T(8,128)(2,1)S(1)} collective-permute-done((bf16[22,16,128]{2,1,0:T(8,128)(2,1)S(1)}, bf16[22,16,128]{2,1,0:T(8,128)(2,1)S(1)}, u32[]{:S(2)}, u32[]{:S(2)}) %collective-permute-start.7) | collective-permute-done | bytes 90144 | tf_op jit(solution)/shard_map/ppermute | solution.py:395
  28.6 1.5 %collective-permute-done.8.refs_0_ = bf16[96,256]{1,0:T(8,128)(2,1)S(1)} collective-permute-done((bf16[96,256]{1,0:T(8,128)(2,1)S(1)}, bf16[96,256]{1,0:T(8,128)(2,1)S(1)}, u32[]{:S(2)}, u32[]{:S(2)}) %collective-permute-start.8) | collective-permute-done | bytes 49184 | tf_op jit(solution)/shard_map/ppermute | solution.py:383
  30.1 2.6 %collective-permute-start.9 = (bf16[22,16,128]{2,1,0:T(8,128)(2,1)S(1)}, bf16[22,16,128]{2,1,0:T(8,128)(2,1)S(1)}, u32[]{:S(2)}, u32[]{:S(2)}) collective-permute-start(bf16[22,16,128]{2,1,0:T(8,128)(2,1)S(1)} %add_convert_fusion.1), channel_id=1, source_target_pairs={{0,16},{8,24},{16,0},{24,8},{1,17},{9,25},{17,1},{25,9},{2,18},{10... | collective-permute-start | bytes 270344 | tf_op jit(solution)/shard_map/ppermute | solution.py:395
  32.7 0.1 turn.1
  32.8 0.7 %collective-permute-start.10 = (bf16[96,64]{1,0:T(8,128)(2,1)S(1)}, bf16[96,64]{1,0:T(8,128)(2,1)S(1)}, u32[]{:S(2)}, u32[]{:S(2)}) collective-permute-start(bf16[96,64]{1,0:T(8,128)(2,1)S(1)} %get-tuple-element.82), channel_id=1, source_target_pairs={{2,4},{6,8},{10,12},{14,16},{18,20},{22,24},{26,28},{4,2},{8,6},{1... | collective-permute-start | bytes 36872 | tf_op jit(solution)/shard_map/ppermute | solution.py:409
  33.5 3.0 %collective-permute-done.9 = bf16[22,16,128]{2,1,0:T(8,128)(2,1)S(1)} collective-permute-done((bf16[22,16,128]{2,1,0:T(8,128)(2,1)S(1)}, bf16[22,16,128]{2,1,0:T(8,128)(2,1)S(1)}, u32[]{:S(2)}, u32[]{:S(2)}) %collective-permute-start.9) | collective-permute-done | bytes 90144 | tf_op jit(solution)/shard_map/ppermute | solution.py:395
  36.5 0.0 collective-permute-done.10.refs_1_
  36.5 2.8 %collective-permute-start.13 = (bf16[22,16,128]{2,1,0:T(8,128)(2,1)S(1)}, bf16[22,16,128]{2,1,0:T(8,128)(2,1)S(1)}, u32[]{:S(2)}, u32[]{:S(2)}) collective-permute-start(bf16[22,16,128]{2,1,0:T(8,128)(2,1)S(1)} %add_convert_fusion.refs_0_), channel_id=1, source_target_pairs={{0,5},{2,7},{1,4},{3,6},{4,1},{6,3},{5,0},{7,2},{8,13},{10,15},{9,... | collective-permute-start | bytes 270344 | tf_op jit(solution)/shard_map/ppermute | solution.py:411
  39.4 0.0 collective-permute-start.12
  39.4 0.8 %collective-permute-start.11 = (bf16[22,16,128]{2,1,0:T(8,128)(2,1)S(1)}, bf16[22,16,128]{2,1,0:T(8,128)(2,1)S(1)}, u32[]{:S(2)}, u32[]{:S(2)}) collective-permute-start(bf16[22,16,128]{2,1,0:T(8,128)(2,1)S(1)} %add_convert_fusion.refs_0_), channel_id=1, source_target_pairs={{0,1},{2,6},{1,0},{3,7},{4,5},{6,2},{5,4},{7,3},{8,9},{10,14},{9,8... | collective-permute-start | bytes 270344 | tf_op jit(solution)/shard_map/ppermute | solution.py:411
  40.2 2.2 %collective-permute-done.13.refs_3_ = bf16[22,16,128]{2,1,0:T(8,128)(2,1)S(1)} collective-permute-done((bf16[22,16,128]{2,1,0:T(8,128)(2,1)S(1)}, bf16[22,16,128]{2,1,0:T(8,128)(2,1)S(1)}, u32[]{:S(2)}, u32[]{:S(2)}) %collective-permute-start.13) | collective-permute-done | bytes 90144 | tf_op jit(solution)/shard_map/ppermute | solution.py:411
  42.4 1.8 %collective-permute-done.12.refs_2_ = bf16[22,16,128]{2,1,0:T(8,128)(2,1)S(1)} collective-permute-done((bf16[22,16,128]{2,1,0:T(8,128)(2,1)S(1)}, bf16[22,16,128]{2,1,0:T(8,128)(2,1)S(1)}, u32[]{:S(2)}, u32[]{:S(2)}) %collective-permute-start.12) | collective-permute-done | bytes 90144 | tf_op jit(solution)/shard_map/ppermute | solution.py:411
  44.2 0.0 collective-permute-done.11.refs_1_
  44.2 0.1 collective-permute-start.14
  44.3 0.8 %copy-done.7 = bf16[768,128]{1,0:T(8,128)(2,1)S(1)} copy-done((bf16[768,128]{1,0:T(8,128)(2,1)S(1)}, bf16[768,128]{1,0:T(8,128)(2,1)}, u32[]{:S(2)}) %copy-start.7) | copy-done | bytes 196632
  45.1 1.1 %coarse.1 = bf16[64,128]{1,0:T(8,128)(2,1)} custom-call(bf16[8,64,256]{2,1,0:T(8,128)(2,1)S(1)} %get-tuple-element.54.refs_2_.pick_ref, bf16[96,256]{1,0:T(8,128)(2,1)S(1)} %get-tuple-element.59.hidden_ref, bf16[768,128]{1,0:T(8,128)(2,1)S(1)} %copy-done.7), custom_call_target="tpu_custom_call" | custom-call | flops 2000000000 | bytes 10000000 | tf_op jit(solution)/shard_map/coarse/pallas_call | solution.py:384
  46.3 0.0 collective-permute-done.14.other_ref
  46.3 1.2 %final.1 = (f32[96,2592]{1,0:T(8,128)}, f32[768,128]{1,0:T(8,128)}, f32[96,256]{1,0:T(8,128)}) custom-call(s32[1]{0:T(128)} %bitcast.3.core_ref, bf16[94,16,128]{2,1,0:T(8,128)(2,1)S(1)} %join.1.mine_ref, bf16[94,16,128]{2,1,0:T(8,128)(2,1)S(1)} %collective-permute-done.14.other_ref, f32[96,256]{1,0:T(8,128)S(1)} %get-tuple-element.85.refs_0_, ...), custom_call_target="tpu_custom_call" | custom-call | tf_op jit(solution)/shard_map/final/pallas_call | solution.py:420
  (15 shorter events, 0.1 us)
Async XLA Ops:
  0.6 5.6 %collective-permute-start = (bf16[96,256]{1,0:T(8,128)(2,1)}, bf16[96,256]{1,0:T(8,128)(2,1)S(1)}, u32[]{:S(2)}, u32[]{:S(2)}) collective-permute-start(bf16[96,256]{1,0:T(8,128)(2,1)} %bitcast.10), channel_id=1, source_target_pairs={{0,1},{1,0},{2,3},{3,2},{4,5},{5,4},{6,7},{7,6},{8,9},{9,8},{10,11... | collective-permute-start | bytes 147464 | tf_op jit(solution)/shard_map/ppermute | solution.py:297
  3.7 0.8 %copy-start.1 = (bf16[256,96]{0,1:T(8,128)(2,1)S(1)}, bf16[256,96]{0,1:T(8,128)(2,1)}, u32[]{:S(2)}) copy-start(bf16[256,96]{0,1:T(8,128)(2,1)} %param.6) | copy-start | bytes 147460
  4.5 0.8 %copy-start.3 = (s32[256,27]{0,1:T(8,128)S(1)}, s32[256,27]{0,1:T(8,128)}, u32[]{:S(2)}) copy-start(s32[256,27]{0,1:T(8,128)} %param.7) | copy-start | bytes 82948
  5.3 1.8 %copy-start.6 = (bf16[768,128]{1,0:T(8,128)(2,1)S(1)}, bf16[768,128]{1,0:T(8,128)(2,1)}, u32[]{:S(2)}) copy-start(bf16[768,128]{1,0:T(8,128)(2,1)} %wd_ref.3) | copy-start | bytes 589828
  6.3 0.8 %copy-start.5 = (bf16[64,128]{1,0:T(8,128)(2,1)S(1)}, bf16[64,128]{1,0:T(8,128)(2,1)}, u32[]{:S(2)}) copy-start(bf16[64,128]{1,0:T(8,128)(2,1)} %cgrad_ref.3) | copy-start | bytes 49156
  6.3 0.8 %copy-start.8 = (s32[64,8]{0,1:T(8,128)S(1)}, s32[64,8]{0,1:T(8,128)}, u32[]{:S(2)}) copy-start(s32[64,8]{0,1:T(8,128)} %param.8) | copy-start | bytes 6148
  6.4 4.5 %collective-permute-start.2 = (bf16[96,128]{1,0:T(8,128)(2,1)S(1)}, bf16[96,128]{1,0:T(8,128)(2,1)S(1)}, u32[]{:S(2)}, u32[]{:S(2)}) collective-permute-start(bf16[96,128]{1,0:T(8,128)(2,1)S(1)} %pad_maximum_fusion), channel_id=1, source_target_pairs={{2,4},{6,8},{10,12},{14,16},{18,20},{22,24},{26,28},{4,2},{8,6},{1... | collective-permute-start | bytes 73736 | tf_op jit(solution)/shard_map/ppermute | solution.py:312
  7.1 4.7 %copy-start = (bf16[2592,96]{0,1:T(8,128)(2,1)S(1)}, bf16[2592,96]{0,1:T(8,128)(2,1)}, u32[]{:S(2)}) copy-start(bf16[2592,96]{0,1:T(8,128)(2,1)} %param.9) | copy-start | bytes 1492996
  7.1 4.7 %copy-start.2 = (bf16[256,96]{0,1:T(8,128)(2,1)S(1)}, bf16[256,96]{0,1:T(8,128)(2,1)}, u32[]{:S(2)}) copy-start(bf16[256,96]{0,1:T(8,128)(2,1)} %param.6) | copy-start | bytes 147460
  7.1 4.7 %copy-start.4 = (s32[256,27]{0,1:T(8,128)S(1)}, s32[256,27]{0,1:T(8,128)}, u32[]{:S(2)}) copy-start(s32[256,27]{0,1:T(8,128)} %param.7) | copy-start | bytes 82948
  7.8 3.9 %collective-permute-start.1 = (bf16[96,128]{1,0:T(8,128)(2,1)S(1)}, bf16[96,128]{1,0:T(8,128)(2,1)S(1)}, u32[]{:S(2)}, u32[]{:S(2)}) collective-permute-start(bf16[96,128]{1,0:T(8,128)(2,1)S(1)} %pad_maximum_fusion), channel_id=1, source_target_pairs={{0,2},{2,0},{4,6},{6,4},{8,10},{10,8},{12,14},{14,12},{16,18},{18,... | collective-permute-start | bytes 73736 | tf_op jit(solution)/shard_map/ppermute | solution.py:325
  14.0 1.8 %collective-permute-start.3 = (bf16[88,16,128]{2,1,0:T(8,128)(2,1)S(1)}, bf16[88,16,128]{2,1,0:T(8,128)(2,1)S(1)}, u32[]{:S(2)}, u32[]{:S(2)}) collective-permute-start(bf16[88,16,128]{2,1,0:T(8,128)(2,1)S(1)} %get-tuple-element.61), channel_id=1, source_target_pairs={{0,2},{2,0},{1,3},{3,1},{4,6},{6,4},{5,7},{7,5},{8,10},{10,8},{9,1... | collective-permute-start | bytes 1081352 | tf_op jit(solution)/shard_map/ppermute | solution.py:349
  15.9 5.9 %collective-permute-start.4 = (bf16[22,16,128]{2,1,0:T(8,128)(2,1)S(1)}, bf16[22,16,128]{2,1,0:T(8,128)(2,1)S(1)}, u32[]{:S(2)}, u32[]{:S(2)}) collective-permute-start(bf16[22,16,128]{2,1,0:T(8,128)(2,1)S(1)} %get-tuple-element.67), channel_id=1, source_target_pairs={{0,5},{2,7},{1,4},{3,6},{4,1},{6,3},{5,0},{7,2},{8,13},{10,15},{9,... | collective-permute-start | bytes 270344 | tf_op jit(solution)/shard_map/ppermute | solution.py:361
  18.5 5.2 %collective-permute-start.5 = (bf16[22,16,128]{2,1,0:T(8,128)(2,1)S(1)}, bf16[22,16,128]{2,1,0:T(8,128)(2,1)S(1)}, u32[]{:S(2)}, u32[]{:S(2)}) collective-permute-start(bf16[22,16,128]{2,1,0:T(8,128)(2,1)S(1)} %get-tuple-element.68), channel_id=1, source_target_pairs={{0,4},{2,3},{1,5},{3,2},{4,0},{6,7},{5,1},{7,6},{8,12},{10,11},{9,... | collective-permute-start | bytes 270344 | tf_op jit(solution)/shard_map/ppermute | solution.py:361
  18.9 4.8 %collective-permute-start.6 = (bf16[22,16,128]{2,1,0:T(8,128)(2,1)S(1)}, bf16[22,16,128]{2,1,0:T(8,128)(2,1)S(1)}, u32[]{:S(2)}, u32[]{:S(2)}) collective-permute-start(bf16[22,16,128]{2,1,0:T(8,128)(2,1)S(1)} %get-tuple-element.69), channel_id=1, source_target_pairs={{0,1},{2,6},{1,0},{3,7},{4,5},{6,2},{5,4},{7,3},{8,9},{10,14},{9,8... | collective-permute-start | bytes 270344 | tf_op jit(solution)/shard_map/ppermute | solution.py:361
  23.8 4.8 %collective-permute-start.7 = (bf16[22,16,128]{2,1,0:T(8,128)(2,1)S(1)}, bf16[22,16,128]{2,1,0:T(8,128)(2,1)S(1)}, u32[]{:S(2)}, u32[]{:S(2)}) collective-permute-start(bf16[22,16,128]{2,1,0:T(8,128)(2,1)S(1)} %add_convert_fusion.2), channel_id=1, source_target_pairs={{0,8},{8,0},{16,24},{24,16},{1,9},{9,1},{17,25},{25,17},{2,10},{10... | collective-permute-start | bytes 270344 | tf_op jit(solution)/shard_map/ppermute | solution.py:395
  26.0 4.1 %collective-permute-start.8 = (bf16[96,256]{1,0:T(8,128)(2,1)S(1)}, bf16[96,256]{1,0:T(8,128)(2,1)S(1)}, u32[]{:S(2)}, u32[]{:S(2)}) collective-permute-start(bf16[96,256]{1,0:T(8,128)(2,1)S(1)} %get-tuple-element.77), channel_id=1, source_target_pairs={{0,1},{1,0},{2,3},{3,2},{4,5},{5,4},{6,7},{7,6},{8,9},{9,8},{10,11... | collective-permute-start | bytes 147464 | tf_op jit(solution)/shard_map/ppermute | solution.py:383
  30.1 6.4 %collective-permute-start.9 = (bf16[22,16,128]{2,1,0:T(8,128)(2,1)S(1)}, bf16[22,16,128]{2,1,0:T(8,128)(2,1)S(1)}, u32[]{:S(2)}, u32[]{:S(2)}) collective-permute-start(bf16[22,16,128]{2,1,0:T(8,128)(2,1)S(1)} %add_convert_fusion.1), channel_id=1, source_target_pairs={{0,16},{8,24},{16,0},{24,8},{1,17},{9,25},{17,1},{25,9},{2,18},{10... | collective-permute-start | bytes 270344 | tf_op jit(solution)/shard_map/ppermute | solution.py:395
  32.8 3.7 %collective-permute-start.10 = (bf16[96,64]{1,0:T(8,128)(2,1)S(1)}, bf16[96,64]{1,0:T(8,128)(2,1)S(1)}, u32[]{:S(2)}, u32[]{:S(2)}) collective-permute-start(bf16[96,64]{1,0:T(8,128)(2,1)S(1)} %get-tuple-element.82), channel_id=1, source_target_pairs={{2,4},{6,8},{10,12},{14,16},{18,20},{22,24},{26,28},{4,2},{8,6},{1... | collective-permute-start | bytes 36872 | tf_op jit(solution)/shard_map/ppermute | solution.py:409
  36.5 5.9 %collective-permute-start.13 = (bf16[22,16,128]{2,1,0:T(8,128)(2,1)S(1)}, bf16[22,16,128]{2,1,0:T(8,128)(2,1)S(1)}, u32[]{:S(2)}, u32[]{:S(2)}) collective-permute-start(bf16[22,16,128]{2,1,0:T(8,128)(2,1)S(1)} %add_convert_fusion.refs_0_), channel_id=1, source_target_pairs={{0,5},{2,7},{1,4},{3,6},{4,1},{6,3},{5,0},{7,2},{8,13},{10,15},{9,... | collective-permute-start | bytes 270344 | tf_op jit(solution)/shard_map/ppermute | solution.py:411
  39.4 4.8 %collective-permute-start.12 = (bf16[22,16,128]{2,1,0:T(8,128)(2,1)S(1)}, bf16[22,16,128]{2,1,0:T(8,128)(2,1)S(1)}, u32[]{:S(2)}, u32[]{:S(2)}) collective-permute-start(bf16[22,16,128]{2,1,0:T(8,128)(2,1)S(1)} %add_convert_fusion.refs_0_), channel_id=1, source_target_pairs={{0,4},{2,3},{1,5},{3,2},{4,0},{6,7},{5,1},{7,6},{8,12},{10,11},{9,... | collective-permute-start | bytes 270344 | tf_op jit(solution)/shard_map/ppermute | solution.py:411
  39.4 4.8 %collective-permute-start.11 = (bf16[22,16,128]{2,1,0:T(8,128)(2,1)S(1)}, bf16[22,16,128]{2,1,0:T(8,128)(2,1)S(1)}, u32[]{:S(2)}, u32[]{:S(2)}) collective-permute-start(bf16[22,16,128]{2,1,0:T(8,128)(2,1)S(1)} %add_convert_fusion.refs_0_), channel_id=1, source_target_pairs={{0,1},{2,6},{1,0},{3,7},{4,5},{6,2},{5,4},{7,3},{8,9},{10,14},{9,8... | collective-permute-start | bytes 270344 | tf_op jit(solution)/shard_map/ppermute | solution.py:411
  44.2 0.9 %copy-start.7 = (bf16[768,128]{1,0:T(8,128)(2,1)S(1)}, bf16[768,128]{1,0:T(8,128)(2,1)}, u32[]{:S(2)}) copy-start(bf16[768,128]{1,0:T(8,128)(2,1)} %wd_ref.3) | copy-start | bytes 589828
  44.2 2.0 %collective-permute-start.14 = (bf16[94,16,128]{2,1,0:T(8,128)(2,1)S(1)}, bf16[94,16,128]{2,1,0:T(8,128)(2,1)S(1)}, u32[]{:S(2)}, u32[]{:S(2)}) collective-permute-start(bf16[94,16,128]{2,1,0:T(8,128)(2,1)S(1)} %join.1.mine_ref), channel_id=1, source_target_pairs={{0,2},{2,0},{1,3},{3,1},{4,6},{6,4},{5,7},{7,5},{8,10},{10,8},{9,1... | collective-permute-start | bytes 1155080 | tf_op jit(solution)/shard_map/ppermute | solution.py:419

commit v10 on v9

--- a/solution.py
+++ b/solution.py
@@ -156,8 +156,7 @@
 
 
 def backward_kernel(slabs, core_ref, near_ref, hgrad_ref, grad_ref, w_ref, *refs):
-    base_ref, keep_ref, *refs = refs
-    cross_refs, (drt, drt_far, hot, far, w_back) = refs[:-5], refs[-5:]
+    base_ref, mate_ref, beside_ref, cross_ref, drt, drt_far, hot, far, w_back = refs
     channels, voxels = hgrad_ref.shape
     offsets = near_ref.shape[0]
     lanes = table_lanes(near_ref[...], voxels, slabs, core_ref[0])
@@ -176,27 +175,36 @@
     base_ref[...] = hgrad_ref[...] + mm(drt[...], hot[...], NT)
     back_t = mm(drt_far[...], far[...], NT)
     rims = 2 if slabs == 2 else 3
-    mid = 0 if slabs == 2 else 1
-    rim = [back_t[:, i * RIM : (i + 1) * RIM] for i in range(2 * rims + len(cross_refs))]
-    keep_ref[...] = jnp.concatenate([rim[mid], rim[rims + mid]], axis=1)
-    for i, ref in enumerate(cross_refs):
-        place = 1 if slabs == 2 else 2 * i
-        parts = [rim[place], rim[rims + place], rim[2 * rims + i], jnp.zeros_like(rim[0])]
-        ref[...] = jnp.concatenate(parts, axis=1).astype(BF16)
-
-
-def turn_kernel(base_ref, keep_ref, *refs):
-    got_refs, (sum_ref, cross_ref, mate_ref) = refs[:-3], refs[-3:]
+    rim = [back_t[:, i * RIM : (i + 1) * RIM] for i in range(3 * rims - 1)]
+    mate, cross, side = rim[:rims], rim[rims : 2 * rims], rim[2 * rims :]
+    own, away = (0, (1,)) if slabs == 2 else (1, (0, 2))
+    mate_ref[...] = mate[own]
+    parts = []
+    for place, part in zip(away, side):
+        parts += [mate[place], part]
+    beside_ref[...] = jnp.concatenate(parts, axis=1)
+    cross_ref[...] = jnp.concatenate(cross, axis=1).astype(BF16)
+
+
+def cross_turn_kernel(own, beside_ref, got_ref, home_ref, *edge_refs):
+    got = got_ref[...].astype(F32)
+    rim = [got[:, i * RIM : (i + 1) * RIM] for i in range(got.shape[1] // RIM)]
+    home_ref[...] = rim.pop(own)
+    for i, (ref, part) in enumerate(zip(edge_refs, rim)):
+        mine = beside_ref[:, 2 * i * RIM : 2 * (i + 1) * RIM]
+        ref[...] = (mine + jnp.concatenate([jnp.zeros_like(part), part], axis=1)).astype(BF16)
+
+
+def slab_turn_kernel(mate_ref, home_ref, *refs):
+    got_refs, (rider_ref, sum_ref) = refs[:-2], refs[-2:]
     got = got_refs[0][...].astype(F32)
     for ref in got_refs[1:]:
         got += ref[...].astype(F32)
-    sum_ref[:, RIM:] = base_ref[:, RIM:]
-    sum_ref[:, :RIM] = base_ref[:, :RIM] + got[:, 2 * RIM : 3 * RIM]
-    pair = keep_ref[...] + got[:, : 2 * RIM]
-    cross_ref[...] = pair[:, RIM:].astype(BF16)
-    pair = pair.astype(BF16)
-    for i in range(mate_ref.shape[0]):
-        mate_ref[i] = pair[i * TILE : (i + 1) * TILE, :]
+    mate = mate_ref[...] + got[:, :RIM]
+    sum_ref[...] = home_ref[...] + got[:, RIM:]
+    pair = jnp.concatenate([mate, jnp.zeros_like(mate)], axis=1).astype(BF16)
+    for i in range(rider_ref.shape[0]):
+        rider_ref[i] = pair[i * TILE : (i + 1) * TILE, :]
 
 
 def step_of(steps, core):
@@ -220,12 +228,12 @@
 
 
 def final_kernel(taps, size, core_ref, mine_ref, other_ref, *refs):
-    base_ref, cross_ref, conv_ref, down_ref, grad_ref = refs
+    base_ref, home_ref, conv_ref, down_ref, grad_ref = refs
     channels, conv_columns = conv_ref.shape
     grad_ref[:, RIM:] = base_ref[:, RIM:]
     for i in range(channels // TILE):
         rows = slice(i * TILE, (i + 1) * TILE)
-        total = base_ref[rows, :RIM] + cross_ref[rows, :].astype(F32)
+        total = base_ref[rows, :RIM] + home_ref[rows, :]
         grad_ref[rows, :RIM] = total + other_ref[size + i][:, :RIM].astype(F32)
     for core in range(2):
 
@@ -359,13 +367,14 @@
     )(core, here, keep, got)
     sent, grad = lax.optimization_barrier((sent, grad))
     got = [lax.ppermute(x, SPLIT, route) for x, route in zip(sent, routes)]
-    base, stay, *edges = pl.pallas_call(
+    base, mate, stay, cross = pl.pallas_call(
         functools.partial(backward_kernel, slabs),
-        out_shape=[
+        out_shape=(
             jax.ShapeDtypeStruct((channels, voxels), F32),
-            jax.ShapeDtypeStruct((channels, 2 * RIM), F32),
-        ]
-        + [jax.ShapeDtypeStruct((channels, 4 * RIM), BF16)] * len(beside),
+            jax.ShapeDtypeStruct((channels, RIM), F32),
+            jax.ShapeDtypeStruct((channels, 2 * len(beside) * RIM), F32),
+            jax.ShapeDtypeStruct((channels, row.shape[1]), BF16),
+        ),
         in_specs=[smem] + [vmem] * 4,
         scratch_shapes=[
             pltpu.VMEM((channels, offsets * voxels), BF16),
@@ -378,9 +387,7 @@
         cost_estimate=light,
         name="backward",
     )(core, neighbours_t, hgrad, grad, w_conv_t)
-    got, stay, edges, base = lax.optimization_barrier((got, stay, edges, base))
-    back = beside if slabs == 2 else beside[::-1]
-    edges = [lax.ppermute(x, "slab", p) for x, p in zip(edges, back)]
+    got, cross, base = lax.optimization_barrier((got, cross, base))
     coarse = pl.pallas_call(
         coarse_kernel,
         out_shape=jax.ShapeDtypeStruct(coarse_grad.shape, BF16),
@@ -389,25 +396,34 @@
         name="coarse",
     )(pick, hidden, w_down)
     total = functools.reduce(lambda x, y: x + y.astype(F32), got, keep).astype(BF16)
-    far_bits = sizes["far"].bit_length() - 1
-    for bit in range(far_bits):
-        pairs = [(i, i ^ (1 << bit)) for i in range(sizes["far"])]
-        got = lax.ppermute(total, "far", pairs)
-        total = (total.astype(F32) + got.astype(F32)).astype(BF16)
-        if bit == 0:
-            total, edges = lax.optimization_barrier((total, edges))
-    base, cross, mate = pl.pallas_call(
-        turn_kernel,
-        out_shape=(
-            jax.ShapeDtypeStruct((channels, voxels), F32),
-            jax.ShapeDtypeStruct((channels, RIM), BF16),
+    parts = [total]
+    for step in range(1, sizes["far"]):
+        parts.append(lax.ppermute(total, "far", [(i, i ^ step) for i in range(sizes["far"])]))
+    cross = lax.ppermute(cross, RING, crossings)
+    parts = [x.astype(F32) for x in parts]
+    while len(parts) > 1:
+        parts = [x + y for x, y in zip(parts[0::2], parts[1::2])]
+    total = parts[0].astype(BF16)
+    total, cross = lax.optimization_barrier((total, cross))
+    home, *edges = pl.pallas_call(
+        functools.partial(cross_turn_kernel, 0 if slabs == 2 else 1),
+        out_shape=[jax.ShapeDtypeStruct((channels, RIM), F32)]
+        + [jax.ShapeDtypeStruct((channels, 2 * RIM), BF16)] * len(beside),
+        compiler_params=params,
+        name="cross_turn",
+    )(stay, cross)
+    back = beside if slabs == 2 else beside[::-1]
+    edges = [lax.ppermute(x, "slab", p) for x, p in zip(edges, back)]
+    edges, coarse = lax.optimization_barrier((edges, coarse))
+    mate, home = pl.pallas_call(
+        slab_turn_kernel,
+        out_shape=(
             jax.ShapeDtypeStruct((channels // TILE, TILE, LANES), BF16),
-        ),
-        compiler_params=params,
-        name="turn",
-    )(base, stay, *edges)
-    cross = lax.ppermute(cross, RING, crossings)
-    total, cross = lax.optimization_barrier((total, cross))
+            jax.ShapeDtypeStruct((channels, RIM), F32),
+        ),
+        compiler_params=params,
+        name="slab_turn",
+    )(mate, home, *edges)
     got = [lax.ppermute(total, SPLIT, route) for route in routes[::-1]]
     mine = pl.pallas_call(
         functools.partial(join_kernel, orders[::-1]),
@@ -427,7 +443,7 @@
         in_specs=[smem] + [vmem] * 4,
         compiler_params=params,
         name="final",
-    )(core, mine, other, base, cross)
+    )(core, mine, other, base, home)
     return coarse, grad_input_t.T, conv_wgrad_t.T, down_wgrad
 
 

time: 47.8 us -> 46.3 us (0.969)
  waiting for transfers between devices: 14.1 us -> 12.9 us
  local copies, waits for them, and re-layouts: 2.45 us -> 1.64 us
    ppermute x3, waiting for transfers between devices: 4.01 us -> 0.01 us  [on_device(): got = [lax.ppermute(total, SPLIT, route) for route in routes[::-1]]]
    ppermute x1, waiting for transfers between devices: 0.01 us -> 1.7 us  [on_device(): other = lax.ppermute(mine, 'core', swap)]
    ppermute x2 -> x3, waiting for transfers between devices: 4.37 us -> 5.73 us  [on_device(): lax.ppermute(total, 'far', [(i, i ^ step) for i in range(sizes['far'])])]
    unnamed x18, local copies, waits for them, and re-layouts: 2.44 us -> 1.63 us
    pallas_call x2 -> x3, Pallas kernels: 2.39 us -> 2.61 us  [the longest x1 2.53 us: on_device(): pl.pallas_call(functools.partial(backward_kernel, slabs), out_shape=(jax....]
    ppermute x2 -> x3, starting transfers between devices: 4.84 us -> 4.92 us  [on_device(): lax.ppermute(total, 'far', [(i, i ^ step) for i in range(sizes['far'])])]
  transfers between devices with their start and end apart: 15 -> 16, of which waited for: 9 -> 7; matrix products, arithmetic and copies ran while one was open for 0% -> 0% of each run, Pallas kernels for 11% -> 12%
where the time goes in v10:
time: 46.3 us; the launch traced here: 46 us
  starting transfers between devices  21.4 us (46%)
  waiting for transfers between devices  12.9 us (28%)
  Pallas kernels  8.99 us (19%)
  local copies, waits for them, and re-layouts  1.64 us (4%)
  between operations  0.85 us (2%)
    ppermute x3, waiting for transfers between devices, on_device(): lax.ppermute(total, 'far', [(i, i ^ step) for i in range(sizes['far'])])  5.73 us
    ppermute x3, starting transfers between devices, on_device(): lax.ppermute(total, 'far', [(i, i ^ step) for i in range(sizes['far'])])  4.92 us
    ppermute x3, starting transfers between devices, on_device(): got = [lax.ppermute(x, SPLIT, route) for x, route in zip(sent, routes)]  3.57 us
    ppermute x3, starting transfers between devices, on_device(): got = [lax.ppermute(total, SPLIT, route) for route in routes[::-1]]  3.55 us
    ppermute x1, starting transfers between devices, on_device(): mate = lax.ppermute(row, RING, mates)  3.08 us
    ppermute x1, starting transfers between devices, on_device(): side = [lax.ppermute(features_t, 'slab', pairs) for pairs in beside]  3.03 us
    pallas_call x1, Pallas kernels, on_device(): pl.pallas_call(functools.partial(backward_kernel, slabs), out_shape=(jax....  2.53 us
    pallas_call x1, Pallas kernels, on_device(): pl.pallas_call(functools.partial(forward_kernel, slabs), out_shape=(jax.S...  2.23 us
  transfers between devices with their start and end apart: 16, of which 7 were waited for; matrix products, arithmetic and copies ran while one was open for 0% of the time, Pallas kernels for 12%

profile of v10, /device:TPU:0, one launch (start us, length us, event | category | flops | bytes accessed | tf_op | source)
XLA Modules:
  0.0 46.0 jit_solution(17757041780576371172)
XLA Ops:
  0.6 3.0 %collective-permute-start = (bf16[96,256]{1,0:T(8,128)(2,1)}, bf16[96,256]{1,0:T(8,128)(2,1)S(1)}, u32[]{:S(2)}, u32[]{:S(2)}) collective-permute-start(bf16[96,256]{1,0:T(8,128)(2,1)} %bitcast.10), channel_id=1, source_target_pairs={{0,1},{1,0},{2,3},{3,2},{4,5},{5,4},{6,7},{7,6},{8,9},{9,8},{10,11... | collective-permute-start | bytes 147464 | tf_op jit(solution)/shard_map/ppermute | solution.py:305
  3.7 0.8 %copy-done.1 = bf16[256,96]{0,1:T(8,128)(2,1)S(1)} copy-done((bf16[256,96]{0,1:T(8,128)(2,1)S(1)}, bf16[256,96]{0,1:T(8,128)(2,1)}, u32[]{:S(2)}) %copy-start.1) | copy-done | bytes 49176
  4.5 0.8 %copy-done.3 = s32[256,27]{0,1:T(8,128)S(1)} copy-done((s32[256,27]{0,1:T(8,128)S(1)}, s32[256,27]{0,1:T(8,128)}, u32[]{:S(2)}) %copy-start.3) | copy-done | bytes 27672
  5.3 1.0 %gather.1 = (bf16[2592,128]{1,0:T(8,128)(2,1)S(1)}, bf16[2592,128]{1,0:T(8,128)(2,1)S(1)}) custom-call(bf16[96,256]{1,0:T(8,128)(2,1)S(1)} %bitcast.11, s32[27,256]{1,0:T(8,128)S(1)} %bitcast.14), custom_call_target="tpu_custom_call" | custom-call | flops 2000000000 | bytes 10000000 | tf_op jit(solution)/shard_map/gather/pallas_call | solution.py:306
  6.2 0.0 collective-permute-done
  6.3 0.0 copy-start.5
  6.3 0.0 copy-start.8
  6.3 0.1 pad_maximum_fusion
  6.4 0.7 %collective-permute-start.2 = (bf16[96,128]{1,0:T(8,128)(2,1)S(1)}, bf16[96,128]{1,0:T(8,128)(2,1)S(1)}, u32[]{:S(2)}, u32[]{:S(2)}) collective-permute-start(bf16[96,128]{1,0:T(8,128)(2,1)S(1)} %pad_maximum_fusion), channel_id=1, source_target_pairs={{2,4},{6,8},{10,12},{14,16},{18,20},{22,24},{26,28},{4,2},{8,6},{1... | collective-permute-start | bytes 73736 | tf_op jit(solution)/shard_map/ppermute | solution.py:320
  7.1 0.0 copy-start
  7.1 0.0 copy-start.2
  7.1 0.0 copy-start.4
  7.1 0.7 %taps.1 = (bf16[8,64,256]{2,1,0:T(8,128)(2,1)S(1)}, f32[96,256]{1,0:T(8,128)S(1)}) custom-call(s32[8,64]{1,0:T(8,128)S(1)} %bitcast.17, bf16[64,128]{1,0:T(8,128)(2,1)S(1)} %copy-done.5, bf16[768,128]{1,0:T(8,128)(2,1)S(1)} %copy-done.6), custom_call_target="tpu_custom_call" | custom-call | flops 2000000000 | bytes 10000000 | tf_op jit(solution)/shard_map/taps/pallas_call | solution.py:322
  7.8 3.1 %collective-permute-start.1 = (bf16[96,128]{1,0:T(8,128)(2,1)S(1)}, bf16[96,128]{1,0:T(8,128)(2,1)S(1)}, u32[]{:S(2)}, u32[]{:S(2)}) collective-permute-start(bf16[96,128]{1,0:T(8,128)(2,1)S(1)} %pad_maximum_fusion), channel_id=1, source_target_pairs={{0,2},{2,0},{4,6},{6,4},{8,10},{10,8},{12,14},{14,12},{16,18},{18,... | collective-permute-start | bytes 73736 | tf_op jit(solution)/shard_map/ppermute | solution.py:333
  10.9 0.0 collective-permute-done.2.refs_5_
  10.9 0.8 %collective-permute-done.1.refs_4_ = bf16[96,128]{1,0:T(8,128)(2,1)S(1)} collective-permute-done((bf16[96,128]{1,0:T(8,128)(2,1)S(1)}, bf16[96,128]{1,0:T(8,128)(2,1)S(1)}, u32[]{:S(2)}, u32[]{:S(2)}) %collective-permute-start.1) | collective-permute-done | bytes 24608 | tf_op jit(solution)/shard_map/ppermute | solution.py:333
  11.8 2.2 %forward.1 = (bf16[96,256]{1,0:T(8,128)(2,1)S(1)}, bf16[96,256]{1,0:T(8,128)(2,1)S(1)}, f32[88,16,128]{2,1,0:T(8,128)S(1)}, bf16[88,16,128]{2,1,0:T(8,128)(2,1)S(1)}) custom-call(s32[1]{0:T(128)} %bitcast.core_ref, bf16[96,256]{1,0:T(8,128)(2,1)S(1)} %bitcast.13, s32[27,256]{1,0:T(8,128)S(1)} %bitcast.15, bf16[64,128]{1,0:T(8,128)(2,1)S(1)} %copy-done.5, ...), custom_call_target="tpu_custom_call" | custom-call | tf_op jit(solution)/shard_map/forward/pallas_call | solution.py:339
  14.0 0.5 %collective-permute-start.3 = (bf16[88,16,128]{2,1,0:T(8,128)(2,1)S(1)}, bf16[88,16,128]{2,1,0:T(8,128)(2,1)S(1)}, u32[]{:S(2)}, u32[]{:S(2)}) collective-permute-start(bf16[88,16,128]{2,1,0:T(8,128)(2,1)S(1)} %get-tuple-element.61), channel_id=1, source_target_pairs={{0,2},{2,0},{1,3},{3,1},{4,6},{6,4},{5,7},{7,5},{8,10},{10,8},{9,1... | collective-permute-start | bytes 1081352 | tf_op jit(solution)/shard_map/ppermute | solution.py:357
  14.5 1.3 %collective-permute-done.3.got_ref = bf16[88,16,128]{2,1,0:T(8,128)(2,1)S(1)} collective-permute-done((bf16[88,16,128]{2,1,0:T(8,128)(2,1)S(1)}, bf16[88,16,128]{2,1,0:T(8,128)(2,1)S(1)}, u32[]{:S(2)}, u32[]{:S(2)}) %collective-permute-start.3) | collective-permute-done | bytes 360480 | tf_op jit(solution)/shard_map/ppermute | solution.py:357
  15.8 0.1 split.1
  15.9 2.7 %collective-permute-start.4 = (bf16[22,16,128]{2,1,0:T(8,128)(2,1)S(1)}, bf16[22,16,128]{2,1,0:T(8,128)(2,1)S(1)}, u32[]{:S(2)}, u32[]{:S(2)}) collective-permute-start(bf16[22,16,128]{2,1,0:T(8,128)(2,1)S(1)} %get-tuple-element.69), channel_id=1, source_target_pairs={{0,5},{2,7},{1,4},{3,6},{4,1},{6,3},{5,0},{7,2},{8,13},{10,15},{9,... | collective-permute-start | bytes 270344 | tf_op jit(solution)/shard_map/ppermute | solution.py:369
  18.5 0.4 collective-permute-start.5
  18.9 0.5 %collective-permute-start.6 = (bf16[22,16,128]{2,1,0:T(8,128)(2,1)S(1)}, bf16[22,16,128]{2,1,0:T(8,128)(2,1)S(1)}, u32[]{:S(2)}, u32[]{:S(2)}) collective-permute-start(bf16[22,16,128]{2,1,0:T(8,128)(2,1)S(1)} %get-tuple-element.71), channel_id=1, source_target_pairs={{0,1},{2,6},{1,0},{3,7},{4,5},{6,2},{5,4},{7,3},{8,9},{10,14},{9,8... | collective-permute-start | bytes 270344 | tf_op jit(solution)/shard_map/ppermute | solution.py:369
  19.4 2.5 %backward.1 = (f32[96,256]{1,0:T(8,128)S(1)}, f32[96,64]{1,0:T(8,128)S(1)}, f32[96,128]{1,0:T(8,128)S(1)}, bf16[96,128]{1,0:T(8,128)(2,1)S(1)}) custom-call(s32[1]{0:T(128)} %bitcast.core_ref, s32[27,256]{1,0:T(8,128)S(1)} %bitcast.16, f32[96,256]{1,0:T(8,128)S(1)} %get-tuple-element.55.refs_3_.hgrad_ref, bf16[96,256]{1,0:T(8,128)(2,1)S(1)} %get-tuple-element.66.grad_ref, ...), custom_call_target="tpu_custom_call" | custom-call | flops 2000000000 | bytes 10000000 | tf_op jit(solution)/shard_map/backward/pallas_call | solution.py:370
  22.0 1.7 %collective-permute-done.5 = bf16[22,16,128]{2,1,0:T(8,128)(2,1)S(1)} collective-permute-done((bf16[22,16,128]{2,1,0:T(8,128)(2,1)S(1)}, bf16[22,16,128]{2,1,0:T(8,128)(2,1)S(1)}, u32[]{:S(2)}, u32[]{:S(2)}) %collective-permute-start.5) | collective-permute-done | bytes 90144 | tf_op jit(solution)/shard_map/ppermute | solution.py:369
  23.7 0.0 collective-permute-done.6
  23.7 0.1 add_convert_fusion.1
  23.8 0.0 copy-start.7
  23.8 4.3 %collective-permute-start.9 = (bf16[22,16,128]{2,1,0:T(8,128)(2,1)S(1)}, bf16[22,16,128]{2,1,0:T(8,128)(2,1)S(1)}, u32[]{:S(2)}, u32[]{:S(2)}) collective-permute-start(bf16[22,16,128]{2,1,0:T(8,128)(2,1)S(1)} %add_convert_fusion.1), channel_id=1, source_target_pairs={{0,24},{8,16},{16,8},{24,0},{1,25},{9,17},{17,9},{25,1},{2,26},{10... | collective-permute-start | bytes 270344 | tf_op jit(solution)/shard_map/ppermute | solution.py:401
  28.1 0.6 %collective-permute-start.7 = (bf16[22,16,128]{2,1,0:T(8,128)(2,1)S(1)}, bf16[22,16,128]{2,1,0:T(8,128)(2,1)S(1)}, u32[]{:S(2)}, u32[]{:S(2)}) collective-permute-start(bf16[22,16,128]{2,1,0:T(8,128)(2,1)S(1)} %add_convert_fusion.1), channel_id=1, source_target_pairs={{0,8},{8,0},{16,24},{24,16},{1,9},{9,1},{17,25},{25,17},{2,10},{10... | collective-permute-start | bytes 270344 | tf_op jit(solution)/shard_map/ppermute | solution.py:401
  28.7 0.7 %collective-permute-start.10 = (bf16[96,128]{1,0:T(8,128)(2,1)S(1)}, bf16[96,128]{1,0:T(8,128)(2,1)S(1)}, u32[]{:S(2)}, u32[]{:S(2)}) collective-permute-start(bf16[96,128]{1,0:T(8,128)(2,1)S(1)} %get-tuple-element.77), channel_id=1, source_target_pairs={{2,4},{6,8},{10,12},{14,16},{18,20},{22,24},{26,28},{4,2},{8,6},{1... | collective-permute-start | bytes 73736 | tf_op jit(solution)/shard_map/ppermute | solution.py:402
  29.4 2.2 %collective-permute-done.9 = bf16[22,16,128]{2,1,0:T(8,128)(2,1)S(1)} collective-permute-done((bf16[22,16,128]{2,1,0:T(8,128)(2,1)S(1)}, bf16[22,16,128]{2,1,0:T(8,128)(2,1)S(1)}, u32[]{:S(2)}, u32[]{:S(2)}) %collective-permute-start.9) | collective-permute-done | bytes 90144 | tf_op jit(solution)/shard_map/ppermute | solution.py:401
  31.6 3.5 %collective-permute-done.8 = bf16[22,16,128]{2,1,0:T(8,128)(2,1)S(1)} collective-permute-done((bf16[22,16,128]{2,1,0:T(8,128)(2,1)S(1)}, bf16[22,16,128]{2,1,0:T(8,128)(2,1)S(1)}, u32[]{:S(2)}, u32[]{:S(2)}) %collective-permute-start.8) | collective-permute-done | bytes 90144 | tf_op jit(solution)/shard_map/ppermute | solution.py:401
  35.1 0.0 collective-permute-done.7
  35.1 0.1 add_convert_fusion.refs_0_
  35.1 0.0 collective-permute-done.10.got_ref
  35.2 2.0 %collective-permute-start.14 = (bf16[22,16,128]{2,1,0:T(8,128)(2,1)S(1)}, bf16[22,16,128]{2,1,0:T(8,128)(2,1)S(1)}, u32[]{:S(2)}, u32[]{:S(2)}) collective-permute-start(bf16[22,16,128]{2,1,0:T(8,128)(2,1)S(1)} %add_convert_fusion.refs_0_), channel_id=1, source_target_pairs={{0,5},{2,7},{1,4},{3,6},{4,1},{6,3},{5,0},{7,2},{8,13},{10,15},{9,... | collective-permute-start | bytes 270344 | tf_op jit(solution)/shard_map/ppermute | solution.py:427
  37.2 0.9 %collective-permute-start.13 = (bf16[22,16,128]{2,1,0:T(8,128)(2,1)S(1)}, bf16[22,16,128]{2,1,0:T(8,128)(2,1)S(1)}, u32[]{:S(2)}, u32[]{:S(2)}) collective-permute-start(bf16[22,16,128]{2,1,0:T(8,128)(2,1)S(1)} %add_convert_fusion.refs_0_), channel_id=1, source_target_pairs={{0,4},{2,3},{1,5},{3,2},{4,0},{6,7},{5,1},{7,6},{8,12},{10,11},{9,... | collective-permute-start | bytes 270344 | tf_op jit(solution)/shard_map/ppermute | solution.py:427
  38.1 0.6 %collective-permute-start.12 = (bf16[22,16,128]{2,1,0:T(8,128)(2,1)S(1)}, bf16[22,16,128]{2,1,0:T(8,128)(2,1)S(1)}, u32[]{:S(2)}, u32[]{:S(2)}) collective-permute-start(bf16[22,16,128]{2,1,0:T(8,128)(2,1)S(1)} %add_convert_fusion.refs_0_), channel_id=1, source_target_pairs={{0,1},{2,6},{1,0},{3,7},{4,5},{6,2},{5,4},{7,3},{8,9},{10,14},{9,8... | collective-permute-start | bytes 270344 | tf_op jit(solution)/shard_map/ppermute | solution.py:427
  38.7 1.4 %collective-permute-start.11 = (bf16[96,128]{1,0:T(8,128)(2,1)S(1)}, bf16[96,128]{1,0:T(8,128)(2,1)S(1)}, u32[]{:S(2)}, u32[]{:S(2)}) collective-permute-start(bf16[96,128]{1,0:T(8,128)(2,1)S(1)} %get-tuple-element.79), channel_id=1, source_target_pairs={{0,1},{1,0},{2,3},{3,2},{4,5},{5,4},{6,7},{7,6},{8,9},{9,8},{10,11... | collective-permute-start | bytes 73736 | tf_op jit(solution)/shard_map/ppermute | solution.py:416
  40.2 1.1 %coarse.1 = bf16[64,128]{1,0:T(8,128)(2,1)} custom-call(bf16[8,64,256]{2,1,0:T(8,128)(2,1)S(1)} %get-tuple-element.58.refs_2_.pick_ref, bf16[96,256]{1,0:T(8,128)(2,1)S(1)} %get-tuple-element.80.hidden_ref, bf16[768,128]{1,0:T(8,128)(2,1)S(1)} %copy-done.7), custom_call_target="tpu_custom_call" | custom-call | flops 2000000000 | bytes 10000000 | tf_op jit(solution)/shard_map/coarse/pallas_call | solution.py:391
  41.3 1.5 %collective-permute-done.11.refs_0_ = bf16[96,128]{1,0:T(8,128)(2,1)S(1)} collective-permute-done((bf16[96,128]{1,0:T(8,128)(2,1)S(1)}, bf16[96,128]{1,0:T(8,128)(2,1)S(1)}, u32[]{:S(2)}, u32[]{:S(2)}) %collective-permute-start.11) | collective-permute-done | bytes 24608 | tf_op jit(solution)/shard_map/ppermute | solution.py:416
  42.9 0.1 slab_turn.1
  42.9 0.0 collective-permute-done.14.refs_3_
  42.9 0.0 collective-permute-done.12.refs_1_
  43.0 0.1 collective-permute-start.15
  43.1 1.7 %collective-permute-done.15.other_ref = bf16[94,16,128]{2,1,0:T(8,128)(2,1)S(1)} collective-permute-done((bf16[94,16,128]{2,1,0:T(8,128)(2,1)S(1)}, bf16[94,16,128]{2,1,0:T(8,128)(2,1)S(1)}, u32[]{:S(2)}, u32[]{:S(2)}) %collective-permute-start.15) | collective-permute-done | bytes 385056 | tf_op jit(solution)/shard_map/ppermute | solution.py:435
  44.8 1.2 %final.1 = (f32[96,2592]{1,0:T(8,128)}, f32[768,128]{1,0:T(8,128)}, f32[96,256]{1,0:T(8,128)}) custom-call(s32[1]{0:T(128)} %bitcast.core_ref, bf16[94,16,128]{2,1,0:T(8,128)(2,1)S(1)} %join.1.mine_ref, bf16[94,16,128]{2,1,0:T(8,128)(2,1)S(1)} %collective-permute-done.15.other_ref, f32[96,256]{1,0:T(8,128)S(1)} %get-tuple-element.87.refs_0_, ...), custom_call_target="tpu_custom_call" | custom-call | tf_op jit(solution)/shard_map/final/pallas_call | solution.py:436
  (17 shorter events, 0.1 us)
Async XLA Ops:
  0.6 5.6 %collective-permute-start = (bf16[96,256]{1,0:T(8,128)(2,1)}, bf16[96,256]{1,0:T(8,128)(2,1)S(1)}, u32[]{:S(2)}, u32[]{:S(2)}) collective-permute-start(bf16[96,256]{1,0:T(8,128)(2,1)} %bitcast.10), channel_id=1, source_target_pairs={{0,1},{1,0},{2,3},{3,2},{4,5},{5,4},{6,7},{7,6},{8,9},{9,8},{10,11... | collective-permute-start | bytes 147464 | tf_op jit(solution)/shard_map/ppermute | solution.py:305
  3.7 0.8 %copy-start.1 = (bf16[256,96]{0,1:T(8,128)(2,1)S(1)}, bf16[256,96]{0,1:T(8,128)(2,1)}, u32[]{:S(2)}) copy-start(bf16[256,96]{0,1:T(8,128)(2,1)} %param.6) | copy-start | bytes 147460
  4.5 0.8 %copy-start.3 = (s32[256,27]{0,1:T(8,128)S(1)}, s32[256,27]{0,1:T(8,128)}, u32[]{:S(2)}) copy-start(s32[256,27]{0,1:T(8,128)} %param.7) | copy-start | bytes 82948
  5.3 1.8 %copy-start.6 = (bf16[768,128]{1,0:T(8,128)(2,1)S(1)}, bf16[768,128]{1,0:T(8,128)(2,1)}, u32[]{:S(2)}) copy-start(bf16[768,128]{1,0:T(8,128)(2,1)} %wd_ref.3) | copy-start | bytes 589828
  6.3 0.8 %copy-start.5 = (bf16[64,128]{1,0:T(8,128)(2,1)S(1)}, bf16[64,128]{1,0:T(8,128)(2,1)}, u32[]{:S(2)}) copy-start(bf16[64,128]{1,0:T(8,128)(2,1)} %cgrad_ref.3) | copy-start | bytes 49156
  6.3 0.8 %copy-start.8 = (s32[64,8]{0,1:T(8,128)S(1)}, s32[64,8]{0,1:T(8,128)}, u32[]{:S(2)}) copy-start(s32[64,8]{0,1:T(8,128)} %param.8) | copy-start | bytes 6148
  6.4 4.5 %collective-permute-start.2 = (bf16[96,128]{1,0:T(8,128)(2,1)S(1)}, bf16[96,128]{1,0:T(8,128)(2,1)S(1)}, u32[]{:S(2)}, u32[]{:S(2)}) collective-permute-start(bf16[96,128]{1,0:T(8,128)(2,1)S(1)} %pad_maximum_fusion), channel_id=1, source_target_pairs={{2,4},{6,8},{10,12},{14,16},{18,20},{22,24},{26,28},{4,2},{8,6},{1... | collective-permute-start | bytes 73736 | tf_op jit(solution)/shard_map/ppermute | solution.py:320
  7.1 4.7 %copy-start = (bf16[2592,96]{0,1:T(8,128)(2,1)S(1)}, bf16[2592,96]{0,1:T(8,128)(2,1)}, u32[]{:S(2)}) copy-start(bf16[2592,96]{0,1:T(8,128)(2,1)} %param.9) | copy-start | bytes 1492996
  7.1 4.7 %copy-start.2 = (bf16[256,96]{0,1:T(8,128)(2,1)S(1)}, bf16[256,96]{0,1:T(8,128)(2,1)}, u32[]{:S(2)}) copy-start(bf16[256,96]{0,1:T(8,128)(2,1)} %param.6) | copy-start | bytes 147460
  7.1 4.7 %copy-start.4 = (s32[256,27]{0,1:T(8,128)S(1)}, s32[256,27]{0,1:T(8,128)}, u32[]{:S(2)}) copy-start(s32[256,27]{0,1:T(8,128)} %param.7) | copy-start | bytes 82948
  7.8 3.9 %collective-permute-start.1 = (bf16[96,128]{1,0:T(8,128)(2,1)S(1)}, bf16[96,128]{1,0:T(8,128)(2,1)S(1)}, u32[]{:S(2)}, u32[]{:S(2)}) collective-permute-start(bf16[96,128]{1,0:T(8,128)(2,1)S(1)} %pad_maximum_fusion), channel_id=1, source_target_pairs={{0,2},{2,0},{4,6},{6,4},{8,10},{10,8},{12,14},{14,12},{16,18},{18,... | collective-permute-start | bytes 73736 | tf_op jit(solution)/shard_map/ppermute | solution.py:333
  14.0 1.8 %collective-permute-start.3 = (bf16[88,16,128]{2,1,0:T(8,128)(2,1)S(1)}, bf16[88,16,128]{2,1,0:T(8,128)(2,1)S(1)}, u32[]{:S(2)}, u32[]{:S(2)}) collective-permute-start(bf16[88,16,128]{2,1,0:T(8,128)(2,1)S(1)} %get-tuple-element.61), channel_id=1, source_target_pairs={{0,2},{2,0},{1,3},{3,1},{4,6},{6,4},{5,7},{7,5},{8,10},{10,8},{9,1... | collective-permute-start | bytes 1081352 | tf_op jit(solution)/shard_map/ppermute | solution.py:357
  15.9 6.1 %collective-permute-start.4 = (bf16[22,16,128]{2,1,0:T(8,128)(2,1)S(1)}, bf16[22,16,128]{2,1,0:T(8,128)(2,1)S(1)}, u32[]{:S(2)}, u32[]{:S(2)}) collective-permute-start(bf16[22,16,128]{2,1,0:T(8,128)(2,1)S(1)} %get-tuple-element.69), channel_id=1, source_target_pairs={{0,5},{2,7},{1,4},{3,6},{4,1},{6,3},{5,0},{7,2},{8,13},{10,15},{9,... | collective-permute-start | bytes 270344 | tf_op jit(solution)/shard_map/ppermute | solution.py:369
  18.5 5.2 %collective-permute-start.5 = (bf16[22,16,128]{2,1,0:T(8,128)(2,1)S(1)}, bf16[22,16,128]{2,1,0:T(8,128)(2,1)S(1)}, u32[]{:S(2)}, u32[]{:S(2)}) collective-permute-start(bf16[22,16,128]{2,1,0:T(8,128)(2,1)S(1)} %get-tuple-element.70), channel_id=1, source_target_pairs={{0,4},{2,3},{1,5},{3,2},{4,0},{6,7},{5,1},{7,6},{8,12},{10,11},{9,... | collective-permute-start | bytes 270344 | tf_op jit(solution)/shard_map/ppermute | solution.py:369
  18.9 4.8 %collective-permute-start.6 = (bf16[22,16,128]{2,1,0:T(8,128)(2,1)S(1)}, bf16[22,16,128]{2,1,0:T(8,128)(2,1)S(1)}, u32[]{:S(2)}, u32[]{:S(2)}) collective-permute-start(bf16[22,16,128]{2,1,0:T(8,128)(2,1)S(1)} %get-tuple-element.71), channel_id=1, source_target_pairs={{0,1},{2,6},{1,0},{3,7},{4,5},{6,2},{5,4},{7,3},{8,9},{10,14},{9,8... | collective-permute-start | bytes 270344 | tf_op jit(solution)/shard_map/ppermute | solution.py:369
  23.8 16.4 %copy-start.7 = (bf16[768,128]{1,0:T(8,128)(2,1)S(1)}, bf16[768,128]{1,0:T(8,128)(2,1)}, u32[]{:S(2)}) copy-start(bf16[768,128]{1,0:T(8,128)(2,1)} %wd_ref.3) | copy-start | bytes 589828
  23.8 7.8 %collective-permute-start.9 = (bf16[22,16,128]{2,1,0:T(8,128)(2,1)S(1)}, bf16[22,16,128]{2,1,0:T(8,128)(2,1)S(1)}, u32[]{:S(2)}, u32[]{:S(2)}) collective-permute-start(bf16[22,16,128]{2,1,0:T(8,128)(2,1)S(1)} %add_convert_fusion.1), channel_id=1, source_target_pairs={{0,24},{8,16},{16,8},{24,0},{1,25},{9,17},{17,9},{25,1},{2,26},{10... | collective-permute-start | bytes 270344 | tf_op jit(solution)/shard_map/ppermute | solution.py:401
  28.1 7.0 %collective-permute-start.8 = (bf16[22,16,128]{2,1,0:T(8,128)(2,1)S(1)}, bf16[22,16,128]{2,1,0:T(8,128)(2,1)S(1)}, u32[]{:S(2)}, u32[]{:S(2)}) collective-permute-start(bf16[22,16,128]{2,1,0:T(8,128)(2,1)S(1)} %add_convert_fusion.1), channel_id=1, source_target_pairs={{0,16},{8,24},{16,0},{24,8},{1,17},{9,25},{17,1},{25,9},{2,18},{10... | collective-permute-start | bytes 270344 | tf_op jit(solution)/shard_map/ppermute | solution.py:401
  28.1 7.0 %collective-permute-start.7 = (bf16[22,16,128]{2,1,0:T(8,128)(2,1)S(1)}, bf16[22,16,128]{2,1,0:T(8,128)(2,1)S(1)}, u32[]{:S(2)}, u32[]{:S(2)}) collective-permute-start(bf16[22,16,128]{2,1,0:T(8,128)(2,1)S(1)} %add_convert_fusion.1), channel_id=1, source_target_pairs={{0,8},{8,0},{16,24},{24,16},{1,9},{9,1},{17,25},{25,17},{2,10},{10... | collective-permute-start | bytes 270344 | tf_op jit(solution)/shard_map/ppermute | solution.py:401
  28.7 6.4 %collective-permute-start.10 = (bf16[96,128]{1,0:T(8,128)(2,1)S(1)}, bf16[96,128]{1,0:T(8,128)(2,1)S(1)}, u32[]{:S(2)}, u32[]{:S(2)}) collective-permute-start(bf16[96,128]{1,0:T(8,128)(2,1)S(1)} %get-tuple-element.77), channel_id=1, source_target_pairs={{2,4},{6,8},{10,12},{14,16},{18,20},{22,24},{26,28},{4,2},{8,6},{1... | collective-permute-start | bytes 73736 | tf_op jit(solution)/shard_map/ppermute | solution.py:402
  35.2 7.8 %collective-permute-start.14 = (bf16[22,16,128]{2,1,0:T(8,128)(2,1)S(1)}, bf16[22,16,128]{2,1,0:T(8,128)(2,1)S(1)}, u32[]{:S(2)}, u32[]{:S(2)}) collective-permute-start(bf16[22,16,128]{2,1,0:T(8,128)(2,1)S(1)} %add_convert_fusion.refs_0_), channel_id=1, source_target_pairs={{0,5},{2,7},{1,4},{3,6},{4,1},{6,3},{5,0},{7,2},{8,13},{10,15},{9,... | collective-permute-start | bytes 270344 | tf_op jit(solution)/shard_map/ppermute | solution.py:427
  37.2 5.8 %collective-permute-start.13 = (bf16[22,16,128]{2,1,0:T(8,128)(2,1)S(1)}, bf16[22,16,128]{2,1,0:T(8,128)(2,1)S(1)}, u32[]{:S(2)}, u32[]{:S(2)}) collective-permute-start(bf16[22,16,128]{2,1,0:T(8,128)(2,1)S(1)} %add_convert_fusion.refs_0_), channel_id=1, source_target_pairs={{0,4},{2,3},{1,5},{3,2},{4,0},{6,7},{5,1},{7,6},{8,12},{10,11},{9,... | collective-permute-start | bytes 270344 | tf_op jit(solution)/shard_map/ppermute | solution.py:427
  38.1 4.9 %collective-permute-start.12 = (bf16[22,16,128]{2,1,0:T(8,128)(2,1)S(1)}, bf16[22,16,128]{2,1,0:T(8,128)(2,1)S(1)}, u32[]{:S(2)}, u32[]{:S(2)}) collective-permute-start(bf16[22,16,128]{2,1,0:T(8,128)(2,1)S(1)} %add_convert_fusion.refs_0_), channel_id=1, source_target_pairs={{0,1},{2,6},{1,0},{3,7},{4,5},{6,2},{5,4},{7,3},{8,9},{10,14},{9,8... | collective-permute-start | bytes 270344 | tf_op jit(solution)/shard_map/ppermute | solution.py:427
  38.7 4.1 %collective-permute-start.11 = (bf16[96,128]{1,0:T(8,128)(2,1)S(1)}, bf16[96,128]{1,0:T(8,128)(2,1)S(1)}, u32[]{:S(2)}, u32[]{:S(2)}) collective-permute-start(bf16[96,128]{1,0:T(8,128)(2,1)S(1)} %get-tuple-element.79), channel_id=1, source_target_pairs={{0,1},{1,0},{2,3},{3,2},{4,5},{5,4},{6,7},{7,6},{8,9},{9,8},{10,11... | collective-permute-start | bytes 73736 | tf_op jit(solution)/shard_map/ppermute | solution.py:416
  43.0 1.8 %collective-permute-start.15 = (bf16[94,16,128]{2,1,0:T(8,128)(2,1)S(1)}, bf16[94,16,128]{2,1,0:T(8,128)(2,1)S(1)}, u32[]{:S(2)}, u32[]{:S(2)}) collective-permute-start(bf16[94,16,128]{2,1,0:T(8,128)(2,1)S(1)} %join.1.mine_ref), channel_id=1, source_target_pairs={{0,2},{2,0},{1,3},{3,1},{4,6},{6,4},{5,7},{7,5},{8,10},{10,8},{9,1... | collective-permute-start | bytes 1155080 | tf_op jit(solution)/shard_map/ppermute | solution.py:435

commit v11 on v10

--- a/solution.py
+++ b/solution.py
@@ -42,12 +42,12 @@
     return jnp.where(code > 8, -1, lane)
 
 
-def payload_tiles(channels, conv_columns, taps):
+def half_tiles(channels, conv_columns, taps):
     tiles = []
     for column in range(0, conv_columns, LANES):
-        for row in range(0, channels, TILE):
+        for row in range(0, channels // 2, TILE):
             tiles.append((0, row, column, min(LANES, conv_columns - column)))
-    for row in range(0, taps * channels, TILE):
+    for row in range(0, taps * channels // 2, TILE):
         tiles.append((1, row, 0, LANES))
     return tiles
 
@@ -129,21 +129,17 @@
         picked_t = mm(hidden_t, pick_ref[t], NT).astype(BF16)
         down_w[t * channels : (t + 1) * channels, :] = mm(picked_t, cgrad)
 
-    tiles = payload_tiles(channels, conv_columns, taps)
-    size = keep_ref.shape[0]
-    for core in range(2):
-
-        @pl.when(core_ref[0] == core)
-        def _(core=core):
-            for i in range(2 * size):
-                ref = keep_ref if i // size == core else send_ref
-                if i < len(tiles):
-                    kind, row, column, _ = tiles[i]
-                    source = down_w if kind else conv_w
-                    value = source[row : row + TILE, column : column + LANES]
-                else:
-                    value = jnp.zeros((TILE, LANES), F32)
-                ref[i % size] = value.astype(ref.dtype)
+    tiles = half_tiles(channels, conv_columns, taps)
+    for ref, half in ((keep_ref, core_ref[0]), (send_ref, 1 - core_ref[0])):
+        for i in range(ref.shape[0]):
+            if i < len(tiles):
+                kind, row, column, _ = tiles[i]
+                source = down_w if kind else conv_w
+                start = pl.multiple_of(half * (source.shape[0] // 2) + row, TILE)
+                value = source[pl.ds(start, TILE), column : column + LANES]
+            else:
+                value = jnp.zeros((TILE, LANES), F32)
+            ref[i] = value.astype(ref.dtype)
 
 
 def coarse_kernel(pick_ref, hidden_ref, wd_ref, coarse_ref):
@@ -227,24 +223,38 @@
     full_ref[len(piece_refs) * length :] = rider_ref[...]
 
 
-def final_kernel(taps, size, core_ref, mine_ref, other_ref, *refs):
-    base_ref, home_ref, conv_ref, down_ref, grad_ref = refs
+def write_half(taps, half, tiles_ref, conv_ref, down_ref, conv_half, down_half, sems):
     channels, conv_columns = conv_ref.shape
+    tiles = half_tiles(channels, conv_columns, taps)
+    copies = []
+    for wanted, buffer, whole in ((1, down_half, down_ref), (0, conv_half, conv_ref)):
+        for i, (kind, row, column, columns) in enumerate(tiles):
+            if kind == wanted:
+                value = tiles_ref[i].astype(F32)[:, :columns]
+                buffer[row : row + TILE, column : column + columns] = value
+        rows = buffer.shape[0]
+        start = pl.multiple_of(half * rows, TILE)
+        copy = pltpu.make_async_copy(buffer, whole.at[pl.ds(start, rows)], sems.at[wanted])
+        copy.start()
+        copies.append(copy)
+    return copies
+
+
+def first_half_kernel(taps, core_ref, mine_ref, conv_ref, down_ref, *scratch):
+    for copy in write_half(taps, core_ref[0], mine_ref, conv_ref, down_ref, *scratch):
+        copy.wait()
+
+
+def other_half_kernel(taps, size, core_ref, other_ref, base_ref, home_ref, *refs):
+    _, _, conv_ref, down_ref, grad_ref, *scratch = refs
+    copies = write_half(taps, 1 - core_ref[0], other_ref, conv_ref, down_ref, *scratch)
     grad_ref[:, RIM:] = base_ref[:, RIM:]
-    for i in range(channels // TILE):
+    for i in range(base_ref.shape[0] // TILE):
         rows = slice(i * TILE, (i + 1) * TILE)
         total = base_ref[rows, :RIM] + home_ref[rows, :]
         grad_ref[rows, :RIM] = total + other_ref[size + i][:, :RIM].astype(F32)
-    for core in range(2):
-
-        @pl.when(core_ref[0] == core)
-        def _(core=core):
-            for i, tile in enumerate(payload_tiles(channels, conv_columns, taps)):
-                kind, row, column, columns = tile
-                source = mine_ref if i // size == core else other_ref
-                value = source[i % size].astype(F32)
-                target = down_ref if kind else conv_ref
-                target[row : row + TILE, column : column + columns] = value[:, :columns]
+    for copy in copies:
+        copy.wait()
 
 
 def shifts(count, step):
@@ -329,13 +339,12 @@
         cost_estimate=light,
         name="taps",
     )(down_t, coarse_grad, w_down)
-    row, pick, hgrad = lax.optimization_barrier((row, pick, hgrad))
     mate = lax.ppermute(row, RING, mates)
     halos = [mate, cross, *side]
     far_rows = -(-sum(x.shape[1] for x in halos) // LANES) * LANES
 
-    tiles = len(payload_tiles(channels, conv_columns, taps))
-    size = -(-tiles // (2 * squares)) * squares
+    tiles = len(half_tiles(channels, conv_columns, taps))
+    size = -(-tiles // squares) * squares
     grad, hidden, keep, send = pl.pallas_call(
         functools.partial(forward_kernel, slabs),
         out_shape=(
@@ -433,17 +442,32 @@
         name="join",
     )(core, here, total, *got, mate)
     other = lax.ppermute(mine, "core", swap)
+    weights = (
+        jax.ShapeDtypeStruct((channels, conv_columns), F32),
+        jax.ShapeDtypeStruct((taps * channels, LANES), F32),
+    )
+    halves = [pltpu.VMEM((x.shape[0] // 2, x.shape[1]), F32) for x in weights]
+    scratch = halves + [pltpu.SemaphoreType.DMA((2,))]
+    whole = pl.BlockSpec(memory_space=pl.ANY)
+    conv_wgrad_t, down_wgrad = pl.pallas_call(
+        functools.partial(first_half_kernel, taps),
+        out_shape=weights,
+        in_specs=[smem, vmem],
+        out_specs=(whole, whole),
+        scratch_shapes=scratch,
+        compiler_params=params,
+        name="first_half",
+    )(core, mine)
     conv_wgrad_t, down_wgrad, grad_input_t = pl.pallas_call(
-        functools.partial(final_kernel, taps, size),
-        out_shape=(
-            jax.ShapeDtypeStruct((channels, conv_columns), F32),
-            jax.ShapeDtypeStruct((taps * channels, LANES), F32),
-            jax.ShapeDtypeStruct((channels, voxels), F32),
-        ),
-        in_specs=[smem] + [vmem] * 4,
-        compiler_params=params,
-        name="final",
-    )(core, mine, other, base, home)
+        functools.partial(other_half_kernel, taps, size),
+        out_shape=(*weights, jax.ShapeDtypeStruct((channels, voxels), F32)),
+        in_specs=[smem, vmem, vmem, vmem, whole, whole],
+        out_specs=(whole, whole, vmem),
+        input_output_aliases={4: 0, 5: 1},
+        scratch_shapes=scratch,
+        compiler_params=params,
+        name="other_half",
+    )(core, other, base, home, conv_wgrad_t, down_wgrad)
     return coarse, grad_input_t.T, conv_wgrad_t.T, down_wgrad
 
 

time: 46.3 us -> 47.5 us (1.026)
  waiting for transfers between devices: 12.9 us -> 11.2 us
  local copies, waits for them, and re-layouts: 1.64 us -> 2.88 us
  Pallas kernels: 8.99 us -> 10.2 us
  starting transfers between devices: 21.4 us -> 21.9 us
    unnamed x18 -> x24, local copies, waits for them, and re-layouts: 1.63 us -> 2.87 us
    pallas_call x1 -> x2, Pallas kernels: 1.22 us -> 2.41 us  [the longest x1 1.52 us: on_device(): pl.pallas_call(functools.partial(other_half_kernel, taps, size), out_shap...]
    ppermute x1, waiting for transfers between devices: 1.7 us -> 0.81 us  [on_device(): other = lax.ppermute(mine, 'core', swap)]
    ppermute x1, waiting for transfers between devices: 0.85 us -> 0.13 us  [on_device(): mate = lax.ppermute(row, RING, mates)]
  transfers between devices with their start and end apart: 16 -> 16, of which waited for: 7 -> 8; matrix products, arithmetic and copies ran while one was open for 0% -> 0% of each run, Pallas kernels for 12% -> 13%
where the time goes in v11:
time: 47.5 us; the launch traced here: 47.2 us
  starting transfers between devices  21.9 us (46%)
  waiting for transfers between devices  11.2 us (24%)
  Pallas kernels  10.2 us (21%)
  local copies, waits for them, and re-layouts  2.88 us (6%)
  between operations  0.86 us (2%)
    ppermute x3, waiting for transfers between devices, on_device(): lax.ppermute(total, 'far', [(i, i ^ step) for i in range(sizes['far'])])  5.73 us
    ppermute x3, starting transfers between devices, on_device(): lax.ppermute(total, 'far', [(i, i ^ step) for i in range(sizes['far'])])  5.24 us
    ppermute x3, starting transfers between devices, on_device(): got = [lax.ppermute(x, SPLIT, route) for x, route in zip(sent, routes)]  3.91 us
    ppermute x3, starting transfers between devices, on_device(): got = [lax.ppermute(total, SPLIT, route) for route in routes[::-1]]  3.55 us
    ppermute x1, starting transfers between devices, on_device(): mate = lax.ppermute(row, RING, mates)  3.07 us
    ppermute x1, starting transfers between devices, on_device(): side = [lax.ppermute(features_t, 'slab', pairs) for pairs in beside]  3.03 us
    unnamed x24, local copies, waits for them, and re-layouts  2.87 us
    pallas_call x1, Pallas kernels, on_device(): pl.pallas_call(functools.partial(backward_kernel, slabs), out_shape=(jax....  2.53 us
  transfers between devices with their start and end apart: 16, of which 8 were waited for; matrix products, arithmetic and copies ran while one was open for 0% of the time, Pallas kernels for 13%

profile of v11, /device:TPU:0, one launch (start us, length us, event | category | flops | bytes accessed | tf_op | source)
XLA Modules:
  0.0 47.2 jit_solution(18322700468101919255)
XLA Ops:
  0.6 3.0 %collective-permute-start = (bf16[96,256]{1,0:T(8,128)(2,1)}, bf16[96,256]{1,0:T(8,128)(2,1)S(1)}, u32[]{:S(2)}, u32[]{:S(2)}) collective-permute-start(bf16[96,256]{1,0:T(8,128)(2,1)} %bitcast.10), channel_id=1, source_target_pairs={{0,1},{1,0},{2,3},{3,2},{4,5},{5,4},{6,7},{7,6},{8,9},{9,8},{10,11... | collective-permute-start | bytes 147464 | tf_op jit(solution)/shard_map/ppermute | solution.py:315
  3.7 0.8 %copy-done.1 = bf16[256,96]{0,1:T(8,128)(2,1)S(1)} copy-done((bf16[256,96]{0,1:T(8,128)(2,1)S(1)}, bf16[256,96]{0,1:T(8,128)(2,1)}, u32[]{:S(2)}) %copy-start.1) | copy-done | bytes 49176
  4.5 0.8 %copy-done.3 = s32[256,27]{0,1:T(8,128)S(1)} copy-done((s32[256,27]{0,1:T(8,128)S(1)}, s32[256,27]{0,1:T(8,128)}, u32[]{:S(2)}) %copy-start.3) | copy-done | bytes 27672
  5.3 1.0 %gather.1 = (bf16[2592,128]{1,0:T(8,128)(2,1)S(1)}, bf16[2592,128]{1,0:T(8,128)(2,1)S(1)}) custom-call(bf16[96,256]{1,0:T(8,128)(2,1)S(1)} %bitcast.11, s32[27,256]{1,0:T(8,128)S(1)} %bitcast.14), custom_call_target="tpu_custom_call" | custom-call | flops 2000000000 | bytes 10000000 | tf_op jit(solution)/shard_map/gather/pallas_call | solution.py:316
  6.3 0.0 collective-permute-done
  6.3 0.0 copy-start.5
  6.3 0.0 copy-start.11
  6.3 0.1 pad_maximum_fusion
  6.4 0.7 %collective-permute-start.2 = (bf16[96,128]{1,0:T(8,128)(2,1)S(1)}, bf16[96,128]{1,0:T(8,128)(2,1)S(1)}, u32[]{:S(2)}, u32[]{:S(2)}) collective-permute-start(bf16[96,128]{1,0:T(8,128)(2,1)S(1)} %pad_maximum_fusion), channel_id=1, source_target_pairs={{2,4},{6,8},{10,12},{14,16},{18,20},{22,24},{26,28},{4,2},{8,6},{1... | collective-permute-start | bytes 73736 | tf_op jit(solution)/shard_map/ppermute | solution.py:330
  7.0 0.0 copy-start
  7.1 0.0 copy-start.2
  7.1 0.0 copy-start.4
  7.1 3.1 %collective-permute-start.1 = (bf16[96,128]{1,0:T(8,128)(2,1)S(1)}, bf16[96,128]{1,0:T(8,128)(2,1)S(1)}, u32[]{:S(2)}, u32[]{:S(2)}) collective-permute-start(bf16[96,128]{1,0:T(8,128)(2,1)S(1)} %pad_maximum_fusion), channel_id=1, source_target_pairs={{0,2},{2,0},{4,6},{6,4},{8,10},{10,8},{12,14},{14,12},{16,18},{18,... | collective-permute-start | bytes 73736 | tf_op jit(solution)/shard_map/ppermute | solution.py:342
  10.2 0.7 %taps.1 = (bf16[8,64,256]{2,1,0:T(8,128)(2,1)S(1)}, f32[96,256]{1,0:T(8,128)S(1)}) custom-call(s32[8,64]{1,0:T(8,128)S(1)} %bitcast.17, bf16[64,128]{1,0:T(8,128)(2,1)S(1)} %copy-done.5, bf16[768,128]{1,0:T(8,128)(2,1)S(1)} %copy-done.6), custom_call_target="tpu_custom_call" | custom-call | flops 2000000000 | bytes 10000000 | tf_op jit(solution)/shard_map/taps/pallas_call | solution.py:332
  10.9 0.1 collective-permute-done.1.refs_4_
  11.0 2.2 %forward.1 = (bf16[96,256]{1,0:T(8,128)(2,1)S(1)}, bf16[96,256]{1,0:T(8,128)(2,1)S(1)}, f32[88,16,128]{2,1,0:T(8,128)S(1)}, bf16[88,16,128]{2,1,0:T(8,128)(2,1)S(1)}) custom-call(s32[1]{0:T(128)} %bitcast.core_ref, bf16[96,256]{1,0:T(8,128)(2,1)S(1)} %bitcast.13, s32[27,256]{1,0:T(8,128)S(1)} %bitcast.15, bf16[64,128]{1,0:T(8,128)(2,1)S(1)} %copy-done.5, ...), custom_call_target="tpu_custom_call" | custom-call | tf_op jit(solution)/shard_map/forward/pallas_call | solution.py:348
  13.3 0.0 copy-start.7
  13.3 0.6 %copy-done.7 = bf16[96,256]{1,0:T(8,128)(2,1)} copy-done((bf16[96,256]{1,0:T(8,128)(2,1)}, bf16[96,256]{1,0:T(8,128)(2,1)S(1)}, u32[]{:S(2)}) %copy-start.7) | copy-done | bytes 49176
  13.9 0.6 %copy-done.9 = bf16[96,256]{1,0:T(8,128)(2,1)} copy-done((bf16[96,256]{1,0:T(8,128)(2,1)}, bf16[96,256]{1,0:T(8,128)(2,1)S(1)}, u32[]{:S(2)}) %copy-start.9) | copy-done | bytes 49176
  14.5 0.6 %collective-permute-start.3 = (bf16[88,16,128]{2,1,0:T(8,128)(2,1)S(1)}, bf16[88,16,128]{2,1,0:T(8,128)(2,1)S(1)}, u32[]{:S(2)}, u32[]{:S(2)}) collective-permute-start(bf16[88,16,128]{2,1,0:T(8,128)(2,1)S(1)} %get-tuple-element.57), channel_id=1, source_target_pairs={{0,2},{2,0},{1,3},{3,1},{4,6},{6,4},{5,7},{7,5},{8,10},{10,8},{9,1... | collective-permute-start | bytes 1081352 | tf_op jit(solution)/shard_map/ppermute | solution.py:366
  15.1 1.3 %collective-permute-done.3.got_ref = bf16[88,16,128]{2,1,0:T(8,128)(2,1)S(1)} collective-permute-done((bf16[88,16,128]{2,1,0:T(8,128)(2,1)S(1)}, bf16[88,16,128]{2,1,0:T(8,128)(2,1)S(1)}, u32[]{:S(2)}, u32[]{:S(2)}) %collective-permute-start.3) | collective-permute-done | bytes 360480 | tf_op jit(solution)/shard_map/ppermute | solution.py:366
  16.4 0.1 split.1
  16.4 3.3 %collective-permute-start.4 = (bf16[22,16,128]{2,1,0:T(8,128)(2,1)S(1)}, bf16[22,16,128]{2,1,0:T(8,128)(2,1)S(1)}, u32[]{:S(2)}, u32[]{:S(2)}) collective-permute-start(bf16[22,16,128]{2,1,0:T(8,128)(2,1)S(1)} %get-tuple-element.65), channel_id=1, source_target_pairs={{0,5},{2,7},{1,4},{3,6},{4,1},{6,3},{5,0},{7,2},{8,13},{10,15},{9,... | collective-permute-start | bytes 270344 | tf_op jit(solution)/shard_map/ppermute | solution.py:378
  19.7 0.0 collective-permute-start.5
  19.7 0.6 %collective-permute-start.6 = (bf16[22,16,128]{2,1,0:T(8,128)(2,1)S(1)}, bf16[22,16,128]{2,1,0:T(8,128)(2,1)S(1)}, u32[]{:S(2)}, u32[]{:S(2)}) collective-permute-start(bf16[22,16,128]{2,1,0:T(8,128)(2,1)S(1)} %get-tuple-element.67), channel_id=1, source_target_pairs={{0,1},{2,6},{1,0},{3,7},{4,5},{6,2},{5,4},{7,3},{8,9},{10,14},{9,8... | collective-permute-start | bytes 270344 | tf_op jit(solution)/shard_map/ppermute | solution.py:378
  20.4 2.5 %backward.1 = (f32[96,256]{1,0:T(8,128)S(1)}, f32[96,64]{1,0:T(8,128)S(1)}, f32[96,128]{1,0:T(8,128)S(1)}, bf16[96,128]{1,0:T(8,128)(2,1)S(1)}) custom-call(s32[1]{0:T(128)} %bitcast.core_ref, s32[27,256]{1,0:T(8,128)S(1)} %bitcast.16, f32[96,256]{1,0:T(8,128)S(1)} %get-tuple-element.51.refs_3_.hgrad_ref, bf16[96,256]{1,0:T(8,128)(2,1)S(1)} %copy-done.10, ...), custom_call_target="tpu_custom_call" | custom-call | flops 2000000000 | bytes 10000000 | tf_op jit(solution)/shard_map/backward/pallas_call | solution.py:379
  22.9 1.4 %collective-permute-done.5 = bf16[22,16,128]{2,1,0:T(8,128)(2,1)S(1)} collective-permute-done((bf16[22,16,128]{2,1,0:T(8,128)(2,1)S(1)}, bf16[22,16,128]{2,1,0:T(8,128)(2,1)S(1)}, u32[]{:S(2)}, u32[]{:S(2)}) %collective-permute-start.5) | collective-permute-done | bytes 90144 | tf_op jit(solution)/shard_map/ppermute | solution.py:378
  24.3 0.3 collective-permute-done.6
  24.6 0.1 add_convert_fusion.1
  24.6 4.6 %collective-permute-start.9 = (bf16[22,16,128]{2,1,0:T(8,128)(2,1)S(1)}, bf16[22,16,128]{2,1,0:T(8,128)(2,1)S(1)}, u32[]{:S(2)}, u32[]{:S(2)}) collective-permute-start(bf16[22,16,128]{2,1,0:T(8,128)(2,1)S(1)} %add_convert_fusion.1), channel_id=1, source_target_pairs={{0,24},{8,16},{16,8},{24,0},{1,25},{9,17},{17,9},{25,1},{2,26},{10... | collective-permute-start | bytes 270344 | tf_op jit(solution)/shard_map/ppermute | solution.py:410
  29.2 0.6 %collective-permute-start.7 = (bf16[22,16,128]{2,1,0:T(8,128)(2,1)S(1)}, bf16[22,16,128]{2,1,0:T(8,128)(2,1)S(1)}, u32[]{:S(2)}, u32[]{:S(2)}) collective-permute-start(bf16[22,16,128]{2,1,0:T(8,128)(2,1)S(1)} %add_convert_fusion.1), channel_id=1, source_target_pairs={{0,8},{8,0},{16,24},{24,16},{1,9},{9,1},{17,25},{25,17},{2,10},{10... | collective-permute-start | bytes 270344 | tf_op jit(solution)/shard_map/ppermute | solution.py:410
  29.9 0.7 %collective-permute-start.10 = (bf16[96,128]{1,0:T(8,128)(2,1)S(1)}, bf16[96,128]{1,0:T(8,128)(2,1)S(1)}, u32[]{:S(2)}, u32[]{:S(2)}) collective-permute-start(bf16[96,128]{1,0:T(8,128)(2,1)S(1)} %get-tuple-element.73), channel_id=1, source_target_pairs={{2,4},{6,8},{10,12},{14,16},{18,20},{22,24},{26,28},{4,2},{8,6},{1... | collective-permute-start | bytes 73736 | tf_op jit(solution)/shard_map/ppermute | solution.py:411
  30.5 2.2 %collective-permute-done.9 = bf16[22,16,128]{2,1,0:T(8,128)(2,1)S(1)} collective-permute-done((bf16[22,16,128]{2,1,0:T(8,128)(2,1)S(1)}, bf16[22,16,128]{2,1,0:T(8,128)(2,1)S(1)}, u32[]{:S(2)}, u32[]{:S(2)}) %collective-permute-start.9) | collective-permute-done | bytes 90144 | tf_op jit(solution)/shard_map/ppermute | solution.py:410
  32.7 3.5 %collective-permute-done.8 = bf16[22,16,128]{2,1,0:T(8,128)(2,1)S(1)} collective-permute-done((bf16[22,16,128]{2,1,0:T(8,128)(2,1)S(1)}, bf16[22,16,128]{2,1,0:T(8,128)(2,1)S(1)}, u32[]{:S(2)}, u32[]{:S(2)}) %collective-permute-start.8) | collective-permute-done | bytes 90144 | tf_op jit(solution)/shard_map/ppermute | solution.py:410
  36.2 0.0 collective-permute-done.7
  36.2 0.1 add_convert_fusion.refs_0_
  36.3 0.0 copy-start.8
  36.3 2.2 %collective-permute-start.14 = (bf16[22,16,128]{2,1,0:T(8,128)(2,1)S(1)}, bf16[22,16,128]{2,1,0:T(8,128)(2,1)S(1)}, u32[]{:S(2)}, u32[]{:S(2)}) collective-permute-start(bf16[22,16,128]{2,1,0:T(8,128)(2,1)S(1)} %add_convert_fusion.refs_0_), channel_id=1, source_target_pairs={{0,5},{2,7},{1,4},{3,6},{4,1},{6,3},{5,0},{7,2},{8,13},{10,15},{9,... | collective-permute-start | bytes 270344 | tf_op jit(solution)/shard_map/ppermute | solution.py:436
  38.5 0.5 %collective-permute-start.13 = (bf16[22,16,128]{2,1,0:T(8,128)(2,1)S(1)}, bf16[22,16,128]{2,1,0:T(8,128)(2,1)S(1)}, u32[]{:S(2)}, u32[]{:S(2)}) collective-permute-start(bf16[22,16,128]{2,1,0:T(8,128)(2,1)S(1)} %add_convert_fusion.refs_0_), channel_id=1, source_target_pairs={{0,4},{2,3},{1,5},{3,2},{4,0},{6,7},{5,1},{7,6},{8,12},{10,11},{9,... | collective-permute-start | bytes 270344 | tf_op jit(solution)/shard_map/ppermute | solution.py:436
  39.0 0.9 %collective-permute-start.12 = (bf16[22,16,128]{2,1,0:T(8,128)(2,1)S(1)}, bf16[22,16,128]{2,1,0:T(8,128)(2,1)S(1)}, u32[]{:S(2)}, u32[]{:S(2)}) collective-permute-start(bf16[22,16,128]{2,1,0:T(8,128)(2,1)S(1)} %add_convert_fusion.refs_0_), channel_id=1, source_target_pairs={{0,1},{2,6},{1,0},{3,7},{4,5},{6,2},{5,4},{7,3},{8,9},{10,14},{9,8... | collective-permute-start | bytes 270344 | tf_op jit(solution)/shard_map/ppermute | solution.py:436
  39.9 1.2 %collective-permute-start.11 = (bf16[96,128]{1,0:T(8,128)(2,1)S(1)}, bf16[96,128]{1,0:T(8,128)(2,1)S(1)}, u32[]{:S(2)}, u32[]{:S(2)}) collective-permute-start(bf16[96,128]{1,0:T(8,128)(2,1)S(1)} %get-tuple-element.75), channel_id=1, source_target_pairs={{0,1},{1,0},{2,3},{3,2},{4,5},{5,4},{6,7},{7,6},{8,9},{9,8},{10,11... | collective-permute-start | bytes 73736 | tf_op jit(solution)/shard_map/ppermute | solution.py:425
  41.1 1.1 %coarse.1 = bf16[64,128]{1,0:T(8,128)(2,1)} custom-call(bf16[8,64,256]{2,1,0:T(8,128)(2,1)S(1)} %get-tuple-element.54.refs_2_.pick_ref, bf16[96,256]{1,0:T(8,128)(2,1)S(1)} %copy-done.8, bf16[768,128]{1,0:T(8,128)(2,1)S(1)} %copy-done.6), custom_call_target="tpu_custom_call" | custom-call | flops 2000000000 | bytes 10000000 | tf_op jit(solution)/shard_map/coarse/pallas_call | solution.py:400
  42.2 1.6 %collective-permute-done.11.refs_0_ = bf16[96,128]{1,0:T(8,128)(2,1)S(1)} collective-permute-done((bf16[96,128]{1,0:T(8,128)(2,1)S(1)}, bf16[96,128]{1,0:T(8,128)(2,1)S(1)}, u32[]{:S(2)}, u32[]{:S(2)}) %collective-permute-start.11) | collective-permute-done | bytes 24608 | tf_op jit(solution)/shard_map/ppermute | solution.py:425
  43.8 0.1 slab_turn.1
  43.9 0.1 collective-permute-start.15
  44.0 0.9 %first_half.1 = (f32[96,2592]{1,0:T(8,128)}, f32[768,128]{1,0:T(8,128)}) custom-call(s32[1]{0:T(128)} %bitcast.core_ref, bf16[94,16,128]{2,1,0:T(8,128)(2,1)S(1)} %join.1.mine_ref), custom_call_target="tpu_custom_call" | custom-call | tf_op jit(solution)/shard_map/first_half/pallas_call | solution.py:452
  44.9 0.8 %collective-permute-done.15.other_ref = bf16[94,16,128]{2,1,0:T(8,128)(2,1)S(1)} collective-permute-done((bf16[94,16,128]{2,1,0:T(8,128)(2,1)S(1)}, bf16[94,16,128]{2,1,0:T(8,128)(2,1)S(1)}, u32[]{:S(2)}, u32[]{:S(2)}) %collective-permute-start.15) | collective-permute-done | bytes 385056 | tf_op jit(solution)/shard_map/ppermute | solution.py:444
  45.7 1.5 %other_half.1 = (f32[96,2592]{1,0:T(8,128)}, f32[768,128]{1,0:T(8,128)}, f32[96,256]{1,0:T(8,128)}) custom-call(s32[1]{0:T(128)} %bitcast.core_ref, bf16[94,16,128]{2,1,0:T(8,128)(2,1)S(1)} %collective-permute-done.15.other_ref, f32[96,256]{1,0:T(8,128)S(1)} %get-tuple-element.83.base_ref, ...), custom_call_target="tpu_custom_call", output_to_operand_aliasing={{0}: (4, {}), {1}: (5, {})} | custom-call | tf_op jit(solution)/shard_map/other_half/pallas_call | solution.py:461
  (24 shorter events, 0.1 us)
Async XLA Ops:
  0.6 5.6 %collective-permute-start = (bf16[96,256]{1,0:T(8,128)(2,1)}, bf16[96,256]{1,0:T(8,128)(2,1)S(1)}, u32[]{:S(2)}, u32[]{:S(2)}) collective-permute-start(bf16[96,256]{1,0:T(8,128)(2,1)} %bitcast.10), channel_id=1, source_target_pairs={{0,1},{1,0},{2,3},{3,2},{4,5},{5,4},{6,7},{7,6},{8,9},{9,8},{10,11... | collective-permute-start | bytes 147464 | tf_op jit(solution)/shard_map/ppermute | solution.py:315
  3.7 0.8 %copy-start.1 = (bf16[256,96]{0,1:T(8,128)(2,1)S(1)}, bf16[256,96]{0,1:T(8,128)(2,1)}, u32[]{:S(2)}) copy-start(bf16[256,96]{0,1:T(8,128)(2,1)} %param.6) | copy-start | bytes 147460
  4.5 0.8 %copy-start.3 = (s32[256,27]{0,1:T(8,128)S(1)}, s32[256,27]{0,1:T(8,128)}, u32[]{:S(2)}) copy-start(s32[256,27]{0,1:T(8,128)} %param.7) | copy-start | bytes 82948
  5.3 4.9 %copy-start.6 = (bf16[768,128]{1,0:T(8,128)(2,1)S(1)}, bf16[768,128]{1,0:T(8,128)(2,1)}, u32[]{:S(2)}) copy-start(bf16[768,128]{1,0:T(8,128)(2,1)} %wd_ref.3) | copy-start | bytes 589828
  6.3 3.9 %copy-start.5 = (bf16[64,128]{1,0:T(8,128)(2,1)S(1)}, bf16[64,128]{1,0:T(8,128)(2,1)}, u32[]{:S(2)}) copy-start(bf16[64,128]{1,0:T(8,128)(2,1)} %cgrad_ref.3) | copy-start | bytes 49156
  6.3 3.9 %copy-start.11 = (s32[64,8]{0,1:T(8,128)S(1)}, s32[64,8]{0,1:T(8,128)}, u32[]{:S(2)}) copy-start(s32[64,8]{0,1:T(8,128)} %param.8) | copy-start | bytes 6148
  6.4 4.6 %collective-permute-start.2 = (bf16[96,128]{1,0:T(8,128)(2,1)S(1)}, bf16[96,128]{1,0:T(8,128)(2,1)S(1)}, u32[]{:S(2)}, u32[]{:S(2)}) collective-permute-start(bf16[96,128]{1,0:T(8,128)(2,1)S(1)} %pad_maximum_fusion), channel_id=1, source_target_pairs={{2,4},{6,8},{10,12},{14,16},{18,20},{22,24},{26,28},{4,2},{8,6},{1... | collective-permute-start | bytes 73736 | tf_op jit(solution)/shard_map/ppermute | solution.py:330
  7.0 4.0 %copy-start = (bf16[2592,96]{0,1:T(8,128)(2,1)S(1)}, bf16[2592,96]{0,1:T(8,128)(2,1)}, u32[]{:S(2)}) copy-start(bf16[2592,96]{0,1:T(8,128)(2,1)} %param.9) | copy-start | bytes 1492996
  7.1 4.0 %copy-start.2 = (bf16[256,96]{0,1:T(8,128)(2,1)S(1)}, bf16[256,96]{0,1:T(8,128)(2,1)}, u32[]{:S(2)}) copy-start(bf16[256,96]{0,1:T(8,128)(2,1)} %param.6) | copy-start | bytes 147460
  7.1 3.9 %copy-start.4 = (s32[256,27]{0,1:T(8,128)S(1)}, s32[256,27]{0,1:T(8,128)}, u32[]{:S(2)}) copy-start(s32[256,27]{0,1:T(8,128)} %param.7) | copy-start | bytes 82948
  7.1 3.9 %collective-permute-start.1 = (bf16[96,128]{1,0:T(8,128)(2,1)S(1)}, bf16[96,128]{1,0:T(8,128)(2,1)S(1)}, u32[]{:S(2)}, u32[]{:S(2)}) collective-permute-start(bf16[96,128]{1,0:T(8,128)(2,1)S(1)} %pad_maximum_fusion), channel_id=1, source_target_pairs={{0,2},{2,0},{4,6},{6,4},{8,10},{10,8},{12,14},{14,12},{16,18},{18,... | collective-permute-start | bytes 73736 | tf_op jit(solution)/shard_map/ppermute | solution.py:342
  13.3 0.6 %copy-start.7 = (bf16[96,256]{1,0:T(8,128)(2,1)}, bf16[96,256]{1,0:T(8,128)(2,1)S(1)}, u32[]{:S(2)}) copy-start(bf16[96,256]{1,0:T(8,128)(2,1)S(1)} %get-tuple-element.76.hidden_ref) | copy-start | bytes 147460
  13.9 0.6 %copy-start.9 = (bf16[96,256]{1,0:T(8,128)(2,1)}, bf16[96,256]{1,0:T(8,128)(2,1)S(1)}, u32[]{:S(2)}) copy-start(bf16[96,256]{1,0:T(8,128)(2,1)S(1)} %get-tuple-element.62.grad_ref) | copy-start | bytes 147460
  14.5 1.9 %collective-permute-start.3 = (bf16[88,16,128]{2,1,0:T(8,128)(2,1)S(1)}, bf16[88,16,128]{2,1,0:T(8,128)(2,1)S(1)}, u32[]{:S(2)}, u32[]{:S(2)}) collective-permute-start(bf16[88,16,128]{2,1,0:T(8,128)(2,1)S(1)} %get-tuple-element.57), channel_id=1, source_target_pairs={{0,2},{2,0},{1,3},{3,1},{4,6},{6,4},{5,7},{7,5},{8,10},{10,8},{9,1... | collective-permute-start | bytes 1081352 | tf_op jit(solution)/shard_map/ppermute | solution.py:366
  16.4 4.0 %copy-start.10 = (bf16[96,256]{1,0:T(8,128)(2,1)S(1)}, bf16[96,256]{1,0:T(8,128)(2,1)}, u32[]{:S(2)}) copy-start(bf16[96,256]{1,0:T(8,128)(2,1)} %copy-done.9) | copy-start | bytes 147460
  16.4 6.5 %collective-permute-start.4 = (bf16[22,16,128]{2,1,0:T(8,128)(2,1)S(1)}, bf16[22,16,128]{2,1,0:T(8,128)(2,1)S(1)}, u32[]{:S(2)}, u32[]{:S(2)}) collective-permute-start(bf16[22,16,128]{2,1,0:T(8,128)(2,1)S(1)} %get-tuple-element.65), channel_id=1, source_target_pairs={{0,5},{2,7},{1,4},{3,6},{4,1},{6,3},{5,0},{7,2},{8,13},{10,15},{9,... | collective-permute-start | bytes 270344 | tf_op jit(solution)/shard_map/ppermute | solution.py:378
  19.7 4.6 %collective-permute-start.5 = (bf16[22,16,128]{2,1,0:T(8,128)(2,1)S(1)}, bf16[22,16,128]{2,1,0:T(8,128)(2,1)S(1)}, u32[]{:S(2)}, u32[]{:S(2)}) collective-permute-start(bf16[22,16,128]{2,1,0:T(8,128)(2,1)S(1)} %get-tuple-element.66), channel_id=1, source_target_pairs={{0,4},{2,3},{1,5},{3,2},{4,0},{6,7},{5,1},{7,6},{8,12},{10,11},{9,... | collective-permute-start | bytes 270344 | tf_op jit(solution)/shard_map/ppermute | solution.py:378
  19.7 4.8 %collective-permute-start.6 = (bf16[22,16,128]{2,1,0:T(8,128)(2,1)S(1)}, bf16[22,16,128]{2,1,0:T(8,128)(2,1)S(1)}, u32[]{:S(2)}, u32[]{:S(2)}) collective-permute-start(bf16[22,16,128]{2,1,0:T(8,128)(2,1)S(1)} %get-tuple-element.67), channel_id=1, source_target_pairs={{0,1},{2,6},{1,0},{3,7},{4,5},{6,2},{5,4},{7,3},{8,9},{10,14},{9,8... | collective-permute-start | bytes 270344 | tf_op jit(solution)/shard_map/ppermute | solution.py:378
  24.6 8.1 %collective-permute-start.9 = (bf16[22,16,128]{2,1,0:T(8,128)(2,1)S(1)}, bf16[22,16,128]{2,1,0:T(8,128)(2,1)S(1)}, u32[]{:S(2)}, u32[]{:S(2)}) collective-permute-start(bf16[22,16,128]{2,1,0:T(8,128)(2,1)S(1)} %add_convert_fusion.1), channel_id=1, source_target_pairs={{0,24},{8,16},{16,8},{24,0},{1,25},{9,17},{17,9},{25,1},{2,26},{10... | collective-permute-start | bytes 270344 | tf_op jit(solution)/shard_map/ppermute | solution.py:410
  29.2 7.0 %collective-permute-start.8 = (bf16[22,16,128]{2,1,0:T(8,128)(2,1)S(1)}, bf16[22,16,128]{2,1,0:T(8,128)(2,1)S(1)}, u32[]{:S(2)}, u32[]{:S(2)}) collective-permute-start(bf16[22,16,128]{2,1,0:T(8,128)(2,1)S(1)} %add_convert_fusion.1), channel_id=1, source_target_pairs={{0,16},{8,24},{16,0},{24,8},{1,17},{9,25},{17,1},{25,9},{2,18},{10... | collective-permute-start | bytes 270344 | tf_op jit(solution)/shard_map/ppermute | solution.py:410
  29.2 7.0 %collective-permute-start.7 = (bf16[22,16,128]{2,1,0:T(8,128)(2,1)S(1)}, bf16[22,16,128]{2,1,0:T(8,128)(2,1)S(1)}, u32[]{:S(2)}, u32[]{:S(2)}) collective-permute-start(bf16[22,16,128]{2,1,0:T(8,128)(2,1)S(1)} %add_convert_fusion.1), channel_id=1, source_target_pairs={{0,8},{8,0},{16,24},{24,16},{1,9},{9,1},{17,25},{25,17},{2,10},{10... | collective-permute-start | bytes 270344 | tf_op jit(solution)/shard_map/ppermute | solution.py:410
  29.9 6.5 %collective-permute-start.10 = (bf16[96,128]{1,0:T(8,128)(2,1)S(1)}, bf16[96,128]{1,0:T(8,128)(2,1)S(1)}, u32[]{:S(2)}, u32[]{:S(2)}) collective-permute-start(bf16[96,128]{1,0:T(8,128)(2,1)S(1)} %get-tuple-element.73), channel_id=1, source_target_pairs={{2,4},{6,8},{10,12},{14,16},{18,20},{22,24},{26,28},{4,2},{8,6},{1... | collective-permute-start | bytes 73736 | tf_op jit(solution)/shard_map/ppermute | solution.py:411
  36.3 4.8 %copy-start.8 = (bf16[96,256]{1,0:T(8,128)(2,1)S(1)}, bf16[96,256]{1,0:T(8,128)(2,1)}, u32[]{:S(2)}) copy-start(bf16[96,256]{1,0:T(8,128)(2,1)} %copy-done.7) | copy-start | bytes 147460
  36.3 7.5 %collective-permute-start.14 = (bf16[22,16,128]{2,1,0:T(8,128)(2,1)S(1)}, bf16[22,16,128]{2,1,0:T(8,128)(2,1)S(1)}, u32[]{:S(2)}, u32[]{:S(2)}) collective-permute-start(bf16[22,16,128]{2,1,0:T(8,128)(2,1)S(1)} %add_convert_fusion.refs_0_), channel_id=1, source_target_pairs={{0,5},{2,7},{1,4},{3,6},{4,1},{6,3},{5,0},{7,2},{8,13},{10,15},{9,... | collective-permute-start | bytes 270344 | tf_op jit(solution)/shard_map/ppermute | solution.py:436
  38.5 5.4 %collective-permute-start.13 = (bf16[22,16,128]{2,1,0:T(8,128)(2,1)S(1)}, bf16[22,16,128]{2,1,0:T(8,128)(2,1)S(1)}, u32[]{:S(2)}, u32[]{:S(2)}) collective-permute-start(bf16[22,16,128]{2,1,0:T(8,128)(2,1)S(1)} %add_convert_fusion.refs_0_), channel_id=1, source_target_pairs={{0,4},{2,3},{1,5},{3,2},{4,0},{6,7},{5,1},{7,6},{8,12},{10,11},{9,... | collective-permute-start | bytes 270344 | tf_op jit(solution)/shard_map/ppermute | solution.py:436
  39.0 4.9 %collective-permute-start.12 = (bf16[22,16,128]{2,1,0:T(8,128)(2,1)S(1)}, bf16[22,16,128]{2,1,0:T(8,128)(2,1)S(1)}, u32[]{:S(2)}, u32[]{:S(2)}) collective-permute-start(bf16[22,16,128]{2,1,0:T(8,128)(2,1)S(1)} %add_convert_fusion.refs_0_), channel_id=1, source_target_pairs={{0,1},{2,6},{1,0},{3,7},{4,5},{6,2},{5,4},{7,3},{8,9},{10,14},{9,8... | collective-permute-start | bytes 270344 | tf_op jit(solution)/shard_map/ppermute | solution.py:436
  39.9 3.9 %collective-permute-start.11 = (bf16[96,128]{1,0:T(8,128)(2,1)S(1)}, bf16[96,128]{1,0:T(8,128)(2,1)S(1)}, u32[]{:S(2)}, u32[]{:S(2)}) collective-permute-start(bf16[96,128]{1,0:T(8,128)(2,1)S(1)} %get-tuple-element.75), channel_id=1, source_target_pairs={{0,1},{1,0},{2,3},{3,2},{4,5},{5,4},{6,7},{7,6},{8,9},{9,8},{10,11... | collective-permute-start | bytes 73736 | tf_op jit(solution)/shard_map/ppermute | solution.py:425
  43.9 1.8 %collective-permute-start.15 = (bf16[94,16,128]{2,1,0:T(8,128)(2,1)S(1)}, bf16[94,16,128]{2,1,0:T(8,128)(2,1)S(1)}, u32[]{:S(2)}, u32[]{:S(2)}) collective-permute-start(bf16[94,16,128]{2,1,0:T(8,128)(2,1)S(1)} %join.1.mine_ref), channel_id=1, source_target_pairs={{0,2},{2,0},{1,3},{3,1},{4,6},{6,4},{5,7},{7,5},{8,10},{10,8},{9,1... | collective-permute-start | bytes 1155080 | tf_op jit(solution)/shard_map/ppermute | solution.py:444

commit v12 on v10

--- a/solution.py
+++ b/solution.py
@@ -104,13 +104,17 @@
     conv_columns = offsets * channels
     halo_t = padded_halo(halo_refs)
     lanes = table_lanes(near_ref[:, :LANES], voxels, slabs, core_ref[0])
-    for pair in range(0, offsets, 2):
-        pair = range(pair, min(pair + 2, offsets))
-        away = mm(halo_t, far_one_hots(lanes, halo_t.shape[1], voxels, pair))
-        for i, o in enumerate(pair):
+    pack = 2 * LANES // RIM
+    iota = lax.broadcasted_iota(jnp.int32, (halo_t.shape[1], 2 * LANES), 0) + voxels
+    empty = jnp.zeros((channels, LANES - RIM), F32)
+    for start in range(0, offsets, pack):
+        group = [lanes[min(o, offsets - 1) : min(o, offsets - 1) + 1, :RIM] for o in range(start, start + pack)]
+        hot = jnp.where(iota == jnp.concatenate(group, axis=1), 1.0, 0.0).astype(BF16)
+        away = mm(halo_t, hot)
+        for i, o in enumerate(range(start, min(start + pack, offsets))):
             rows = slice(o * channels, (o + 1) * channels)
-            first = first_ref[rows, :].astype(F32) + away[:, i * LANES : (i + 1) * LANES]
-            rt[rows, :LANES] = first.astype(BF16)
+            part = jnp.concatenate([away[:, i * RIM : (i + 1) * RIM], empty], axis=1)
+            rt[rows, :LANES] = (first_ref[rows, :].astype(F32) + part).astype(BF16)
             rt[rows, LANES:] = rest_ref[rows, :]
 
     out_t = mm(w_ref[...], rt[...])

time: 46.3 us -> 46.3 us (level)
  no operation moved by 1% of the time
where the time goes in v12:
time: 46.3 us; the launch traced here: 46 us
  starting transfers between devices  21.4 us (46%)
  waiting for transfers between devices  12.9 us (28%)
  Pallas kernels  9.02 us (19%)
  local copies, waits for them, and re-layouts  1.64 us (4%)
  between operations  0.85 us (2%)
    ppermute x3, waiting for transfers between devices, on_device(): lax.ppermute(total, 'far', [(i, i ^ step) for i in range(sizes['far'])])  5.74 us
    ppermute x3, starting transfers between devices, on_device(): lax.ppermute(total, 'far', [(i, i ^ step) for i in range(sizes['far'])])  4.92 us
    ppermute x3, starting transfers between devices, on_device(): got = [lax.ppermute(x, SPLIT, route) for x, route in zip(sent, routes)]  3.57 us
    ppermute x3, starting transfers between devices, on_device(): got = [lax.ppermute(total, SPLIT, route) for route in routes[::-1]]  3.55 us
    ppermute x1, starting transfers between devices, on_device(): mate = lax.ppermute(row, RING, mates)  3.08 us
    ppermute x1, starting transfers between devices, on_device(): side = [lax.ppermute(features_t, 'slab', pairs) for pairs in beside]  3.03 us
    pallas_call x1, Pallas kernels, on_device(): pl.pallas_call(functools.partial(backward_kernel, slabs), out_shape=(jax....  2.53 us
    pallas_call x1, Pallas kernels, on_device(): pl.pallas_call(functools.partial(forward_kernel, slabs), out_shape=(jax.S...  2.27 us
  transfers between devices with their start and end apart: 16, of which 7 were waited for; matrix products, arithmetic and copies ran while one was open for 0% of the time, Pallas kernels for 12%

profile of v12, /device:TPU:0, one launch (start us, length us, event | category | flops | bytes accessed | tf_op | source)
XLA Modules:
  0.0 46.0 jit_solution(5710149402269632573)
XLA Ops:
  0.6 3.0 %collective-permute-start = (bf16[96,256]{1,0:T(8,128)(2,1)}, bf16[96,256]{1,0:T(8,128)(2,1)S(1)}, u32[]{:S(2)}, u32[]{:S(2)}) collective-permute-start(bf16[96,256]{1,0:T(8,128)(2,1)} %bitcast.10), channel_id=1, source_target_pairs={{0,1},{1,0},{2,3},{3,2},{4,5},{5,4},{6,7},{7,6},{8,9},{9,8},{10,11... | collective-permute-start | bytes 147464 | tf_op jit(solution)/shard_map/ppermute | solution.py:309
  3.7 0.8 %copy-done.1 = bf16[256,96]{0,1:T(8,128)(2,1)S(1)} copy-done((bf16[256,96]{0,1:T(8,128)(2,1)S(1)}, bf16[256,96]{0,1:T(8,128)(2,1)}, u32[]{:S(2)}) %copy-start.1) | copy-done | bytes 49176
  4.5 0.8 %copy-done.3 = s32[256,27]{0,1:T(8,128)S(1)} copy-done((s32[256,27]{0,1:T(8,128)S(1)}, s32[256,27]{0,1:T(8,128)}, u32[]{:S(2)}) %copy-start.3) | copy-done | bytes 27672
  5.3 1.0 %gather.1 = (bf16[2592,128]{1,0:T(8,128)(2,1)S(1)}, bf16[2592,128]{1,0:T(8,128)(2,1)S(1)}) custom-call(bf16[96,256]{1,0:T(8,128)(2,1)S(1)} %bitcast.11, s32[27,256]{1,0:T(8,128)S(1)} %bitcast.14), custom_call_target="tpu_custom_call" | custom-call | flops 2000000000 | bytes 10000000 | tf_op jit(solution)/shard_map/gather/pallas_call | solution.py:310
  6.2 0.0 collective-permute-done
  6.3 0.0 copy-start.5
  6.3 0.0 copy-start.8
  6.3 0.1 pad_maximum_fusion
  6.4 0.7 %collective-permute-start.2 = (bf16[96,128]{1,0:T(8,128)(2,1)S(1)}, bf16[96,128]{1,0:T(8,128)(2,1)S(1)}, u32[]{:S(2)}, u32[]{:S(2)}) collective-permute-start(bf16[96,128]{1,0:T(8,128)(2,1)S(1)} %pad_maximum_fusion), channel_id=1, source_target_pairs={{2,4},{6,8},{10,12},{14,16},{18,20},{22,24},{26,28},{4,2},{8,6},{1... | collective-permute-start | bytes 73736 | tf_op jit(solution)/shard_map/ppermute | solution.py:324
  7.1 0.0 copy-start
  7.1 0.0 copy-start.2
  7.1 0.0 copy-start.4
  7.1 0.7 %taps.1 = (bf16[8,64,256]{2,1,0:T(8,128)(2,1)S(1)}, f32[96,256]{1,0:T(8,128)S(1)}) custom-call(s32[8,64]{1,0:T(8,128)S(1)} %bitcast.17, bf16[64,128]{1,0:T(8,128)(2,1)S(1)} %copy-done.5, bf16[768,128]{1,0:T(8,128)(2,1)S(1)} %copy-done.6), custom_call_target="tpu_custom_call" | custom-call | flops 2000000000 | bytes 10000000 | tf_op jit(solution)/shard_map/taps/pallas_call | solution.py:326
  7.8 3.1 %collective-permute-start.1 = (bf16[96,128]{1,0:T(8,128)(2,1)S(1)}, bf16[96,128]{1,0:T(8,128)(2,1)S(1)}, u32[]{:S(2)}, u32[]{:S(2)}) collective-permute-start(bf16[96,128]{1,0:T(8,128)(2,1)S(1)} %pad_maximum_fusion), channel_id=1, source_target_pairs={{0,2},{2,0},{4,6},{6,4},{8,10},{10,8},{12,14},{14,12},{16,18},{18,... | collective-permute-start | bytes 73736 | tf_op jit(solution)/shard_map/ppermute | solution.py:337
  10.9 0.0 collective-permute-done.2.refs_5_
  10.9 0.8 %collective-permute-done.1.refs_4_ = bf16[96,128]{1,0:T(8,128)(2,1)S(1)} collective-permute-done((bf16[96,128]{1,0:T(8,128)(2,1)S(1)}, bf16[96,128]{1,0:T(8,128)(2,1)S(1)}, u32[]{:S(2)}, u32[]{:S(2)}) %collective-permute-start.1) | collective-permute-done | bytes 24608 | tf_op jit(solution)/shard_map/ppermute | solution.py:337
  11.8 2.3 %forward.1 = (bf16[96,256]{1,0:T(8,128)(2,1)S(1)}, bf16[96,256]{1,0:T(8,128)(2,1)S(1)}, f32[88,16,128]{2,1,0:T(8,128)S(1)}, bf16[88,16,128]{2,1,0:T(8,128)(2,1)S(1)}) custom-call(s32[1]{0:T(128)} %bitcast.core_ref, bf16[96,256]{1,0:T(8,128)(2,1)S(1)} %bitcast.13, s32[27,256]{1,0:T(8,128)S(1)} %bitcast.15, bf16[64,128]{1,0:T(8,128)(2,1)S(1)} %copy-done.5, ...), custom_call_target="tpu_custom_call" | custom-call | tf_op jit(solution)/shard_map/forward/pallas_call | solution.py:343
  14.0 0.5 %collective-permute-start.3 = (bf16[88,16,128]{2,1,0:T(8,128)(2,1)S(1)}, bf16[88,16,128]{2,1,0:T(8,128)(2,1)S(1)}, u32[]{:S(2)}, u32[]{:S(2)}) collective-permute-start(bf16[88,16,128]{2,1,0:T(8,128)(2,1)S(1)} %get-tuple-element.61), channel_id=1, source_target_pairs={{0,2},{2,0},{1,3},{3,1},{4,6},{6,4},{5,7},{7,5},{8,10},{10,8},{9,1... | collective-permute-start | bytes 1081352 | tf_op jit(solution)/shard_map/ppermute | solution.py:361
  14.5 1.3 %collective-permute-done.3.got_ref = bf16[88,16,128]{2,1,0:T(8,128)(2,1)S(1)} collective-permute-done((bf16[88,16,128]{2,1,0:T(8,128)(2,1)S(1)}, bf16[88,16,128]{2,1,0:T(8,128)(2,1)S(1)}, u32[]{:S(2)}, u32[]{:S(2)}) %collective-permute-start.3) | collective-permute-done | bytes 360480 | tf_op jit(solution)/shard_map/ppermute | solution.py:361
  15.8 0.1 split.1
  15.9 2.7 %collective-permute-start.4 = (bf16[22,16,128]{2,1,0:T(8,128)(2,1)S(1)}, bf16[22,16,128]{2,1,0:T(8,128)(2,1)S(1)}, u32[]{:S(2)}, u32[]{:S(2)}) collective-permute-start(bf16[22,16,128]{2,1,0:T(8,128)(2,1)S(1)} %get-tuple-element.69), channel_id=1, source_target_pairs={{0,5},{2,7},{1,4},{3,6},{4,1},{6,3},{5,0},{7,2},{8,13},{10,15},{9,... | collective-permute-start | bytes 270344 | tf_op jit(solution)/shard_map/ppermute | solution.py:373
  18.6 0.4 collective-permute-start.5
  18.9 0.5 %collective-permute-start.6 = (bf16[22,16,128]{2,1,0:T(8,128)(2,1)S(1)}, bf16[22,16,128]{2,1,0:T(8,128)(2,1)S(1)}, u32[]{:S(2)}, u32[]{:S(2)}) collective-permute-start(bf16[22,16,128]{2,1,0:T(8,128)(2,1)S(1)} %get-tuple-element.71), channel_id=1, source_target_pairs={{0,1},{2,6},{1,0},{3,7},{4,5},{6,2},{5,4},{7,3},{8,9},{10,14},{9,8... | collective-permute-start | bytes 270344 | tf_op jit(solution)/shard_map/ppermute | solution.py:373
  19.5 2.5 %backward.1 = (f32[96,256]{1,0:T(8,128)S(1)}, f32[96,64]{1,0:T(8,128)S(1)}, f32[96,128]{1,0:T(8,128)S(1)}, bf16[96,128]{1,0:T(8,128)(2,1)S(1)}) custom-call(s32[1]{0:T(128)} %bitcast.core_ref, s32[27,256]{1,0:T(8,128)S(1)} %bitcast.16, f32[96,256]{1,0:T(8,128)S(1)} %get-tuple-element.55.refs_3_.hgrad_ref, bf16[96,256]{1,0:T(8,128)(2,1)S(1)} %get-tuple-element.66.grad_ref, ...), custom_call_target="tpu_custom_call" | custom-call | flops 2000000000 | bytes 10000000 | tf_op jit(solution)/shard_map/backward/pallas_call | solution.py:374
  22.0 0.0 collective-permute-done.4
  22.0 1.7 %collective-permute-done.5 = bf16[22,16,128]{2,1,0:T(8,128)(2,1)S(1)} collective-permute-done((bf16[22,16,128]{2,1,0:T(8,128)(2,1)S(1)}, bf16[22,16,128]{2,1,0:T(8,128)(2,1)S(1)}, u32[]{:S(2)}, u32[]{:S(2)}) %collective-permute-start.5) | collective-permute-done | bytes 90144 | tf_op jit(solution)/shard_map/ppermute | solution.py:373
  23.7 0.0 collective-permute-done.6
  23.7 0.1 add_convert_fusion.1
  23.8 0.0 copy-start.7
  23.8 4.3 %collective-permute-start.9 = (bf16[22,16,128]{2,1,0:T(8,128)(2,1)S(1)}, bf16[22,16,128]{2,1,0:T(8,128)(2,1)S(1)}, u32[]{:S(2)}, u32[]{:S(2)}) collective-permute-start(bf16[22,16,128]{2,1,0:T(8,128)(2,1)S(1)} %add_convert_fusion.1), channel_id=1, source_target_pairs={{0,24},{8,16},{16,8},{24,0},{1,25},{9,17},{17,9},{25,1},{2,26},{10... | collective-permute-start | bytes 270344 | tf_op jit(solution)/shard_map/ppermute | solution.py:405
  28.1 0.0 collective-permute-start.8
  28.1 0.6 %collective-permute-start.7 = (bf16[22,16,128]{2,1,0:T(8,128)(2,1)S(1)}, bf16[22,16,128]{2,1,0:T(8,128)(2,1)S(1)}, u32[]{:S(2)}, u32[]{:S(2)}) collective-permute-start(bf16[22,16,128]{2,1,0:T(8,128)(2,1)S(1)} %add_convert_fusion.1), channel_id=1, source_target_pairs={{0,8},{8,0},{16,24},{24,16},{1,9},{9,1},{17,25},{25,17},{2,10},{10... | collective-permute-start | bytes 270344 | tf_op jit(solution)/shard_map/ppermute | solution.py:405
  28.7 0.7 %collective-permute-start.10 = (bf16[96,128]{1,0:T(8,128)(2,1)S(1)}, bf16[96,128]{1,0:T(8,128)(2,1)S(1)}, u32[]{:S(2)}, u32[]{:S(2)}) collective-permute-start(bf16[96,128]{1,0:T(8,128)(2,1)S(1)} %get-tuple-element.77), channel_id=1, source_target_pairs={{2,4},{6,8},{10,12},{14,16},{18,20},{22,24},{26,28},{4,2},{8,6},{1... | collective-permute-start | bytes 73736 | tf_op jit(solution)/shard_map/ppermute | solution.py:406
  29.4 2.2 %collective-permute-done.9 = bf16[22,16,128]{2,1,0:T(8,128)(2,1)S(1)} collective-permute-done((bf16[22,16,128]{2,1,0:T(8,128)(2,1)S(1)}, bf16[22,16,128]{2,1,0:T(8,128)(2,1)S(1)}, u32[]{:S(2)}, u32[]{:S(2)}) %collective-permute-start.9) | collective-permute-done | bytes 90144 | tf_op jit(solution)/shard_map/ppermute | solution.py:405
  31.6 3.5 %collective-permute-done.8 = bf16[22,16,128]{2,1,0:T(8,128)(2,1)S(1)} collective-permute-done((bf16[22,16,128]{2,1,0:T(8,128)(2,1)S(1)}, bf16[22,16,128]{2,1,0:T(8,128)(2,1)S(1)}, u32[]{:S(2)}, u32[]{:S(2)}) %collective-permute-start.8) | collective-permute-done | bytes 90144 | tf_op jit(solution)/shard_map/ppermute | solution.py:405
  35.1 0.0 collective-permute-done.7
  35.1 0.1 add_convert_fusion.refs_0_
  35.2 2.0 %collective-permute-start.14 = (bf16[22,16,128]{2,1,0:T(8,128)(2,1)S(1)}, bf16[22,16,128]{2,1,0:T(8,128)(2,1)S(1)}, u32[]{:S(2)}, u32[]{:S(2)}) collective-permute-start(bf16[22,16,128]{2,1,0:T(8,128)(2,1)S(1)} %add_convert_fusion.refs_0_), channel_id=1, source_target_pairs={{0,5},{2,7},{1,4},{3,6},{4,1},{6,3},{5,0},{7,2},{8,13},{10,15},{9,... | collective-permute-start | bytes 270344 | tf_op jit(solution)/shard_map/ppermute | solution.py:431
  37.2 0.9 %collective-permute-start.13 = (bf16[22,16,128]{2,1,0:T(8,128)(2,1)S(1)}, bf16[22,16,128]{2,1,0:T(8,128)(2,1)S(1)}, u32[]{:S(2)}, u32[]{:S(2)}) collective-permute-start(bf16[22,16,128]{2,1,0:T(8,128)(2,1)S(1)} %add_convert_fusion.refs_0_), channel_id=1, source_target_pairs={{0,4},{2,3},{1,5},{3,2},{4,0},{6,7},{5,1},{7,6},{8,12},{10,11},{9,... | collective-permute-start | bytes 270344 | tf_op jit(solution)/shard_map/ppermute | solution.py:431
  38.1 0.7 %collective-permute-start.12 = (bf16[22,16,128]{2,1,0:T(8,128)(2,1)S(1)}, bf16[22,16,128]{2,1,0:T(8,128)(2,1)S(1)}, u32[]{:S(2)}, u32[]{:S(2)}) collective-permute-start(bf16[22,16,128]{2,1,0:T(8,128)(2,1)S(1)} %add_convert_fusion.refs_0_), channel_id=1, source_target_pairs={{0,1},{2,6},{1,0},{3,7},{4,5},{6,2},{5,4},{7,3},{8,9},{10,14},{9,8... | collective-permute-start | bytes 270344 | tf_op jit(solution)/shard_map/ppermute | solution.py:431
  38.8 1.4 %collective-permute-start.11 = (bf16[96,128]{1,0:T(8,128)(2,1)S(1)}, bf16[96,128]{1,0:T(8,128)(2,1)S(1)}, u32[]{:S(2)}, u32[]{:S(2)}) collective-permute-start(bf16[96,128]{1,0:T(8,128)(2,1)S(1)} %get-tuple-element.79), channel_id=1, source_target_pairs={{0,1},{1,0},{2,3},{3,2},{4,5},{5,4},{6,7},{7,6},{8,9},{9,8},{10,11... | collective-permute-start | bytes 73736 | tf_op jit(solution)/shard_map/ppermute | solution.py:420
  40.2 1.1 %coarse.1 = bf16[64,128]{1,0:T(8,128)(2,1)} custom-call(bf16[8,64,256]{2,1,0:T(8,128)(2,1)S(1)} %get-tuple-element.58.refs_2_.pick_ref, bf16[96,256]{1,0:T(8,128)(2,1)S(1)} %get-tuple-element.80.hidden_ref, bf16[768,128]{1,0:T(8,128)(2,1)S(1)} %copy-done.7), custom_call_target="tpu_custom_call" | custom-call | flops 2000000000 | bytes 10000000 | tf_op jit(solution)/shard_map/coarse/pallas_call | solution.py:395
  41.3 1.5 %collective-permute-done.11.refs_0_ = bf16[96,128]{1,0:T(8,128)(2,1)S(1)} collective-permute-done((bf16[96,128]{1,0:T(8,128)(2,1)S(1)}, bf16[96,128]{1,0:T(8,128)(2,1)S(1)}, u32[]{:S(2)}, u32[]{:S(2)}) %collective-permute-start.11) | collective-permute-done | bytes 24608 | tf_op jit(solution)/shard_map/ppermute | solution.py:420
  42.9 0.1 slab_turn.1
  43.0 0.0 collective-permute-done.13.refs_2_
  43.0 0.1 collective-permute-start.15
  43.1 1.7 %collective-permute-done.15.other_ref = bf16[94,16,128]{2,1,0:T(8,128)(2,1)S(1)} collective-permute-done((bf16[94,16,128]{2,1,0:T(8,128)(2,1)S(1)}, bf16[94,16,128]{2,1,0:T(8,128)(2,1)S(1)}, u32[]{:S(2)}, u32[]{:S(2)}) %collective-permute-start.15) | collective-permute-done | bytes 385056 | tf_op jit(solution)/shard_map/ppermute | solution.py:439
  44.8 1.2 %final.1 = (f32[96,2592]{1,0:T(8,128)}, f32[768,128]{1,0:T(8,128)}, f32[96,256]{1,0:T(8,128)}) custom-call(s32[1]{0:T(128)} %bitcast.core_ref, bf16[94,16,128]{2,1,0:T(8,128)(2,1)S(1)} %join.1.mine_ref, bf16[94,16,128]{2,1,0:T(8,128)(2,1)S(1)} %collective-permute-done.15.other_ref, f32[96,256]{1,0:T(8,128)S(1)} %get-tuple-element.87.refs_0_, ...), custom_call_target="tpu_custom_call" | custom-call | tf_op jit(solution)/shard_map/final/pallas_call | solution.py:440
  (17 shorter events, 0.1 us)
Async XLA Ops:
  0.6 5.6 %collective-permute-start = (bf16[96,256]{1,0:T(8,128)(2,1)}, bf16[96,256]{1,0:T(8,128)(2,1)S(1)}, u32[]{:S(2)}, u32[]{:S(2)}) collective-permute-start(bf16[96,256]{1,0:T(8,128)(2,1)} %bitcast.10), channel_id=1, source_target_pairs={{0,1},{1,0},{2,3},{3,2},{4,5},{5,4},{6,7},{7,6},{8,9},{9,8},{10,11... | collective-permute-start | bytes 147464 | tf_op jit(solution)/shard_map/ppermute | solution.py:309
  3.7 0.8 %copy-start.1 = (bf16[256,96]{0,1:T(8,128)(2,1)S(1)}, bf16[256,96]{0,1:T(8,128)(2,1)}, u32[]{:S(2)}) copy-start(bf16[256,96]{0,1:T(8,128)(2,1)} %param.6) | copy-start | bytes 147460
  4.5 0.8 %copy-start.3 = (s32[256,27]{0,1:T(8,128)S(1)}, s32[256,27]{0,1:T(8,128)}, u32[]{:S(2)}) copy-start(s32[256,27]{0,1:T(8,128)} %param.7) | copy-start | bytes 82948
  5.3 1.8 %copy-start.6 = (bf16[768,128]{1,0:T(8,128)(2,1)S(1)}, bf16[768,128]{1,0:T(8,128)(2,1)}, u32[]{:S(2)}) copy-start(bf16[768,128]{1,0:T(8,128)(2,1)} %wd_ref.3) | copy-start | bytes 589828
  6.3 0.8 %copy-start.5 = (bf16[64,128]{1,0:T(8,128)(2,1)S(1)}, bf16[64,128]{1,0:T(8,128)(2,1)}, u32[]{:S(2)}) copy-start(bf16[64,128]{1,0:T(8,128)(2,1)} %cgrad_ref.3) | copy-start | bytes 49156
  6.3 0.8 %copy-start.8 = (s32[64,8]{0,1:T(8,128)S(1)}, s32[64,8]{0,1:T(8,128)}, u32[]{:S(2)}) copy-start(s32[64,8]{0,1:T(8,128)} %param.8) | copy-start | bytes 6148
  6.4 4.5 %collective-permute-start.2 = (bf16[96,128]{1,0:T(8,128)(2,1)S(1)}, bf16[96,128]{1,0:T(8,128)(2,1)S(1)}, u32[]{:S(2)}, u32[]{:S(2)}) collective-permute-start(bf16[96,128]{1,0:T(8,128)(2,1)S(1)} %pad_maximum_fusion), channel_id=1, source_target_pairs={{2,4},{6,8},{10,12},{14,16},{18,20},{22,24},{26,28},{4,2},{8,6},{1... | collective-permute-start | bytes 73736 | tf_op jit(solution)/shard_map/ppermute | solution.py:324
  7.1 4.7 %copy-start = (bf16[2592,96]{0,1:T(8,128)(2,1)S(1)}, bf16[2592,96]{0,1:T(8,128)(2,1)}, u32[]{:S(2)}) copy-start(bf16[2592,96]{0,1:T(8,128)(2,1)} %param.9) | copy-start | bytes 1492996
  7.1 4.7 %copy-start.2 = (bf16[256,96]{0,1:T(8,128)(2,1)S(1)}, bf16[256,96]{0,1:T(8,128)(2,1)}, u32[]{:S(2)}) copy-start(bf16[256,96]{0,1:T(8,128)(2,1)} %param.6) | copy-start | bytes 147460
  7.1 4.7 %copy-start.4 = (s32[256,27]{0,1:T(8,128)S(1)}, s32[256,27]{0,1:T(8,128)}, u32[]{:S(2)}) copy-start(s32[256,27]{0,1:T(8,128)} %param.7) | copy-start | bytes 82948
  7.8 3.9 %collective-permute-start.1 = (bf16[96,128]{1,0:T(8,128)(2,1)S(1)}, bf16[96,128]{1,0:T(8,128)(2,1)S(1)}, u32[]{:S(2)}, u32[]{:S(2)}) collective-permute-start(bf16[96,128]{1,0:T(8,128)(2,1)S(1)} %pad_maximum_fusion), channel_id=1, source_target_pairs={{0,2},{2,0},{4,6},{6,4},{8,10},{10,8},{12,14},{14,12},{16,18},{18,... | collective-permute-start | bytes 73736 | tf_op jit(solution)/shard_map/ppermute | solution.py:337
  14.0 1.8 %collective-permute-start.3 = (bf16[88,16,128]{2,1,0:T(8,128)(2,1)S(1)}, bf16[88,16,128]{2,1,0:T(8,128)(2,1)S(1)}, u32[]{:S(2)}, u32[]{:S(2)}) collective-permute-start(bf16[88,16,128]{2,1,0:T(8,128)(2,1)S(1)} %get-tuple-element.61), channel_id=1, source_target_pairs={{0,2},{2,0},{1,3},{3,1},{4,6},{6,4},{5,7},{7,5},{8,10},{10,8},{9,1... | collective-permute-start | bytes 1081352 | tf_op jit(solution)/shard_map/ppermute | solution.py:361
  15.9 6.1 %collective-permute-start.4 = (bf16[22,16,128]{2,1,0:T(8,128)(2,1)S(1)}, bf16[22,16,128]{2,1,0:T(8,128)(2,1)S(1)}, u32[]{:S(2)}, u32[]{:S(2)}) collective-permute-start(bf16[22,16,128]{2,1,0:T(8,128)(2,1)S(1)} %get-tuple-element.69), channel_id=1, source_target_pairs={{0,5},{2,7},{1,4},{3,6},{4,1},{6,3},{5,0},{7,2},{8,13},{10,15},{9,... | collective-permute-start | bytes 270344 | tf_op jit(solution)/shard_map/ppermute | solution.py:373
  18.6 5.2 %collective-permute-start.5 = (bf16[22,16,128]{2,1,0:T(8,128)(2,1)S(1)}, bf16[22,16,128]{2,1,0:T(8,128)(2,1)S(1)}, u32[]{:S(2)}, u32[]{:S(2)}) collective-permute-start(bf16[22,16,128]{2,1,0:T(8,128)(2,1)S(1)} %get-tuple-element.70), channel_id=1, source_target_pairs={{0,4},{2,3},{1,5},{3,2},{4,0},{6,7},{5,1},{7,6},{8,12},{10,11},{9,... | collective-permute-start | bytes 270344 | tf_op jit(solution)/shard_map/ppermute | solution.py:373
  18.9 4.8 %collective-permute-start.6 = (bf16[22,16,128]{2,1,0:T(8,128)(2,1)S(1)}, bf16[22,16,128]{2,1,0:T(8,128)(2,1)S(1)}, u32[]{:S(2)}, u32[]{:S(2)}) collective-permute-start(bf16[22,16,128]{2,1,0:T(8,128)(2,1)S(1)} %get-tuple-element.71), channel_id=1, source_target_pairs={{0,1},{2,6},{1,0},{3,7},{4,5},{6,2},{5,4},{7,3},{8,9},{10,14},{9,8... | collective-permute-start | bytes 270344 | tf_op jit(solution)/shard_map/ppermute | solution.py:373
  23.8 16.4 %copy-start.7 = (bf16[768,128]{1,0:T(8,128)(2,1)S(1)}, bf16[768,128]{1,0:T(8,128)(2,1)}, u32[]{:S(2)}) copy-start(bf16[768,128]{1,0:T(8,128)(2,1)} %wd_ref.3) | copy-start | bytes 589828
  23.8 7.8 %collective-permute-start.9 = (bf16[22,16,128]{2,1,0:T(8,128)(2,1)S(1)}, bf16[22,16,128]{2,1,0:T(8,128)(2,1)S(1)}, u32[]{:S(2)}, u32[]{:S(2)}) collective-permute-start(bf16[22,16,128]{2,1,0:T(8,128)(2,1)S(1)} %add_convert_fusion.1), channel_id=1, source_target_pairs={{0,24},{8,16},{16,8},{24,0},{1,25},{9,17},{17,9},{25,1},{2,26},{10... | collective-permute-start | bytes 270344 | tf_op jit(solution)/shard_map/ppermute | solution.py:405
  28.1 7.0 %collective-permute-start.8 = (bf16[22,16,128]{2,1,0:T(8,128)(2,1)S(1)}, bf16[22,16,128]{2,1,0:T(8,128)(2,1)S(1)}, u32[]{:S(2)}, u32[]{:S(2)}) collective-permute-start(bf16[22,16,128]{2,1,0:T(8,128)(2,1)S(1)} %add_convert_fusion.1), channel_id=1, source_target_pairs={{0,16},{8,24},{16,0},{24,8},{1,17},{9,25},{17,1},{25,9},{2,18},{10... | collective-permute-start | bytes 270344 | tf_op jit(solution)/shard_map/ppermute | solution.py:405
  28.1 7.0 %collective-permute-start.7 = (bf16[22,16,128]{2,1,0:T(8,128)(2,1)S(1)}, bf16[22,16,128]{2,1,0:T(8,128)(2,1)S(1)}, u32[]{:S(2)}, u32[]{:S(2)}) collective-permute-start(bf16[22,16,128]{2,1,0:T(8,128)(2,1)S(1)} %add_convert_fusion.1), channel_id=1, source_target_pairs={{0,8},{8,0},{16,24},{24,16},{1,9},{9,1},{17,25},{25,17},{2,10},{10... | collective-permute-start | bytes 270344 | tf_op jit(solution)/shard_map/ppermute | solution.py:405
  28.7 6.5 %collective-permute-start.10 = (bf16[96,128]{1,0:T(8,128)(2,1)S(1)}, bf16[96,128]{1,0:T(8,128)(2,1)S(1)}, u32[]{:S(2)}, u32[]{:S(2)}) collective-permute-start(bf16[96,128]{1,0:T(8,128)(2,1)S(1)} %get-tuple-element.77), channel_id=1, source_target_pairs={{2,4},{6,8},{10,12},{14,16},{18,20},{22,24},{26,28},{4,2},{8,6},{1... | collective-permute-start | bytes 73736 | tf_op jit(solution)/shard_map/ppermute | solution.py:406
  35.2 7.8 %collective-permute-start.14 = (bf16[22,16,128]{2,1,0:T(8,128)(2,1)S(1)}, bf16[22,16,128]{2,1,0:T(8,128)(2,1)S(1)}, u32[]{:S(2)}, u32[]{:S(2)}) collective-permute-start(bf16[22,16,128]{2,1,0:T(8,128)(2,1)S(1)} %add_convert_fusion.refs_0_), channel_id=1, source_target_pairs={{0,5},{2,7},{1,4},{3,6},{4,1},{6,3},{5,0},{7,2},{8,13},{10,15},{9,... | collective-permute-start | bytes 270344 | tf_op jit(solution)/shard_map/ppermute | solution.py:431
  37.2 5.7 %collective-permute-start.13 = (bf16[22,16,128]{2,1,0:T(8,128)(2,1)S(1)}, bf16[22,16,128]{2,1,0:T(8,128)(2,1)S(1)}, u32[]{:S(2)}, u32[]{:S(2)}) collective-permute-start(bf16[22,16,128]{2,1,0:T(8,128)(2,1)S(1)} %add_convert_fusion.refs_0_), channel_id=1, source_target_pairs={{0,4},{2,3},{1,5},{3,2},{4,0},{6,7},{5,1},{7,6},{8,12},{10,11},{9,... | collective-permute-start | bytes 270344 | tf_op jit(solution)/shard_map/ppermute | solution.py:431
  38.1 4.9 %collective-permute-start.12 = (bf16[22,16,128]{2,1,0:T(8,128)(2,1)S(1)}, bf16[22,16,128]{2,1,0:T(8,128)(2,1)S(1)}, u32[]{:S(2)}, u32[]{:S(2)}) collective-permute-start(bf16[22,16,128]{2,1,0:T(8,128)(2,1)S(1)} %add_convert_fusion.refs_0_), channel_id=1, source_target_pairs={{0,1},{2,6},{1,0},{3,7},{4,5},{6,2},{5,4},{7,3},{8,9},{10,14},{9,8... | collective-permute-start | bytes 270344 | tf_op jit(solution)/shard_map/ppermute | solution.py:431
  38.8 4.1 %collective-permute-start.11 = (bf16[96,128]{1,0:T(8,128)(2,1)S(1)}, bf16[96,128]{1,0:T(8,128)(2,1)S(1)}, u32[]{:S(2)}, u32[]{:S(2)}) collective-permute-start(bf16[96,128]{1,0:T(8,128)(2,1)S(1)} %get-tuple-element.79), channel_id=1, source_target_pairs={{0,1},{1,0},{2,3},{3,2},{4,5},{5,4},{6,7},{7,6},{8,9},{9,8},{10,11... | collective-permute-start | bytes 73736 | tf_op jit(solution)/shard_map/ppermute | solution.py:420
  43.0 1.8 %collective-permute-start.15 = (bf16[94,16,128]{2,1,0:T(8,128)(2,1)S(1)}, bf16[94,16,128]{2,1,0:T(8,128)(2,1)S(1)}, u32[]{:S(2)}, u32[]{:S(2)}) collective-permute-start(bf16[94,16,128]{2,1,0:T(8,128)(2,1)S(1)} %join.1.mine_ref), channel_id=1, source_target_pairs={{0,2},{2,0},{1,3},{3,1},{4,6},{6,4},{5,7},{7,5},{8,10},{10,8},{9,1... | collective-permute-start | bytes 1155080 | tf_op jit(solution)/shard_map/ppermute | solution.py:439

commit v13 on v12

--- a/solution.py
+++ b/solution.py
@@ -408,7 +408,6 @@
     while len(parts) > 1:
         parts = [x + y for x, y in zip(parts[0::2], parts[1::2])]
     total = parts[0].astype(BF16)
-    total, cross = lax.optimization_barrier((total, cross))
     home, *edges = pl.pallas_call(
         functools.partial(cross_turn_kernel, 0 if slabs == 2 else 1),
         out_shape=[jax.ShapeDtypeStruct((channels, RIM), F32)]

time: 46.3 us -> 46 us (level)
    ppermute x3, waiting for transfers between devices: 0.01 us -> 2.69 us  [on_device(): got = [lax.ppermute(total, SPLIT, route) for route in routes[::-1]]]
    ppermute x1, waiting for transfers between devices: 1.55 us -> 0.01 us  [on_device(): edges = [lax.ppermute(x, 'slab', p) for x, p in zip(edges, back)]]
    ppermute x3, waiting for transfers between devices: 5.74 us -> 4.64 us  [on_device(): lax.ppermute(total, 'far', [(i, i ^ step) for i in range(sizes['far'])])]
  transfers between devices with their start and end apart: 16 -> 16, of which waited for: 7 -> 9; matrix products, arithmetic and copies ran while one was open for 0% -> 0% of each run, Pallas kernels for 12% -> 12%
where the time goes in v13:
time: 46 us; the launch traced here: 45.7 us
  starting transfers between devices  21.1 us (46%)
  waiting for transfers between devices  12.9 us (28%)
  Pallas kernels  9.02 us (20%)
  local copies, waits for them, and re-layouts  1.64 us (4%)
  between operations  0.84 us (2%)
    ppermute x3, starting transfers between devices, on_device(): lax.ppermute(total, 'far', [(i, i ^ step) for i in range(sizes['far'])])  4.92 us
    ppermute x3, waiting for transfers between devices, on_device(): lax.ppermute(total, 'far', [(i, i ^ step) for i in range(sizes['far'])])  4.64 us
    ppermute x3, starting transfers between devices, on_device(): got = [lax.ppermute(x, SPLIT, route) for x, route in zip(sent, routes)]  3.57 us
    ppermute x3, starting transfers between devices, on_device(): got = [lax.ppermute(total, SPLIT, route) for route in routes[::-1]]  3.55 us
    ppermute x1, starting transfers between devices, on_device(): mate = lax.ppermute(row, RING, mates)  3.08 us
    ppermute x1, starting transfers between devices, on_device(): side = [lax.ppermute(features_t, 'slab', pairs) for pairs in beside]  3.03 us
    ppermute x3, waiting for transfers between devices, on_device(): got = [lax.ppermute(total, SPLIT, route) for route in routes[::-1]]  2.69 us
    pallas_call x1, Pallas kernels, on_device(): pl.pallas_call(functools.partial(backward_kernel, slabs), out_shape=(jax....  2.53 us
  transfers between devices with their start and end apart: 16, of which 9 were waited for; matrix products, arithmetic and copies ran while one was open for 0% of the time, Pallas kernels for 12%

profile of v13, /device:TPU:0, one launch (start us, length us, event | category | flops | bytes accessed | tf_op | source)
XLA Modules:
  0.0 45.7 jit_solution(10061938059926768097)
XLA Ops:
  0.6 3.0 %collective-permute-start = (bf16[96,256]{1,0:T(8,128)(2,1)}, bf16[96,256]{1,0:T(8,128)(2,1)S(1)}, u32[]{:S(2)}, u32[]{:S(2)}) collective-permute-start(bf16[96,256]{1,0:T(8,128)(2,1)} %bitcast.10), channel_id=1, source_target_pairs={{0,1},{1,0},{2,3},{3,2},{4,5},{5,4},{6,7},{7,6},{8,9},{9,8},{10,11... | collective-permute-start | bytes 147464 | tf_op jit(solution)/shard_map/ppermute | solution.py:309
  3.7 0.8 %copy-done.1 = bf16[256,96]{0,1:T(8,128)(2,1)S(1)} copy-done((bf16[256,96]{0,1:T(8,128)(2,1)S(1)}, bf16[256,96]{0,1:T(8,128)(2,1)}, u32[]{:S(2)}) %copy-start.1) | copy-done | bytes 49176
  4.5 0.8 %copy-done.3 = s32[256,27]{0,1:T(8,128)S(1)} copy-done((s32[256,27]{0,1:T(8,128)S(1)}, s32[256,27]{0,1:T(8,128)}, u32[]{:S(2)}) %copy-start.3) | copy-done | bytes 27672
  5.3 1.0 %gather.1 = (bf16[2592,128]{1,0:T(8,128)(2,1)S(1)}, bf16[2592,128]{1,0:T(8,128)(2,1)S(1)}) custom-call(bf16[96,256]{1,0:T(8,128)(2,1)S(1)} %bitcast.11, s32[27,256]{1,0:T(8,128)S(1)} %bitcast.14), custom_call_target="tpu_custom_call" | custom-call | flops 2000000000 | bytes 10000000 | tf_op jit(solution)/shard_map/gather/pallas_call | solution.py:310
  6.2 0.0 collective-permute-done
  6.3 0.0 copy-start.5
  6.3 0.0 copy-start.8
  6.3 0.1 pad_maximum_fusion
  6.4 0.7 %collective-permute-start.2 = (bf16[96,128]{1,0:T(8,128)(2,1)S(1)}, bf16[96,128]{1,0:T(8,128)(2,1)S(1)}, u32[]{:S(2)}, u32[]{:S(2)}) collective-permute-start(bf16[96,128]{1,0:T(8,128)(2,1)S(1)} %pad_maximum_fusion), channel_id=1, source_target_pairs={{2,4},{6,8},{10,12},{14,16},{18,20},{22,24},{26,28},{4,2},{8,6},{1... | collective-permute-start | bytes 73736 | tf_op jit(solution)/shard_map/ppermute | solution.py:324
  7.1 0.0 copy-start
  7.1 0.0 copy-start.2
  7.1 0.0 copy-start.4
  7.1 0.7 %taps.1 = (bf16[8,64,256]{2,1,0:T(8,128)(2,1)S(1)}, f32[96,256]{1,0:T(8,128)S(1)}) custom-call(s32[8,64]{1,0:T(8,128)S(1)} %bitcast.17, bf16[64,128]{1,0:T(8,128)(2,1)S(1)} %copy-done.5, bf16[768,128]{1,0:T(8,128)(2,1)S(1)} %copy-done.6), custom_call_target="tpu_custom_call" | custom-call | flops 2000000000 | bytes 10000000 | tf_op jit(solution)/shard_map/taps/pallas_call | solution.py:326
  7.8 3.1 %collective-permute-start.1 = (bf16[96,128]{1,0:T(8,128)(2,1)S(1)}, bf16[96,128]{1,0:T(8,128)(2,1)S(1)}, u32[]{:S(2)}, u32[]{:S(2)}) collective-permute-start(bf16[96,128]{1,0:T(8,128)(2,1)S(1)} %pad_maximum_fusion), channel_id=1, source_target_pairs={{0,2},{2,0},{4,6},{6,4},{8,10},{10,8},{12,14},{14,12},{16,18},{18,... | collective-permute-start | bytes 73736 | tf_op jit(solution)/shard_map/ppermute | solution.py:337
  10.9 0.0 collective-permute-done.2.refs_5_
  10.9 0.8 %collective-permute-done.1.refs_4_ = bf16[96,128]{1,0:T(8,128)(2,1)S(1)} collective-permute-done((bf16[96,128]{1,0:T(8,128)(2,1)S(1)}, bf16[96,128]{1,0:T(8,128)(2,1)S(1)}, u32[]{:S(2)}, u32[]{:S(2)}) %collective-permute-start.1) | collective-permute-done | bytes 24608 | tf_op jit(solution)/shard_map/ppermute | solution.py:337
  11.8 2.3 %forward.1 = (bf16[96,256]{1,0:T(8,128)(2,1)S(1)}, bf16[96,256]{1,0:T(8,128)(2,1)S(1)}, f32[88,16,128]{2,1,0:T(8,128)S(1)}, bf16[88,16,128]{2,1,0:T(8,128)(2,1)S(1)}) custom-call(s32[1]{0:T(128)} %bitcast.core_ref, bf16[96,256]{1,0:T(8,128)(2,1)S(1)} %bitcast.13, s32[27,256]{1,0:T(8,128)S(1)} %bitcast.15, bf16[64,128]{1,0:T(8,128)(2,1)S(1)} %copy-done.5, ...), custom_call_target="tpu_custom_call" | custom-call | tf_op jit(solution)/shard_map/forward/pallas_call | solution.py:343
  14.0 0.5 %collective-permute-start.3 = (bf16[88,16,128]{2,1,0:T(8,128)(2,1)S(1)}, bf16[88,16,128]{2,1,0:T(8,128)(2,1)S(1)}, u32[]{:S(2)}, u32[]{:S(2)}) collective-permute-start(bf16[88,16,128]{2,1,0:T(8,128)(2,1)S(1)} %get-tuple-element.59), channel_id=1, source_target_pairs={{0,2},{2,0},{1,3},{3,1},{4,6},{6,4},{5,7},{7,5},{8,10},{10,8},{9,1... | collective-permute-start | bytes 1081352 | tf_op jit(solution)/shard_map/ppermute | solution.py:361
  14.5 1.3 %collective-permute-done.3.got_ref = bf16[88,16,128]{2,1,0:T(8,128)(2,1)S(1)} collective-permute-done((bf16[88,16,128]{2,1,0:T(8,128)(2,1)S(1)}, bf16[88,16,128]{2,1,0:T(8,128)(2,1)S(1)}, u32[]{:S(2)}, u32[]{:S(2)}) %collective-permute-start.3) | collective-permute-done | bytes 360480 | tf_op jit(solution)/shard_map/ppermute | solution.py:361
  15.8 0.1 split.1
  15.9 2.7 %collective-permute-start.4 = (bf16[22,16,128]{2,1,0:T(8,128)(2,1)S(1)}, bf16[22,16,128]{2,1,0:T(8,128)(2,1)S(1)}, u32[]{:S(2)}, u32[]{:S(2)}) collective-permute-start(bf16[22,16,128]{2,1,0:T(8,128)(2,1)S(1)} %get-tuple-element.66), channel_id=1, source_target_pairs={{0,5},{2,7},{1,4},{3,6},{4,1},{6,3},{5,0},{7,2},{8,13},{10,15},{9,... | collective-permute-start | bytes 270344 | tf_op jit(solution)/shard_map/ppermute | solution.py:373
  18.6 0.4 collective-permute-start.5
  18.9 0.5 %collective-permute-start.6 = (bf16[22,16,128]{2,1,0:T(8,128)(2,1)S(1)}, bf16[22,16,128]{2,1,0:T(8,128)(2,1)S(1)}, u32[]{:S(2)}, u32[]{:S(2)}) collective-permute-start(bf16[22,16,128]{2,1,0:T(8,128)(2,1)S(1)} %get-tuple-element.68), channel_id=1, source_target_pairs={{0,1},{2,6},{1,0},{3,7},{4,5},{6,2},{5,4},{7,3},{8,9},{10,14},{9,8... | collective-permute-start | bytes 270344 | tf_op jit(solution)/shard_map/ppermute | solution.py:373
  19.5 2.5 %backward.1 = (f32[96,256]{1,0:T(8,128)S(1)}, f32[96,64]{1,0:T(8,128)S(1)}, f32[96,128]{1,0:T(8,128)S(1)}, bf16[96,128]{1,0:T(8,128)(2,1)S(1)}) custom-call(s32[1]{0:T(128)} %bitcast.core_ref, s32[27,256]{1,0:T(8,128)S(1)} %bitcast.16, f32[96,256]{1,0:T(8,128)S(1)} %get-tuple-element.53.refs_3_.hgrad_ref, bf16[96,256]{1,0:T(8,128)(2,1)S(1)} %get-tuple-element.64.grad_ref, ...), custom_call_target="tpu_custom_call" | custom-call | flops 2000000000 | bytes 10000000 | tf_op jit(solution)/shard_map/backward/pallas_call | solution.py:374
  22.0 0.0 collective-permute-done.4
  22.0 1.7 %collective-permute-done.5 = bf16[22,16,128]{2,1,0:T(8,128)(2,1)S(1)} collective-permute-done((bf16[22,16,128]{2,1,0:T(8,128)(2,1)S(1)}, bf16[22,16,128]{2,1,0:T(8,128)(2,1)S(1)}, u32[]{:S(2)}, u32[]{:S(2)}) %collective-permute-start.5) | collective-permute-done | bytes 90144 | tf_op jit(solution)/shard_map/ppermute | solution.py:373
  23.7 0.0 collective-permute-done.6
  23.7 0.1 add_convert_fusion.1
  23.8 4.3 %collective-permute-start.11 = (bf16[22,16,128]{2,1,0:T(8,128)(2,1)S(1)}, bf16[22,16,128]{2,1,0:T(8,128)(2,1)S(1)}, u32[]{:S(2)}, u32[]{:S(2)}) collective-permute-start(bf16[22,16,128]{2,1,0:T(8,128)(2,1)S(1)} %add_convert_fusion.1), channel_id=1, source_target_pairs={{0,24},{8,16},{16,8},{24,0},{1,25},{9,17},{17,9},{25,1},{2,26},{10... | collective-permute-start | bytes 270344 | tf_op jit(solution)/shard_map/ppermute | solution.py:405
  28.1 0.6 %collective-permute-start.9 = (bf16[22,16,128]{2,1,0:T(8,128)(2,1)S(1)}, bf16[22,16,128]{2,1,0:T(8,128)(2,1)S(1)}, u32[]{:S(2)}, u32[]{:S(2)}) collective-permute-start(bf16[22,16,128]{2,1,0:T(8,128)(2,1)S(1)} %add_convert_fusion.1), channel_id=1, source_target_pairs={{0,8},{8,0},{16,24},{24,16},{1,9},{9,1},{17,25},{25,17},{2,10},{10... | collective-permute-start | bytes 270344 | tf_op jit(solution)/shard_map/ppermute | solution.py:405
  28.7 0.7 %collective-permute-start.7 = (bf16[96,128]{1,0:T(8,128)(2,1)S(1)}, bf16[96,128]{1,0:T(8,128)(2,1)S(1)}, u32[]{:S(2)}, u32[]{:S(2)}) collective-permute-start(bf16[96,128]{1,0:T(8,128)(2,1)S(1)} %get-tuple-element.71), channel_id=1, source_target_pairs={{2,4},{6,8},{10,12},{14,16},{18,20},{22,24},{26,28},{4,2},{8,6},{1... | collective-permute-start | bytes 73736 | tf_op jit(solution)/shard_map/ppermute | solution.py:406
  29.4 0.0 copy-start.7
  29.4 1.1 %collective-permute-start.8 = (bf16[96,128]{1,0:T(8,128)(2,1)S(1)}, bf16[96,128]{1,0:T(8,128)(2,1)S(1)}, u32[]{:S(2)}, u32[]{:S(2)}) collective-permute-start(bf16[96,128]{1,0:T(8,128)(2,1)S(1)} %get-tuple-element.72), channel_id=1, source_target_pairs={{0,1},{1,0},{2,3},{3,2},{4,5},{5,4},{6,7},{7,6},{8,9},{9,8},{10,11... | collective-permute-start | bytes 73736 | tf_op jit(solution)/shard_map/ppermute | solution.py:419
  30.5 1.1 %collective-permute-done.11 = bf16[22,16,128]{2,1,0:T(8,128)(2,1)S(1)} collective-permute-done((bf16[22,16,128]{2,1,0:T(8,128)(2,1)S(1)}, bf16[22,16,128]{2,1,0:T(8,128)(2,1)S(1)}, u32[]{:S(2)}, u32[]{:S(2)}) %collective-permute-start.11) | collective-permute-done | bytes 90144 | tf_op jit(solution)/shard_map/ppermute | solution.py:405
  31.6 3.5 %collective-permute-done.10 = bf16[22,16,128]{2,1,0:T(8,128)(2,1)S(1)} collective-permute-done((bf16[22,16,128]{2,1,0:T(8,128)(2,1)S(1)}, bf16[22,16,128]{2,1,0:T(8,128)(2,1)S(1)}, u32[]{:S(2)}, u32[]{:S(2)}) %collective-permute-start.10) | collective-permute-done | bytes 90144 | tf_op jit(solution)/shard_map/ppermute | solution.py:405
  35.1 0.0 collective-permute-done.9
  35.1 0.1 add_convert_fusion.refs_0_
  35.2 2.0 %collective-permute-start.14 = (bf16[22,16,128]{2,1,0:T(8,128)(2,1)S(1)}, bf16[22,16,128]{2,1,0:T(8,128)(2,1)S(1)}, u32[]{:S(2)}, u32[]{:S(2)}) collective-permute-start(bf16[22,16,128]{2,1,0:T(8,128)(2,1)S(1)} %add_convert_fusion.refs_0_), channel_id=1, source_target_pairs={{0,5},{2,7},{1,4},{3,6},{4,1},{6,3},{5,0},{7,2},{8,13},{10,15},{9,... | collective-permute-start | bytes 270344 | tf_op jit(solution)/shard_map/ppermute | solution.py:430
  37.2 0.9 %collective-permute-start.13 = (bf16[22,16,128]{2,1,0:T(8,128)(2,1)S(1)}, bf16[22,16,128]{2,1,0:T(8,128)(2,1)S(1)}, u32[]{:S(2)}, u32[]{:S(2)}) collective-permute-start(bf16[22,16,128]{2,1,0:T(8,128)(2,1)S(1)} %add_convert_fusion.refs_0_), channel_id=1, source_target_pairs={{0,4},{2,3},{1,5},{3,2},{4,0},{6,7},{5,1},{7,6},{8,12},{10,11},{9,... | collective-permute-start | bytes 270344 | tf_op jit(solution)/shard_map/ppermute | solution.py:430
  38.1 0.7 %collective-permute-start.12 = (bf16[22,16,128]{2,1,0:T(8,128)(2,1)S(1)}, bf16[22,16,128]{2,1,0:T(8,128)(2,1)S(1)}, u32[]{:S(2)}, u32[]{:S(2)}) collective-permute-start(bf16[22,16,128]{2,1,0:T(8,128)(2,1)S(1)} %add_convert_fusion.refs_0_), channel_id=1, source_target_pairs={{0,1},{2,6},{1,0},{3,7},{4,5},{6,2},{5,4},{7,3},{8,9},{10,14},{9,8... | collective-permute-start | bytes 270344 | tf_op jit(solution)/shard_map/ppermute | solution.py:430
  38.7 1.1 %coarse.1 = bf16[64,128]{1,0:T(8,128)(2,1)} custom-call(bf16[8,64,256]{2,1,0:T(8,128)(2,1)S(1)} %get-tuple-element.56.refs_2_.pick_ref, bf16[96,256]{1,0:T(8,128)(2,1)S(1)} %get-tuple-element.73.hidden_ref, bf16[768,128]{1,0:T(8,128)(2,1)S(1)} %copy-done.7), custom_call_target="tpu_custom_call" | custom-call | flops 2000000000 | bytes 10000000 | tf_op jit(solution)/shard_map/coarse/pallas_call | solution.py:395
  39.9 0.1 slab_turn.1
  39.9 0.8 %collective-permute-done.14.refs_3_ = bf16[22,16,128]{2,1,0:T(8,128)(2,1)S(1)} collective-permute-done((bf16[22,16,128]{2,1,0:T(8,128)(2,1)S(1)}, bf16[22,16,128]{2,1,0:T(8,128)(2,1)S(1)}, u32[]{:S(2)}, u32[]{:S(2)}) %collective-permute-start.14) | collective-permute-done | bytes 90144 | tf_op jit(solution)/shard_map/ppermute | solution.py:430
  40.7 1.8 %collective-permute-done.13.refs_2_ = bf16[22,16,128]{2,1,0:T(8,128)(2,1)S(1)} collective-permute-done((bf16[22,16,128]{2,1,0:T(8,128)(2,1)S(1)}, bf16[22,16,128]{2,1,0:T(8,128)(2,1)S(1)}, u32[]{:S(2)}, u32[]{:S(2)}) %collective-permute-start.13) | collective-permute-done | bytes 90144 | tf_op jit(solution)/shard_map/ppermute | solution.py:430
  42.5 0.1 collective-permute-done.12.refs_1_
  42.7 0.1 collective-permute-start.15
  42.7 1.7 %collective-permute-done.15.other_ref = bf16[94,16,128]{2,1,0:T(8,128)(2,1)S(1)} collective-permute-done((bf16[94,16,128]{2,1,0:T(8,128)(2,1)S(1)}, bf16[94,16,128]{2,1,0:T(8,128)(2,1)S(1)}, u32[]{:S(2)}, u32[]{:S(2)}) %collective-permute-start.15) | collective-permute-done | bytes 385056 | tf_op jit(solution)/shard_map/ppermute | solution.py:438
  44.4 1.2 %final.1 = (f32[96,2592]{1,0:T(8,128)}, f32[768,128]{1,0:T(8,128)}, f32[96,256]{1,0:T(8,128)}) custom-call(s32[1]{0:T(128)} %bitcast.core_ref, bf16[94,16,128]{2,1,0:T(8,128)(2,1)S(1)} %join.1.mine_ref, bf16[94,16,128]{2,1,0:T(8,128)(2,1)S(1)} %collective-permute-done.15.other_ref, f32[96,256]{1,0:T(8,128)S(1)} %get-tuple-element.83.refs_0_, ...), custom_call_target="tpu_custom_call" | custom-call | tf_op jit(solution)/shard_map/final/pallas_call | solution.py:439
  (17 shorter events, 0.1 us)
Async XLA Ops:
  0.6 5.6 %collective-permute-start = (bf16[96,256]{1,0:T(8,128)(2,1)}, bf16[96,256]{1,0:T(8,128)(2,1)S(1)}, u32[]{:S(2)}, u32[]{:S(2)}) collective-permute-start(bf16[96,256]{1,0:T(8,128)(2,1)} %bitcast.10), channel_id=1, source_target_pairs={{0,1},{1,0},{2,3},{3,2},{4,5},{5,4},{6,7},{7,6},{8,9},{9,8},{10,11... | collective-permute-start | bytes 147464 | tf_op jit(solution)/shard_map/ppermute | solution.py:309
  3.7 0.8 %copy-start.1 = (bf16[256,96]{0,1:T(8,128)(2,1)S(1)}, bf16[256,96]{0,1:T(8,128)(2,1)}, u32[]{:S(2)}) copy-start(bf16[256,96]{0,1:T(8,128)(2,1)} %param.6) | copy-start | bytes 147460
  4.5 0.8 %copy-start.3 = (s32[256,27]{0,1:T(8,128)S(1)}, s32[256,27]{0,1:T(8,128)}, u32[]{:S(2)}) copy-start(s32[256,27]{0,1:T(8,128)} %param.7) | copy-start | bytes 82948
  5.3 1.8 %copy-start.6 = (bf16[768,128]{1,0:T(8,128)(2,1)S(1)}, bf16[768,128]{1,0:T(8,128)(2,1)}, u32[]{:S(2)}) copy-start(bf16[768,128]{1,0:T(8,128)(2,1)} %wd_ref.3) | copy-start | bytes 589828
  6.3 0.8 %copy-start.5 = (bf16[64,128]{1,0:T(8,128)(2,1)S(1)}, bf16[64,128]{1,0:T(8,128)(2,1)}, u32[]{:S(2)}) copy-start(bf16[64,128]{1,0:T(8,128)(2,1)} %cgrad_ref.3) | copy-start | bytes 49156
  6.3 0.8 %copy-start.8 = (s32[64,8]{0,1:T(8,128)S(1)}, s32[64,8]{0,1:T(8,128)}, u32[]{:S(2)}) copy-start(s32[64,8]{0,1:T(8,128)} %param.8) | copy-start | bytes 6148
  6.4 4.5 %collective-permute-start.2 = (bf16[96,128]{1,0:T(8,128)(2,1)S(1)}, bf16[96,128]{1,0:T(8,128)(2,1)S(1)}, u32[]{:S(2)}, u32[]{:S(2)}) collective-permute-start(bf16[96,128]{1,0:T(8,128)(2,1)S(1)} %pad_maximum_fusion), channel_id=1, source_target_pairs={{2,4},{6,8},{10,12},{14,16},{18,20},{22,24},{26,28},{4,2},{8,6},{1... | collective-permute-start | bytes 73736 | tf_op jit(solution)/shard_map/ppermute | solution.py:324
  7.1 4.7 %copy-start = (bf16[2592,96]{0,1:T(8,128)(2,1)S(1)}, bf16[2592,96]{0,1:T(8,128)(2,1)}, u32[]{:S(2)}) copy-start(bf16[2592,96]{0,1:T(8,128)(2,1)} %param.9) | copy-start | bytes 1492996
  7.1 4.7 %copy-start.2 = (bf16[256,96]{0,1:T(8,128)(2,1)S(1)}, bf16[256,96]{0,1:T(8,128)(2,1)}, u32[]{:S(2)}) copy-start(bf16[256,96]{0,1:T(8,128)(2,1)} %param.6) | copy-start | bytes 147460
  7.1 4.7 %copy-start.4 = (s32[256,27]{0,1:T(8,128)S(1)}, s32[256,27]{0,1:T(8,128)}, u32[]{:S(2)}) copy-start(s32[256,27]{0,1:T(8,128)} %param.7) | copy-start | bytes 82948
  7.8 3.9 %collective-permute-start.1 = (bf16[96,128]{1,0:T(8,128)(2,1)S(1)}, bf16[96,128]{1,0:T(8,128)(2,1)S(1)}, u32[]{:S(2)}, u32[]{:S(2)}) collective-permute-start(bf16[96,128]{1,0:T(8,128)(2,1)S(1)} %pad_maximum_fusion), channel_id=1, source_target_pairs={{0,2},{2,0},{4,6},{6,4},{8,10},{10,8},{12,14},{14,12},{16,18},{18,... | collective-permute-start | bytes 73736 | tf_op jit(solution)/shard_map/ppermute | solution.py:337
  14.0 1.8 %collective-permute-start.3 = (bf16[88,16,128]{2,1,0:T(8,128)(2,1)S(1)}, bf16[88,16,128]{2,1,0:T(8,128)(2,1)S(1)}, u32[]{:S(2)}, u32[]{:S(2)}) collective-permute-start(bf16[88,16,128]{2,1,0:T(8,128)(2,1)S(1)} %get-tuple-element.59), channel_id=1, source_target_pairs={{0,2},{2,0},{1,3},{3,1},{4,6},{6,4},{5,7},{7,5},{8,10},{10,8},{9,1... | collective-permute-start | bytes 1081352 | tf_op jit(solution)/shard_map/ppermute | solution.py:361
  15.9 6.1 %collective-permute-start.4 = (bf16[22,16,128]{2,1,0:T(8,128)(2,1)S(1)}, bf16[22,16,128]{2,1,0:T(8,128)(2,1)S(1)}, u32[]{:S(2)}, u32[]{:S(2)}) collective-permute-start(bf16[22,16,128]{2,1,0:T(8,128)(2,1)S(1)} %get-tuple-element.66), channel_id=1, source_target_pairs={{0,5},{2,7},{1,4},{3,6},{4,1},{6,3},{5,0},{7,2},{8,13},{10,15},{9,... | collective-permute-start | bytes 270344 | tf_op jit(solution)/shard_map/ppermute | solution.py:373
  18.6 5.2 %collective-permute-start.5 = (bf16[22,16,128]{2,1,0:T(8,128)(2,1)S(1)}, bf16[22,16,128]{2,1,0:T(8,128)(2,1)S(1)}, u32[]{:S(2)}, u32[]{:S(2)}) collective-permute-start(bf16[22,16,128]{2,1,0:T(8,128)(2,1)S(1)} %get-tuple-element.67), channel_id=1, source_target_pairs={{0,4},{2,3},{1,5},{3,2},{4,0},{6,7},{5,1},{7,6},{8,12},{10,11},{9,... | collective-permute-start | bytes 270344 | tf_op jit(solution)/shard_map/ppermute | solution.py:373
  18.9 4.8 %collective-permute-start.6 = (bf16[22,16,128]{2,1,0:T(8,128)(2,1)S(1)}, bf16[22,16,128]{2,1,0:T(8,128)(2,1)S(1)}, u32[]{:S(2)}, u32[]{:S(2)}) collective-permute-start(bf16[22,16,128]{2,1,0:T(8,128)(2,1)S(1)} %get-tuple-element.68), channel_id=1, source_target_pairs={{0,1},{2,6},{1,0},{3,7},{4,5},{6,2},{5,4},{7,3},{8,9},{10,14},{9,8... | collective-permute-start | bytes 270344 | tf_op jit(solution)/shard_map/ppermute | solution.py:373
  23.8 7.8 %collective-permute-start.11 = (bf16[22,16,128]{2,1,0:T(8,128)(2,1)S(1)}, bf16[22,16,128]{2,1,0:T(8,128)(2,1)S(1)}, u32[]{:S(2)}, u32[]{:S(2)}) collective-permute-start(bf16[22,16,128]{2,1,0:T(8,128)(2,1)S(1)} %add_convert_fusion.1), channel_id=1, source_target_pairs={{0,24},{8,16},{16,8},{24,0},{1,25},{9,17},{17,9},{25,1},{2,26},{10... | collective-permute-start | bytes 270344 | tf_op jit(solution)/shard_map/ppermute | solution.py:405
  28.1 7.0 %collective-permute-start.10 = (bf16[22,16,128]{2,1,0:T(8,128)(2,1)S(1)}, bf16[22,16,128]{2,1,0:T(8,128)(2,1)S(1)}, u32[]{:S(2)}, u32[]{:S(2)}) collective-permute-start(bf16[22,16,128]{2,1,0:T(8,128)(2,1)S(1)} %add_convert_fusion.1), channel_id=1, source_target_pairs={{0,16},{8,24},{16,0},{24,8},{1,17},{9,25},{17,1},{25,9},{2,18},{10... | collective-permute-start | bytes 270344 | tf_op jit(solution)/shard_map/ppermute | solution.py:405
  28.1 7.0 %collective-permute-start.9 = (bf16[22,16,128]{2,1,0:T(8,128)(2,1)S(1)}, bf16[22,16,128]{2,1,0:T(8,128)(2,1)S(1)}, u32[]{:S(2)}, u32[]{:S(2)}) collective-permute-start(bf16[22,16,128]{2,1,0:T(8,128)(2,1)S(1)} %add_convert_fusion.1), channel_id=1, source_target_pairs={{0,8},{8,0},{16,24},{24,16},{1,9},{9,1},{17,25},{25,17},{2,10},{10... | collective-permute-start | bytes 270344 | tf_op jit(solution)/shard_map/ppermute | solution.py:405
  28.7 0.7 %collective-permute-start.7 = (bf16[96,128]{1,0:T(8,128)(2,1)S(1)}, bf16[96,128]{1,0:T(8,128)(2,1)S(1)}, u32[]{:S(2)}, u32[]{:S(2)}) collective-permute-start(bf16[96,128]{1,0:T(8,128)(2,1)S(1)} %get-tuple-element.71), channel_id=1, source_target_pairs={{2,4},{6,8},{10,12},{14,16},{18,20},{22,24},{26,28},{4,2},{8,6},{1... | collective-permute-start | bytes 73736 | tf_op jit(solution)/shard_map/ppermute | solution.py:406
  29.4 9.3 %copy-start.7 = (bf16[768,128]{1,0:T(8,128)(2,1)S(1)}, bf16[768,128]{1,0:T(8,128)(2,1)}, u32[]{:S(2)}) copy-start(bf16[768,128]{1,0:T(8,128)(2,1)} %wd_ref.3) | copy-start | bytes 589828
  29.4 10.4 %collective-permute-start.8 = (bf16[96,128]{1,0:T(8,128)(2,1)S(1)}, bf16[96,128]{1,0:T(8,128)(2,1)S(1)}, u32[]{:S(2)}, u32[]{:S(2)}) collective-permute-start(bf16[96,128]{1,0:T(8,128)(2,1)S(1)} %get-tuple-element.72), channel_id=1, source_target_pairs={{0,1},{1,0},{2,3},{3,2},{4,5},{5,4},{6,7},{7,6},{8,9},{9,8},{10,11... | collective-permute-start | bytes 73736 | tf_op jit(solution)/shard_map/ppermute | solution.py:419
  35.2 5.6 %collective-permute-start.14 = (bf16[22,16,128]{2,1,0:T(8,128)(2,1)S(1)}, bf16[22,16,128]{2,1,0:T(8,128)(2,1)S(1)}, u32[]{:S(2)}, u32[]{:S(2)}) collective-permute-start(bf16[22,16,128]{2,1,0:T(8,128)(2,1)S(1)} %add_convert_fusion.refs_0_), channel_id=1, source_target_pairs={{0,5},{2,7},{1,4},{3,6},{4,1},{6,3},{5,0},{7,2},{8,13},{10,15},{9,... | collective-permute-start | bytes 270344 | tf_op jit(solution)/shard_map/ppermute | solution.py:430
  37.2 5.3 %collective-permute-start.13 = (bf16[22,16,128]{2,1,0:T(8,128)(2,1)S(1)}, bf16[22,16,128]{2,1,0:T(8,128)(2,1)S(1)}, u32[]{:S(2)}, u32[]{:S(2)}) collective-permute-start(bf16[22,16,128]{2,1,0:T(8,128)(2,1)S(1)} %add_convert_fusion.refs_0_), channel_id=1, source_target_pairs={{0,4},{2,3},{1,5},{3,2},{4,0},{6,7},{5,1},{7,6},{8,12},{10,11},{9,... | collective-permute-start | bytes 270344 | tf_op jit(solution)/shard_map/ppermute | solution.py:430
  38.1 4.6 %collective-permute-start.12 = (bf16[22,16,128]{2,1,0:T(8,128)(2,1)S(1)}, bf16[22,16,128]{2,1,0:T(8,128)(2,1)S(1)}, u32[]{:S(2)}, u32[]{:S(2)}) collective-permute-start(bf16[22,16,128]{2,1,0:T(8,128)(2,1)S(1)} %add_convert_fusion.refs_0_), channel_id=1, source_target_pairs={{0,1},{2,6},{1,0},{3,7},{4,5},{6,2},{5,4},{7,3},{8,9},{10,14},{9,8... | collective-permute-start | bytes 270344 | tf_op jit(solution)/shard_map/ppermute | solution.py:430
  42.7 1.8 %collective-permute-start.15 = (bf16[94,16,128]{2,1,0:T(8,128)(2,1)S(1)}, bf16[94,16,128]{2,1,0:T(8,128)(2,1)S(1)}, u32[]{:S(2)}, u32[]{:S(2)}) collective-permute-start(bf16[94,16,128]{2,1,0:T(8,128)(2,1)S(1)} %join.1.mine_ref), channel_id=1, source_target_pairs={{0,2},{2,0},{1,3},{3,1},{4,6},{6,4},{5,7},{7,5},{8,10},{10,8},{9,1... | collective-permute-start | bytes 1155080 | tf_op jit(solution)/shard_map/ppermute | solution.py:438

commit v14 on v13

--- a/solution.py
+++ b/solution.py
@@ -400,14 +400,22 @@
         name="coarse",
     )(pick, hidden, w_down)
     total = functools.reduce(lambda x, y: x + y.astype(F32), got, keep).astype(BF16)
+    late, coarse = lax.optimization_barrier((total, coarse))
     parts = [total]
     for step in range(1, sizes["far"]):
-        parts.append(lax.ppermute(total, "far", [(i, i ^ step) for i in range(sizes["far"])]))
+        sent = late if step == 1 else total
+        parts.append(lax.ppermute(sent, "far", [(i, i ^ step) for i in range(sizes["far"])]))
     cross = lax.ppermute(cross, RING, crossings)
     parts = [x.astype(F32) for x in parts]
-    while len(parts) > 1:
-        parts = [x + y for x, y in zip(parts[0::2], parts[1::2])]
-    total = parts[0].astype(BF16)
+    blocks, start = [], 2
+    while start < len(parts):
+        block = parts[start : 2 * start]
+        while len(block) > 1:
+            block = [x + y for x, y in zip(block[0::2], block[1::2])]
+        blocks += block
+        start *= 2
+    blocks, cross = lax.optimization_barrier((blocks, cross))
+    total = sum(parts[1:2] + blocks, parts[0]).astype(BF16)
     home, *edges = pl.pallas_call(
         functools.partial(cross_turn_kernel, 0 if slabs == 2 else 1),
         out_shape=[jax.ShapeDtypeStruct((channels, RIM), F32)]
@@ -417,7 +425,6 @@
     )(stay, cross)
     back = beside if slabs == 2 else beside[::-1]
     edges = [lax.ppermute(x, "slab", p) for x, p in zip(edges, back)]
-    edges, coarse = lax.optimization_barrier((edges, coarse))
     mate, home = pl.pallas_call(
         slab_turn_kernel,
         out_shape=(

time: 46 us -> 48.7 us (1.059)
  starting transfers between devices: 21.1 us -> 23 us
  waiting for transfers between devices: 12.9 us -> 13.6 us
    ppermute x1, waiting for transfers between devices: 0.01 us -> 2.95 us  [on_device(): edges = [lax.ppermute(x, 'slab', p) for x, p in zip(edges, back)]]
    ppermute x3, waiting for transfers between devices: 2.69 us -> 0.01 us  [on_device(): got = [lax.ppermute(total, SPLIT, route) for route in routes[::-1]]]
    ppermute x3, starting transfers between devices: 4.92 us -> 6.42 us  [on_device(): lax.ppermute(sent, 'far', [(i, i ^ step) for i in range(sizes['far'])])]
    ppermute x1, starting transfers between devices: 1.06 us -> 1.55 us  [on_device(): edges = [lax.ppermute(x, 'slab', p) for x, p in zip(edges, back)]]
  transfers between devices with their start and end apart: 16 -> 16, of which waited for: 9 -> 7; matrix products, arithmetic and copies ran while one was open for 0% -> 0% of each run, Pallas kernels for 12% -> 11%
where the time goes in v14:
time: 48.7 us; the launch traced here: 48.4 us
  starting transfers between devices  23 us (47%)
  waiting for transfers between devices  13.6 us (28%)
  Pallas kernels  9.02 us (19%)
  local copies, waits for them, and re-layouts  1.64 us (3%)
  between operations  0.85 us (2%)
    ppermute x3, starting transfers between devices, on_device(): lax.ppermute(sent, 'far', [(i, i ^ step) for i in range(sizes['far'])])  6.42 us
    ppermute x3, waiting for transfers between devices, on_device(): lax.ppermute(sent, 'far', [(i, i ^ step) for i in range(sizes['far'])])  5.05 us
    ppermute x3, starting transfers between devices, on_device(): got = [lax.ppermute(x, SPLIT, route) for x, route in zip(sent, routes)]  3.57 us
    ppermute x3, starting transfers between devices, on_device(): got = [lax.ppermute(total, SPLIT, route) for route in routes[::-1]]  3.55 us
    ppermute x1, starting transfers between devices, on_device(): mate = lax.ppermute(row, RING, mates)  3.08 us
    ppermute x1, starting transfers between devices, on_device(): side = [lax.ppermute(features_t, 'slab', pairs) for pairs in beside]  3.03 us
    ppermute x1, waiting for transfers between devices, on_device(): edges = [lax.ppermute(x, 'slab', p) for x, p in zip(edges, back)]  2.95 us
    pallas_call x1, Pallas kernels, on_device(): pl.pallas_call(functools.partial(backward_kernel, slabs), out_shape=(jax....  2.53 us
  transfers between devices with their start and end apart: 16, of which 7 were waited for; matrix products, arithmetic and copies ran while one was open for 0% of the time, Pallas kernels for 11%

profile of v14, /device:TPU:0, one launch (start us, length us, event | category | flops | bytes accessed | tf_op | source)
XLA Modules:
  0.0 48.4 jit_solution(8837634823986306581)
XLA Ops:
  0.6 3.0 %collective-permute-start = (bf16[96,256]{1,0:T(8,128)(2,1)}, bf16[96,256]{1,0:T(8,128)(2,1)S(1)}, u32[]{:S(2)}, u32[]{:S(2)}) collective-permute-start(bf16[96,256]{1,0:T(8,128)(2,1)} %bitcast.10), channel_id=1, source_target_pairs={{0,1},{1,0},{2,3},{3,2},{4,5},{5,4},{6,7},{7,6},{8,9},{9,8},{10,11... | collective-permute-start | bytes 147464 | tf_op jit(solution)/shard_map/ppermute | solution.py:309
  3.7 0.8 %copy-done.1 = bf16[256,96]{0,1:T(8,128)(2,1)S(1)} copy-done((bf16[256,96]{0,1:T(8,128)(2,1)S(1)}, bf16[256,96]{0,1:T(8,128)(2,1)}, u32[]{:S(2)}) %copy-start.1) | copy-done | bytes 49176
  4.5 0.8 %copy-done.3 = s32[256,27]{0,1:T(8,128)S(1)} copy-done((s32[256,27]{0,1:T(8,128)S(1)}, s32[256,27]{0,1:T(8,128)}, u32[]{:S(2)}) %copy-start.3) | copy-done | bytes 27672
  5.3 1.0 %gather.1 = (bf16[2592,128]{1,0:T(8,128)(2,1)S(1)}, bf16[2592,128]{1,0:T(8,128)(2,1)S(1)}) custom-call(bf16[96,256]{1,0:T(8,128)(2,1)S(1)} %bitcast.11, s32[27,256]{1,0:T(8,128)S(1)} %bitcast.14), custom_call_target="tpu_custom_call" | custom-call | flops 2000000000 | bytes 10000000 | tf_op jit(solution)/shard_map/gather/pallas_call | solution.py:310
  6.2 0.0 collective-permute-done
  6.3 0.0 copy-start.5
  6.3 0.0 copy-start.8
  6.3 0.1 pad_maximum_fusion
  6.4 0.7 %collective-permute-start.2 = (bf16[96,128]{1,0:T(8,128)(2,1)S(1)}, bf16[96,128]{1,0:T(8,128)(2,1)S(1)}, u32[]{:S(2)}, u32[]{:S(2)}) collective-permute-start(bf16[96,128]{1,0:T(8,128)(2,1)S(1)} %pad_maximum_fusion), channel_id=1, source_target_pairs={{2,4},{6,8},{10,12},{14,16},{18,20},{22,24},{26,28},{4,2},{8,6},{1... | collective-permute-start | bytes 73736 | tf_op jit(solution)/shard_map/ppermute | solution.py:324
  7.1 0.0 copy-start
  7.1 0.0 copy-start.2
  7.1 0.0 copy-start.4
  7.1 0.7 %taps.1 = (bf16[8,64,256]{2,1,0:T(8,128)(2,1)S(1)}, f32[96,256]{1,0:T(8,128)S(1)}) custom-call(s32[8,64]{1,0:T(8,128)S(1)} %bitcast.17, bf16[64,128]{1,0:T(8,128)(2,1)S(1)} %copy-done.5, bf16[768,128]{1,0:T(8,128)(2,1)S(1)} %copy-done.6), custom_call_target="tpu_custom_call" | custom-call | flops 2000000000 | bytes 10000000 | tf_op jit(solution)/shard_map/taps/pallas_call | solution.py:326
  7.8 3.1 %collective-permute-start.1 = (bf16[96,128]{1,0:T(8,128)(2,1)S(1)}, bf16[96,128]{1,0:T(8,128)(2,1)S(1)}, u32[]{:S(2)}, u32[]{:S(2)}) collective-permute-start(bf16[96,128]{1,0:T(8,128)(2,1)S(1)} %pad_maximum_fusion), channel_id=1, source_target_pairs={{0,2},{2,0},{4,6},{6,4},{8,10},{10,8},{12,14},{14,12},{16,18},{18,... | collective-permute-start | bytes 73736 | tf_op jit(solution)/shard_map/ppermute | solution.py:337
  10.9 0.0 collective-permute-done.2.refs_5_
  10.9 0.8 %collective-permute-done.1.refs_4_ = bf16[96,128]{1,0:T(8,128)(2,1)S(1)} collective-permute-done((bf16[96,128]{1,0:T(8,128)(2,1)S(1)}, bf16[96,128]{1,0:T(8,128)(2,1)S(1)}, u32[]{:S(2)}, u32[]{:S(2)}) %collective-permute-start.1) | collective-permute-done | bytes 24608 | tf_op jit(solution)/shard_map/ppermute | solution.py:337
  11.8 2.3 %forward.1 = (bf16[96,256]{1,0:T(8,128)(2,1)S(1)}, bf16[96,256]{1,0:T(8,128)(2,1)S(1)}, f32[88,16,128]{2,1,0:T(8,128)S(1)}, bf16[88,16,128]{2,1,0:T(8,128)(2,1)S(1)}) custom-call(s32[1]{0:T(128)} %bitcast.core_ref, bf16[96,256]{1,0:T(8,128)(2,1)S(1)} %bitcast.13, s32[27,256]{1,0:T(8,128)S(1)} %bitcast.15, bf16[64,128]{1,0:T(8,128)(2,1)S(1)} %copy-done.5, ...), custom_call_target="tpu_custom_call" | custom-call | tf_op jit(solution)/shard_map/forward/pallas_call | solution.py:343
  14.0 0.5 collective-permute-start.3
  14.5 1.3 %collective-permute-done.3.got_ref = bf16[88,16,128]{2,1,0:T(8,128)(2,1)S(1)} collective-permute-done((bf16[88,16,128]{2,1,0:T(8,128)(2,1)S(1)}, bf16[88,16,128]{2,1,0:T(8,128)(2,1)S(1)}, u32[]{:S(2)}, u32[]{:S(2)}) %collective-permute-start.3) | collective-permute-done | bytes 360480 | tf_op jit(solution)/shard_map/ppermute | solution.py:361
  15.8 0.1 split.1
  15.9 2.7 %collective-permute-start.4 = (bf16[22,16,128]{2,1,0:T(8,128)(2,1)S(1)}, bf16[22,16,128]{2,1,0:T(8,128)(2,1)S(1)}, u32[]{:S(2)}, u32[]{:S(2)}) collective-permute-start(bf16[22,16,128]{2,1,0:T(8,128)(2,1)S(1)} %get-tuple-element.67), channel_id=1, source_target_pairs={{0,5},{2,7},{1,4},{3,6},{4,1},{6,3},{5,0},{7,2},{8,13},{10,15},{9,... | collective-permute-start | bytes 270344 | tf_op jit(solution)/shard_map/ppermute | solution.py:373
  18.6 0.4 collective-permute-start.5
  18.9 0.5 %collective-permute-start.6 = (bf16[22,16,128]{2,1,0:T(8,128)(2,1)S(1)}, bf16[22,16,128]{2,1,0:T(8,128)(2,1)S(1)}, u32[]{:S(2)}, u32[]{:S(2)}) collective-permute-start(bf16[22,16,128]{2,1,0:T(8,128)(2,1)S(1)} %get-tuple-element.69), channel_id=1, source_target_pairs={{0,1},{2,6},{1,0},{3,7},{4,5},{6,2},{5,4},{7,3},{8,9},{10,14},{9,8... | collective-permute-start | bytes 270344 | tf_op jit(solution)/shard_map/ppermute | solution.py:373
  19.5 2.5 %backward.1 = (f32[96,256]{1,0:T(8,128)S(1)}, f32[96,64]{1,0:T(8,128)S(1)}, f32[96,128]{1,0:T(8,128)S(1)}, bf16[96,128]{1,0:T(8,128)(2,1)S(1)}) custom-call(s32[1]{0:T(128)} %bitcast.core_ref, s32[27,256]{1,0:T(8,128)S(1)} %bitcast.16, f32[96,256]{1,0:T(8,128)S(1)} %get-tuple-element.58.refs_3_.hgrad_ref, bf16[96,256]{1,0:T(8,128)(2,1)S(1)} %get-tuple-element.70.grad_ref, ...), custom_call_target="tpu_custom_call" | custom-call | flops 2000000000 | bytes 10000000 | tf_op jit(solution)/shard_map/backward/pallas_call | solution.py:374
  22.0 0.0 collective-permute-done.4
  22.0 1.7 %collective-permute-done.5 = bf16[22,16,128]{2,1,0:T(8,128)(2,1)S(1)} collective-permute-done((bf16[22,16,128]{2,1,0:T(8,128)(2,1)S(1)}, bf16[22,16,128]{2,1,0:T(8,128)(2,1)S(1)}, u32[]{:S(2)}, u32[]{:S(2)}) %collective-permute-start.5) | collective-permute-done | bytes 90144 | tf_op jit(solution)/shard_map/ppermute | solution.py:373
  23.7 0.0 collective-permute-done.6
  23.7 0.1 add_convert_fusion.1
  23.8 4.3 %collective-permute-start.9 = (bf16[22,16,128]{2,1,0:T(8,128)(2,1)S(1)}, bf16[22,16,128]{2,1,0:T(8,128)(2,1)S(1)}, u32[]{:S(2)}, u32[]{:S(2)}) collective-permute-start(bf16[22,16,128]{2,1,0:T(8,128)(2,1)S(1)} %add_convert_fusion.1), channel_id=1, source_target_pairs={{0,24},{8,16},{16,8},{24,0},{1,25},{9,17},{17,9},{25,1},{2,26},{10... | collective-permute-start | bytes 270344 | tf_op jit(solution)/shard_map/ppermute | solution.py:407
  28.1 0.0 collective-permute-start.8
  28.1 1.1 %coarse.1 = bf16[64,128]{1,0:T(8,128)(2,1)} custom-call(bf16[8,64,256]{2,1,0:T(8,128)(2,1)S(1)} %get-tuple-element.57.refs_2_.pick_ref, bf16[96,256]{1,0:T(8,128)(2,1)S(1)} %get-tuple-element.76.hidden_ref, bf16[768,128]{1,0:T(8,128)(2,1)S(1)} %copy-done.7), custom_call_target="tpu_custom_call" | custom-call | flops 2000000000 | bytes 10000000 | tf_op jit(solution)/shard_map/coarse/pallas_call | solution.py:395
  29.2 0.7 %collective-permute-start.10 = (bf16[96,128]{1,0:T(8,128)(2,1)S(1)}, bf16[96,128]{1,0:T(8,128)(2,1)S(1)}, u32[]{:S(2)}, u32[]{:S(2)}) collective-permute-start(bf16[96,128]{1,0:T(8,128)(2,1)S(1)} %get-tuple-element.79), channel_id=1, source_target_pairs={{2,4},{6,8},{10,12},{14,16},{18,20},{22,24},{26,28},{4,2},{8,6},{1... | collective-permute-start | bytes 73736 | tf_op jit(solution)/shard_map/ppermute | solution.py:408
  29.9 2.1 %collective-permute-start.7 = (bf16[22,16,128]{2,1,0:T(8,128)(2,1)S(1)}, bf16[22,16,128]{2,1,0:T(8,128)(2,1)S(1)}, u32[]{:S(2)}, u32[]{:S(2)}) collective-permute-start(bf16[22,16,128]{2,1,0:T(8,128)(2,1)S(1)} %add_convert_fusion.1), channel_id=1, source_target_pairs={{0,8},{8,0},{16,24},{24,16},{1,9},{9,1},{17,25},{25,17},{2,10},{10... | collective-permute-start | bytes 270344 | tf_op jit(solution)/shard_map/ppermute | solution.py:407
  32.0 0.0 collective-permute-done.9
  32.0 3.2 %collective-permute-done.8 = bf16[22,16,128]{2,1,0:T(8,128)(2,1)S(1)} collective-permute-done((bf16[22,16,128]{2,1,0:T(8,128)(2,1)S(1)}, bf16[22,16,128]{2,1,0:T(8,128)(2,1)S(1)}, u32[]{:S(2)}, u32[]{:S(2)}) %collective-permute-start.8) | collective-permute-done | bytes 90144 | tf_op jit(solution)/shard_map/ppermute | solution.py:407
  35.2 0.0 collective-permute-done.10.got_ref
  35.3 1.9 %collective-permute-done.7 = bf16[22,16,128]{2,1,0:T(8,128)(2,1)S(1)} collective-permute-done((bf16[22,16,128]{2,1,0:T(8,128)(2,1)S(1)}, bf16[22,16,128]{2,1,0:T(8,128)(2,1)S(1)}, u32[]{:S(2)}, u32[]{:S(2)}) %collective-permute-start.7) | collective-permute-done | bytes 90144 | tf_op jit(solution)/shard_map/ppermute | solution.py:407
  37.1 1.7 %collective-permute-start.13 = (bf16[22,16,128]{2,1,0:T(8,128)(2,1)S(1)}, bf16[22,16,128]{2,1,0:T(8,128)(2,1)S(1)}, u32[]{:S(2)}, u32[]{:S(2)}) collective-permute-start(bf16[22,16,128]{2,1,0:T(8,128)(2,1)S(1)} %add_convert_fusion.refs_0_), channel_id=1, source_target_pairs={{0,5},{2,7},{1,4},{3,6},{4,1},{6,3},{5,0},{7,2},{8,13},{10,15},{9,... | collective-permute-start | bytes 270344 | tf_op jit(solution)/shard_map/ppermute | solution.py:437
  38.8 1.4 %collective-permute-start.12 = (bf16[22,16,128]{2,1,0:T(8,128)(2,1)S(1)}, bf16[22,16,128]{2,1,0:T(8,128)(2,1)S(1)}, u32[]{:S(2)}, u32[]{:S(2)}) collective-permute-start(bf16[22,16,128]{2,1,0:T(8,128)(2,1)S(1)} %add_convert_fusion.refs_0_), channel_id=1, source_target_pairs={{0,4},{2,3},{1,5},{3,2},{4,0},{6,7},{5,1},{7,6},{8,12},{10,11},{9,... | collective-permute-start | bytes 270344 | tf_op jit(solution)/shard_map/ppermute | solution.py:437
  40.2 0.5 %collective-permute-start.11 = (bf16[22,16,128]{2,1,0:T(8,128)(2,1)S(1)}, bf16[22,16,128]{2,1,0:T(8,128)(2,1)S(1)}, u32[]{:S(2)}, u32[]{:S(2)}) collective-permute-start(bf16[22,16,128]{2,1,0:T(8,128)(2,1)S(1)} %add_convert_fusion.refs_0_), channel_id=1, source_target_pairs={{0,1},{2,6},{1,0},{3,7},{4,5},{6,2},{5,4},{7,3},{8,9},{10,14},{9,8... | collective-permute-start | bytes 270344 | tf_op jit(solution)/shard_map/ppermute | solution.py:437
  40.7 1.5 %collective-permute-start.14 = (bf16[96,128]{1,0:T(8,128)(2,1)S(1)}, bf16[96,128]{1,0:T(8,128)(2,1)S(1)}, u32[]{:S(2)}, u32[]{:S(2)}) collective-permute-start(bf16[96,128]{1,0:T(8,128)(2,1)S(1)} %get-tuple-element.85), channel_id=1, source_target_pairs={{0,1},{1,0},{2,3},{3,2},{4,5},{5,4},{6,7},{7,6},{8,9},{9,8},{10,11... | collective-permute-start | bytes 73736 | tf_op jit(solution)/shard_map/ppermute | solution.py:427
  42.3 2.9 %collective-permute-done.14.refs_0_ = bf16[96,128]{1,0:T(8,128)(2,1)S(1)} collective-permute-done((bf16[96,128]{1,0:T(8,128)(2,1)S(1)}, bf16[96,128]{1,0:T(8,128)(2,1)S(1)}, u32[]{:S(2)}, u32[]{:S(2)}) %collective-permute-start.14) | collective-permute-done | bytes 24608 | tf_op jit(solution)/shard_map/ppermute | solution.py:427
  45.2 0.1 slab_turn.1
  45.3 0.0 collective-permute-done.13.refs_3_
  45.3 0.0 collective-permute-done.12.refs_2_
  45.4 0.1 collective-permute-start.15
  45.4 1.7 %collective-permute-done.15.other_ref = bf16[94,16,128]{2,1,0:T(8,128)(2,1)S(1)} collective-permute-done((bf16[94,16,128]{2,1,0:T(8,128)(2,1)S(1)}, bf16[94,16,128]{2,1,0:T(8,128)(2,1)S(1)}, u32[]{:S(2)}, u32[]{:S(2)}) %collective-permute-start.15) | collective-permute-done | bytes 385056 | tf_op jit(solution)/shard_map/ppermute | solution.py:445
  47.1 1.2 %final.1 = (f32[96,2592]{1,0:T(8,128)}, f32[768,128]{1,0:T(8,128)}, f32[96,256]{1,0:T(8,128)}) custom-call(s32[1]{0:T(128)} %bitcast.core_ref, bf16[94,16,128]{2,1,0:T(8,128)(2,1)S(1)} %join.1.mine_ref, bf16[94,16,128]{2,1,0:T(8,128)(2,1)S(1)} %collective-permute-done.15.other_ref, f32[96,256]{1,0:T(8,128)S(1)} %get-tuple-element.87.refs_0_, ...), custom_call_target="tpu_custom_call" | custom-call | tf_op jit(solution)/shard_map/final/pallas_call | solution.py:446
  (18 shorter events, 0.1 us)
Async XLA Ops:
  0.6 5.6 %collective-permute-start = (bf16[96,256]{1,0:T(8,128)(2,1)}, bf16[96,256]{1,0:T(8,128)(2,1)S(1)}, u32[]{:S(2)}, u32[]{:S(2)}) collective-permute-start(bf16[96,256]{1,0:T(8,128)(2,1)} %bitcast.10), channel_id=1, source_target_pairs={{0,1},{1,0},{2,3},{3,2},{4,5},{5,4},{6,7},{7,6},{8,9},{9,8},{10,11... | collective-permute-start | bytes 147464 | tf_op jit(solution)/shard_map/ppermute | solution.py:309
  3.7 0.8 %copy-start.1 = (bf16[256,96]{0,1:T(8,128)(2,1)S(1)}, bf16[256,96]{0,1:T(8,128)(2,1)}, u32[]{:S(2)}) copy-start(bf16[256,96]{0,1:T(8,128)(2,1)} %param.6) | copy-start | bytes 147460
  4.5 0.8 %copy-start.3 = (s32[256,27]{0,1:T(8,128)S(1)}, s32[256,27]{0,1:T(8,128)}, u32[]{:S(2)}) copy-start(s32[256,27]{0,1:T(8,128)} %param.7) | copy-start | bytes 82948
  5.3 1.8 %copy-start.6 = (bf16[768,128]{1,0:T(8,128)(2,1)S(1)}, bf16[768,128]{1,0:T(8,128)(2,1)}, u32[]{:S(2)}) copy-start(bf16[768,128]{1,0:T(8,128)(2,1)} %wd_ref.3) | copy-start | bytes 589828
  6.3 0.8 %copy-start.5 = (bf16[64,128]{1,0:T(8,128)(2,1)S(1)}, bf16[64,128]{1,0:T(8,128)(2,1)}, u32[]{:S(2)}) copy-start(bf16[64,128]{1,0:T(8,128)(2,1)} %cgrad_ref.3) | copy-start | bytes 49156
  6.3 0.8 %copy-start.8 = (s32[64,8]{0,1:T(8,128)S(1)}, s32[64,8]{0,1:T(8,128)}, u32[]{:S(2)}) copy-start(s32[64,8]{0,1:T(8,128)} %param.8) | copy-start | bytes 6148
  6.4 4.5 %collective-permute-start.2 = (bf16[96,128]{1,0:T(8,128)(2,1)S(1)}, bf16[96,128]{1,0:T(8,128)(2,1)S(1)}, u32[]{:S(2)}, u32[]{:S(2)}) collective-permute-start(bf16[96,128]{1,0:T(8,128)(2,1)S(1)} %pad_maximum_fusion), channel_id=1, source_target_pairs={{2,4},{6,8},{10,12},{14,16},{18,20},{22,24},{26,28},{4,2},{8,6},{1... | collective-permute-start | bytes 73736 | tf_op jit(solution)/shard_map/ppermute | solution.py:324
  7.1 4.7 %copy-start = (bf16[2592,96]{0,1:T(8,128)(2,1)S(1)}, bf16[2592,96]{0,1:T(8,128)(2,1)}, u32[]{:S(2)}) copy-start(bf16[2592,96]{0,1:T(8,128)(2,1)} %param.9) | copy-start | bytes 1492996
  7.1 4.7 %copy-start.2 = (bf16[256,96]{0,1:T(8,128)(2,1)S(1)}, bf16[256,96]{0,1:T(8,128)(2,1)}, u32[]{:S(2)}) copy-start(bf16[256,96]{0,1:T(8,128)(2,1)} %param.6) | copy-start | bytes 147460
  7.1 4.7 %copy-start.4 = (s32[256,27]{0,1:T(8,128)S(1)}, s32[256,27]{0,1:T(8,128)}, u32[]{:S(2)}) copy-start(s32[256,27]{0,1:T(8,128)} %param.7) | copy-start | bytes 82948
  7.8 3.9 %collective-permute-start.1 = (bf16[96,128]{1,0:T(8,128)(2,1)S(1)}, bf16[96,128]{1,0:T(8,128)(2,1)S(1)}, u32[]{:S(2)}, u32[]{:S(2)}) collective-permute-start(bf16[96,128]{1,0:T(8,128)(2,1)S(1)} %pad_maximum_fusion), channel_id=1, source_target_pairs={{0,2},{2,0},{4,6},{6,4},{8,10},{10,8},{12,14},{14,12},{16,18},{18,... | collective-permute-start | bytes 73736 | tf_op jit(solution)/shard_map/ppermute | solution.py:337
  14.0 1.8 %collective-permute-start.3 = (bf16[88,16,128]{2,1,0:T(8,128)(2,1)S(1)}, bf16[88,16,128]{2,1,0:T(8,128)(2,1)S(1)}, u32[]{:S(2)}, u32[]{:S(2)}) collective-permute-start(bf16[88,16,128]{2,1,0:T(8,128)(2,1)S(1)} %get-tuple-element.61), channel_id=1, source_target_pairs={{0,2},{2,0},{1,3},{3,1},{4,6},{6,4},{5,7},{7,5},{8,10},{10,8},{9,1... | collective-permute-start | bytes 1081352 | tf_op jit(solution)/shard_map/ppermute | solution.py:361
  15.9 6.1 %collective-permute-start.4 = (bf16[22,16,128]{2,1,0:T(8,128)(2,1)S(1)}, bf16[22,16,128]{2,1,0:T(8,128)(2,1)S(1)}, u32[]{:S(2)}, u32[]{:S(2)}) collective-permute-start(bf16[22,16,128]{2,1,0:T(8,128)(2,1)S(1)} %get-tuple-element.67), channel_id=1, source_target_pairs={{0,5},{2,7},{1,4},{3,6},{4,1},{6,3},{5,0},{7,2},{8,13},{10,15},{9,... | collective-permute-start | bytes 270344 | tf_op jit(solution)/shard_map/ppermute | solution.py:373
  18.6 5.2 %collective-permute-start.5 = (bf16[22,16,128]{2,1,0:T(8,128)(2,1)S(1)}, bf16[22,16,128]{2,1,0:T(8,128)(2,1)S(1)}, u32[]{:S(2)}, u32[]{:S(2)}) collective-permute-start(bf16[22,16,128]{2,1,0:T(8,128)(2,1)S(1)} %get-tuple-element.68), channel_id=1, source_target_pairs={{0,4},{2,3},{1,5},{3,2},{4,0},{6,7},{5,1},{7,6},{8,12},{10,11},{9,... | collective-permute-start | bytes 270344 | tf_op jit(solution)/shard_map/ppermute | solution.py:373
  18.9 4.8 %collective-permute-start.6 = (bf16[22,16,128]{2,1,0:T(8,128)(2,1)S(1)}, bf16[22,16,128]{2,1,0:T(8,128)(2,1)S(1)}, u32[]{:S(2)}, u32[]{:S(2)}) collective-permute-start(bf16[22,16,128]{2,1,0:T(8,128)(2,1)S(1)} %get-tuple-element.69), channel_id=1, source_target_pairs={{0,1},{2,6},{1,0},{3,7},{4,5},{6,2},{5,4},{7,3},{8,9},{10,14},{9,8... | collective-permute-start | bytes 270344 | tf_op jit(solution)/shard_map/ppermute | solution.py:373
  23.7 4.3 %copy-start.7 = (bf16[768,128]{1,0:T(8,128)(2,1)S(1)}, bf16[768,128]{1,0:T(8,128)(2,1)}, u32[]{:S(2)}) copy-start(bf16[768,128]{1,0:T(8,128)(2,1)} %wd_ref.3) | copy-start | bytes 589828
  23.8 8.2 %collective-permute-start.9 = (bf16[22,16,128]{2,1,0:T(8,128)(2,1)S(1)}, bf16[22,16,128]{2,1,0:T(8,128)(2,1)S(1)}, u32[]{:S(2)}, u32[]{:S(2)}) collective-permute-start(bf16[22,16,128]{2,1,0:T(8,128)(2,1)S(1)} %add_convert_fusion.1), channel_id=1, source_target_pairs={{0,24},{8,16},{16,8},{24,0},{1,25},{9,17},{17,9},{25,1},{2,26},{10... | collective-permute-start | bytes 270344 | tf_op jit(solution)/shard_map/ppermute | solution.py:407
  28.1 7.1 %collective-permute-start.8 = (bf16[22,16,128]{2,1,0:T(8,128)(2,1)S(1)}, bf16[22,16,128]{2,1,0:T(8,128)(2,1)S(1)}, u32[]{:S(2)}, u32[]{:S(2)}) collective-permute-start(bf16[22,16,128]{2,1,0:T(8,128)(2,1)S(1)} %add_convert_fusion.1), channel_id=1, source_target_pairs={{0,16},{8,24},{16,0},{24,8},{1,17},{9,25},{17,1},{25,9},{2,18},{10... | collective-permute-start | bytes 270344 | tf_op jit(solution)/shard_map/ppermute | solution.py:407
  29.2 6.0 %collective-permute-start.10 = (bf16[96,128]{1,0:T(8,128)(2,1)S(1)}, bf16[96,128]{1,0:T(8,128)(2,1)S(1)}, u32[]{:S(2)}, u32[]{:S(2)}) collective-permute-start(bf16[96,128]{1,0:T(8,128)(2,1)S(1)} %get-tuple-element.79), channel_id=1, source_target_pairs={{2,4},{6,8},{10,12},{14,16},{18,20},{22,24},{26,28},{4,2},{8,6},{1... | collective-permute-start | bytes 73736 | tf_op jit(solution)/shard_map/ppermute | solution.py:408
  29.9 7.2 %collective-permute-start.7 = (bf16[22,16,128]{2,1,0:T(8,128)(2,1)S(1)}, bf16[22,16,128]{2,1,0:T(8,128)(2,1)S(1)}, u32[]{:S(2)}, u32[]{:S(2)}) collective-permute-start(bf16[22,16,128]{2,1,0:T(8,128)(2,1)S(1)} %add_convert_fusion.1), channel_id=1, source_target_pairs={{0,8},{8,0},{16,24},{24,16},{1,9},{9,1},{17,25},{25,17},{2,10},{10... | collective-permute-start | bytes 270344 | tf_op jit(solution)/shard_map/ppermute | solution.py:407
  37.1 8.1 %collective-permute-start.13 = (bf16[22,16,128]{2,1,0:T(8,128)(2,1)S(1)}, bf16[22,16,128]{2,1,0:T(8,128)(2,1)S(1)}, u32[]{:S(2)}, u32[]{:S(2)}) collective-permute-start(bf16[22,16,128]{2,1,0:T(8,128)(2,1)S(1)} %add_convert_fusion.refs_0_), channel_id=1, source_target_pairs={{0,5},{2,7},{1,4},{3,6},{4,1},{6,3},{5,0},{7,2},{8,13},{10,15},{9,... | collective-permute-start | bytes 270344 | tf_op jit(solution)/shard_map/ppermute | solution.py:437
  38.8 6.5 %collective-permute-start.12 = (bf16[22,16,128]{2,1,0:T(8,128)(2,1)S(1)}, bf16[22,16,128]{2,1,0:T(8,128)(2,1)S(1)}, u32[]{:S(2)}, u32[]{:S(2)}) collective-permute-start(bf16[22,16,128]{2,1,0:T(8,128)(2,1)S(1)} %add_convert_fusion.refs_0_), channel_id=1, source_target_pairs={{0,4},{2,3},{1,5},{3,2},{4,0},{6,7},{5,1},{7,6},{8,12},{10,11},{9,... | collective-permute-start | bytes 270344 | tf_op jit(solution)/shard_map/ppermute | solution.py:437
  40.2 5.1 %collective-permute-start.11 = (bf16[22,16,128]{2,1,0:T(8,128)(2,1)S(1)}, bf16[22,16,128]{2,1,0:T(8,128)(2,1)S(1)}, u32[]{:S(2)}, u32[]{:S(2)}) collective-permute-start(bf16[22,16,128]{2,1,0:T(8,128)(2,1)S(1)} %add_convert_fusion.refs_0_), channel_id=1, source_target_pairs={{0,1},{2,6},{1,0},{3,7},{4,5},{6,2},{5,4},{7,3},{8,9},{10,14},{9,8... | collective-permute-start | bytes 270344 | tf_op jit(solution)/shard_map/ppermute | solution.py:437
  40.7 4.5 %collective-permute-start.14 = (bf16[96,128]{1,0:T(8,128)(2,1)S(1)}, bf16[96,128]{1,0:T(8,128)(2,1)S(1)}, u32[]{:S(2)}, u32[]{:S(2)}) collective-permute-start(bf16[96,128]{1,0:T(8,128)(2,1)S(1)} %get-tuple-element.85), channel_id=1, source_target_pairs={{0,1},{1,0},{2,3},{3,2},{4,5},{5,4},{6,7},{7,6},{8,9},{9,8},{10,11... | collective-permute-start | bytes 73736 | tf_op jit(solution)/shard_map/ppermute | solution.py:427
  45.4 1.8 %collective-permute-start.15 = (bf16[94,16,128]{2,1,0:T(8,128)(2,1)S(1)}, bf16[94,16,128]{2,1,0:T(8,128)(2,1)S(1)}, u32[]{:S(2)}, u32[]{:S(2)}) collective-permute-start(bf16[94,16,128]{2,1,0:T(8,128)(2,1)S(1)} %join.1.mine_ref), channel_id=1, source_target_pairs={{0,2},{2,0},{1,3},{3,1},{4,6},{6,4},{5,7},{7,5},{8,10},{10,8},{9,1... | collective-permute-start | bytes 1155080 | tf_op jit(solution)/shard_map/ppermute | solution.py:445
